TPU v7x, 512 devices: a whole 4x4x16 slice. The times are simulated.
512 devices in a mesh: grp: 16 (over y_hi, x, core), seq: 32 (over y_lo, z).
Axes of the slice: x: 4, y: 4 (y_hi: 2, y_lo: 2; y = y_hi * 2 + y_lo), z: 16, core: 2. Of those that a mesh axis runs over, the one named last changes fastest.
Arguments:
- inputs: bfloat16 [16, 4096, 1024], P('grp', 'seq'), may hold values from -6 to 6
- q_heads: bfloat16 [16, 4096, 512], P('grp', 'seq'), may hold values from -5.2 to 5.2
- k_heads: bfloat16 [16, 4096, 512], P('grp', 'seq'), may hold values from -5.2 to 5.2
- v_heads: bfloat16 [16, 4096, 512], P('grp', 'seq'), may hold values from -6 to 6
- w_out: bfloat16 [512, 1024], replicated, may hold values from -0.25 to 0.25
- group_lens: int32 [16, 8], P('grp'), may hold values from 1 to 1024, 4096 in all within a row
- query_emb: bfloat16 [8192, 1024], P(('grp', 'seq')), may hold values from -6 to 6
- positive: int32 [8192], P(('grp', 'seq')), may hold values from 0 to 127
Outputs:
- mean_loss: float32 [], replicated
- grad_inputs: bfloat16 [16, 4096, 1024], P('grp', 'seq')
- grad_q: bfloat16 [16, 4096, 512], P('grp', 'seq')
- grad_k: bfloat16 [16, 4096, 512], P('grp', 'seq')
- grad_v: bfloat16 [16, 4096, 512], P('grp', 'seq')
- grad_w_out: float32 [512, 1024], replicated
All inputs are finite; a program needn't handle non-finite values.
Results may differ from a plain program's by a relative error of at most 0.02.
Values may be sent and summed in bfloat16 or wider, within the bound.
No kernel may reach another device: no remote copies, remote signals or barrier semaphores. Data moves between devices by JAX's collectives and lax.ppermute only.
A program may use at most 64 MiB of HBM per device.

v0:
```python
import jax
import jax.numpy as jnp
from jax import lax
from jax.sharding import PartitionSpec as P

HEAD_COUNT = 8
HEAD_DIM = 64


RECIPROCAL_TEMP = 20.0
GRADIENT_FACTOR = 64.0
NORM_EPS = 1e-06
NEG_LARGE = -1e30
EXACT_MATMUL = lax.Precision.HIGHEST


def group_member(positions, lengths):
    group_ends = jnp.cumsum(lengths)
    starts = group_ends - lengths
    inside = (positions[:, None] >= starts[None, :]) & (positions[:, None] < group_ends[None, :])
    return inside.astype(jnp.float32)


def group_number(positions, lengths):
    group_ends = jnp.cumsum(lengths)
    passed = (positions[:, None] >= group_ends[None, :]).astype(jnp.int32)
    return jnp.minimum(jnp.sum(passed, axis=1), lengths.shape[0] - 1)


def head_scores(query_rows, key_rows):
    queries = query_rows.reshape(query_rows.shape[0], HEAD_COUNT, HEAD_DIM)
    keys = key_rows.reshape(key_rows.shape[0], HEAD_COUNT, HEAD_DIM)
    return jnp.einsum(
        "ihd,jhd->hij", queries, keys, preferred_element_type=jnp.float32
    ) * HEAD_DIM ** (-0.5)


def blockwise(step, carry, pieces, dims, start):
    extent = pieces[0].shape[dims[0]]
    block_rows = 512

    def advance(state, index):
        offset = index * block_rows
        parts = tuple(
            (
                lax.dynamic_slice_in_dim(piece, offset, block_rows, dim)
                for piece, dim in zip(pieces, dims)
            )
        )
        return (step(state, parts, start + offset), None)

    carry, unused = lax.scan(advance, carry, jnp.arange(extent // block_rows, dtype=jnp.int32))
    return carry


def body(inputs, q_heads, k_heads, v_heads, w_out, group_lens, query_emb, positive):
    tok_rows = q_heads.shape[1]
    my_first = lax.axis_index("seq") * tok_rows
    doc_index = lax.axis_index("grp")
    lengths = group_lens[0]
    group_count = lengths.shape[0]
    length_f32 = lengths.astype(jnp.float32)
    local_positions = my_first + jnp.arange(tok_rows, dtype=jnp.int32)
    local_member = group_member(local_positions, lengths)
    local_group = group_number(local_positions, lengths)
    member_bf16 = local_member.astype(jnp.bfloat16)
    queries = q_heads[0]
    keys_local = k_heads[0]
    values_local = v_heads[0]
    score_scale = HEAD_DIM ** (-0.5)

    def stats_step(state, parts, start):
        row_max, row_sum = state
        scores = head_scores(queries, parts[0])
        new_max = jnp.maximum(row_max, jnp.max(scores, axis=2))
        row_sum = row_sum * jnp.exp(row_max - new_max) + jnp.sum(
            jnp.exp(scores - new_max[:, :, None]), axis=2
        )
        return (new_max, row_sum)

    stats_init = (
        jnp.full((HEAD_COUNT, tok_rows), NEG_LARGE, jnp.float32),
        jnp.zeros((HEAD_COUNT, tok_rows), jnp.float32),
    )
    keys_all = lax.all_gather(keys_local, "seq", axis=0, tiled=True)
    row_max, row_sum = blockwise(stats_step, stats_init, (keys_all,), (0,), 0)
    log_total = row_max + jnp.log(row_sum)

    def value_step(state, parts, start):
        count_rows = parts[0].shape[0]
        key_rows = lax.dynamic_slice_in_dim(keys_all, start, count_rows, 0)
        prob_bf16 = jnp.exp(head_scores(queries, key_rows) - log_total[:, :, None]).astype(
            jnp.bfloat16
        )
        values = parts[0].reshape(count_rows, HEAD_COUNT, HEAD_DIM)
        return state + jnp.einsum(
            "hij,jhd->ihd", prob_bf16, values, preferred_element_type=jnp.float32
        )

    attn_sum = blockwise(
        value_step,
        jnp.zeros((tok_rows, HEAD_COUNT, HEAD_DIM), jnp.float32),
        (lax.all_gather(values_local, "seq", axis=0, tiled=True),),
        (0,),
        jnp.int32(0),
    )
    attention = attn_sum.reshape(tok_rows, HEAD_COUNT * HEAD_DIM).astype(jnp.bfloat16)
    mean_inputs = (
        jnp.dot(member_bf16.T, inputs[0], preferred_element_type=jnp.float32) / length_f32[:, None]
    )
    mean_attn = (
        jnp.dot(member_bf16.T, attention, preferred_element_type=jnp.float32) / length_f32[:, None]
    )
    doc_inputs, doc_attn = lax.psum((mean_inputs, mean_attn), "seq")
    doc_pooled = doc_inputs + jnp.dot(
        doc_attn, w_out, precision=EXACT_MATMUL, preferred_element_type=jnp.float32
    )
    pooled = lax.all_gather(doc_pooled, "grp", axis=0, tiled=True)
    row_norms = jnp.sqrt(jnp.sum(pooled * pooled, axis=1) + NORM_EPS)
    group_embedding = pooled / row_norms[:, None]
    query_f32 = query_emb.astype(jnp.float32)
    query_normalized = (
        query_f32 / jnp.sqrt(jnp.sum(query_f32 * query_f32, axis=1) + NORM_EPS)[:, None]
    )
    similarity_logits = RECIPROCAL_TEMP * jnp.dot(
        query_normalized, group_embedding.T, precision=EXACT_MATMUL
    )
    exp_logits = jnp.exp(similarity_logits)
    totals = jnp.sum(exp_logits, axis=1)
    target = (
        jnp.arange(similarity_logits.shape[1], dtype=jnp.int32)[None, :] == positive[:, None]
    ).astype(jnp.float32)
    losses = jnp.log(totals) - jnp.sum(target * similarity_logits, axis=1)
    softmax_weight = exp_logits / totals[:, None] - target
    embedding_gradient = (
        GRADIENT_FACTOR
        * RECIPROCAL_TEMP
        * jnp.dot(softmax_weight.T, query_normalized, precision=EXACT_MATMUL)
    )
    embedding_gradient, loss_total = lax.psum((embedding_gradient, jnp.sum(losses)), ("grp", "seq"))
    query_count = positive.shape[0] * lax.axis_size("grp") * lax.axis_size("seq")
    mean_loss = loss_total / query_count
    pooled_grad = (
        embedding_gradient
        - group_embedding * jnp.sum(group_embedding * embedding_gradient, axis=1)[:, None]
    ) / row_norms[:, None]
    doc_grad = lax.dynamic_slice_in_dim(pooled_grad, doc_index * group_count, group_count, 0)
    weight_term = jnp.dot(doc_attn.T, doc_grad, precision=EXACT_MATMUL)
    grad_w_out = lax.psum(weight_term, "grp")
    group_grad = doc_grad / length_f32[:, None]
    grad_inputs = jnp.dot(local_member, group_grad, precision=EXACT_MATMUL).astype(jnp.bfloat16)
    group_dattn = jnp.einsum(
        "cd,kd->ck", group_grad, w_out, precision=EXACT_MATMUL, preferred_element_type=jnp.float32
    ).astype(jnp.bfloat16)
    token_dattn = jnp.dot(member_bf16, group_dattn, preferred_element_type=jnp.float32)
    delta = jnp.sum(
        (token_dattn * attention.astype(jnp.float32)).reshape(tok_rows, HEAD_COUNT, HEAD_DIM),
        axis=2,
    )
    dattn_heads = group_dattn.reshape(group_count, HEAD_COUNT, HEAD_DIM)
    value_terms = jnp.einsum(
        "chd,jhd->chj",
        dattn_heads,
        values_local.reshape(tok_rows, HEAD_COUNT, HEAD_DIM),
        preferred_element_type=jnp.float32,
    ).reshape(group_count * HEAD_COUNT, tok_rows)
    local_terms = value_terms.reshape(group_count, HEAD_COUNT, tok_rows)
    stats_all = (
        lax.all_gather(log_total.T, "seq", axis=0, tiled=True),
        lax.all_gather(delta, "seq", axis=0, tiled=True),
    )

    def query_step(state, parts, start):
        key_grad, prob_mass = state
        query_piece = parts[0]
        row_count = query_piece.shape[0]
        remote_total = lax.dynamic_slice_in_dim(stats_all[0], start, row_count, 0)
        remote_delta = lax.dynamic_slice_in_dim(stats_all[1], start, row_count, 0)
        remote_positions = start + jnp.arange(row_count, dtype=jnp.int32)
        remote_member = group_member(remote_positions, lengths)
        remote_group = group_number(remote_positions, lengths)
        prob_f32 = jnp.exp(head_scores(query_piece, keys_local) - remote_total.T[:, :, None])
        prob_bf16 = prob_f32.astype(jnp.bfloat16)
        prob_mass = prob_mass + jnp.einsum(
            "ic,hij->chj",
            remote_member.astype(jnp.bfloat16),
            prob_bf16,
            preferred_element_type=jnp.float32,
        )
        prob_grad = jnp.take(local_terms, remote_group, axis=0).transpose(1, 0, 2)
        score_grad = (prob_f32 * (prob_grad - remote_delta.T[:, :, None])).astype(jnp.bfloat16)
        key_grad = key_grad + jnp.einsum(
            "hij,ihd->jhd",
            score_grad,
            query_piece.reshape(row_count, HEAD_COUNT, HEAD_DIM),
            preferred_element_type=jnp.float32,
        )
        return (key_grad, prob_mass)

    query_init = (
        jnp.zeros((tok_rows, HEAD_COUNT, HEAD_DIM), jnp.float32),
        jnp.zeros((group_count, HEAD_COUNT, tok_rows), jnp.float32),
    )
    key_grad, prob_mass = blockwise(
        query_step,
        query_init,
        (lax.all_gather(queries, "seq", axis=0, tiled=True),),
        (0,),
        jnp.int32(0),
    )
    grad_k = (key_grad * score_scale).reshape(tok_rows, HEAD_COUNT * HEAD_DIM).astype(jnp.bfloat16)
    grad_v = (
        jnp.einsum(
            "chj,chd->jhd", prob_mass, dattn_heads.astype(jnp.float32), precision=EXACT_MATMUL
        )
        .reshape(tok_rows, HEAD_COUNT * HEAD_DIM)
        .astype(jnp.bfloat16)
    )
    local_delta = delta.T

    def term_step(state, parts, start):
        term_piece = parts[0]
        col_count = term_piece.shape[1]
        key_rows = lax.dynamic_slice_in_dim(keys_all, start, col_count, 0)
        prob_f32 = jnp.exp(head_scores(queries, key_rows) - log_total[:, :, None])
        prob_grad = jnp.take(
            term_piece.reshape(group_count, HEAD_COUNT, col_count), local_group, axis=0
        ).transpose(1, 0, 2)
        score_grad = (prob_f32 * (prob_grad - local_delta[:, :, None])).astype(jnp.bfloat16)
        return state + jnp.einsum(
            "hij,jhd->ihd",
            score_grad,
            key_rows.reshape(col_count, HEAD_COUNT, HEAD_DIM),
            preferred_element_type=jnp.float32,
        )

    query_grad = blockwise(
        term_step,
        jnp.zeros((tok_rows, HEAD_COUNT, HEAD_DIM), jnp.float32),
        (lax.all_gather(value_terms, "seq", axis=1, tiled=True),),
        (1,),
        jnp.int32(0),
    )
    grad_q = (
        (query_grad * score_scale).reshape(tok_rows, HEAD_COUNT * HEAD_DIM).astype(jnp.bfloat16)
    )
    return (mean_loss, grad_inputs[None], grad_q[None], grad_k[None], grad_v[None], grad_w_out)


def solution(mesh):
    return jax.shard_map(
        body,
        mesh=mesh,
        in_specs=(
            P("grp", "seq", None),
            P("grp", "seq", None),
            P("grp", "seq", None),
            P("grp", "seq", None),
            P(),
            P("grp", None),
            P(("grp", "seq"), None),
            P(("grp", "seq")),
        ),
        out_specs=(
            P(),
            P("grp", "seq", None),
            P("grp", "seq", None),
            P("grp", "seq", None),
            P("grp", "seq", None),
            P(),
        ),
        check_vma=False,
    )
```

profile of v0, /device:TPU:1, one launch (start us, length us, event | category | flops | bytes accessed | tf_op | source)
XLA Modules:
  0.0 1370.8 jit_solution(14375397415587914440)
XLA Ops:
  16.5 121.3 %all-gather.12.cloned.1.call-done = bf16[1,4096,512]{1,2,0:T(8,128)(2,1)} async-done(((bf16[1,128,512]{1,2,0:T(8,128)(2,1)}), bf16[1,4096,512]{1,2,0:T(8,128)(2,1)}) %all-gather.12.cloned.1.call-update) | async-done | bytes 4194320 | tf_op jit(solution)/shard_map/all_gather | solution.py:85
  137.8 26.1 %while.50 = (s32[]{:T(128)}, f32[8,128]{1,0:T(8,128)S(1)}, f32[8,128]{1,0:T(8,128)S(1)}, s32[8]{0:T(128)S(1)}, bf16[4096,512]{0,1:T(8,128)(2,1)}, /*index=5*/bf1...) while((s32[]{:T(128)}, f32[8,128]{1,0:T(8,128)S(1)}, ...), condition=%wide.region_6.7_spmd.clone, body=%wide.region_3.0_spmd.clone.sunk | while | flops 69735432 | bytes 5951670 | solution.py:52
  163.9 114.8 %all-gather.10.cloned.1.call-done = bf16[1,4096,512]{1,2,0:T(8,128)(2,1)} async-done(((bf16[1,128,512]{1,2,0:T(8,128)(2,1)}), bf16[1,4096,512]{1,2,0:T(8,128)(2,1)}) %all-gather.10.cloned.1.call-update) | async-done | bytes 4194320 | tf_op jit(solution)/shard_map/all_gather | solution.py:103
  278.7 32.2 %while.51 = (s32[]{:T(128)}, f32[128,8,64]{0,2,1:T(8,128)}, s32[8]{0:T(128)S(1)}, bf16[4096,512]{0,1:T(8,128)(2,1)}, bf16[4096,512]{0,1:T(8,128)(2,1)}, /*index=...) while((s32[]{:T(128)}, f32[128,8,64]{0,2,1:T(8,128)}, ...), condition=%wide.region_8.9_spmd.clone, body=%wide.region_7.8_spmd.clone.sunk | while | flops 135921664 | bytes 5902581 | solution.py:52
  312.7 92.2 %all-reduce = (f32[8,1024]{1,0:T(8,128)S(1)}, f32[8,512]{1,0:T(8,128)S(1)}) all-reduce(f32[8,1024]{1,0:T(8,128)S(1)} %convolution_divide_fusion, f32[8,512]{1,0:T(8,128)S(1)} %convolution_divide_fusion.1), channel_id=1, replica_groups=mesh['grp'=16,'seq'=32] {'seq'}, use_global_device_ids=true, to_apply=%region_2.3 | all-reduce | flops 12288 | bytes 98304 | tf_op jit(solution)/shard_map/psum | solution.py:114
  406.0 75.8 %all_gather.23 = f32[128,1024]{1,0:T(8,128)S(1)} all-gather(f32[8,1024]{1,0:T(8,128)S(1)} %convolution_add_fusion.1), channel_id=1, replica_groups=mesh['grp'=16,'seq'=32] {'grp'}, dimensions={0}, use_global_device_ids=true | all-gather | bytes 557056 | tf_op jit(solution)/shard_map/all_gather | solution.py:118
  486.8 99.0 %psum.37 = f32[]{:T(128)} all-reduce(f32[]{:T(128)} %subtract_reduce_fusion), channel_id=1, replica_groups=mesh['grp'=16,'seq'=32] {'grp','seq'}, use_global_device_ids=true, to_apply=%region_14.15 | all-reduce | flops 1 | bytes 8 | tf_op jit(solution)/shard_map/psum | solution.py:140
  586.7 51.8 %all_gather.26 = f32[4096,8]{0,1:T(8,128)} all-gather(f32[128,8]{0,1:T(8,128)S(1)} %bitcast.231), channel_id=1, replica_groups=mesh['grp'=16,'seq'=32] {'seq'}, dimensions={0}, use_global_device_ids=true | all-gather | bytes 135168 | tf_op jit(solution)/shard_map/all_gather | solution.py:169
  638.5 290.1 %all-reduce.4.cloned.1.call-done = f32[128,1024]{1,0:T(8,128)} async-done(((f32[128,1024]{1,0:T(8,128)}), f32[128,1024]{1,0:T(8,128)}) %all-reduce.4.cloned.1.call-update) | async-done | bytes 524304 | tf_op jit(solution)/shard_map/psum | solution.py:140
  934.2 54.8 %all_gather.27 = f32[4096,8]{0,1:T(8,128)} all-gather(f32[128,8]{0,1:T(8,128)S(1)} %bitcast_reduce_fusion.1), channel_id=1, replica_groups=mesh['grp'=16,'seq'=32] {'seq'}, dimensions={0}, use_global_device_ids=true | all-gather | bytes 135168 | tf_op jit(solution)/shard_map/all_gather | solution.py:170
  989.3 60.4 %all-gather.14.cloned.1.call-done = bf16[1,4096,512]{1,2,0:T(8,128)(2,1)} async-done(((bf16[1,128,512]{1,2,0:T(8,128)(2,1)}), bf16[1,4096,512]{1,2,0:T(8,128)(2,1)}) %all-gather.14.cloned.1.call-update) | async-done | bytes 4194320 | tf_op jit(solution)/shard_map/all_gather | solution.py:207
  1050.3 125.5 %while.53 = (s32[]{:T(128)}, f32[128,8,64]{0,2,1:T(8,128)S(1)}, f32[8,8,128]{2,0,1:T(8,128)}, s32[8]{0:T(128)}, bf16[4096,512]{0,1:T(8,128)(2,1)}, /*index=5*/bf...) while((s32[]{:T(128)}, f32[128,8,64]{0,2,1:T(8,128)S(1)}, ...), condition=%wide.region_23.24_spmd.clone, body=%wide.region_21.23_spmd.clone.sunk | while | flops 147511808 | bytes 15969802 | solution.py:52
  1060.9 3.1 fusion.134
  1076.6 3.1 fusion.134
  1092.3 3.1 fusion.134
  1108.0 3.1 fusion.134
  1123.6 3.1 fusion.134
  1139.3 3.1 fusion.134
  1155.0 3.1 fusion.134
  1170.7 3.1 fusion.134
  1178.5 4.0 fusion.70
  1184.6 83.6 %while.52 = (s32[]{:T(128)}, f32[128,8,64]{0,2,1:T(8,128)}, s32[8]{0:T(128)S(1)}, bf16[4096,512]{0,1:T(8,128)(2,1)}, bf16[1,128,512]{1,2,0:T(8,128)(2,1)S(1)}, /...) while((s32[]{:T(128)}, f32[128,8,64]{0,2,1:T(8,128)}, ...), condition=%wide.region_20.21_spmd.clone, body=%wide.region_19.20_spmd.clone.sunk | while | flops 137496704 | bytes 12991441 | solution.py:52
  1191.4 3.6 fusion.126
  1201.9 3.6 fusion.126
  1212.3 3.6 fusion.126
  1222.7 3.6 fusion.126
  1233.2 3.7 fusion.126
  1243.7 3.6 fusion.126
  1254.1 3.6 fusion.126
  1264.6 3.6 fusion.126
  1269.9 89.8 %all-reduce.6.cloned.1.call-done = f32[512,1024]{1,0:T(8,128)} async-done(((f32[512,1024]{1,0:T(8,128)}), f32[512,1024]{1,0:T(8,128)}) %all-reduce.6.cloned.1.call-update) | async-done | bytes 2097168 | tf_op jit(solution)/shard_map/psum | solution.py:149
  1359.7 3.2 copy.117
  (492 shorter events, 221.4 us)
Async XLA Ops:
  7.2 398.3 %copy-start = (bf16[512,1024]{1,0:T(8,128)(2,1)S(1)}, bf16[512,1024]{1,0:T(8,128)(2,1)}, u32[]{:S(2)}) copy-start(bf16[512,1024]{1,0:T(8,128)(2,1)} %param.20) | copy-start | bytes 3145732
  7.2 130.6 %all-gather.12.cloned.1.call-start = ((), (), s32[]{:S(2)}) async-start(), calls=%async_computation.4 | async-start | bytes 4325376 | tf_op jit(solution)/shard_map/all_gather | solution.py:85
  9.0 269.7 %all-gather.10.cloned.1.call-start = ((), (), s32[]{:S(2)}) async-start(), calls=%async_computation.3 | async-start | bytes 4325376 | tf_op jit(solution)/shard_map/all_gather | solution.py:103
  10.7 917.9 %all-reduce.4.cloned.1.call-start = ((), (), s32[]{:S(2)}) async-start(), calls=%async_computation | async-start | bytes 1048576 | tf_op jit(solution)/shard_map/psum | solution.py:140
  13.4 916.6 %copy-start.26 = (f32[8]{0:T(128)}, f32[8]{0:T(128)S(1)}, u32[]{:S(2)}) copy-start(f32[8]{0:T(128)S(1)} %get-tuple-element.549) | copy-start | bytes 100
  13.4 919.7 %copy-start.28 = (s32[128]{0:T(128)}, s32[128]{0:T(128)S(1)}, u32[]{:S(2)}) copy-start(s32[128]{0:T(128)S(1)} %iota_add_fusion.1) | copy-start | bytes 1540
  310.9 172.0 %copy-start.2 = (bf16[1,128,512]{1,2,0:T(8,128)(2,1)}, bf16[1,128,512]{1,2,0:T(8,128)(2,1)S(1)}, u32[]{:S(2)}) copy-start(bf16[1,128,512]{1,2,0:T(8,128)(2,1)S(1)} %get-tuple-element.932) | copy-start | bytes 393220
  310.9 275.9 %copy-start.20 = (f32[8,128]{1,0:T(8,128)}, f32[8,128]{1,0:T(8,128)S(1)}, u32[]{:S(2)}) copy-start(f32[8,128]{1,0:T(8,128)S(1)} %get-tuple-element.946) | copy-start | bytes 12292
  310.9 171.2 %copy-start.13 = (bf16[16,1024]{1,0:T(8,128)(2,1)S(1)}, bf16[16,1024]{1,0:T(8,128)(2,1)}, u32[]{:S(2)}) copy-start(bf16[16,1024]{1,0:T(8,128)(2,1)} %param.22) | copy-start | bytes 98308
  310.9 171.3 %copy-start.30 = (s32[16]{0:T(128)S(1)}, s32[16]{0:T(128)}, u32[]{:S(2)}) copy-start(s32[16]{0:T(128)} %param.23) | copy-start | bytes 196
  482.1 450.1 %copy-start.5 = (f32[128,1024]{1,0:T(8,128)}, f32[128,1024]{1,0:T(8,128)S(1)}, u32[]{:S(2)}) copy-start(f32[128,1024]{1,0:T(8,128)S(1)} %broadcast_divide_fusion) | copy-start | bytes 1572868
  482.1 450.2 %copy-start.6 = (bf16[1,128,512]{1,2,0:T(8,128)(2,1)S(1)}, bf16[1,128,512]{1,2,0:T(8,128)(2,1)}, u32[]{:S(2)}) copy-start(bf16[1,128,512]{1,2,0:T(8,128)(2,1)} %copy.52) | copy-start | bytes 393220
  484.3 565.4 %all-gather.14.cloned.1.call-start = ((), (), s32[]{:S(2)}) async-start(), calls=%async_computation.5 | async-start | bytes 4325376 | tf_op jit(solution)/shard_map/all_gather | solution.py:207
  484.9 699.6 %all-gather.8.cloned.1.call-start = ((), (), s32[]{:S(2)}) async-start(), calls=%async_computation.1 | async-start | bytes 1081344 | tf_op jit(solution)/shard_map/all_gather | solution.py:240
  585.9 464.4 %copy-start.4 = (bf16[1,128,512]{1,2,0:T(8,128)(2,1)S(1)}, bf16[1,128,512]{1,2,0:T(8,128)(2,1)}, u32[]{:S(2)}) copy-start(bf16[1,128,512]{1,2,0:T(8,128)(2,1)} %copy.53) | copy-start | bytes 393220
  586.1 343.9 %copy-start.22 = (f32[8]{0:T(128)}, f32[8]{0:T(128)S(1)}, u32[]{:S(2)}) copy-start(f32[8]{0:T(128)S(1)} %dynamic-slice.1) | copy-start | bytes 100
  932.3 117.9 %copy-start.16 = (bf16[8,8,64]{2,1,0:T(8,128)(2,1)}, bf16[8,8,64]{2,1,0:T(8,128)(2,1)S(1)}, u32[]{:S(2)}) copy-start(bf16[8,8,64]{2,1,0:T(8,128)(2,1)S(1)} %reshape.195) | copy-start | bytes 24580
  934.2 116.0 %copy-start.18 = (f32[128,8]{0,1:T(8,128)}, f32[128,8]{0,1:T(8,128)S(1)}, u32[]{:S(2)}) copy-start(f32[128,8]{0,1:T(8,128)S(1)} %bitcast_reduce_fusion.1) | copy-start | bytes 12292
  989.1 370.6 %all-reduce.6.cloned.1.call-start = ((), (), s32[]{:S(2)}) async-start(), calls=%async_computation.2 | async-start | bytes 4194304 | tf_op jit(solution)/shard_map/psum | solution.py:149
  1050.3 4.5 copy-start.1
  1066.0 4.5 copy-start.1
  1081.7 4.5 copy-start.1
  1097.3 4.5 copy-start.1
  1113.0 4.5 copy-start.1
  1128.7 4.5 copy-start.1
  1144.4 4.5 copy-start.1
  1160.1 4.5 copy-start.1
  1178.5 4.1 copy-start.29
  1178.5 6.1 copy-start.3
  1178.5 6.1 copy-start.19
  1178.5 6.1 copy-start.21
  1178.5 6.1 copy-start.31
  (69 other events, 166.6 us)
Sparse Core Ops, SparseCore 0:
  10.6 127.1 all-gather.11
  140.3 138.3 all-gather.9
  484.5 444.1 all-reduce.3
  931.3 118.4 all-gather.13
  1051.8 116.7 all-gather.7
  1182.7 177.0 all-reduce.5
where the time goes:
time: 1370 us
  waiting for transfers between devices  677 us (49%)
  blocking collectives  374 us (27%)
  local copies, waits for them, and re-layouts  157 us (11%)
  matrix products  102 us (7%)
  loops' own time  22.5 us (2%)
  other arithmetic  21.9 us (2%)
  between operations  16.2 us (1%)
    psum x1, waiting for transfers between devices, body(): lax.psum((embedding_gradient, jnp.sum(losses)), ('grp', 'seq'))  290 us
    all_gather x1, waiting for transfers between devices, body(): keys_all = lax.all_gather(keys_local, 'seq', axis=0, tiled=True)  121 us
    all_gather x1, waiting for transfers between devices, body(): lax.all_gather(values_local, 'seq', axis=0, tiled=True)  115 us
    psum x1, blocking collectives, body(): lax.psum((embedding_gradient, jnp.sum(losses)), ('grp', 'seq'))  99 us
    psum x1, blocking collectives, body(): doc_inputs, doc_attn = lax.psum((mean_inputs, mean_attn), 'seq')  92.2 us
    psum x1, waiting for transfers between devices, body(): grad_w_out = lax.psum(weight_term, 'grp')  89.8 us
    all_gather x1, blocking collectives, body(): pooled = lax.all_gather(doc_pooled, 'grp', axis=0, tiled=True)  75.8 us
    all_gather x1, waiting for transfers between devices, body(): lax.all_gather(queries, 'seq', axis=0, tiled=True)  60.4 us
  transfers between devices with their start and end apart: 6, of which 5 were waited for; matrix products, arithmetic and copies ran while one was open for 17% of the time, Pallas kernels for 0%

commit v1 on v0

v1 whole, which is shorter than its diff:
```python
import functools

import jax
import jax.numpy as jnp
from jax import lax
from jax.experimental import pallas as pl
from jax.experimental.pallas import tpu as pltpu
from jax.sharding import Mesh, PartitionSpec as P

HEAD_COUNT = 8
HEAD_DIM = 64
GROUPS = 8
DOCS = 16
MODEL = 1024
WIDTH = 512
ROWS = 128
HALF = 64
QUARTER = 1024
PLANE = 16
SCALE = HEAD_DIM ** (-0.5)

RECIPROCAL_TEMP = 20.0
GRADIENT_FACTOR = 64.0
NORM_EPS = 1e-06
QUERY_COUNT = 8192
EXACT = lax.Precision.HIGHEST

BF16 = jnp.bfloat16
F32 = jnp.float32

GRP = ("yh", "xa", "xb", "co")
SEQ = ("yl", "za", "zb", "zc", "zd")
ZED = ("za", "zb", "zc", "zd")
SQUARE = ("yl", "zd")
NT = (((1,), (1,)), ((), ()))
TN = (((0,), (0,)), ((), ()))

VMEM_BYTES = 56 << 20


def params():
    return pltpu.CompilerParams(vmem_limit_bytes=VMEM_BYTES)


def cost(flops, moved, exps=0):
    return pl.CostEstimate(flops=int(flops), bytes_accessed=int(moved), transcendentals=int(exps))


def share(value, axes):
    count = 2 ** len(axes)
    return lax.all_to_all(
        jnp.broadcast_to(value[None], (count,) + value.shape), axes, split_axis=0, concat_axis=0
    )


def swap(value, axes, flip):
    count = 2 ** len(axes)
    return lax.ppermute(value, axes, [(i, i ^ flip) for i in range(count)])


def gather_grp(value):
    for axis in ("co", "xb", "xa", "yh"):
        other = swap(value, (axis,), 1)
        first = lax.axis_index(axis) == 0
        value = jnp.where(
            first,
            jnp.concatenate([value, other], axis=0),
            jnp.concatenate([other, value], axis=0),
        )
    return value


def three(value):
    high = value.astype(BF16)
    rest = value - high.astype(F32)
    middle = rest.astype(BF16)
    low = (rest - middle.astype(F32)).astype(BF16)
    return high, middle, low


def stacked(value):
    parts = [part.astype(F32) for part in three(value)]
    parts.append(jnp.zeros_like(value))
    return jnp.concatenate(parts, axis=0).astype(BF16)


def folded(product):
    return (product[16:24] + product[8:16]) + product[0:8]


def quarter_member(bounds_ref, plane, half):
    row = lax.broadcasted_iota(jnp.int32, (GROUPS, QUARTER), 1)
    position = plane * (PLANE * ROWS) + (row >> 6) * ROWS + half * HALF + (row & 63)
    inside = (position >= bounds_ref[0, :, 0:1]) & (position < bounds_ref[1, :, 0:1])
    return inside.astype(F32)


def local_member(bounds_ref, first):
    position = first + lax.broadcasted_iota(jnp.int32, (GROUPS, ROWS), 1)
    inside = (position >= bounds_ref[0, :, 0:1]) & (position < bounds_ref[1, :, 0:1])
    return inside.astype(F32)


def halves(packed):
    return jnp.concatenate([packed[:, :, 0:64], packed[:, :, 64:128]], axis=1)


def lanes(rows):
    return lax.broadcasted_iota(jnp.int32, (rows, 128), 1)


def pack_kernel(place_ref, q_ref, k_ref, v_ref, inputs_ref, bounds_ref, out_ref):
    mine = local_member(bounds_ref, place_ref[3]).astype(BF16)
    sums = jnp.dot(mine, inputs_ref[...], preferred_element_type=F32)
    high, middle, low = [part.astype(F32) for part in three(sums)]
    zero = jnp.zeros((GROUPS, HALF), F32)
    for head in range(HEAD_COUNT):
        cols = slice(head * HEAD_DIM, (head + 1) * HEAD_DIM)
        for half in range(2):
            rows = slice(half * HALF, (half + 1) * HALF)
            place = 2 * head + half
            out_ref[place, 0:64, :] = jnp.concatenate([k_ref[rows, cols], v_ref[rows, cols]], axis=1)
            query = q_ref[rows, cols] * jnp.asarray(SCALE, BF16)
            out_ref[place, 64:96, :] = jnp.concatenate([query[0:32], query[32:64]], axis=1)
            part = slice(place * HALF, (place + 1) * HALF)
            upper = jnp.concatenate([high[:, part], middle[:, part]], axis=1)
            lower = jnp.concatenate([low[:, part], zero], axis=1)
            out_ref[place, 96:112, :] = jnp.concatenate([upper, lower], axis=0).astype(BF16)


def unpack_kernel(in_ref, q_ref, k_ref, v_ref):
    for pair in range(HEAD_COUNT // 2):
        cols = slice(pair * 128, (pair + 1) * 128)
        for half in range(2):
            one, two = 4 * pair + half, 4 * pair + 2 + half
            rows = slice(half * HALF, (half + 1) * HALF)
            first, second = in_ref[one, 0:64, :], in_ref[two, 0:64, :]
            k_ref[rows, cols] = jnp.concatenate([first[:, 0:64], second[:, 0:64]], axis=1)
            v_ref[rows, cols] = jnp.concatenate([first[:, 64:128], second[:, 64:128]], axis=1)
            first, second = in_ref[one, 64:96, :], in_ref[two, 64:96, :]
            early = jnp.concatenate([first[:, 0:64], second[:, 0:64]], axis=1)
            late = jnp.concatenate([first[:, 64:128], second[:, 64:128]], axis=1)
            q_ref[rows, cols] = jnp.concatenate([early, late], axis=0)


BLOCK = 256
PARTS = BLOCK // 128


def forward_kernel(
    place_ref, own_ref, x_ref, bounds_ref, length_ref, y_ref, lse_ref, means_ref, q_s
):
    queries = halves(own_ref[:, 64:96, :]).reshape(QUARTER, HEAD_DIM)
    q_s[...] = jnp.concatenate([queries, jnp.zeros_like(queries)], axis=1)

    def block(i, carry):
        rows = pl.ds(pl.multiple_of(i * BLOCK, BLOCK), BLOCK)
        scores = lax.dot_general(q_s[rows, :], x_ref[...], NT, preferred_element_type=F32)
        top = jnp.max(scores, axis=1, keepdims=True)
        grown = jnp.exp(scores - top)
        total = jnp.sum(grown, axis=1, keepdims=True)
        prob = (grown * (1.0 / total)).astype(BF16)
        mixed = jnp.dot(prob, x_ref[...], preferred_element_type=F32).astype(BF16)
        y_ref[rows, :] = jnp.where(lanes(BLOCK) < 64, q_s[rows, :], mixed)
        log_total = top + jnp.log(total)
        for part in range(PARTS):
            square = jnp.broadcast_to(log_total[part * 128 : (part + 1) * 128], (128, 128))
            lse_ref[pl.ds(i * PARTS + part, 1), :] = jnp.transpose(square)[0:1, :]
        return carry

    lax.fori_loop(0, QUARTER // BLOCK, block, 0)
    y_ref[QUARTER : QUARTER + 32, :] = stacked(lse_ref[...])
    member = quarter_member(bounds_ref, place_ref[0], place_ref[1]).astype(BF16)
    attn_sums = jnp.dot(member, y_ref[0:QUARTER, :], preferred_element_type=F32)
    sums = jnp.sum(own_ref[:, 96:112, :].astype(F32), axis=0)
    input_sums = (sums[0:8] + pltpu.roll(sums[0:8], 64, 1)) + sums[8:16]
    means = jnp.where(lanes(GROUPS) < 64, input_sums, attn_sums) / length_ref[...]
    means_ref[...] = jnp.broadcast_to(means[None], (2 * PLANE, GROUPS, 128))


def pool_kernel(means_ref, w_ref, pooled_ref, means_out_ref):
    columns, heads = [], []
    for z in range(PLANE):
        both = means_ref[z] + means_ref[PLANE + z]
        columns.append(both[:, 0:64])
        if z % 2 == 0:
            heads.append(both[:, 64:128])
        else:
            heads[-1] = heads[-1] + both[:, 64:128]
    means = jnp.concatenate(heads, axis=1)
    projected = jnp.dot(stacked(means), w_ref[...], preferred_element_type=F32)
    pooled = jnp.concatenate(columns, axis=1) + folded(projected)
    pooled_ref[...] = jnp.broadcast_to(pooled[None], (DOCS, GROUPS, MODEL))
    means_out_ref[...] = means


def query_kernel(query_ref, out_ref):
    query = query_ref[:, :MODEL].astype(F32)
    squares = lax.dot_general(
        jnp.ones((8, MODEL), F32), query * query, NT, precision=EXACT, preferred_element_type=F32
    )
    out_ref[0:8, :] = jnp.sqrt(squares + NORM_EPS)
    out_ref[8:16, :] = lax.dot_general(
        jnp.ones((8, 128), BF16), query_ref[:, MODEL:], NT, preferred_element_type=F32
    )


def loss_kernel(doc_ref, pooled_ref, query_ref, row_ref, w_ref, out_ref, weight_s):
    pooled = pooled_ref[...]
    norms = jnp.sqrt(jnp.sum(pooled * pooled, axis=1, keepdims=True) + NORM_EPS)
    unit = pooled / norms
    query = query_ref[:, :MODEL]
    scale = RECIPROCAL_TEMP / row_ref[0:1, :]
    logits = jnp.zeros((DOCS * GROUPS, 256), F32)
    for part in three(unit)[::-1]:
        logits = logits + lax.dot_general(part, query, NT, preferred_element_type=F32)
    logits = logits * scale
    grown = jnp.exp(logits)
    total = jnp.sum(grown, axis=0, keepdims=True)
    group = lax.broadcasted_iota(jnp.int32, logits.shape, 0)
    target = (group == row_ref[8:9, :].astype(jnp.int32)).astype(F32)
    losses = jnp.log(total) - jnp.sum(target * logits, axis=0, keepdims=True)
    loss = jnp.sum(losses, axis=1, keepdims=True)
    weight_s[...] = (grown / total - target) * (GRADIENT_FACTOR * scale)
    mine = pl.ds(pl.multiple_of(doc_ref[0] * GROUPS, GROUPS), GROUPS)
    grad = folded(jnp.dot(stacked(weight_s[mine, :]), query, preferred_element_type=F32))
    own = pooled_ref[mine, :]
    own_unit = own / jnp.sqrt(jnp.sum(own * own, axis=1, keepdims=True) + NORM_EPS)
    along = jnp.sum(own_unit * grad, axis=1, keepdims=True)
    spread = folded(
        lax.dot_general(stacked(grad), w_ref[...], NT, preferred_element_type=F32)
    )
    extra = jnp.where(lanes(GROUPS) < 64, along, loss)
    for z in range(PLANE):
        head = z // 2
        chunk = jnp.concatenate(
            [
                spread[:, head * HEAD_DIM : (head + 1) * HEAD_DIM],
                grad[:, z * HALF : (z + 1) * HALF],
            ],
            axis=1,
        )
        for plane in range(2):
            out_ref[plane * PLANE + z, 0:8, :] = chunk
            out_ref[plane * PLANE + z, 8:16, :] = extra


def group_kernel(place_ref, terms_ref, pooled_ref, w_ref, length_ref, dattn_ref, grad_ref, loss_ref):
    head = place_ref[2]
    z = 2 * head + place_ref[1]
    sums = terms_ref[0]
    for n in range(1, 2 * PLANE):
        sums = sums + terms_ref[n]
    along = sums[8:16, 0:1]
    loss_ref[...] = sums[8:16, :] / QUERY_COUNT
    pooled = pooled_ref[...]
    norms = jnp.sqrt(jnp.sum(pooled * pooled, axis=1, keepdims=True) + NORM_EPS)
    unit = pooled / norms
    w_head = w_ref[pl.ds(pl.multiple_of(head * HEAD_DIM, HEAD_DIM), HEAD_DIM), :]
    w_twice = jnp.concatenate([w_head, w_head], axis=0)
    shade = folded(lax.dot_general(stacked(unit), w_twice, NT, preferred_element_type=F32))
    raw = jnp.concatenate([sums[0:8, 0:64], sums[0:8, 0:64]], axis=1)
    dattn_ref[...] = (raw - shade * along) / norms / length_ref[...]
    part = jnp.zeros((GROUPS, HALF), F32)
    for n in range(PLANE):
        part = jnp.where(z == n, unit[:, n * HALF : (n + 1) * HALF], part)
    grad = (sums[0:8, 64:128] - part * along) / norms
    wide = jnp.concatenate([grad, grad], axis=1)
    grad_ref[...] = jnp.broadcast_to(wide[None], (PLANE, GROUPS, 128))


def inputs_kernel(place_ref, parts_ref, means_ref, bounds_ref, length_ref, grad_inputs_ref, out_ref):
    grad = jnp.concatenate([parts_ref[z][:, 0:64] for z in range(PLANE)], axis=1)
    mine = local_member(bounds_ref, place_ref[3])
    members = jnp.concatenate([mine, mine, mine, mine], axis=0).astype(BF16)
    grad_inputs_ref[...] = lax.dot_general(
        members, stacked(grad / length_ref[:, 0:1]), TN, preferred_element_type=F32
    ).astype(BF16)
    both = jnp.concatenate([grad, means_ref[...]], axis=1)
    out_ref[...] = jnp.broadcast_to(both[None], (DOCS, GROUPS, MODEL + WIDTH))


def weight_kernel(in_ref, out_ref):
    grads = three(in_ref[:, :MODEL])
    means = three(in_ref[:, MODEL:])
    out_ref[...] = lax.dot_general(
        jnp.concatenate([means[1], means[0], means[0]], axis=0),
        jnp.concatenate([grads[0], grads[1], grads[0]], axis=0),
        TN,
        preferred_element_type=F32,
    )


def row_kernel(place_ref, y_ref, lse_ref, x_ref, dattn_ref, bounds_ref, out_ref, q_s, d_s, delta_s):
    lane = lanes(QUARTER)
    member = quarter_member(bounds_ref, place_ref[0], place_ref[1]).astype(BF16)
    spread = lax.dot_general(
        member, dattn_ref[...].astype(BF16), TN, preferred_element_type=F32
    )
    spread = jnp.where(lane < 64, 0.0, spread)
    mine = y_ref[0:QUARTER, :]
    q_s[...] = jnp.where(lane < 64, mine, jnp.zeros_like(mine))
    d_s[...] = spread.astype(BF16)
    delta_s[...] = jnp.broadcast_to(
        jnp.sum(spread * mine.astype(F32), axis=1, keepdims=True), (QUARTER, 128)
    )

    def block(i, carry):
        rows = pl.ds(pl.multiple_of(i * BLOCK, BLOCK), BLOCK)
        columns = []
        for part in range(PARTS):
            line = lse_ref[pl.ds(i * PARTS + part, 1), :]
            columns.append(jnp.transpose(jnp.broadcast_to(line, (128, 128))))
        log_total = jnp.concatenate(columns, axis=0)[:, 0:1]
        scores = lax.dot_general(q_s[rows, :], x_ref[...], NT, preferred_element_type=F32)
        prob = jnp.exp(scores - log_total)
        prob_grad = lax.dot_general(d_s[rows, :], x_ref[...], NT, preferred_element_type=F32)
        score_grad = (prob * (prob_grad - delta_s[rows, 0:1])).astype(BF16)
        for_query = jnp.dot(score_grad, x_ref[...], preferred_element_type=F32) * SCALE
        count = BLOCK // HALF
        value = for_query[:, 0:64].astype(BF16).reshape(count, HALF, HEAD_DIM)
        out_ref[pl.ds(i * count, count), :, :] = jnp.concatenate(
            [value[:, 0:32], value[:, 32:64]], axis=2
        )
        return carry

    lax.fori_loop(0, QUARTER // BLOCK, block, 0)


def column_kernel(own_ref, y_ref, dattn_ref, bounds_ref, grad_q_ref, out_ref, y_s, k_s, v_s, delta_s, lse_s):
    lane = lanes(QUARTER)
    mine = own_ref[:, 0:64, :].reshape(QUARTER, 128)
    zero = jnp.zeros_like(mine)
    k_s[...] = jnp.where(lane < 64, mine, zero)
    v_s[...] = jnp.where(lane < 64, zero, mine)
    dattn = dattn_ref[...].astype(BF16)
    ones = jnp.ones((8, 128), F32)
    for n in range(4):
        rows = slice(n * QUARTER, (n + 1) * QUARTER)
        member = quarter_member(bounds_ref, n // 2, n % 2).astype(BF16)
        spread = lax.dot_general(member, dattn, TN, preferred_element_type=F32)
        spread = jnp.where(lane < 64, 0.0, spread)
        other = y_ref[n, 0:QUARTER, :]
        y_s[rows, :] = jnp.where(lane < 64, other, spread.astype(BF16))
        delta_s[:, rows] = lax.dot_general(
            ones, spread * other.astype(F32), NT, precision=EXACT, preferred_element_type=F32
        )
        lse = y_ref[n, QUARTER : QUARTER + 32, :].astype(F32)
        lse = (lse[16:24] + lse[8:16]) + lse[0:8]
        for part in range(8):
            lse_s[:, n * QUARTER + part * 128 : n * QUARTER + (part + 1) * 128] = jnp.broadcast_to(
                lse[part : part + 1, :], (8, 128)
            )

    def block(i, carry):
        rows = pl.ds(pl.multiple_of(i * BLOCK, BLOCK), BLOCK)
        scores = lax.dot_general(k_s[rows, :], y_s[...], NT, preferred_element_type=F32)
        prob = jnp.exp(scores - lse_s[0:1, :])
        prob_grad = lax.dot_general(v_s[rows, :], y_s[...], NT, preferred_element_type=F32)
        score_grad = (prob * (prob_grad - delta_s[0:1, :])).astype(BF16)
        for_key = jnp.dot(score_grad, y_s[...], preferred_element_type=F32)
        for_value = jnp.dot(prob.astype(BF16), y_s[...], preferred_element_type=F32)
        both = jnp.where(lanes(BLOCK) < 64, for_key, for_value).astype(BF16)
        count = BLOCK // HALF
        out_ref[pl.ds(i * count, count), 0:64, :] = both.reshape(count, HALF, 128)
        return carry

    lax.fori_loop(0, QUARTER // BLOCK, block, 0)
    out_ref[:, 64:96, :] = grad_q_ref[...]


SMEM = pl.BlockSpec(memory_space=pltpu.SMEM)
VMEM = pl.BlockSpec(memory_space=pltpu.VMEM)


def call(kernel, outs, scalars, arrays, scratch, estimate, name):
    return pl.pallas_call(
        kernel,
        out_shape=outs,
        in_specs=[SMEM] * len(scalars) + [VMEM] * len(arrays),
        out_specs=jax.tree.map(lambda _: VMEM, outs),
        scratch_shapes=scratch,
        compiler_params=params(),
        cost_estimate=estimate,
        name=name,
    )(*scalars, *arrays)


def shape(dims, dtype):
    return jax.ShapeDtypeStruct(dims, dtype)


def body(inputs, q_heads, k_heads, v_heads, w_out, group_lens, query_emb, positive):
    plane = lax.axis_index("yl")
    half = lax.axis_index("zd")
    head = lax.axis_index(("za", "zb", "zc"))
    first = lax.axis_index(SEQ) * ROWS
    doc = lax.axis_index(GRP).reshape(1).astype(jnp.int32)
    place = jnp.stack([plane, half, head, first]).astype(jnp.int32)
    lengths = group_lens[0]
    ends = jnp.cumsum(lengths)
    bounds = jnp.broadcast_to(jnp.stack([ends - lengths, ends])[:, :, None], (2, GROUPS, 128))
    length = jnp.broadcast_to(lengths.astype(F32)[:, None], (GROUPS, 128))

    packed = call(
        pack_kernel, shape((PLANE, 112, 128), BF16), (place,),
        (q_heads[0], k_heads[0], v_heads[0], inputs[0], bounds), (), cost(0, 1000000), "pack",
    )
    own = lax.all_to_all(packed, ZED, split_axis=0, concat_axis=0)
    keys = share(own[:, 0:64, :], SQUARE).reshape(4 * QUARTER, 128)

    tagged = jnp.concatenate(
        [query_emb, jnp.pad(positive.astype(BF16)[:, None], ((0, 0), (0, 127)))], axis=1
    )
    queries = gather_grp(tagged)
    query_rows = call(
        query_kernel, shape((16, 256), F32), (), (queries,), (), cost(6 * 2 * 8 * 256 * 1024, 600000),
        "queries",
    )

    pairs = QUARTER * 4 * QUARTER
    mine, lse, means = call(
        forward_kernel,
        (
            shape((QUARTER + 32, 128), BF16),
            shape((8, 128), F32),
            shape((2 * PLANE, GROUPS, 128), F32),
        ),
        (place,), (own, keys, bounds, length), [pltpu.VMEM((QUARTER, 128), BF16)],
        cost(pairs * 256 * 4, 3000000, pairs), "forward",
    )
    means = lax.all_to_all(means, SEQ, split_axis=0, concat_axis=0)
    others = share(mine, SQUARE)

    pooled, doc_means = call(
        pool_kernel,
        (shape((DOCS, GROUPS, MODEL), F32), shape((GROUPS, WIDTH), F32)),
        (), (means, w_out), (), cost(2 * 32 * 512 * 1024, 1200000), "pool",
    )
    pooled_own = pooled[0]
    pooled_all = lax.all_to_all(pooled, GRP, split_axis=0, concat_axis=0)
    pooled_all = pooled_all.reshape(DOCS * GROUPS, MODEL)
    pooled_all, others = lax.optimization_barrier((pooled_all, others))
    terms = call(
        loss_kernel, shape((2 * PLANE, 16, 128), F32), (doc,),
        (pooled_all, queries, query_rows, w_out), [pltpu.VMEM((DOCS * GROUPS, 256), F32)],
        cost(3 * 2 * 128 * 256 * 1024, 2500000, 40000), "loss",
    )
    terms = lax.all_to_all(terms, SEQ, split_axis=0, concat_axis=0)

    dattn, grad_part, loss = call(
        group_kernel,
        (
            shape((GROUPS, 128), F32),
            shape((PLANE, GROUPS, 128), F32),
            shape((GROUPS, 128), F32),
        ),
        (place,), (terms, pooled_own, w_out, length),
        (), cost(2 * 32 * 128 * 1024, 1500000), "group",
    )
    mean_loss = loss[0, 64]
    grad_parts = lax.all_to_all(grad_part, ZED, split_axis=0, concat_axis=0)
    grad_rows = call(
        row_kernel, shape((PLANE, 32, 128), BF16), (place,),
        (mine, lse, keys, dattn, bounds),
        [
            pltpu.VMEM((QUARTER, 128), BF16),
            pltpu.VMEM((QUARTER, 128), BF16),
            pltpu.VMEM((QUARTER, 128), F32),
        ],
        cost(pairs * 256 * 6, 2000000, pairs), "rows",
    )
    grad_inputs, grads = call(
        inputs_kernel,
        (shape((ROWS, MODEL), BF16), shape((DOCS, GROUPS, MODEL + WIDTH), F32)),
        (place,), (grad_parts, doc_means, bounds, length), (), cost(2 * 32 * 128 * 1024, 1200000),
        "inputs",
    )
    grad_rows, grads = lax.optimization_barrier((grad_rows, grads))
    all_grads = lax.all_to_all(grads, GRP, split_axis=0, concat_axis=0)
    packed_grads = call(
        column_kernel, shape((PLANE, 96, 128), BF16), (), (own, others, dattn, bounds, grad_rows),
        [
            pltpu.VMEM((4 * QUARTER, 128), BF16),
            pltpu.VMEM((QUARTER, 128), BF16),
            pltpu.VMEM((QUARTER, 128), BF16),
            pltpu.VMEM((8, 4 * QUARTER), F32),
            pltpu.VMEM((8, 4 * QUARTER), F32),
        ],
        cost(pairs * 256 * 8, 2500000, pairs), "columns",
    )
    home = lax.all_to_all(packed_grads, ZED, split_axis=0, concat_axis=0)
    out = shape((ROWS, WIDTH), BF16)
    grad_q, grad_k, grad_v = call(
        unpack_kernel, (out, out, out), (), (home,), (), cost(0, 800000), "unpack"
    )
    grad_w_out = call(
        weight_kernel, shape((WIDTH, MODEL), F32), (),
        (all_grads.reshape(DOCS * GROUPS, MODEL + WIDTH),), (),
        cost(2 * 384 * 512 * 1024, 3000000), "weights",
    )
    return (mean_loss, grad_inputs[None], grad_q[None], grad_k[None], grad_v[None], grad_w_out)


def solution(mesh):
    fine = Mesh(mesh.devices.reshape((2,) * 9), GRP + SEQ)
    rows = P(GRP, SEQ, None)
    return jax.shard_map(
        body,
        mesh=fine,
        in_specs=(
            rows,
            rows,
            rows,
            rows,
            P(),
            P(GRP, None),
            P(GRP + SEQ, None),
            P(GRP + SEQ),
        ),
        out_specs=(P(), rows, rows, rows, rows, P()),
        check_vma=False,
    )
```

time: 1370 us -> 266 us (0.19)
  the two profiles are of different devices: /device:TPU:1 before, /device:TPU:2 now
where the time goes in v1:
time: 266 us; the launch traced here: 264 us
  blocking collectives  98 us (37%)
  waiting for transfers between devices  58.9 us (22%)
  Pallas kernels  56.9 us (21%)
  starting transfers between devices  38.7 us (15%)
  local copies, waits for them, and re-layouts  7.54 us (3%)
  other arithmetic  3.32 us (1%)
    pallas_call x11, Pallas kernels, call(): pl.pallas_call(kernel, out_shape=outs, in_specs=[SMEM] * len(scalars) + [...  56.9 us
    all_to_all x1, blocking collectives, body(): own = lax.all_to_all(packed, ZED, split_axis=0, concat_axis=0)  42 us
    all_to_all x1, blocking collectives, body(): means = lax.all_to_all(means, SEQ, split_axis=0, concat_axis=0)  26.1 us
    all_to_all x1, waiting for transfers between devices, body(): home = lax.all_to_all(packed_grads, ZED, split_axis=0, concat_axis=0)  19.8 us
    all_to_all x1, waiting for transfers between devices, body(): terms = lax.all_to_all(terms, SEQ, split_axis=0, concat_axis=0)  19 us
    ppermute x4, waiting for transfers between devices, swap(): return lax.ppermute(value, axes, [(i, i ^ flip) for i in range(count)])  17.5 us
    all_to_all x1, blocking collectives, body(): pooled_all = lax.all_to_all(pooled, GRP, split_axis=0, concat_axis=0)  16.3 us
    all_to_all x1, blocking collectives, share(): lax.all_to_all(jnp.broadcast_to(value[None], (count,) + value.shape), axe...  13.7 us
  transfers between devices with their start and end apart: 9, of which 7 were waited for; matrix products, arithmetic and copies ran while one was open for 1% of the time, Pallas kernels for 11%

profile of v1, /device:TPU:2, one launch (start us, length us, event | category | flops | bytes accessed | tf_op | source)
XLA Modules:
  0.0 264.3 jit_solution(15392500656262967853)
XLA Ops:
  3.6 2.2 pack.1
  5.7 42.0 %all_to_all.45.own_ref = bf16[16,112,128]{2,1,0:T(8,128)(2,1)S(1)} all-to-all(bf16[16,112,128]{2,1,0:T(8,128)(2,1)} %pack.1), channel_id=1, replica_groups=mesh['yh'=2,'xa'=2,'xb'=2,'co'=2,'yl'=2,'za'=2,'zb'=2,'zc'=2,'zd'=2] {'z..., dimensions={0} | all-to-all | bytes 917504 | tf_op jit(solution)/shard_map/all_to_all | solution.py:409
  48.0 13.7 %all_to_all.46 = bf16[4,16,64,128]{3,2,1,0:T(8,128)(2,1)} all-to-all(bf16[4,16,64,128]{3,2,1,0:T(8,128)(2,1)S(1)} %broadcast_in_dim.19), channel_id=1, replica_groups=mesh['yh'=2,'xa'=2,'xb'=2,'co'=2,'yl'=2,'za'=2,'zb'=2,'zc'=2,'zd'=2] {'y..., dimensions={0} | all-to-all | bytes 2097152 | tf_op jit(solution)/shard_map/all_to_all | solution.py:51
  62.4 10.3 %forward.1 = (bf16[1056,128]{1,0:T(8,128)(2,1)}, f32[8,128]{1,0:T(8,128)}, f32[32,8,128]{2,1,0:T(8,128)}) custom-call(s32[4]{0:T(128)} %pad_add_fusion.1.place_ref, bf16[16,112,128]{2,1,0:T(8,128)(2,1)} %copy-done.2, bf16[4096,128]{1,0:T(8,128)(2,1)} %bitcast.25, s32[2,8,128]{2,1,0:T(8,128)} %broadcast_in_dim.18.bounds_ref, f32[8,128]{1,0:T(8,128)} %broadcast_in_dim.20.length_ref), custom_call_target="tpu_custom_call" | custom-call | flops 4294967296 | bytes 3000000 | tf_op jit(solution)/shard_map/forward/pallas_call | solution.py:377
  72.7 26.1 %all_to_all.47.means_ref = f32[32,8,128]{2,1,0:T(8,128)} all-to-all(f32[32,8,128]{2,1,0:T(8,128)} %get-tuple-element.23), channel_id=1, replica_groups=mesh['yh'=2,'xa'=2,'xb'=2,'co'=2,'yl'=2,'za'=2,'zb'=2,'zc'=2,'zd'=2] {'y..., dimensions={0} | all-to-all | bytes 262144 | tf_op jit(solution)/shard_map/all_to_all | solution.py:432
  98.8 2.5 pool.1
  101.3 16.3 %all_to_all.48 = f32[16,8,1024]{2,1,0:T(8,128)} all-to-all(f32[16,8,1024]{2,1,0:T(8,128)} %get-tuple-element.24), channel_id=1, replica_groups=mesh['yh'=2,'xa'=2,'xb'=2,'co'=2,'yl'=2,'za'=2,'zb'=2,'zc'=2,'zd'=2] {'y..., dimensions={0} | all-to-all | bytes 1048576 | tf_op jit(solution)/shard_map/all_to_all | solution.py:441
  118.7 3.7 %all-to-all-start.4 = ((bf16[4,1056,128]{2,1,0:T(8,128)(2,1)}), bf16[4,1056,128]{2,1,0:T(8,128)(2,1)S(1)}, u32[]{:S(2)}, u32[]{:S(2)}) async-start(bf16[4,1056,128]{2,1,0:T(8,128)(2,1)} %broadcast_in_dim.42), calls=%async_computation.4 | async-start | bytes 2162688 | tf_op jit(solution)/shard_map/all_to_all | solution.py:51
  122.5 2.8 %collective-permute-start = (bf16[16,1152]{1,0:T(8,128)(2,1)S(1)}, bf16[16,1152]{1,0:T(8,128)(2,1)S(1)}, u32[]{:S(2)}, u32[]{:S(2)}) collective-permute-start(bf16[16,1152]{1,0:T(8,128)(2,1)S(1)} %pad_maximum_fusion), channel_id=1, source_target_pairs={{0,32},{32,0},{1,33},{33,1},{2,34},{34,2},{3,35},{35,3},{4,36},{36... | collective-permute-start | bytes 110600 | tf_op jit(solution)/shard_map/ppermute | solution.py:58
  126.2 5.1 %collective-permute-start.1 = (bf16[32,1152]{1,0:T(8,128)(2,1)S(1)}, bf16[32,1152]{1,0:T(8,128)(2,1)S(1)}, u32[]{:S(2)}, u32[]{:S(2)}) collective-permute-start(bf16[32,1152]{1,0:T(8,128)(2,1)S(1)} %maximum_select_fusion.3), channel_id=1, source_target_pairs={{0,64},{64,0},{1,65},{65,1},{2,66},{66,2},{3,67},{67,3},{4,68},{68... | collective-permute-start | bytes 221192 | tf_op jit(solution)/shard_map/ppermute | solution.py:58
  131.3 2.6 collective-permute-done.1
  133.9 3.2 %collective-permute-start.2 = (bf16[64,1152]{1,0:T(8,128)(2,1)S(1)}, bf16[64,1152]{1,0:T(8,128)(2,1)S(1)}, u32[]{:S(2)}, u32[]{:S(2)}) collective-permute-start(bf16[64,1152]{1,0:T(8,128)(2,1)S(1)} %maximum_select_fusion.2), channel_id=1, source_target_pairs={{0,128},{128,0},{1,129},{129,1},{2,130},{130,2},{3,131},{131,3},{4... | collective-permute-start | bytes 442376 | tf_op jit(solution)/shard_map/ppermute | solution.py:58
  137.1 5.5 %collective-permute-done.2 = bf16[64,1152]{1,0:T(8,128)(2,1)S(1)} collective-permute-done((bf16[64,1152]{1,0:T(8,128)(2,1)S(1)}, bf16[64,1152]{1,0:T(8,128)(2,1)S(1)}, u32[]{:S(2)}, u32[]{:S(2)}) %collective-permute-start.2) | collective-permute-done | bytes 147488 | tf_op jit(solution)/shard_map/ppermute | solution.py:58
  142.7 2.5 collective-permute-start.3
  145.2 8.6 %collective-permute-done.3 = bf16[128,1152]{1,0:T(8,128)(2,1)S(1)} collective-permute-done((bf16[128,1152]{1,0:T(8,128)(2,1)S(1)}, bf16[128,1152]{1,0:T(8,128)(2,1)S(1)}, u32[]{:S(2)}, u32[]{:S(2)}) %collective-permute-start.3) | collective-permute-done | bytes 294944 | tf_op jit(solution)/shard_map/ppermute | solution.py:58
  154.8 2.6 %queries.1.row_ref = f32[16,256]{1,0:T(8,128)} custom-call(bf16[256,1152]{1,0:T(8,128)(2,1)} %maximum_select_fusion.query_ref), custom_call_target="tpu_custom_call" | custom-call | flops 25165824 | bytes 600000 | tf_op jit(solution)/shard_map/queries/pallas_call | solution.py:377
  157.4 4.5 %loss.1 = f32[32,16,128]{2,1,0:T(8,128)} custom-call(s32[1]{0:T(128)} %bitcast.4.doc_ref, f32[128,1024]{1,0:T(8,128)} %bitcast.24, bf16[256,1152]{1,0:T(8,128)(2,1)} %maximum_select_fusion.query_ref, f32[16,256]{1,0:T(8,128)} %queries.1.row_ref, bf16[512,1024]{1,0:T(8,128)(2,1)} %w_ref.5), custom_call_target="tpu_custom_call" | custom-call | flops 201326592 | bytes 2500000 | tf_op jit(solution)/shard_map/loss/pallas_call | solution.py:377
  161.9 4.6 %all-to-all-start.5 = ((f32[32,16,128]{2,1,0:T(8,128)}), f32[32,16,128]{2,1,0:T(8,128)S(1)}, u32[]{:S(2)}, u32[]{:S(2)}) async-start(f32[32,16,128]{2,1,0:T(8,128)} %loss.1), calls=%async_computation.5 | async-start | bytes 524288 | tf_op jit(solution)/shard_map/all_to_all | solution.py:449
  166.5 1.4 slice_bitcast_fusion.pooled_ref
  167.9 19.0 %all-to-all-done.5.terms_ref = f32[32,16,128]{2,1,0:T(8,128)S(1)} async-done(((f32[32,16,128]{2,1,0:T(8,128)}), f32[32,16,128]{2,1,0:T(8,128)S(1)}, u32[]{:S(2)}, u32[]{:S(2)}) %all-to-all-start.5) | async-done | bytes 262176 | tf_op jit(solution)/shard_map/all_to_all | solution.py:449
  187.6 3.2 %group.1 = (f32[8,128]{1,0:T(8,128)}, f32[16,8,128]{2,1,0:T(8,128)}, f32[8,128]{1,0:T(8,128)}) custom-call(s32[4]{0:T(128)} %pad_add_fusion.1.place_ref, f32[32,16,128]{2,1,0:T(8,128)} %copy-done.4, f32[8,1024]{1,0:T(8,128)} %slice_bitcast_fusion.pooled_ref, bf16[512,1024]{1,0:T(8,128)(2,1)} %w_ref.5, f32[8,128]{1,0:T(8,128)} %broadcast_in_dim.20.length_ref), custom_call_target="tpu_custom_call" | custom-call | flops 8388608 | bytes 1500000 | tf_op jit(solution)/shard_map/group/pallas_call | solution.py:377
  190.8 3.5 %all-to-all-start.6 = ((f32[16,8,128]{2,1,0:T(8,128)}), f32[16,8,128]{2,1,0:T(8,128)S(1)}, u32[]{:S(2)}, u32[]{:S(2)}) async-start(f32[16,8,128]{2,1,0:T(8,128)} %get-tuple-element.28), calls=%async_computation.6 | async-start | bytes 131072 | tf_op jit(solution)/shard_map/all_to_all | solution.py:462
  194.3 10.2 %rows.1.grad_q_ref = bf16[16,32,128]{2,1,0:T(8,128)(2,1)} custom-call(s32[4]{0:T(128)} %pad_add_fusion.1.place_ref, bf16[1056,128]{1,0:T(8,128)(2,1)} %get-tuple-element.25.y_ref, f32[8,128]{1,0:T(8,128)} %get-tuple-element.33.lse_ref, bf16[4096,128]{1,0:T(8,128)(2,1)} %bitcast.26, f32[8,128]{1,0:T(8,128)} %get-tuple-element.32.dattn_ref, ...), custom_call_target="tpu_custom_call" | custom-call | flops 6442450944 | bytes 2000000 | tf_op jit(solution)/shard_map/rows/pallas_call | solution.py:377
  204.5 2.5 all-to-all-done.6.parts_ref
  207.6 2.0 inputs.1
  209.6 4.0 %all-to-all-start.8 = ((f32[16,8,1536]{2,1,0:T(8,128)}), f32[16,8,1536]{2,1,0:T(8,128)S(1)}, u32[]{:S(2)}, u32[]{:S(2)}) async-start(f32[16,8,1536]{2,1,0:T(8,128)} %get-tuple-element.39), calls=%async_computation.8 | async-start | bytes 1572864 | tf_op jit(solution)/shard_map/all_to_all | solution.py:480
  213.6 14.3 %columns.1 = bf16[16,96,128]{2,1,0:T(8,128)(2,1)} custom-call(bf16[16,112,128]{2,1,0:T(8,128)(2,1)} %copy-done.2, bf16[4,1056,128]{2,1,0:T(8,128)(2,1)} %copy-done.3, f32[8,128]{1,0:T(8,128)} %get-tuple-element.32.dattn_ref, s32[2,8,128]{2,1,0:T(8,128)} %broadcast_in_dim.18.bounds_ref, bf16[16,32,128]{2,1,0:T(8,128)(2,1)} %rows.1.grad_q_ref), custom_call_target="tpu_custom_call" | custom-call | flops 8589934592 | bytes 2500000 | tf_op jit(solution)/shard_map/columns/pallas_call | solution.py:377
  227.9 9.4 %all-to-all-start.7 = ((bf16[16,96,128]{2,1,0:T(8,128)(2,1)}), bf16[16,96,128]{2,1,0:T(8,128)(2,1)S(1)}, u32[]{:S(2)}, u32[]{:S(2)}) async-start(bf16[16,96,128]{2,1,0:T(8,128)(2,1)} %columns.1), calls=%async_computation.7 | async-start | bytes 786432 | tf_op jit(solution)/shard_map/all_to_all | solution.py:492
  237.3 1.3 slice.11
  238.6 3.2 %weights.1 = f32[512,1024]{1,0:T(8,128)} custom-call(f32[128,1536]{1,0:T(8,128)} %bitcast.23), custom_call_target="tpu_custom_call" | custom-call | flops 402653184 | bytes 3000000 | tf_op jit(solution)/shard_map/weights/pallas_call | solution.py:377
  241.8 19.8 %all-to-all-done.7.in_ref = bf16[16,96,128]{2,1,0:T(8,128)(2,1)S(1)} async-done(((bf16[16,96,128]{2,1,0:T(8,128)(2,1)}), bf16[16,96,128]{2,1,0:T(8,128)(2,1)S(1)}, u32[]{:S(2)}, u32[]{:S(2)}) %all-to-all-start.7) | async-done | bytes 393248 | tf_op jit(solution)/shard_map/all_to_all | solution.py:492
  262.4 1.9 unpack.1
  (38 shorter events, 9.1 us)
Async XLA Ops:
  47.7 14.0 %copy-start.2 = (bf16[16,112,128]{2,1,0:T(8,128)(2,1)}, bf16[16,112,128]{2,1,0:T(8,128)(2,1)S(1)}, u32[]{:S(2)}) copy-start(bf16[16,112,128]{2,1,0:T(8,128)(2,1)S(1)} %all_to_all.45.own_ref) | copy-start | bytes 1376260
  98.8 18.8 %copy-start.5 = (bf16[1056,128]{1,0:T(8,128)(2,1)S(1)}, bf16[1056,128]{1,0:T(8,128)(2,1)}, u32[]{:S(2)}) copy-start(bf16[1056,128]{1,0:T(8,128)(2,1)} %get-tuple-element.25.y_ref) | copy-start | bytes 811012
  118.7 3.7 %copy-start.8 = (s32[16]{0:T(128)S(1)}, s32[16]{0:T(128)}, u32[]{:S(2)}) copy-start(s32[16]{0:T(128)} %param.15) | copy-start | bytes 196
  118.7 3.8 %copy-start.7 = (bf16[16,1024]{1,0:T(8,128)(2,1)S(1)}, bf16[16,1024]{1,0:T(8,128)(2,1)}, u32[]{:S(2)}) copy-start(bf16[16,1024]{1,0:T(8,128)(2,1)} %param.14) | copy-start | bytes 98308
  118.7 38.7 %all-to-all-start.4 = ((bf16[4,1056,128]{2,1,0:T(8,128)(2,1)}), bf16[4,1056,128]{2,1,0:T(8,128)(2,1)S(1)}, u32[]{:S(2)}, u32[]{:S(2)}) async-start(bf16[4,1056,128]{2,1,0:T(8,128)(2,1)} %broadcast_in_dim.42), calls=%async_computation.4 | async-start | bytes 2162688 | tf_op jit(solution)/shard_map/all_to_all | solution.py:51
  122.5 3.7 %collective-permute-start = (bf16[16,1152]{1,0:T(8,128)(2,1)S(1)}, bf16[16,1152]{1,0:T(8,128)(2,1)S(1)}, u32[]{:S(2)}, u32[]{:S(2)}) collective-permute-start(bf16[16,1152]{1,0:T(8,128)(2,1)S(1)} %pad_maximum_fusion), channel_id=1, source_target_pairs={{0,32},{32,0},{1,33},{33,1},{2,34},{34,2},{3,35},{35,3},{4,36},{36... | collective-permute-start | bytes 110600 | tf_op jit(solution)/shard_map/ppermute | solution.py:58
  126.2 7.6 %collective-permute-start.1 = (bf16[32,1152]{1,0:T(8,128)(2,1)S(1)}, bf16[32,1152]{1,0:T(8,128)(2,1)S(1)}, u32[]{:S(2)}, u32[]{:S(2)}) collective-permute-start(bf16[32,1152]{1,0:T(8,128)(2,1)S(1)} %maximum_select_fusion.3), channel_id=1, source_target_pairs={{0,64},{64,0},{1,65},{65,1},{2,66},{66,2},{3,67},{67,3},{4,68},{68... | collective-permute-start | bytes 221192 | tf_op jit(solution)/shard_map/ppermute | solution.py:58
  133.9 8.8 %collective-permute-start.2 = (bf16[64,1152]{1,0:T(8,128)(2,1)S(1)}, bf16[64,1152]{1,0:T(8,128)(2,1)S(1)}, u32[]{:S(2)}, u32[]{:S(2)}) collective-permute-start(bf16[64,1152]{1,0:T(8,128)(2,1)S(1)} %maximum_select_fusion.2), channel_id=1, source_target_pairs={{0,128},{128,0},{1,129},{129,1},{2,130},{130,2},{3,131},{131,3},{4... | collective-permute-start | bytes 442376 | tf_op jit(solution)/shard_map/ppermute | solution.py:58
  142.7 11.1 %collective-permute-start.3 = (bf16[128,1152]{1,0:T(8,128)(2,1)S(1)}, bf16[128,1152]{1,0:T(8,128)(2,1)S(1)}, u32[]{:S(2)}, u32[]{:S(2)}) collective-permute-start(bf16[128,1152]{1,0:T(8,128)(2,1)S(1)} %maximum_select_fusion.1), channel_id=1, source_target_pairs={{0,256},{256,0},{1,257},{257,1},{2,258},{258,2},{3,259},{259,3},{4... | collective-permute-start | bytes 884744 | tf_op jit(solution)/shard_map/ppermute | solution.py:58
  157.4 4.5 %copy-start.3 = (bf16[4,1056,128]{2,1,0:T(8,128)(2,1)}, bf16[4,1056,128]{2,1,0:T(8,128)(2,1)S(1)}, u32[]{:S(2)}) copy-start(bf16[4,1056,128]{2,1,0:T(8,128)(2,1)S(1)} %all-to-all-done.4.y_ref) | copy-start | bytes 3244036
  161.9 25.0 %all-to-all-start.5 = ((f32[32,16,128]{2,1,0:T(8,128)}), f32[32,16,128]{2,1,0:T(8,128)S(1)}, u32[]{:S(2)}, u32[]{:S(2)}) async-start(f32[32,16,128]{2,1,0:T(8,128)} %loss.1), calls=%async_computation.5 | async-start | bytes 524288 | tf_op jit(solution)/shard_map/all_to_all | solution.py:449
  186.9 0.7 copy-start.4
  190.8 16.2 %all-to-all-start.6 = ((f32[16,8,128]{2,1,0:T(8,128)}), f32[16,8,128]{2,1,0:T(8,128)S(1)}, u32[]{:S(2)}, u32[]{:S(2)}) async-start(f32[16,8,128]{2,1,0:T(8,128)} %get-tuple-element.28), calls=%async_computation.6 | async-start | bytes 131072 | tf_op jit(solution)/shard_map/all_to_all | solution.py:462
  207.0 0.6 copy-start.6
  209.6 18.3 %all-to-all-start.8 = ((f32[16,8,1536]{2,1,0:T(8,128)}), f32[16,8,1536]{2,1,0:T(8,128)S(1)}, u32[]{:S(2)}, u32[]{:S(2)}) async-start(f32[16,8,1536]{2,1,0:T(8,128)} %get-tuple-element.39), calls=%async_computation.8 | async-start | bytes 1572864 | tf_op jit(solution)/shard_map/all_to_all | solution.py:480
  227.9 10.6 %copy-start = (f32[16,8,1536]{2,1,0:T(8,128)}, f32[16,8,1536]{2,1,0:T(8,128)S(1)}, u32[]{:S(2)}) copy-start(f32[16,8,1536]{2,1,0:T(8,128)S(1)} %all-to-all-done.8) | copy-start | bytes 2359300
  227.9 33.7 %all-to-all-start.7 = ((bf16[16,96,128]{2,1,0:T(8,128)(2,1)}), bf16[16,96,128]{2,1,0:T(8,128)(2,1)S(1)}, u32[]{:S(2)}, u32[]{:S(2)}) async-start(bf16[16,96,128]{2,1,0:T(8,128)(2,1)} %columns.1), calls=%async_computation.7 | async-start | bytes 786432 | tf_op jit(solution)/shard_map/all_to_all | solution.py:492
  261.6 0.7 copy-start.1

commit v2 on v1

--- a/solution.py
+++ b/solution.py
@@ -32,6 +32,7 @@
 SEQ = ("yl", "za", "zb", "zc", "zd")
 ZED = ("za", "zb", "zc", "zd")
 SQUARE = ("yl", "zd")
+HEADS = ("za", "zb", "zc")
 NT = (((1,), (1,)), ((), ()))
 TN = (((0,), (0,)), ((), ()))
 
@@ -88,17 +89,35 @@
     return (product[16:24] + product[8:16]) + product[0:8]
 
 
-def quarter_member(bounds_ref, plane, half):
+def column_of(values):
+    row = lax.broadcasted_iota(jnp.int32, (GROUPS, 128), 0)
+    out = jnp.full((GROUPS, 128), values[0])
+    for n in range(1, GROUPS):
+        out = jnp.where(row == n, values[n], out)
+    return out
+
+
+def member_of(position, lens_ref):
+    ends = [lens_ref[0]]
+    for n in range(1, GROUPS):
+        ends.append(ends[-1] + lens_ref[n])
+    last = column_of(ends)
+    first = last - column_of([lens_ref[n] for n in range(GROUPS)])
+    return ((position >= first[:, 0:1]) & (position < last[:, 0:1])).astype(F32)
+
+
+def lengths_of(lens_ref):
+    return column_of([lens_ref[n] for n in range(GROUPS)]).astype(F32)
+
+
+def quarter_member(lens_ref, plane, half):
     row = lax.broadcasted_iota(jnp.int32, (GROUPS, QUARTER), 1)
     position = plane * (PLANE * ROWS) + (row >> 6) * ROWS + half * HALF + (row & 63)
-    inside = (position >= bounds_ref[0, :, 0:1]) & (position < bounds_ref[1, :, 0:1])
-    return inside.astype(F32)
-
-
-def local_member(bounds_ref, first):
-    position = first + lax.broadcasted_iota(jnp.int32, (GROUPS, ROWS), 1)
-    inside = (position >= bounds_ref[0, :, 0:1]) & (position < bounds_ref[1, :, 0:1])
-    return inside.astype(F32)
+    return member_of(position, lens_ref)
+
+
+def local_member(lens_ref, first):
+    return member_of(first + lax.broadcasted_iota(jnp.int32, (GROUPS, ROWS), 1), lens_ref)
 
 
 def halves(packed):
@@ -109,8 +128,8 @@
     return lax.broadcasted_iota(jnp.int32, (rows, 128), 1)
 
 
-def pack_kernel(place_ref, q_ref, k_ref, v_ref, inputs_ref, bounds_ref, out_ref):
-    mine = local_member(bounds_ref, place_ref[3]).astype(BF16)
+def pack_kernel(place_ref, lens_ref, q_ref, k_ref, v_ref, inputs_ref, out_ref):
+    mine = local_member(lens_ref, place_ref[3]).astype(BF16)
     sums = jnp.dot(mine, inputs_ref[...], preferred_element_type=F32)
     high, middle, low = [part.astype(F32) for part in three(sums)]
     zero = jnp.zeros((GROUPS, HALF), F32)
@@ -128,16 +147,22 @@
             out_ref[place, 96:112, :] = jnp.concatenate([upper, lower], axis=0).astype(BF16)
 
 
-def unpack_kernel(in_ref, q_ref, k_ref, v_ref):
+def unpack_pair_kernel(in_ref, k_ref, v_ref):
     for pair in range(HEAD_COUNT // 2):
         cols = slice(pair * 128, (pair + 1) * 128)
         for half in range(2):
-            one, two = 4 * pair + half, 4 * pair + 2 + half
             rows = slice(half * HALF, (half + 1) * HALF)
-            first, second = in_ref[one, 0:64, :], in_ref[two, 0:64, :]
+            first, second = in_ref[4 * pair + half], in_ref[4 * pair + 2 + half]
             k_ref[rows, cols] = jnp.concatenate([first[:, 0:64], second[:, 0:64]], axis=1)
             v_ref[rows, cols] = jnp.concatenate([first[:, 64:128], second[:, 64:128]], axis=1)
-            first, second = in_ref[one, 64:96, :], in_ref[two, 64:96, :]
+
+
+def unpack_query_kernel(in_ref, q_ref):
+    for pair in range(HEAD_COUNT // 2):
+        cols = slice(pair * 128, (pair + 1) * 128)
+        for half in range(2):
+            rows = slice(half * HALF, (half + 1) * HALF)
+            first, second = in_ref[4 * pair + half], in_ref[4 * pair + 2 + half]
             early = jnp.concatenate([first[:, 0:64], second[:, 0:64]], axis=1)
             late = jnp.concatenate([first[:, 64:128], second[:, 64:128]], axis=1)
             q_ref[rows, cols] = jnp.concatenate([early, late], axis=0)
@@ -148,7 +173,7 @@
 
 
 def forward_kernel(
-    place_ref, own_ref, x_ref, bounds_ref, length_ref, y_ref, lse_ref, means_ref, q_s
+    place_ref, lens_ref, own_ref, x_ref, out_ref, lse_ref, means_ref, y_ref, q_s
 ):
     queries = halves(own_ref[:, 64:96, :]).reshape(QUARTER, HEAD_DIM)
     q_s[...] = jnp.concatenate([queries, jnp.zeros_like(queries)], axis=1)
@@ -170,28 +195,50 @@
 
     lax.fori_loop(0, QUARTER // BLOCK, block, 0)
     y_ref[QUARTER : QUARTER + 32, :] = stacked(lse_ref[...])
-    member = quarter_member(bounds_ref, place_ref[0], place_ref[1]).astype(BF16)
+    out_ref[...] = jnp.broadcast_to(y_ref[...][None], (4, QUARTER + 32, 128))
+    member = quarter_member(lens_ref, place_ref[0], place_ref[1]).astype(BF16)
     attn_sums = jnp.dot(member, y_ref[0:QUARTER, :], preferred_element_type=F32)
     sums = jnp.sum(own_ref[:, 96:112, :].astype(F32), axis=0)
     input_sums = (sums[0:8] + pltpu.roll(sums[0:8], 64, 1)) + sums[8:16]
-    means = jnp.where(lanes(GROUPS) < 64, input_sums, attn_sums) / length_ref[...]
-    means_ref[...] = jnp.broadcast_to(means[None], (2 * PLANE, GROUPS, 128))
-
-
-def pool_kernel(means_ref, w_ref, pooled_ref, means_out_ref):
-    columns, heads = [], []
-    for z in range(PLANE):
-        both = means_ref[z] + means_ref[PLANE + z]
-        columns.append(both[:, 0:64])
-        if z % 2 == 0:
-            heads.append(both[:, 64:128])
-        else:
-            heads[-1] = heads[-1] + both[:, 64:128]
-    means = jnp.concatenate(heads, axis=1)
+    means = jnp.where(lanes(GROUPS) < 64, input_sums, attn_sums) / lengths_of(lens_ref)
+    means_ref[...] = jnp.broadcast_to(means[None], (4, GROUPS, 128))
+
+
+def square_kernel(means_ref, out_ref):
+    means = [means_ref[n] for n in range(4)]
+    sums = jnp.concatenate(
+        [(means[0] + means[2])[:, 0:64], (means[1] + means[3])[:, 0:64]], axis=1
+    )
+    attn = (means[0] + means[1]) + (means[2] + means[3])
+    both = jnp.concatenate([sums, attn], axis=0)
+    out_ref[...] = jnp.broadcast_to(both[None], (HEAD_COUNT, 16, 128))
+
+
+def pool_kernel(means_ref, w_ref, pooled_ref, own_ref, means_out_ref):
+    columns = [means_ref[h, 0:8, :] for h in range(HEAD_COUNT)]
+    means = jnp.concatenate([means_ref[h, 8:16, 64:128] for h in range(HEAD_COUNT)], axis=1)
     projected = jnp.dot(stacked(means), w_ref[...], preferred_element_type=F32)
     pooled = jnp.concatenate(columns, axis=1) + folded(projected)
     pooled_ref[...] = jnp.broadcast_to(pooled[None], (DOCS, GROUPS, MODEL))
+    own_ref[...] = pooled
     means_out_ref[...] = means
+
+
+def prepare_kernel(place_ref, pooled_ref, w_ref, out_ref):
+    head = place_ref[2]
+    pooled = pooled_ref[...]
+    norms = jnp.sqrt(jnp.sum(pooled * pooled, axis=1, keepdims=True) + NORM_EPS)
+    unit = pooled / norms
+    w_head = w_ref[pl.ds(pl.multiple_of(head * HEAD_DIM, HEAD_DIM), HEAD_DIM), :]
+    w_twice = jnp.concatenate([w_head, w_head], axis=0)
+    out_ref[0:8, :] = folded(
+        lax.dot_general(stacked(unit), w_twice, NT, preferred_element_type=F32)
+    )
+    part = unit[:, 0:128]
+    for n in range(1, HEAD_COUNT):
+        part = jnp.where(head == n, unit[:, n * 128 : (n + 1) * 128], part)
+    out_ref[8:16, :] = part
+    out_ref[16:24, :] = jnp.broadcast_to(norms, (GROUPS, 128))
 
 
 def query_kernel(query_ref, out_ref):
@@ -231,50 +278,36 @@
         lax.dot_general(stacked(grad), w_ref[...], NT, preferred_element_type=F32)
     )
     extra = jnp.where(lanes(GROUPS) < 64, along, loss)
-    for z in range(PLANE):
-        head = z // 2
-        chunk = jnp.concatenate(
-            [
-                spread[:, head * HEAD_DIM : (head + 1) * HEAD_DIM],
-                grad[:, z * HALF : (z + 1) * HALF],
-            ],
-            axis=1,
-        )
-        for plane in range(2):
-            out_ref[plane * PLANE + z, 0:8, :] = chunk
-            out_ref[plane * PLANE + z, 8:16, :] = extra
-
-
-def group_kernel(place_ref, terms_ref, pooled_ref, w_ref, length_ref, dattn_ref, grad_ref, loss_ref):
-    head = place_ref[2]
-    z = 2 * head + place_ref[1]
-    sums = terms_ref[0]
-    for n in range(1, 2 * PLANE):
-        sums = sums + terms_ref[n]
-    along = sums[8:16, 0:1]
-    loss_ref[...] = sums[8:16, :] / QUERY_COUNT
-    pooled = pooled_ref[...]
-    norms = jnp.sqrt(jnp.sum(pooled * pooled, axis=1, keepdims=True) + NORM_EPS)
-    unit = pooled / norms
-    w_head = w_ref[pl.ds(pl.multiple_of(head * HEAD_DIM, HEAD_DIM), HEAD_DIM), :]
-    w_twice = jnp.concatenate([w_head, w_head], axis=0)
-    shade = folded(lax.dot_general(stacked(unit), w_twice, NT, preferred_element_type=F32))
-    raw = jnp.concatenate([sums[0:8, 0:64], sums[0:8, 0:64]], axis=1)
-    dattn_ref[...] = (raw - shade * along) / norms / length_ref[...]
-    part = jnp.zeros((GROUPS, HALF), F32)
-    for n in range(PLANE):
-        part = jnp.where(z == n, unit[:, n * HALF : (n + 1) * HALF], part)
-    grad = (sums[0:8, 64:128] - part * along) / norms
-    wide = jnp.concatenate([grad, grad], axis=1)
-    grad_ref[...] = jnp.broadcast_to(wide[None], (PLANE, GROUPS, 128))
-
-
-def inputs_kernel(place_ref, parts_ref, means_ref, bounds_ref, length_ref, grad_inputs_ref, out_ref):
-    grad = jnp.concatenate([parts_ref[z][:, 0:64] for z in range(PLANE)], axis=1)
-    mine = local_member(bounds_ref, place_ref[3])
+    for head in range(HEAD_COUNT):
+        part = spread[:, head * HEAD_DIM : (head + 1) * HEAD_DIM]
+        out_ref[head, 0:8, :] = jnp.concatenate([part, part], axis=1)
+        out_ref[head, 8:16, :] = grad[:, head * 128 : (head + 1) * 128]
+        out_ref[head, 16:24, :] = extra
+
+
+def fold_kernel(in_ref, out_ref):
+    terms = [in_ref[n] for n in range(HEAD_COUNT)]
+    while len(terms) > 1:
+        terms = [terms[n] + terms[n + 1] for n in range(0, len(terms), 2)]
+    out_ref[...] = jnp.broadcast_to(terms[0][None], (4, 24, 128))
+
+
+def group_kernel(lens_ref, terms_ref, ready_ref, dattn_ref, grad_ref, loss_ref):
+    sums = (terms_ref[0] + terms_ref[1]) + (terms_ref[2] + terms_ref[3])
+    along = sums[16:24, 0:1]
+    loss_ref[...] = sums[16:24, :] / QUERY_COUNT
+    norms = ready_ref[16:24, :]
+    dattn_ref[...] = (sums[0:8] - ready_ref[0:8, :] * along) / norms / lengths_of(lens_ref)
+    grad = (sums[8:16] - ready_ref[8:16, :] * along) / norms
+    grad_ref[...] = jnp.broadcast_to(grad[None], (HEAD_COUNT, GROUPS, 128))
+
+
+def inputs_kernel(place_ref, lens_ref, parts_ref, means_ref, grad_inputs_ref, out_ref):
+    grad = jnp.concatenate([parts_ref[n] for n in range(HEAD_COUNT)], axis=1)
+    mine = local_member(lens_ref, place_ref[3])
     members = jnp.concatenate([mine, mine, mine, mine], axis=0).astype(BF16)
     grad_inputs_ref[...] = lax.dot_general(
-        members, stacked(grad / length_ref[:, 0:1]), TN, preferred_element_type=F32
+        members, stacked(grad / lengths_of(lens_ref)[:, 0:1]), TN, preferred_element_type=F32
     ).astype(BF16)
     both = jnp.concatenate([grad, means_ref[...]], axis=1)
     out_ref[...] = jnp.broadcast_to(both[None], (DOCS, GROUPS, MODEL + WIDTH))
@@ -291,9 +324,9 @@
     )
 
 
-def row_kernel(place_ref, y_ref, lse_ref, x_ref, dattn_ref, bounds_ref, out_ref, q_s, d_s, delta_s):
+def row_kernel(place_ref, lens_ref, y_ref, lse_ref, x_ref, dattn_ref, out_ref, q_s, d_s, delta_s):
     lane = lanes(QUARTER)
-    member = quarter_member(bounds_ref, place_ref[0], place_ref[1]).astype(BF16)
+    member = quarter_member(lens_ref, place_ref[0], place_ref[1]).astype(BF16)
     spread = lax.dot_general(
         member, dattn_ref[...].astype(BF16), TN, preferred_element_type=F32
     )
@@ -327,7 +360,7 @@
     lax.fori_loop(0, QUARTER // BLOCK, block, 0)
 
 
-def column_kernel(own_ref, y_ref, dattn_ref, bounds_ref, grad_q_ref, out_ref, y_s, k_s, v_s, delta_s, lse_s):
+def column_kernel(lens_ref, own_ref, y_ref, dattn_ref, out_ref, y_s, k_s, v_s, delta_s, lse_s):
     lane = lanes(QUARTER)
     mine = own_ref[:, 0:64, :].reshape(QUARTER, 128)
     zero = jnp.zeros_like(mine)
@@ -337,7 +370,7 @@
     ones = jnp.ones((8, 128), F32)
     for n in range(4):
         rows = slice(n * QUARTER, (n + 1) * QUARTER)
-        member = quarter_member(bounds_ref, n // 2, n % 2).astype(BF16)
+        member = quarter_member(lens_ref, n // 2, n % 2).astype(BF16)
         spread = lax.dot_general(member, dattn, TN, preferred_element_type=F32)
         spread = jnp.where(lane < 64, 0.0, spread)
         other = y_ref[n, 0:QUARTER, :]
@@ -362,11 +395,10 @@
         for_value = jnp.dot(prob.astype(BF16), y_s[...], preferred_element_type=F32)
         both = jnp.where(lanes(BLOCK) < 64, for_key, for_value).astype(BF16)
         count = BLOCK // HALF
-        out_ref[pl.ds(i * count, count), 0:64, :] = both.reshape(count, HALF, 128)
+        out_ref[pl.ds(i * count, count), :, :] = both.reshape(count, HALF, 128)
         return carry
 
     lax.fori_loop(0, QUARTER // BLOCK, block, 0)
-    out_ref[:, 64:96, :] = grad_q_ref[...]
 
 
 SMEM = pl.BlockSpec(memory_space=pltpu.SMEM)
@@ -393,93 +425,88 @@
 def body(inputs, q_heads, k_heads, v_heads, w_out, group_lens, query_emb, positive):
     plane = lax.axis_index("yl")
     half = lax.axis_index("zd")
-    head = lax.axis_index(("za", "zb", "zc"))
+    head = lax.axis_index(HEADS)
     first = lax.axis_index(SEQ) * ROWS
     doc = lax.axis_index(GRP).reshape(1).astype(jnp.int32)
     place = jnp.stack([plane, half, head, first]).astype(jnp.int32)
     lengths = group_lens[0]
-    ends = jnp.cumsum(lengths)
-    bounds = jnp.broadcast_to(jnp.stack([ends - lengths, ends])[:, :, None], (2, GROUPS, 128))
-    length = jnp.broadcast_to(lengths.astype(F32)[:, None], (GROUPS, 128))
+    exchange = functools.partial(lax.all_to_all, split_axis=0, concat_axis=0)
 
     packed = call(
-        pack_kernel, shape((PLANE, 112, 128), BF16), (place,),
-        (q_heads[0], k_heads[0], v_heads[0], inputs[0], bounds), (), cost(0, 1000000), "pack",
-    )
-    own = lax.all_to_all(packed, ZED, split_axis=0, concat_axis=0)
-    keys = share(own[:, 0:64, :], SQUARE).reshape(4 * QUARTER, 128)
-
+        pack_kernel, shape((PLANE, 112, 128), BF16), (place, lengths),
+        (q_heads[0], k_heads[0], v_heads[0], inputs[0]), (), cost(0, 1000000), "pack",
+    )
     tagged = jnp.concatenate(
         [query_emb, jnp.pad(positive.astype(BF16)[:, None], ((0, 0), (0, 127)))], axis=1
     )
+    packed, tagged = lax.optimization_barrier((packed, tagged))
+    own = exchange(packed, ZED)
     queries = gather_grp(tagged)
     query_rows = call(
         query_kernel, shape((16, 256), F32), (), (queries,), (), cost(6 * 2 * 8 * 256 * 1024, 600000),
         "queries",
     )
+    own, queries, query_rows = lax.optimization_barrier((own, queries, query_rows))
+    keys = share(own[:, 0:64, :], SQUARE).reshape(4 * QUARTER, 128)
 
     pairs = QUARTER * 4 * QUARTER
-    mine, lse, means = call(
+    outgoing, lse, means, mine = call(
         forward_kernel,
         (
+            shape((4, QUARTER + 32, 128), BF16),
+            shape((8, 128), F32),
+            shape((4, GROUPS, 128), F32),
             shape((QUARTER + 32, 128), BF16),
-            shape((8, 128), F32),
-            shape((2 * PLANE, GROUPS, 128), F32),
         ),
-        (place,), (own, keys, bounds, length), [pltpu.VMEM((QUARTER, 128), BF16)],
+        (place, lengths), (own, keys), [pltpu.VMEM((QUARTER, 128), BF16)],
         cost(pairs * 256 * 4, 3000000, pairs), "forward",
     )
-    means = lax.all_to_all(means, SEQ, split_axis=0, concat_axis=0)
-    others = share(mine, SQUARE)
-
-    pooled, doc_means = call(
+    means = exchange(means, SQUARE)
+    means = call(
+        square_kernel, shape((HEAD_COUNT, 16, 128), F32), (), (means,), (), cost(0, 100000), "square",
+    )
+    means = exchange(means, HEADS)
+    pooled, pooled_own, doc_means = call(
         pool_kernel,
-        (shape((DOCS, GROUPS, MODEL), F32), shape((GROUPS, WIDTH), F32)),
+        (
+            shape((DOCS, GROUPS, MODEL), F32),
+            shape((GROUPS, MODEL), F32),
+            shape((GROUPS, WIDTH), F32),
+        ),
         (), (means, w_out), (), cost(2 * 32 * 512 * 1024, 1200000), "pool",
     )
-    pooled_own = pooled[0]
-    pooled_all = lax.all_to_all(pooled, GRP, split_axis=0, concat_axis=0)
-    pooled_all = pooled_all.reshape(DOCS * GROUPS, MODEL)
-    pooled_all, others = lax.optimization_barrier((pooled_all, others))
+    pooled, pooled_own, outgoing = lax.optimization_barrier((pooled, pooled_own, outgoing))
+    pooled_all = exchange(pooled, GRP).reshape(DOCS * GROUPS, MODEL)
+    others = exchange(outgoing, SQUARE)
+    ready = call(
+        prepare_kernel, shape((24, 128), F32), (place,), (pooled_own, w_out), (),
+        cost(2 * 32 * 128 * 1024, 1200000), "prepare",
+    )
+    pooled_all, others, ready = lax.optimization_barrier((pooled_all, others, ready))
     terms = call(
-        loss_kernel, shape((2 * PLANE, 16, 128), F32), (doc,),
+        loss_kernel, shape((HEAD_COUNT, 24, 128), F32), (doc,),
         (pooled_all, queries, query_rows, w_out), [pltpu.VMEM((DOCS * GROUPS, 256), F32)],
         cost(3 * 2 * 128 * 256 * 1024, 2500000, 40000), "loss",
     )
-    terms = lax.all_to_all(terms, SEQ, split_axis=0, concat_axis=0)
+    terms = exchange(terms, HEADS)
+    terms = call(
+        fold_kernel, shape((4, 24, 128), F32), (), (terms,), (), cost(0, 150000), "fold",
+    )
+    terms = exchange(terms, SQUARE)
 
     dattn, grad_part, loss = call(
         group_kernel,
         (
             shape((GROUPS, 128), F32),
-            shape((PLANE, GROUPS, 128), F32),
+            shape((HEAD_COUNT, GROUPS, 128), F32),
             shape((GROUPS, 128), F32),
         ),
-        (place,), (terms, pooled_own, w_out, length),
-        (), cost(2 * 32 * 128 * 1024, 1500000), "group",
+        (lengths,), (terms, ready), (), cost(0, 100000), "group",
     )
     mean_loss = loss[0, 64]
-    grad_parts = lax.all_to_all(grad_part, ZED, split_axis=0, concat_axis=0)
-    grad_rows = call(
-        row_kernel, shape((PLANE, 32, 128), BF16), (place,),
-        (mine, lse, keys, dattn, bounds),
-        [
-            pltpu.VMEM((QUARTER, 128), BF16),
-            pltpu.VMEM((QUARTER, 128), BF16),
-            pltpu.VMEM((QUARTER, 128), F32),
-        ],
-        cost(pairs * 256 * 6, 2000000, pairs), "rows",
-    )
-    grad_inputs, grads = call(
-        inputs_kernel,
-        (shape((ROWS, MODEL), BF16), shape((DOCS, GROUPS, MODEL + WIDTH), F32)),
-        (place,), (grad_parts, doc_means, bounds, length), (), cost(2 * 32 * 128 * 1024, 1200000),
-        "inputs",
-    )
-    grad_rows, grads = lax.optimization_barrier((grad_rows, grads))
-    all_grads = lax.all_to_all(grads, GRP, split_axis=0, concat_axis=0)
-    packed_grads = call(
-        column_kernel, shape((PLANE, 96, 128), BF16), (), (own, others, dattn, bounds, grad_rows),
+    grad_parts = exchange(grad_part, HEADS)
+    packed_pair = call(
+        column_kernel, shape((PLANE, HALF, 128), BF16), (lengths,), (own, others, dattn),
         [
             pltpu.VMEM((4 * QUARTER, 128), BF16),
             pltpu.VMEM((QUARTER, 128), BF16),
@@ -489,15 +516,35 @@
         ],
         cost(pairs * 256 * 8, 2500000, pairs), "columns",
     )
-    home = lax.all_to_all(packed_grads, ZED, split_axis=0, concat_axis=0)
+    grad_inputs, grads = call(
+        inputs_kernel,
+        (shape((ROWS, MODEL), BF16), shape((DOCS, GROUPS, MODEL + WIDTH), F32)),
+        (place, lengths), (grad_parts, doc_means), (), cost(2 * 32 * 128 * 1024, 1200000), "inputs",
+    )
+    packed_pair, grads, dattn = lax.optimization_barrier((packed_pair, grads, dattn))
+    home_pair = exchange(packed_pair, ZED)
+    all_grads = exchange(grads, GRP)
+    packed_query = call(
+        row_kernel, shape((PLANE, 32, 128), BF16), (place, lengths), (mine, lse, keys, dattn),
+        [
+            pltpu.VMEM((QUARTER, 128), BF16),
+            pltpu.VMEM((QUARTER, 128), BF16),
+            pltpu.VMEM((QUARTER, 128), F32),
+        ],
+        cost(pairs * 256 * 6, 2000000, pairs), "rows",
+    )
+    home_query = exchange(packed_query, ZED)
     out = shape((ROWS, WIDTH), BF16)
-    grad_q, grad_k, grad_v = call(
-        unpack_kernel, (out, out, out), (), (home,), (), cost(0, 800000), "unpack"
+    grad_k, grad_v = call(
+        unpack_pair_kernel, (out, out), (), (home_pair,), (), cost(0, 500000), "unpack_pair"
     )
     grad_w_out = call(
         weight_kernel, shape((WIDTH, MODEL), F32), (),
         (all_grads.reshape(DOCS * GROUPS, MODEL + WIDTH),), (),
         cost(2 * 384 * 512 * 1024, 3000000), "weights",
+    )
+    grad_q = call(
+        unpack_query_kernel, out, (), (home_query,), (), cost(0, 300000), "unpack_query"
     )
     return (mean_loss, grad_inputs[None], grad_q[None], grad_k[None], grad_v[None], grad_w_out)
 

time: 266 us -> 288 us (1.083)
  the two profiles are of different devices: /device:TPU:2 before, /device:TPU:64 now
where the time goes in v2:
time: 288 us; the launch traced here: 287 us
  blocking collectives  136 us (47%)
  Pallas kernels  61.6 us (21%)
  starting transfers between devices  45.2 us (16%)
  waiting for transfers between devices  37.1 us (13%)
  other arithmetic  3.12 us (1%)
  local copies, waits for them, and re-layouts  2.95 us (1%)
    pallas_call x15, Pallas kernels, call(): pl.pallas_call(kernel, out_shape=outs, in_specs=[SMEM] * len(scalars) + [...  61.6 us
    all_to_all x1, blocking collectives, body(): home_query = exchange(packed_query, ZED)  24 us
    all_to_all x1, blocking collectives, body(): means = exchange(means, HEADS)  23 us
    all_to_all x1, blocking collectives, body(): pooled_all = exchange(pooled, GRP).reshape(DOCS * GROUPS, MODEL)  19.5 us
    all_to_all x1, blocking collectives, body(): all_grads = exchange(grads, GRP)  18.7 us
    all_to_all x1, blocking collectives, body(): terms = exchange(terms, HEADS)  17.7 us
    all_to_all x1, blocking collectives, share(): lax.all_to_all(jnp.broadcast_to(value[None], (count,) + value.shape), axe...  15.5 us
    ppermute x4, starting transfers between devices, swap(): return lax.ppermute(value, axes, [(i, i ^ flip) for i in range(count)])  15.3 us
  transfers between devices with their start and end apart: 8, of which 6 were waited for; matrix products, arithmetic and copies ran while one was open for 1% of the time, Pallas kernels for 8%

profile of v2, /device:TPU:64, one launch (start us, length us, event | category | flops | bytes accessed | tf_op | source)
XLA Modules:
  0.0 286.6 jit_solution(15856616877164498341)
XLA Ops:
  2.8 2.2 pack.1
  5.0 14.8 %all-to-all-start = ((bf16[16,112,128]{2,1,0:T(8,128)(2,1)}), bf16[16,112,128]{2,1,0:T(8,128)(2,1)S(1)}, u32[]{:S(2)}, u32[]{:S(2)}) async-start(bf16[16,112,128]{2,1,0:T(8,128)(2,1)} %pack.1), calls=%async_computation | async-start | bytes 917504 | tf_op jit(solution)/shard_map/all_to_all | solution.py:443
  19.7 1.9 collective-permute-start
  22.8 3.4 %collective-permute-start.1 = (bf16[32,1152]{1,0:T(8,128)(2,1)S(1)}, bf16[32,1152]{1,0:T(8,128)(2,1)S(1)}, u32[]{:S(2)}, u32[]{:S(2)}) collective-permute-start(bf16[32,1152]{1,0:T(8,128)(2,1)S(1)} %maximum_select_fusion.3), channel_id=1, source_target_pairs={{0,64},{64,0},{1,65},{65,1},{2,66},{66,2},{3,67},{67,3},{4,68},{68... | collective-permute-start | bytes 221192 | tf_op jit(solution)/shard_map/ppermute | solution.py:59
  26.2 2.8 collective-permute-done.1
  29.1 4.9 %collective-permute-start.2 = (bf16[64,1152]{1,0:T(8,128)(2,1)S(1)}, bf16[64,1152]{1,0:T(8,128)(2,1)S(1)}, u32[]{:S(2)}, u32[]{:S(2)}) collective-permute-start(bf16[64,1152]{1,0:T(8,128)(2,1)S(1)} %maximum_select_fusion.2), channel_id=1, source_target_pairs={{0,128},{128,0},{1,129},{129,1},{2,130},{130,2},{3,131},{131,3},{4... | collective-permute-start | bytes 442376 | tf_op jit(solution)/shard_map/ppermute | solution.py:59
  34.1 3.6 %collective-permute-done.2 = bf16[64,1152]{1,0:T(8,128)(2,1)S(1)} collective-permute-done((bf16[64,1152]{1,0:T(8,128)(2,1)S(1)}, bf16[64,1152]{1,0:T(8,128)(2,1)S(1)}, u32[]{:S(2)}, u32[]{:S(2)}) %collective-permute-start.2) | collective-permute-done | bytes 147488 | tf_op jit(solution)/shard_map/ppermute | solution.py:59
  37.7 5.1 %collective-permute-start.3 = (bf16[128,1152]{1,0:T(8,128)(2,1)S(1)}, bf16[128,1152]{1,0:T(8,128)(2,1)S(1)}, u32[]{:S(2)}, u32[]{:S(2)}) collective-permute-start(bf16[128,1152]{1,0:T(8,128)(2,1)S(1)} %maximum_select_fusion.1), channel_id=1, source_target_pairs={{0,256},{256,0},{1,257},{257,1},{2,258},{258,2},{3,259},{259,3},{4... | collective-permute-start | bytes 884744 | tf_op jit(solution)/shard_map/ppermute | solution.py:59
  42.8 5.6 %collective-permute-done.3 = bf16[128,1152]{1,0:T(8,128)(2,1)S(1)} collective-permute-done((bf16[128,1152]{1,0:T(8,128)(2,1)S(1)}, bf16[128,1152]{1,0:T(8,128)(2,1)S(1)}, u32[]{:S(2)}, u32[]{:S(2)}) %collective-permute-start.3) | collective-permute-done | bytes 294944 | tf_op jit(solution)/shard_map/ppermute | solution.py:59
  49.4 2.6 queries.1.row_ref
  52.4 15.5 %all_to_all.60 = bf16[4,16,64,128]{3,2,1,0:T(8,128)(2,1)} all-to-all(bf16[4,16,64,128]{3,2,1,0:T(8,128)(2,1)S(1)} %broadcast_in_dim.22), channel_id=1, replica_groups=mesh['yh'=2,'xa'=2,'xb'=2,'co'=2,'yl'=2,'za'=2,'zb'=2,'zc'=2,'zd'=2] {'y..., dimensions={0} | all-to-all | bytes 2097152 | tf_op jit(solution)/shard_map/all_to_all | solution.py:52
  67.9 10.6 %forward.1 = (bf16[4,1056,128]{2,1,0:T(8,128)(2,1)}, f32[8,128]{1,0:T(8,128)}, f32[4,8,128]{2,1,0:T(8,128)}, bf16[1056,128]{1,0:T(8,128)(2,1)}) custom-call(s32[4]{0:T(128)} %pad_add_fusion.place_ref, s32[8]{0:T(128)} %bitcast.30, bf16[16,112,128]{2,1,0:T(8,128)(2,1)} %copy-done, bf16[4096,128]{1,0:T(8,128)(2,1)} %bitcast.22), custom_call_target="tpu_custom_call" | custom-call | flops 4294967296 | bytes 3000000 | tf_op jit(solution)/shard_map/forward/pallas_call | solution.py:409
  78.5 8.6 %all_to_all.61.means_ref = f32[4,8,128]{2,1,0:T(8,128)} all-to-all(f32[4,8,128]{2,1,0:T(8,128)} %get-tuple-element.37), channel_id=1, replica_groups=mesh['yh'=2,'xa'=2,'xb'=2,'co'=2,'yl'=2,'za'=2,'zb'=2,'zc'=2,'zd'=2] {'y..., dimensions={0} | all-to-all | bytes 32768 | tf_op jit(solution)/shard_map/all_to_all | solution.py:464
  88.5 23.0 %all_to_all.62.means_ref = f32[8,16,128]{2,1,0:T(8,128)} all-to-all(f32[8,16,128]{2,1,0:T(8,128)} %square.1), channel_id=1, replica_groups=mesh['yh'=2,'xa'=2,'xb'=2,'co'=2,'yl'=2,'za'=2,'zb'=2,'zc'=2,'zd'=2] {'z..., dimensions={0} | all-to-all | bytes 131072 | tf_op jit(solution)/shard_map/all_to_all | solution.py:468
  111.6 2.4 pool.1
  114.0 19.5 %all_to_all.63 = f32[16,8,1024]{2,1,0:T(8,128)} all-to-all(f32[16,8,1024]{2,1,0:T(8,128)} %get-tuple-element.41), channel_id=1, replica_groups=mesh['yh'=2,'xa'=2,'xb'=2,'co'=2,'yl'=2,'za'=2,'zb'=2,'zc'=2,'zd'=2] {'y..., dimensions={0} | all-to-all | bytes 1048576 | tf_op jit(solution)/shard_map/all_to_all | solution.py:479
  133.5 3.5 %all-to-all-start.5 = ((bf16[4,1056,128]{2,1,0:T(8,128)(2,1)}), bf16[4,1056,128]{2,1,0:T(8,128)(2,1)S(1)}, u32[]{:S(2)}, u32[]{:S(2)}) async-start(bf16[4,1056,128]{2,1,0:T(8,128)(2,1)} %get-tuple-element.42), calls=%async_computation.5 | async-start | bytes 2162688 | tf_op jit(solution)/shard_map/all_to_all | solution.py:480
  137.1 2.1 prepare.1.ready_ref
  139.2 11.7 %all-to-all-done.5.y_ref = bf16[4,1056,128]{2,1,0:T(8,128)(2,1)S(1)} async-done(((bf16[4,1056,128]{2,1,0:T(8,128)(2,1)}), bf16[4,1056,128]{2,1,0:T(8,128)(2,1)S(1)}, u32[]{:S(2)}, u32[]{:S(2)}) %all-to-all-start.5) | async-done | bytes 1081376 | tf_op jit(solution)/shard_map/all_to_all | solution.py:480
  150.9 4.5 %loss.1 = f32[8,24,128]{2,1,0:T(8,128)} custom-call(s32[1]{0:T(128)} %bitcast.1.doc_ref, f32[128,1024]{1,0:T(8,128)} %bitcast.21, bf16[256,1152]{1,0:T(8,128)(2,1)} %maximum_select_fusion.query_ref, f32[16,256]{1,0:T(8,128)} %queries.1.row_ref, bf16[512,1024]{1,0:T(8,128)(2,1)} %w_ref.5), custom_call_target="tpu_custom_call" | custom-call | flops 201326592 | bytes 2500000 | tf_op jit(solution)/shard_map/loss/pallas_call | solution.py:409
  155.3 17.7 %all_to_all.64.in_ref = f32[8,24,128]{2,1,0:T(8,128)} all-to-all(f32[8,24,128]{2,1,0:T(8,128)} %loss.1), channel_id=1, replica_groups=mesh['yh'=2,'xa'=2,'xb'=2,'co'=2,'yl'=2,'za'=2,'zb'=2,'zc'=2,'zd'=2] {'z..., dimensions={0} | all-to-all | bytes 196608 | tf_op jit(solution)/shard_map/all_to_all | solution.py:491
  174.5 8.7 %all_to_all.65.terms_ref = f32[4,24,128]{2,1,0:T(8,128)} all-to-all(f32[4,24,128]{2,1,0:T(8,128)} %fold.1), channel_id=1, replica_groups=mesh['yh'=2,'xa'=2,'xb'=2,'co'=2,'yl'=2,'za'=2,'zb'=2,'zc'=2,'zd'=2] {'y..., dimensions={0} | all-to-all | bytes 98304 | tf_op jit(solution)/shard_map/all_to_all | solution.py:495
  184.8 6.3 %all-to-all-start.8 = ((f32[8,8,128]{2,1,0:T(8,128)}), f32[8,8,128]{2,1,0:T(8,128)S(1)}, u32[]{:S(2)}, u32[]{:S(2)}) async-start(f32[8,8,128]{2,1,0:T(8,128)} %get-tuple-element.49), calls=%async_computation.8 | async-start | bytes 65536 | tf_op jit(solution)/shard_map/all_to_all | solution.py:507
  191.1 14.1 %columns.1 = bf16[16,64,128]{2,1,0:T(8,128)(2,1)} custom-call(s32[8]{0:T(128)} %bitcast.32, bf16[16,112,128]{2,1,0:T(8,128)(2,1)} %copy-done, bf16[4,1056,128]{2,1,0:T(8,128)(2,1)} %copy-done.1, f32[8,128]{1,0:T(8,128)} %get-tuple-element.57.dattn_ref), custom_call_target="tpu_custom_call" | custom-call | flops 8589934592 | bytes 2500000 | tf_op jit(solution)/shard_map/columns/pallas_call | solution.py:409
  205.8 1.8 inputs.1
  207.6 10.2 %rows.1 = bf16[16,32,128]{2,1,0:T(8,128)(2,1)} custom-call(s32[4]{0:T(128)} %pad_add_fusion.place_ref, s32[8]{0:T(128)} %bitcast.34, bf16[1056,128]{1,0:T(8,128)(2,1)} %get-tuple-element.52.y_ref, f32[8,128]{1,0:T(8,128)} %get-tuple-element.53.lse_ref, bf16[4096,128]{1,0:T(8,128)(2,1)} %bitcast.23, f32[8,128]{1,0:T(8,128)} %get-tuple-element.57.dattn_ref), custom_call_target="tpu_custom_call" | custom-call | flops 6442450944 | bytes 2000000 | tf_op jit(solution)/shard_map/rows/pallas_call | solution.py:409
  217.8 24.0 %all_to_all.66.in_ref = bf16[16,32,128]{2,1,0:T(8,128)(2,1)} all-to-all(bf16[16,32,128]{2,1,0:T(8,128)(2,1)} %rows.1), channel_id=1, replica_groups=mesh['yh'=2,'xa'=2,'xb'=2,'co'=2,'yl'=2,'za'=2,'zb'=2,'zc'=2,'zd'=2] {'z..., dimensions={0} | all-to-all | bytes 262144 | tf_op jit(solution)/shard_map/all_to_all | solution.py:536
  241.8 18.7 %all_to_all.67 = f32[16,8,1536]{2,1,0:T(8,128)} all-to-all(f32[16,8,1536]{2,1,0:T(8,128)S(1)} %copy-done.3), channel_id=1, replica_groups=mesh['yh'=2,'xa'=2,'xb'=2,'co'=2,'yl'=2,'za'=2,'zb'=2,'zc'=2,'zd'=2] {'y..., dimensions={0} | all-to-all | bytes 1572864 | tf_op jit(solution)/shard_map/all_to_all | solution.py:526
  260.6 5.3 %all-to-all-start.10 = ((bf16[16,64,128]{2,1,0:T(8,128)(2,1)}), bf16[16,64,128]{2,1,0:T(8,128)(2,1)S(1)}, u32[]{:S(2)}, u32[]{:S(2)}) async-start(bf16[16,64,128]{2,1,0:T(8,128)(2,1)} %columns.1), calls=%async_computation.10 | async-start | bytes 524288 | tf_op jit(solution)/shard_map/all_to_all | solution.py:525
  268.7 3.2 %weights.1 = f32[512,1024]{1,0:T(8,128)} custom-call(f32[128,1536]{1,0:T(8,128)} %bitcast.20), custom_call_target="tpu_custom_call" | custom-call | flops 402653184 | bytes 3000000 | tf_op jit(solution)/shard_map/weights/pallas_call | solution.py:409
  271.9 12.2 %all-to-all-done.10.in_ref = bf16[16,64,128]{2,1,0:T(8,128)(2,1)S(1)} async-done(((bf16[16,64,128]{2,1,0:T(8,128)(2,1)}), bf16[16,64,128]{2,1,0:T(8,128)(2,1)S(1)}, u32[]{:S(2)}, u32[]{:S(2)}) %all-to-all-start.10) | async-done | bytes 262176 | tf_op jit(solution)/shard_map/all_to_all | solution.py:525
  284.8 1.8 unpack_pair.1
  (28 shorter events, 13.3 us)
Async XLA Ops:
  5.0 47.1 %all-to-all-start = ((bf16[16,112,128]{2,1,0:T(8,128)(2,1)}), bf16[16,112,128]{2,1,0:T(8,128)(2,1)S(1)}, u32[]{:S(2)}, u32[]{:S(2)}) async-start(bf16[16,112,128]{2,1,0:T(8,128)(2,1)} %pack.1), calls=%async_computation | async-start | bytes 917504 | tf_op jit(solution)/shard_map/all_to_all | solution.py:443
  19.7 3.1 %collective-permute-start = (bf16[16,1152]{1,0:T(8,128)(2,1)S(1)}, bf16[16,1152]{1,0:T(8,128)(2,1)S(1)}, u32[]{:S(2)}, u32[]{:S(2)}) collective-permute-start(bf16[16,1152]{1,0:T(8,128)(2,1)S(1)} %fusion.1), channel_id=1, source_target_pairs={{0,32},{32,0},{1,33},{33,1},{2,34},{34,2},{3,35},{35,3},{4,36},{36... | collective-permute-start | bytes 110600 | tf_op jit(solution)/shard_map/ppermute | solution.py:59
  22.8 6.2 %collective-permute-start.1 = (bf16[32,1152]{1,0:T(8,128)(2,1)S(1)}, bf16[32,1152]{1,0:T(8,128)(2,1)S(1)}, u32[]{:S(2)}, u32[]{:S(2)}) collective-permute-start(bf16[32,1152]{1,0:T(8,128)(2,1)S(1)} %maximum_select_fusion.3), channel_id=1, source_target_pairs={{0,64},{64,0},{1,65},{65,1},{2,66},{66,2},{3,67},{67,3},{4,68},{68... | collective-permute-start | bytes 221192 | tf_op jit(solution)/shard_map/ppermute | solution.py:59
  29.1 8.5 %collective-permute-start.2 = (bf16[64,1152]{1,0:T(8,128)(2,1)S(1)}, bf16[64,1152]{1,0:T(8,128)(2,1)S(1)}, u32[]{:S(2)}, u32[]{:S(2)}) collective-permute-start(bf16[64,1152]{1,0:T(8,128)(2,1)S(1)} %maximum_select_fusion.2), channel_id=1, source_target_pairs={{0,128},{128,0},{1,129},{129,1},{2,130},{130,2},{3,131},{131,3},{4... | collective-permute-start | bytes 442376 | tf_op jit(solution)/shard_map/ppermute | solution.py:59
  37.7 10.8 %collective-permute-start.3 = (bf16[128,1152]{1,0:T(8,128)(2,1)S(1)}, bf16[128,1152]{1,0:T(8,128)(2,1)S(1)}, u32[]{:S(2)}, u32[]{:S(2)}) collective-permute-start(bf16[128,1152]{1,0:T(8,128)(2,1)S(1)} %maximum_select_fusion.1), channel_id=1, source_target_pairs={{0,256},{256,0},{1,257},{257,1},{2,258},{258,2},{3,259},{259,3},{4... | collective-permute-start | bytes 884744 | tf_op jit(solution)/shard_map/ppermute | solution.py:59
  52.1 15.8 %copy-start = (bf16[16,112,128]{2,1,0:T(8,128)(2,1)}, bf16[16,112,128]{2,1,0:T(8,128)(2,1)S(1)}, u32[]{:S(2)}) copy-start(bf16[16,112,128]{2,1,0:T(8,128)(2,1)S(1)} %all-to-all-done.own_ref) | copy-start | bytes 1376260
  133.5 17.4 %all-to-all-start.5 = ((bf16[4,1056,128]{2,1,0:T(8,128)(2,1)}), bf16[4,1056,128]{2,1,0:T(8,128)(2,1)S(1)}, u32[]{:S(2)}, u32[]{:S(2)}) async-start(bf16[4,1056,128]{2,1,0:T(8,128)(2,1)} %get-tuple-element.42), calls=%async_computation.5 | async-start | bytes 2162688 | tf_op jit(solution)/shard_map/all_to_all | solution.py:480
  150.9 22.1 %copy-start.1 = (bf16[4,1056,128]{2,1,0:T(8,128)(2,1)}, bf16[4,1056,128]{2,1,0:T(8,128)(2,1)S(1)}, u32[]{:S(2)}) copy-start(bf16[4,1056,128]{2,1,0:T(8,128)(2,1)S(1)} %all-to-all-done.5.y_ref) | copy-start | bytes 3244036
  184.8 20.4 %all-to-all-start.8 = ((f32[8,8,128]{2,1,0:T(8,128)}), f32[8,8,128]{2,1,0:T(8,128)S(1)}, u32[]{:S(2)}, u32[]{:S(2)}) async-start(f32[8,8,128]{2,1,0:T(8,128)} %get-tuple-element.49), calls=%async_computation.8 | async-start | bytes 65536 | tf_op jit(solution)/shard_map/all_to_all | solution.py:507
  205.2 0.6 copy-start.4
  207.6 34.2 %copy-start.3 = (f32[16,8,1536]{2,1,0:T(8,128)S(1)}, f32[16,8,1536]{2,1,0:T(8,128)}, u32[]{:S(2)}) copy-start(f32[16,8,1536]{2,1,0:T(8,128)} %get-tuple-element.61) | copy-start | bytes 2359300
  260.6 23.6 %all-to-all-start.10 = ((bf16[16,64,128]{2,1,0:T(8,128)(2,1)}), bf16[16,64,128]{2,1,0:T(8,128)(2,1)S(1)}, u32[]{:S(2)}, u32[]{:S(2)}) async-start(bf16[16,64,128]{2,1,0:T(8,128)(2,1)} %columns.1), calls=%async_computation.10 | async-start | bytes 524288 | tf_op jit(solution)/shard_map/all_to_all | solution.py:525
  284.2 0.7 copy-start.2

commit v3 on v2

v3 whole, which is shorter than its diff:
```python
import functools

import jax
import jax.numpy as jnp
from jax import lax
from jax.experimental import pallas as pl
from jax.experimental.pallas import tpu as pltpu
from jax.sharding import Mesh, PartitionSpec as P

HEAD_COUNT = 8
HEAD_DIM = 64
GROUPS = 8
DOCS = 16
MODEL = 1024
WIDTH = 512
ROWS = 128
HALF = 64
QUARTER = 1024
PLANE = 16
SCALE = HEAD_DIM ** (-0.5)

RECIPROCAL_TEMP = 20.0
GRADIENT_FACTOR = 64.0
NORM_EPS = 1e-06
QUERY_COUNT = 8192
EXACT = lax.Precision.HIGHEST

BF16 = jnp.bfloat16
F32 = jnp.float32

GRP = ("yh", "xa", "xb", "co")
SEQ = ("yl", "za", "zb", "zc", "zd")
ZED = ("za", "zb", "zc", "zd")
SQUARE = ("yl", "zd")
HEADS = ("za", "zb", "zc")
NT = (((1,), (1,)), ((), ()))
TN = (((0,), (0,)), ((), ()))

VMEM_BYTES = 56 << 20


def params():
    return pltpu.CompilerParams(vmem_limit_bytes=VMEM_BYTES)


def cost(flops, moved, exps=0):
    return pl.CostEstimate(flops=int(flops), bytes_accessed=int(moved), transcendentals=int(exps))


def share(value, axes):
    count = 2 ** len(axes)
    return lax.all_to_all(
        jnp.broadcast_to(value[None], (count,) + value.shape), axes, split_axis=0, concat_axis=0
    )


def swap(value, axes, flip):
    count = 2 ** len(axes)
    return lax.ppermute(value, axes, [(i, i ^ flip) for i in range(count)])


def gather_step(value, axis):
    other = swap(value, (axis,), 1)
    first = lax.axis_index(axis) == 0
    return jnp.where(
        first,
        jnp.concatenate([value, other], axis=0),
        jnp.concatenate([other, value], axis=0),
    )


def three(value):
    high = value.astype(BF16)
    rest = value - high.astype(F32)
    middle = rest.astype(BF16)
    low = (rest - middle.astype(F32)).astype(BF16)
    return high, middle, low


def stacked(value):
    parts = [part.astype(F32) for part in three(value)]
    parts.append(jnp.zeros_like(value))
    return jnp.concatenate(parts, axis=0).astype(BF16)


def folded(product):
    return (product[16:24] + product[8:16]) + product[0:8]


def column_of(values):
    row = lax.broadcasted_iota(jnp.int32, (GROUPS, 128), 0)
    out = jnp.full((GROUPS, 128), values[0])
    for n in range(1, GROUPS):
        out = jnp.where(row == n, values[n], out)
    return out


def member_of(position, lens_ref):
    ends = [lens_ref[0]]
    for n in range(1, GROUPS):
        ends.append(ends[-1] + lens_ref[n])
    last = column_of(ends)
    first = last - column_of([lens_ref[n] for n in range(GROUPS)])
    return ((position >= first[:, 0:1]) & (position < last[:, 0:1])).astype(F32)


def lengths_of(lens_ref):
    return column_of([lens_ref[n] for n in range(GROUPS)]).astype(F32)


def quarter_member(lens_ref, plane, half):
    row = lax.broadcasted_iota(jnp.int32, (GROUPS, QUARTER), 1)
    position = plane * (PLANE * ROWS) + (row >> 6) * ROWS + half * HALF + (row & 63)
    return member_of(position, lens_ref)


def local_member(lens_ref, first):
    return member_of(first + lax.broadcasted_iota(jnp.int32, (GROUPS, ROWS), 1), lens_ref)


def halves(packed):
    return jnp.concatenate([packed[:, :, 0:64], packed[:, :, 64:128]], axis=1)


def lanes(rows):
    return lax.broadcasted_iota(jnp.int32, (rows, 128), 1)


def pack_kernel(place_ref, lens_ref, q_ref, k_ref, v_ref, inputs_ref, out_ref):
    mine = local_member(lens_ref, place_ref[3]).astype(BF16)
    sums = jnp.dot(mine, inputs_ref[...], preferred_element_type=F32)
    high, middle, low = [part.astype(F32) for part in three(sums)]
    zero = jnp.zeros((GROUPS, HALF), F32)
    for head in range(HEAD_COUNT):
        cols = slice(head * HEAD_DIM, (head + 1) * HEAD_DIM)
        for half in range(2):
            rows = slice(half * HALF, (half + 1) * HALF)
            place = 2 * head + half
            out_ref[place, 0:64, :] = jnp.concatenate([k_ref[rows, cols], v_ref[rows, cols]], axis=1)
            query = q_ref[rows, cols] * jnp.asarray(SCALE, BF16)
            out_ref[place, 64:96, :] = jnp.concatenate([query[0:32], query[32:64]], axis=1)
            part = slice(place * HALF, (place + 1) * HALF)
            upper = jnp.concatenate([high[:, part], middle[:, part]], axis=1)
            lower = jnp.concatenate([low[:, part], zero], axis=1)
            out_ref[place, 96:112, :] = jnp.concatenate([upper, lower], axis=0).astype(BF16)


def unpack_kernel(in_ref, q_ref, k_ref):
    for pair in range(HEAD_COUNT // 2):
        cols = slice(pair * 128, (pair + 1) * 128)
        for half in range(2):
            rows = slice(half * HALF, (half + 1) * HALF)
            first, second = in_ref[4 * pair + half], in_ref[4 * pair + 2 + half]
            k_ref[rows, cols] = jnp.concatenate([first[:, 0:64], second[:, 0:64]], axis=1)
            q_ref[rows, cols] = jnp.concatenate([first[:, 64:128], second[:, 64:128]], axis=1)


BLOCK = 256
PARTS = BLOCK // 128


STEPS = QUARTER // BLOCK
KEYS = 4 * QUARTER


def forward_kernel(
    place_ref, lens_ref, own_ref, x_ref, prob_ref, y_ref, lse_ref, means_ref, q_s
):
    i = pl.program_id(0)

    @pl.when(i == 0)
    def start():
        queries = halves(own_ref[:, 64:96, :]).reshape(QUARTER, HEAD_DIM)
        q_s[...] = jnp.concatenate([queries, jnp.zeros_like(queries)], axis=1)

    rows = pl.ds(pl.multiple_of(i * BLOCK, BLOCK), BLOCK)
    scores = lax.dot_general(q_s[rows, :], x_ref[...], NT, preferred_element_type=F32)
    top = jnp.max(scores, axis=1, keepdims=True)
    grown = jnp.exp(scores - top)
    total = jnp.sum(grown, axis=1, keepdims=True)
    prob_ref[...] = (grown * (1.0 / total)).astype(BF16)
    mixed = jnp.dot(prob_ref[...], x_ref[...], preferred_element_type=F32).astype(BF16)
    y_ref[rows, :] = jnp.where(lanes(BLOCK) < 64, q_s[rows, :], mixed)
    log_total = top + jnp.log(total)
    for part in range(PARTS):
        square = jnp.broadcast_to(log_total[part * 128 : (part + 1) * 128], (128, 128))
        lse_ref[pl.ds(i * PARTS + part, 1), :] = jnp.transpose(square)[0:1, :]

    @pl.when(i == STEPS - 1)
    def finish():
        y_ref[QUARTER : QUARTER + 32, :] = stacked(lse_ref[...])
        member = quarter_member(lens_ref, place_ref[0], place_ref[1]).astype(BF16)
        attn_sums = jnp.dot(member, y_ref[0:QUARTER, :], preferred_element_type=F32)
        sums = jnp.sum(own_ref[:, 96:112, :].astype(F32), axis=0)
        input_sums = (sums[0:8] + pltpu.roll(sums[0:8], 64, 1)) + sums[8:16]
        means = jnp.where(lanes(GROUPS) < 64, input_sums, attn_sums) / lengths_of(lens_ref)
        means_ref[...] = jnp.broadcast_to(means[None], (2 * PLANE, GROUPS, 128))


def pool_kernel(means_ref, w_ref, pooled_ref, own_ref, means_out_ref):
    columns, heads = [], []
    for z in range(PLANE):
        both = means_ref[z] + means_ref[PLANE + z]
        columns.append(both[:, 0:64])
        if z % 2 == 0:
            heads.append(both[:, 64:128])
        else:
            heads[-1] = heads[-1] + both[:, 64:128]
    means = jnp.concatenate(heads, axis=1)
    projected = jnp.dot(stacked(means), w_ref[...], preferred_element_type=F32)
    pooled = jnp.concatenate(columns, axis=1) + folded(projected)
    pooled_ref[...] = jnp.broadcast_to(pooled[None], (DOCS, GROUPS, MODEL))
    own_ref[...] = pooled
    means_out_ref[...] = means


def prepare_kernel(place_ref, pooled_ref, w_ref, out_ref):
    head = place_ref[2]
    pooled = pooled_ref[...]
    norms = jnp.sqrt(jnp.sum(pooled * pooled, axis=1, keepdims=True) + NORM_EPS)
    unit = pooled / norms
    w_head = w_ref[pl.ds(pl.multiple_of(head * HEAD_DIM, HEAD_DIM), HEAD_DIM), :]
    w_twice = jnp.concatenate([w_head, w_head], axis=0)
    out_ref[0:8, :] = folded(
        lax.dot_general(stacked(unit), w_twice, NT, preferred_element_type=F32)
    )
    z = 2 * head + place_ref[1]
    part = unit[:, 0:64]
    for n in range(1, PLANE):
        part = jnp.where(z == n, unit[:, n * HALF : (n + 1) * HALF], part)
    out_ref[8:16, :] = jnp.concatenate([part, part], axis=1)
    out_ref[16:24, :] = jnp.broadcast_to(norms, (GROUPS, 128))


def query_kernel(query_ref, out_ref):
    query = query_ref[:, :MODEL].astype(F32)
    squares = lax.dot_general(
        jnp.ones((8, MODEL), F32), query * query, NT, precision=EXACT, preferred_element_type=F32
    )
    out_ref[0:8, :] = jnp.sqrt(squares + NORM_EPS)
    out_ref[8:16, :] = lax.dot_general(
        jnp.ones((8, 128), BF16), query_ref[:, MODEL:], NT, preferred_element_type=F32
    )


def loss_kernel(doc_ref, pooled_ref, query_ref, row_ref, w_ref, out_ref, weight_s):
    pooled = pooled_ref[...]
    norms = jnp.sqrt(jnp.sum(pooled * pooled, axis=1, keepdims=True) + NORM_EPS)
    unit = pooled / norms
    query = query_ref[:, :MODEL]
    scale = RECIPROCAL_TEMP / row_ref[0:1, :]
    logits = jnp.zeros((DOCS * GROUPS, 256), F32)
    for part in three(unit)[::-1]:
        logits = logits + lax.dot_general(part, query, NT, preferred_element_type=F32)
    logits = logits * scale
    grown = jnp.exp(logits)
    total = jnp.sum(grown, axis=0, keepdims=True)
    group = lax.broadcasted_iota(jnp.int32, logits.shape, 0)
    target = (group == row_ref[8:9, :].astype(jnp.int32)).astype(F32)
    losses = jnp.log(total) - jnp.sum(target * logits, axis=0, keepdims=True)
    loss = jnp.sum(losses, axis=1, keepdims=True)
    weight_s[...] = (grown / total - target) * (GRADIENT_FACTOR * scale)
    mine = pl.ds(pl.multiple_of(doc_ref[0] * GROUPS, GROUPS), GROUPS)
    grad = folded(jnp.dot(stacked(weight_s[mine, :]), query, preferred_element_type=F32))
    own = pooled_ref[mine, :]
    own_unit = own / jnp.sqrt(jnp.sum(own * own, axis=1, keepdims=True) + NORM_EPS)
    along = jnp.sum(own_unit * grad, axis=1, keepdims=True)
    spread = folded(
        lax.dot_general(stacked(grad), w_ref[...], NT, preferred_element_type=F32)
    )
    extra = jnp.where(lanes(GROUPS) < 64, along, loss)
    for z in range(PLANE):
        head = z // 2
        chunk = jnp.concatenate(
            [
                spread[:, head * HEAD_DIM : (head + 1) * HEAD_DIM],
                grad[:, z * HALF : (z + 1) * HALF],
            ],
            axis=1,
        )
        for plane in range(2):
            out_ref[plane * PLANE + z, 0:8, :] = chunk
            out_ref[plane * PLANE + z, 8:16, :] = extra


def mass_kernel(lens_ref, own_ref, y_ref, prob_ref, mass_ref, k_s, lse_s, member_s):
    i = pl.program_id(0)

    @pl.when(i == 0)
    def start():
        mine = own_ref[:, 0:64, :].reshape(QUARTER, 128)
        k_s[...] = jnp.where(lanes(QUARTER) < 64, mine, jnp.zeros_like(mine))
        for n in range(4):
            lse = y_ref[n * (QUARTER + 32) + QUARTER : (n + 1) * (QUARTER + 32), :].astype(F32)
            lse = (lse[16:24] + lse[8:16]) + lse[0:8]
            for part in range(8):
                at = n * QUARTER + part * 128
                lse_s[:, at : at + 128] = jnp.broadcast_to(lse[part : part + 1, :], (8, 128))
            member = quarter_member(lens_ref, n // 2, n % 2)
            padded = jnp.concatenate([member, jnp.zeros((120, QUARTER), F32)], axis=0)
            member_s[:, n * QUARTER : (n + 1) * QUARTER] = padded.astype(BF16)

    rows = pl.ds(pl.multiple_of(i * BLOCK, BLOCK), BLOCK)
    sums = jnp.zeros((BLOCK, 128), F32)
    for n in range(4):
        cols = slice(n * QUARTER, (n + 1) * QUARTER)
        other = y_ref[n * (QUARTER + 32) : n * (QUARTER + 32) + QUARTER, :]
        scores = lax.dot_general(k_s[rows, :], other, NT, preferred_element_type=F32)
        prob_ref[:, cols] = jnp.exp(scores - lse_s[0:1, cols]).astype(BF16)
        sums = sums + lax.dot_general(
            prob_ref[:, cols], member_s[:, cols], NT, preferred_element_type=F32
        )
    for part in range(PARTS):
        mass_ref[i * PARTS + part] = jnp.transpose(sums[part * 128 : (part + 1) * 128])[0:8, :]


def group_kernel(lens_ref, terms_ref, ready_ref, mass_ref, dattn_ref, grad_ref, loss_ref):
    sums = terms_ref[0]
    for n in range(1, 2 * PLANE):
        sums = sums + terms_ref[n]
    along = sums[8:16, 0:1]
    loss_ref[...] = sums[8:16, :] / QUERY_COUNT
    norms = ready_ref[16:24, :]
    raw = jnp.concatenate([sums[0:8, 0:64], sums[0:8, 0:64]], axis=1)
    dattn_ref[...] = (raw - ready_ref[0:8, :] * along) / norms / lengths_of(lens_ref)
    grad = (sums[0:8, 64:128] - ready_ref[8:16, 0:64] * along) / norms[:, 0:64]
    for z in range(PLANE):
        half = (z % 2) * HALF
        grad_ref[z] = jnp.concatenate([grad, mass_ref[z // 2, :, half : half + HALF]], axis=1)


def inputs_kernel(place_ref, lens_ref, parts_ref, means_ref, grad_inputs_ref, out_ref):
    grad = jnp.concatenate([parts_ref[z, :, 0:64] for z in range(PLANE)], axis=1)
    mine = local_member(lens_ref, place_ref[3])
    members = jnp.concatenate([mine, mine, mine, mine], axis=0).astype(BF16)
    grad_inputs_ref[...] = lax.dot_general(
        members, stacked(grad / lengths_of(lens_ref)[:, 0:1]), TN, preferred_element_type=F32
    ).astype(BF16)
    both = jnp.concatenate([grad, means_ref[...]], axis=1)
    out_ref[...] = jnp.broadcast_to(both[None], (DOCS, GROUPS, MODEL + WIDTH))


def value_kernel(lens_ref, parts_ref, w_ref, grad_v_ref):
    grad = jnp.concatenate([parts_ref[z, :, 0:64] for z in range(PLANE)], axis=1)
    grad = grad / lengths_of(lens_ref)[:, 0:1]
    dattn = folded(lax.dot_general(stacked(grad), w_ref[...], NT, preferred_element_type=F32))
    dattn = dattn.astype(BF16).astype(F32)
    dattn = jnp.concatenate([dattn, dattn, dattn, jnp.zeros_like(dattn)], axis=0).astype(BF16)
    for pair in range(HEAD_COUNT // 2):
        cols = slice(pair * 128, (pair + 1) * 128)
        both = []
        for head in (2 * pair, 2 * pair + 1):
            mass = jnp.concatenate(
                [parts_ref[2 * head, :, 64:128], parts_ref[2 * head + 1, :, 64:128]], axis=1
            )
            both.append(
                lax.dot_general(stacked(mass), dattn[:, cols], TN, preferred_element_type=F32)
            )
        grad_v_ref[:, cols] = jnp.where(lanes(ROWS) < 64, both[0], both[1]).astype(BF16)


def weight_kernel(in_ref, out_ref):
    grads = three(in_ref[:, :MODEL])
    means = three(in_ref[:, MODEL:])
    out_ref[...] = lax.dot_general(
        jnp.concatenate([means[1], means[0], means[0]], axis=0),
        jnp.concatenate([grads[0], grads[1], grads[0]], axis=0),
        TN,
        preferred_element_type=F32,
    )


def row_kernel(place_ref, lens_ref, prob_ref, y_ref, x_ref, dattn_ref, out_ref, d_s, delta_s):
    i = pl.program_id(0)

    @pl.when(i == 0)
    def start():
        member = quarter_member(lens_ref, place_ref[0], place_ref[1]).astype(BF16)
        spread = lax.dot_general(
            member, dattn_ref[...].astype(BF16), TN, preferred_element_type=F32
        )
        spread = jnp.where(lanes(QUARTER) < 64, 0.0, spread)
        d_s[...] = spread.astype(BF16)
        delta_s[...] = jnp.broadcast_to(
            jnp.sum(spread * y_ref[0:QUARTER, :].astype(F32), axis=1, keepdims=True),
            (QUARTER, 128),
        )

    rows = pl.ds(pl.multiple_of(i * BLOCK, BLOCK), BLOCK)
    prob_grad = lax.dot_general(d_s[rows, :], x_ref[...], NT, preferred_element_type=F32)
    score_grad = (prob_ref[...].astype(F32) * (prob_grad - delta_s[rows, 0:1])).astype(BF16)
    for_query = jnp.dot(score_grad, x_ref[...], preferred_element_type=F32) * SCALE
    out_ref[rows, :] = jnp.concatenate([for_query[:, 0:64]] * 2, axis=1).astype(BF16)


def column_kernel(
    lens_ref, prob_ref, own_ref, y_ref, dattn_ref, grad_q_ref, out_ref, y_s, v_s, delta_s
):
    i = pl.program_id(0)

    @pl.when(i == 0)
    def start():
        lane = lanes(QUARTER)
        mine = own_ref[:, 0:64, :].reshape(QUARTER, 128)
        v_s[...] = jnp.where(lane < 64, jnp.zeros_like(mine), mine)
        dattn = dattn_ref[...].astype(BF16)
        ones = jnp.ones((8, 128), F32)
        for n in range(4):
            rows = slice(n * QUARTER, (n + 1) * QUARTER)
            member = quarter_member(lens_ref, n // 2, n % 2).astype(BF16)
            spread = lax.dot_general(member, dattn, TN, preferred_element_type=F32)
            spread = jnp.where(lane < 64, 0.0, spread)
            other = y_ref[n * (QUARTER + 32) : n * (QUARTER + 32) + QUARTER, :]
            y_s[rows, :] = jnp.where(lane < 64, other, spread.astype(BF16))
            delta_s[:, rows] = lax.dot_general(
                ones, spread * other.astype(F32), NT, precision=EXACT, preferred_element_type=F32
            )

    rows = pl.ds(pl.multiple_of(i * BLOCK, BLOCK), BLOCK)
    prob_grad = lax.dot_general(v_s[rows, :], y_s[...], NT, preferred_element_type=F32)
    score_grad = (prob_ref[...].astype(F32) * (prob_grad - delta_s[0:1, :])).astype(BF16)
    for_key = jnp.dot(score_grad, y_s[...], preferred_element_type=F32).astype(BF16)
    both = jnp.where(lanes(BLOCK) < 64, for_key, grad_q_ref[rows, :])
    count = BLOCK // HALF
    out_ref[pl.ds(i * count, count), :, :] = both.reshape(count, HALF, 128)


SMEM = pl.BlockSpec(memory_space=pltpu.SMEM)
VMEM = pl.BlockSpec(memory_space=pltpu.VMEM)


def call(kernel, outs, scalars, arrays, scratch, estimate, name):
    return pl.pallas_call(
        kernel,
        out_shape=outs,
        in_specs=[SMEM] * len(scalars) + [VMEM] * len(arrays),
        out_specs=jax.tree.map(lambda _: VMEM, outs),
        scratch_shapes=scratch,
        compiler_params=params(),
        cost_estimate=estimate,
        name=name,
    )(*scalars, *arrays)


def whole(array):
    rank = len(array.shape)
    return pl.BlockSpec(array.shape, lambda i: (0,) * rank)


PROB = pl.BlockSpec((BLOCK, KEYS), lambda i: (i, 0))


def sweep(kernel, outs, scalars, arrays, scratch, estimate, name):
    def spec(array):
        return PROB if array.shape == (QUARTER, KEYS) else whole(array)

    return pl.pallas_call(
        kernel,
        out_shape=outs,
        grid=(STEPS,),
        in_specs=[SMEM] * len(scalars) + [spec(array) for array in arrays],
        out_specs=jax.tree.map(spec, outs),
        scratch_shapes=scratch,
        compiler_params=params(),
        cost_estimate=estimate,
        name=name,
    )(*scalars, *arrays)


def shape(dims, dtype):
    return jax.ShapeDtypeStruct(dims, dtype)


def body(inputs, q_heads, k_heads, v_heads, w_out, group_lens, query_emb, positive):
    plane = lax.axis_index("yl")
    half = lax.axis_index("zd")
    head = lax.axis_index(HEADS)
    first = lax.axis_index(SEQ) * ROWS
    doc = lax.axis_index(GRP).reshape(1).astype(jnp.int32)
    place = jnp.stack([plane, half, head, first]).astype(jnp.int32)
    lengths = group_lens[0]
    exchange = functools.partial(lax.all_to_all, split_axis=0, concat_axis=0)
    barrier = lax.optimization_barrier
    pairs = QUARTER * KEYS

    packed = call(
        pack_kernel, shape((PLANE, 112, 128), BF16), (place, lengths),
        (q_heads[0], k_heads[0], v_heads[0], inputs[0]), (), cost(0, 1000000), "pack",
    )
    tagged = jnp.concatenate(
        [query_emb, jnp.pad(positive.astype(BF16)[:, None], ((0, 0), (0, 127)))], axis=1
    )
    packed, tagged = barrier((packed, tagged))
    own = exchange(packed, ZED)
    queries = gather_step(gather_step(gather_step(tagged, "co"), "xb"), "xa")
    own, queries = barrier((own, queries))
    keys = share(own[:, 0:64, :], SQUARE).reshape(KEYS, 128)

    prob, mine, lse, means = sweep(
        forward_kernel,
        (
            shape((QUARTER, KEYS), BF16),
            shape((QUARTER + 32, 128), BF16),
            shape((8, 128), F32),
            shape((2 * PLANE, GROUPS, 128), F32),
        ),
        (place, lengths), (own, keys), [pltpu.VMEM((QUARTER, 128), BF16)],
        cost(pairs * 256 * 4, 11000000, pairs), "forward",
    )
    mine, means, queries = barrier((mine, means, queries))
    means = exchange(means, SEQ)
    queries = gather_step(queries, "yh")
    around = [swap(mine, SQUARE, flip) for flip in (1, 2, 3)]
    means, queries, around = barrier((means, queries, around))
    pooled, pooled_own, doc_means = call(
        pool_kernel,
        (
            shape((DOCS, GROUPS, MODEL), F32),
            shape((GROUPS, MODEL), F32),
            shape((GROUPS, WIDTH), F32),
        ),
        (), (means, w_out), (), cost(2 * 32 * 512 * 1024, 1200000), "pool",
    )
    pooled_all = exchange(pooled, GRP).reshape(DOCS * GROUPS, MODEL)
    square = [mine] + around
    rotated = [jnp.where(half == 0, square[n], square[n ^ 1]) for n in range(4)]
    ordered = [jnp.where(plane == 0, rotated[n], rotated[n ^ 2]) for n in range(4)]
    others = jnp.concatenate(ordered, axis=0)
    query_rows = call(
        query_kernel, shape((16, 256), F32), (), (queries,), (), cost(6 * 2 * 8 * 256 * 1024, 600000),
        "queries",
    )
    ready = call(
        prepare_kernel, shape((24, 128), F32), (place,), (pooled_own, w_out), (),
        cost(2 * 32 * 128 * 1024, 1200000), "prepare",
    )
    pooled_all, others, ready, query_rows = barrier((pooled_all, others, ready, query_rows))
    terms = call(
        loss_kernel, shape((2 * PLANE, 16, 128), F32), (doc,),
        (pooled_all, queries, query_rows, w_out), [pltpu.VMEM((DOCS * GROUPS, 256), F32)],
        cost(3 * 2 * 128 * 256 * 1024, 2500000, 40000), "loss",
    )
    terms, own, others = barrier((terms, own, others))
    terms = exchange(terms, SEQ)
    turned, mass = sweep(
        mass_kernel,
        (shape((QUARTER, KEYS), BF16), shape((GROUPS, 8, 128), F32)),
        (lengths,), (own, others),
        [
            pltpu.VMEM((QUARTER, 128), BF16),
            pltpu.VMEM((8, KEYS), F32),
            pltpu.VMEM((128, KEYS), BF16),
        ],
        cost(pairs * 256 * 4, 11000000, pairs), "mass",
    )
    terms, turned, mass = barrier((terms, turned, mass))

    dattn, grad_part, loss = call(
        group_kernel,
        (
            shape((GROUPS, 128), F32),
            shape((PLANE, GROUPS, 128), F32),
            shape((GROUPS, 128), F32),
        ),
        (lengths,), (terms, ready, mass), (), cost(0, 100000), "group",
    )
    mean_loss = loss[0, 64]
    grad_parts = exchange(grad_part, ZED)
    grad_rows = sweep(
        row_kernel, shape((QUARTER, 128), BF16), (place, lengths), (prob, mine, keys, dattn),
        [pltpu.VMEM((QUARTER, 128), BF16), pltpu.VMEM((QUARTER, 128), F32)],
        cost(pairs * 256 * 4, 11000000), "rows",
    )
    grad_inputs, grads = call(
        inputs_kernel,
        (shape((ROWS, MODEL), BF16), shape((DOCS, GROUPS, MODEL + WIDTH), F32)),
        (place, lengths), (grad_parts, doc_means), (), cost(2 * 32 * 128 * 1024, 1200000), "inputs",
    )
    grad_rows, grads = barrier((grad_rows, grads))
    all_grads = exchange(grads, GRP)
    packed_grads = sweep(
        column_kernel, shape((PLANE, HALF, 128), BF16), (lengths,),
        (turned, own, others, dattn, grad_rows),
        [
            pltpu.VMEM((KEYS, 128), BF16),
            pltpu.VMEM((QUARTER, 128), BF16),
            pltpu.VMEM((8, KEYS), F32),
        ],
        cost(pairs * 256 * 4, 11000000), "columns",
    )
    packed_grads, grad_parts = barrier((packed_grads, grad_parts))
    home = exchange(packed_grads, ZED)
    out = shape((ROWS, WIDTH), BF16)
    grad_v = call(
        value_kernel, out, (lengths,), (grad_parts, w_out), (), cost(2 * 32 * 512 * 1024, 1300000),
        "values",
    )
    grad_w_out = call(
        weight_kernel, shape((WIDTH, MODEL), F32), (),
        (all_grads.reshape(DOCS * GROUPS, MODEL + WIDTH),), (),
        cost(2 * 384 * 512 * 1024, 3000000), "weights",
    )
    grad_q, grad_k = call(
        unpack_kernel, (out, out), (), (home,), (), cost(0, 500000), "unpack"
    )
    return (mean_loss, grad_inputs[None], grad_q[None], grad_k[None], grad_v[None], grad_w_out)


def solution(mesh):
    fine = Mesh(mesh.devices.reshape((2,) * 9), GRP + SEQ)
    rows = P(GRP, SEQ, None)
    return jax.shard_map(
        body,
        mesh=fine,
        in_specs=(
            rows,
            rows,
            rows,
            rows,
            P(),
            P(GRP, None),
            P(GRP + SEQ, None),
            P(GRP + SEQ),
        ),
        out_specs=(P(), rows, rows, rows, rows, P()),
        check_vma=False,
    )
```

time: 288 us -> 236 us (0.82)
  blocking collectives: 136 us -> 15.8 us
  starting transfers between devices: 45.2 us -> 84 us
  waiting for transfers between devices: 37.1 us -> 59 us
  Pallas kernels: 61.6 us -> 66.2 us
    all_to_all x7 -> x0, blocking collectives: 120 us -> none  [the longest x1 24 us: body(): home_query = exchange(packed_query, ZED)]
    pallas_call x0 -> x4, Pallas kernels: none -> 40.4 us  [sweep(): pl.pallas_call(kernel, out_shape=outs, grid=(STEPS,), in_specs=[SMEM] * l...]
    pallas_call x15 -> x10, Pallas kernels: 61.6 us -> 25.8 us  [call(): pl.pallas_call(kernel, out_shape=outs, in_specs=[SMEM] * len(scalars) + [...]
    all_to_all x3 -> x6, starting transfers between devices: 15.1 us -> 45 us  [the longest x1 10.2 us: body(): terms = exchange(terms, SEQ)]
    all_to_all x3 -> x6, waiting for transfers between devices: 23.9 us -> 35.5 us  [the longest x1 11.1 us: body(): home = exchange(packed_grads, ZED)]
    ppermute x4 -> x7, starting transfers between devices: 15.3 us -> 24.3 us  [swap(): return lax.ppermute(value, axes, [(i, i ^ flip) for i in range(count)])]
    all_to_all x1, waiting for transfers between devices: 0.01 us -> 7.07 us  [body(): own = exchange(packed, ZED)]
    ppermute x4 -> x7, waiting for transfers between devices: 13.2 us -> 16.4 us  [swap(): return lax.ppermute(value, axes, [(i, i ^ flip) for i in range(count)])]
  transfers between devices with their start and end apart: 8 -> 14, of which waited for: 6 -> 12; matrix products, arithmetic and copies ran while one was open for 1% -> 1% of each run, Pallas kernels for 8% -> 16%
where the time goes in v3:
time: 236 us; the launch traced here: 234 us
  starting transfers between devices  84 us (36%)
  Pallas kernels  66.2 us (28%)
  waiting for transfers between devices  59 us (25%)
  blocking collectives  15.8 us (7%)
  local copies, waits for them, and re-layouts  4.44 us (2%)
  other arithmetic  4.24 us (2%)
    pallas_call x4, Pallas kernels, sweep(): pl.pallas_call(kernel, out_shape=outs, grid=(STEPS,), in_specs=[SMEM] * l...  40.4 us
    pallas_call x10, Pallas kernels, call(): pl.pallas_call(kernel, out_shape=outs, in_specs=[SMEM] * len(scalars) + [...  25.8 us
    ppermute x7, starting transfers between devices, swap(): return lax.ppermute(value, axes, [(i, i ^ flip) for i in range(count)])  24.3 us
    ppermute x7, waiting for transfers between devices, swap(): return lax.ppermute(value, axes, [(i, i ^ flip) for i in range(count)])  16.4 us
    all_to_all x1, blocking collectives, share(): lax.all_to_all(jnp.broadcast_to(value[None], (count,) + value.shape), axe...  15.8 us
    all_to_all x1, starting transfers between devices, body(): own = exchange(packed, ZED)  14.8 us
    all_to_all x1, waiting for transfers between devices, body(): home = exchange(packed_grads, ZED)  11.1 us
    all_to_all x1, starting transfers between devices, body(): terms = exchange(terms, SEQ)  10.2 us
  transfers between devices with their start and end apart: 14, of which 12 were waited for; matrix products, arithmetic and copies ran while one was open for 1% of the time, Pallas kernels for 16%

profile of v3, /device:TPU:64, one launch (start us, length us, event | category | flops | bytes accessed | tf_op | source)
XLA Modules:
  0.0 234.5 jit_solution(4664873077983843828)
XLA Ops:
  4.9 14.8 %all-to-all-start = ((bf16[16,112,128]{2,1,0:T(8,128)(2,1)}), bf16[16,112,128]{2,1,0:T(8,128)(2,1)S(1)}, u32[]{:S(2)}, u32[]{:S(2)}) async-start(bf16[16,112,128]{2,1,0:T(8,128)(2,1)} %pack.1), calls=%async_computation | async-start | bytes 917504 | tf_op jit(solution)/shard_map/all_to_all | solution.py:494
  22.8 3.4 %collective-permute-start.1 = (bf16[32,1152]{1,0:T(8,128)(2,1)S(1)}, bf16[32,1152]{1,0:T(8,128)(2,1)S(1)}, u32[]{:S(2)}, u32[]{:S(2)}) collective-permute-start(bf16[32,1152]{1,0:T(8,128)(2,1)S(1)} %maximum_select_fusion.3), channel_id=1, source_target_pairs={{0,64},{64,0},{1,65},{65,1},{2,66},{66,2},{3,67},{67,3},{4,68},{68... | collective-permute-start | bytes 221192 | tf_op jit(solution)/shard_map/ppermute | solution.py:59
  26.2 2.8 %collective-permute-done.1 = bf16[32,1152]{1,0:T(8,128)(2,1)S(1)} collective-permute-done((bf16[32,1152]{1,0:T(8,128)(2,1)S(1)}, bf16[32,1152]{1,0:T(8,128)(2,1)S(1)}, u32[]{:S(2)}, u32[]{:S(2)}) %collective-permute-start.1) | collective-permute-done | bytes 73760 | tf_op jit(solution)/shard_map/ppermute | solution.py:59
  29.1 4.9 %collective-permute-start.2 = (bf16[64,1152]{1,0:T(8,128)(2,1)S(1)}, bf16[64,1152]{1,0:T(8,128)(2,1)S(1)}, u32[]{:S(2)}, u32[]{:S(2)}) collective-permute-start(bf16[64,1152]{1,0:T(8,128)(2,1)S(1)} %maximum_select_fusion.2), channel_id=1, source_target_pairs={{0,128},{128,0},{1,129},{129,1},{2,130},{130,2},{3,131},{131,3},{4... | collective-permute-start | bytes 442376 | tf_op jit(solution)/shard_map/ppermute | solution.py:59
  34.0 3.6 %collective-permute-done.2 = bf16[64,1152]{1,0:T(8,128)(2,1)S(1)} collective-permute-done((bf16[64,1152]{1,0:T(8,128)(2,1)S(1)}, bf16[64,1152]{1,0:T(8,128)(2,1)S(1)}, u32[]{:S(2)}, u32[]{:S(2)}) %collective-permute-start.2) | collective-permute-done | bytes 147488 | tf_op jit(solution)/shard_map/ppermute | solution.py:59
  37.7 7.1 %all-to-all-done.own_ref = bf16[16,112,128]{2,1,0:T(8,128)(2,1)S(1)} async-done(((bf16[16,112,128]{2,1,0:T(8,128)(2,1)}), bf16[16,112,128]{2,1,0:T(8,128)(2,1)S(1)}, u32[]{:S(2)}, u32[]{:S(2)}) %all-to-all-start) | async-done | bytes 458784 | tf_op jit(solution)/shard_map/all_to_all | solution.py:494
  45.0 15.8 %all_to_all.40 = bf16[4,16,64,128]{3,2,1,0:T(8,128)(2,1)} all-to-all(bf16[4,16,64,128]{3,2,1,0:T(8,128)(2,1)S(1)} %broadcast_in_dim.22), channel_id=1, replica_groups=mesh['yh'=2,'xa'=2,'xb'=2,'co'=2,'yl'=2,'za'=2,'zb'=2,'zc'=2,'zd'=2] {'y..., dimensions={0} | all-to-all | bytes 2097152 | tf_op jit(solution)/shard_map/all_to_all | solution.py:52
  60.8 11.5 %forward.1 = (bf16[1024,4096]{1,0:T(8,128)(2,1)}, bf16[1056,128]{1,0:T(8,128)(2,1)}, f32[8,128]{1,0:T(8,128)}, f32[32,8,128]{2,1,0:T(8,128)}) custom-call(s32[4]{0:T(128)} %pad_add_fusion.place_ref, s32[8]{0:T(128)} %bitcast.30, bf16[16,112,128]{2,1,0:T(8,128)(2,1)} %copy-done.2, bf16[4096,128]{1,0:T(8,128)(2,1)} %bitcast.22), custom_call_target="tpu_custom_call" | custom-call | flops 4294967296 | bytes 11000000 | tf_op jit(solution)/shard_map/forward/pallas_call | solution.py:457
  72.3 4.8 %collective-permute-start.3 = (bf16[128,1152]{1,0:T(8,128)(2,1)S(1)}, bf16[128,1152]{1,0:T(8,128)(2,1)S(1)}, u32[]{:S(2)}, u32[]{:S(2)}) collective-permute-start(bf16[128,1152]{1,0:T(8,128)(2,1)S(1)} %maximum_select_fusion.1), channel_id=1, source_target_pairs={{0,256},{256,0},{1,257},{257,1},{2,258},{258,2},{3,259},{259,3},{4... | collective-permute-start | bytes 884744 | tf_op jit(solution)/shard_map/ppermute | solution.py:59
  77.1 9.6 %all-to-all-start.2 = ((f32[32,8,128]{2,1,0:T(8,128)}), f32[32,8,128]{2,1,0:T(8,128)S(1)}, u32[]{:S(2)}, u32[]{:S(2)}) async-start(f32[32,8,128]{2,1,0:T(8,128)} %get-tuple-element.53), calls=%async_computation.2 | async-start | bytes 262144 | tf_op jit(solution)/shard_map/all_to_all | solution.py:511
  86.7 4.3 %collective-permute-start.6 = (bf16[1056,128]{1,0:T(8,128)(2,1)}, bf16[1056,128]{1,0:T(8,128)(2,1)S(1)}, u32[]{:S(2)}, u32[]{:S(2)}) collective-permute-start(bf16[1056,128]{1,0:T(8,128)(2,1)} %get-tuple-element.55.y_ref), channel_id=1, source_target_pairs={{0,17},{1,16},{16,1},{17,0},{2,19},{3,18},{18,3},{19,2},{4,21},{5,... | collective-permute-start | bytes 811016 | tf_op jit(solution)/shard_map/ppermute | solution.py:59
  93.5 2.5 %collective-permute-start.4 = (bf16[1056,128]{1,0:T(8,128)(2,1)}, bf16[1056,128]{1,0:T(8,128)(2,1)S(1)}, u32[]{:S(2)}, u32[]{:S(2)}) collective-permute-start(bf16[1056,128]{1,0:T(8,128)(2,1)} %get-tuple-element.55.y_ref), channel_id=1, source_target_pairs={{0,1},{1,0},{16,17},{17,16},{2,3},{3,2},{18,19},{19,18},{4,5},{5,4... | collective-permute-start | bytes 811016 | tf_op jit(solution)/shard_map/ppermute | solution.py:59
  97.0 4.6 %collective-permute-done.6 = bf16[1056,128]{1,0:T(8,128)(2,1)S(1)} collective-permute-done((bf16[1056,128]{1,0:T(8,128)(2,1)}, bf16[1056,128]{1,0:T(8,128)(2,1)S(1)}, u32[]{:S(2)}, u32[]{:S(2)}) %collective-permute-start.6) | collective-permute-done | bytes 270368 | tf_op jit(solution)/shard_map/ppermute | solution.py:59
  101.5 2.8 %collective-permute-done.5 = bf16[1056,128]{1,0:T(8,128)(2,1)S(1)} collective-permute-done((bf16[1056,128]{1,0:T(8,128)(2,1)}, bf16[1056,128]{1,0:T(8,128)(2,1)S(1)}, u32[]{:S(2)}, u32[]{:S(2)}) %collective-permute-start.5) | collective-permute-done | bytes 270368 | tf_op jit(solution)/shard_map/ppermute | solution.py:59
  105.8 2.7 %queries.1.row_ref = f32[16,256]{1,0:T(8,128)} custom-call(bf16[256,1152]{1,0:T(8,128)(2,1)} %maximum_select_fusion.query_ref), custom_call_target="tpu_custom_call" | custom-call | flops 25165824 | bytes 600000 | tf_op jit(solution)/shard_map/queries/pallas_call | solution.py:433
  108.5 2.5 %pool.1 = (f32[16,8,1024]{2,1,0:T(8,128)}, f32[8,1024]{1,0:T(8,128)}, f32[8,512]{1,0:T(8,128)}) custom-call(f32[32,8,128]{2,1,0:T(8,128)} %copy-done.6, bf16[512,1024]{1,0:T(8,128)(2,1)} %w_ref.7), custom_call_target="tpu_custom_call" | custom-call | flops 33554432 | bytes 1200000 | tf_op jit(solution)/shard_map/pool/pallas_call | solution.py:433
  110.9 5.3 %all-to-all-start.3 = ((f32[16,8,1024]{2,1,0:T(8,128)}), f32[16,8,1024]{2,1,0:T(8,128)S(1)}, u32[]{:S(2)}, u32[]{:S(2)}) async-start(f32[16,8,1024]{2,1,0:T(8,128)} %get-tuple-element.57), calls=%async_computation.3 | async-start | bytes 1048576 | tf_op jit(solution)/shard_map/all_to_all | solution.py:524
  116.2 3.0 %prepare.1.ready_ref = f32[24,128]{1,0:T(8,128)} custom-call(s32[4]{0:T(128)} %pad_add_fusion.place_ref, f32[8,1024]{1,0:T(8,128)} %get-tuple-element.61.pooled_ref, bf16[512,1024]{1,0:T(8,128)(2,1)} %w_ref.7), custom_call_target="tpu_custom_call" | custom-call | flops 8388608 | bytes 1200000 | tf_op jit(solution)/shard_map/prepare/pallas_call | solution.py:433
  120.4 8.2 %all-to-all-done.3 = f32[16,8,1024]{2,1,0:T(8,128)S(1)} async-done(((f32[16,8,1024]{2,1,0:T(8,128)}), f32[16,8,1024]{2,1,0:T(8,128)S(1)}, u32[]{:S(2)}, u32[]{:S(2)}) %all-to-all-start.3) | async-done | bytes 524320 | tf_op jit(solution)/shard_map/all_to_all | solution.py:524
  129.4 4.1 %loss.1 = f32[32,16,128]{2,1,0:T(8,128)} custom-call(s32[1]{0:T(128)} %bitcast.1.doc_ref, f32[128,1024]{1,0:T(8,128)} %bitcast.21, bf16[256,1152]{1,0:T(8,128)(2,1)} %maximum_select_fusion.query_ref, f32[16,256]{1,0:T(8,128)} %queries.1.row_ref, bf16[512,1024]{1,0:T(8,128)(2,1)} %w_ref.7), custom_call_target="tpu_custom_call" | custom-call | flops 201326592 | bytes 2500000 | tf_op jit(solution)/shard_map/loss/pallas_call | solution.py:433
  133.5 10.2 %all-to-all-start.4 = ((f32[32,16,128]{2,1,0:T(8,128)}), f32[32,16,128]{2,1,0:T(8,128)S(1)}, u32[]{:S(2)}, u32[]{:S(2)}) async-start(f32[32,16,128]{2,1,0:T(8,128)} %loss.1), calls=%async_computation.4 | async-start | bytes 524288 | tf_op jit(solution)/shard_map/all_to_all | solution.py:544
  143.7 9.4 %mass.1 = (bf16[1024,4096]{1,0:T(8,128)(2,1)}, f32[8,8,128]{2,1,0:T(8,128)}) custom-call(s32[8]{0:T(128)} %bitcast.31, bf16[16,112,128]{2,1,0:T(8,128)(2,1)} %copy-done.2, bf16[4224,128]{1,0:T(8,128)(2,1)} %pad_maximum_fusion.y_ref), custom_call_target="tpu_custom_call" | custom-call | flops 4294967296 | bytes 11000000 | tf_op jit(solution)/shard_map/mass/pallas_call | solution.py:457
  153.0 9.7 %all-to-all-done.4.terms_ref = f32[32,16,128]{2,1,0:T(8,128)S(1)} async-done(((f32[32,16,128]{2,1,0:T(8,128)}), f32[32,16,128]{2,1,0:T(8,128)S(1)}, u32[]{:S(2)}, u32[]{:S(2)}) %all-to-all-start.4) | async-done | bytes 262176 | tf_op jit(solution)/shard_map/all_to_all | solution.py:544
  165.3 6.5 %all-to-all-start.5 = ((f32[16,8,128]{2,1,0:T(8,128)}), f32[16,8,128]{2,1,0:T(8,128)S(1)}, u32[]{:S(2)}, u32[]{:S(2)}) async-start(f32[16,8,128]{2,1,0:T(8,128)} %get-tuple-element.75), calls=%async_computation.5 | async-start | bytes 131072 | tf_op jit(solution)/shard_map/all_to_all | solution.py:568
  171.7 8.8 %rows.1.grad_q_ref = bf16[1024,128]{1,0:T(8,128)(2,1)} custom-call(s32[4]{0:T(128)} %pad_add_fusion.place_ref, s32[8]{0:T(128)} %bitcast.33, bf16[1024,4096]{1,0:T(8,128)(2,1)} %get-tuple-element.80.prob_ref, bf16[1056,128]{1,0:T(8,128)(2,1)} %get-tuple-element.55.y_ref, bf16[4096,128]{1,0:T(8,128)(2,1)} %bitcast.23, f32[8,128]{1,0:T(8,128)} %get-tuple-element.79.dattn_ref), custom_call_target="tpu_custom_call" | custom-call | flops 4294967296 | bytes 11000000 | tf_op jit(solution)/shard_map/rows/pallas_call | solution.py:457
  185.4 3.8 %all-to-all-start.7 = ((f32[16,8,1536]{2,1,0:T(8,128)}), f32[16,8,1536]{2,1,0:T(8,128)S(1)}, u32[]{:S(2)}, u32[]{:S(2)}) async-start(f32[16,8,1536]{2,1,0:T(8,128)} %get-tuple-element.87), calls=%async_computation.7 | async-start | bytes 1572864 | tf_op jit(solution)/shard_map/all_to_all | solution.py:580
  189.2 10.8 %columns.1 = bf16[16,64,128]{2,1,0:T(8,128)(2,1)} custom-call(s32[8]{0:T(128)} %bitcast.35, bf16[1024,4096]{1,0:T(8,128)(2,1)} %get-tuple-element.78.prob_ref, bf16[16,112,128]{2,1,0:T(8,128)(2,1)} %copy-done.2, bf16[4224,128]{1,0:T(8,128)(2,1)} %pad_maximum_fusion.y_ref, f32[8,128]{1,0:T(8,128)} %get-tuple-element.79.dattn_ref, ...), custom_call_target="tpu_custom_call" | custom-call | flops 4294967296 | bytes 11000000 | tf_op jit(solution)/shard_map/columns/pallas_call | solution.py:457
  200.0 4.2 %all-to-all-done.7 = f32[16,8,1536]{2,1,0:T(8,128)S(1)} async-done(((f32[16,8,1536]{2,1,0:T(8,128)}), f32[16,8,1536]{2,1,0:T(8,128)S(1)}, u32[]{:S(2)}, u32[]{:S(2)}) %all-to-all-start.7) | async-done | bytes 786464 | tf_op jit(solution)/shard_map/all_to_all | solution.py:580
  204.2 9.7 %all-to-all-start.6 = ((bf16[16,64,128]{2,1,0:T(8,128)(2,1)}), bf16[16,64,128]{2,1,0:T(8,128)(2,1)S(1)}, u32[]{:S(2)}, u32[]{:S(2)}) async-start(bf16[16,64,128]{2,1,0:T(8,128)(2,1)} %columns.1), calls=%async_computation.6 | async-start | bytes 524288 | tf_op jit(solution)/shard_map/all_to_all | solution.py:592
  215.2 2.6 %values.1 = bf16[128,512]{1,0:T(8,128)(2,1)} custom-call(s32[8]{0:T(128)} %bitcast.36, f32[16,8,128]{2,1,0:T(8,128)} %copy-done.5, bf16[512,1024]{1,0:T(8,128)(2,1)} %w_ref.7), custom_call_target="tpu_custom_call" | custom-call | flops 33554432 | bytes 1300000 | tf_op jit(solution)/shard_map/values/pallas_call | solution.py:433
  217.7 3.2 %weights.1 = f32[512,1024]{1,0:T(8,128)} custom-call(f32[128,1536]{1,0:T(8,128)} %bitcast.20), custom_call_target="tpu_custom_call" | custom-call | flops 402653184 | bytes 3000000 | tf_op jit(solution)/shard_map/weights/pallas_call | solution.py:433
  220.9 11.1 %all-to-all-done.6.in_ref = bf16[16,64,128]{2,1,0:T(8,128)(2,1)S(1)} async-done(((bf16[16,64,128]{2,1,0:T(8,128)(2,1)}), bf16[16,64,128]{2,1,0:T(8,128)(2,1)S(1)}, u32[]{:S(2)}, u32[]{:S(2)}) %all-to-all-start.6) | async-done | bytes 262176 | tf_op jit(solution)/shard_map/all_to_all | solution.py:592
  (40 shorter events, 25.7 us)
Async XLA Ops:
  4.9 39.8 %all-to-all-start = ((bf16[16,112,128]{2,1,0:T(8,128)(2,1)}), bf16[16,112,128]{2,1,0:T(8,128)(2,1)S(1)}, u32[]{:S(2)}, u32[]{:S(2)}) async-start(bf16[16,112,128]{2,1,0:T(8,128)(2,1)} %pack.1), calls=%async_computation | async-start | bytes 917504 | tf_op jit(solution)/shard_map/all_to_all | solution.py:494
  19.7 3.1 %collective-permute-start = (bf16[16,1152]{1,0:T(8,128)(2,1)S(1)}, bf16[16,1152]{1,0:T(8,128)(2,1)S(1)}, u32[]{:S(2)}, u32[]{:S(2)}) collective-permute-start(bf16[16,1152]{1,0:T(8,128)(2,1)S(1)} %fusion.1), channel_id=1, source_target_pairs={{0,32},{32,0},{1,33},{33,1},{2,34},{34,2},{3,35},{35,3},{4,36},{36... | collective-permute-start | bytes 110600 | tf_op jit(solution)/shard_map/ppermute | solution.py:59
  22.8 6.2 %collective-permute-start.1 = (bf16[32,1152]{1,0:T(8,128)(2,1)S(1)}, bf16[32,1152]{1,0:T(8,128)(2,1)S(1)}, u32[]{:S(2)}, u32[]{:S(2)}) collective-permute-start(bf16[32,1152]{1,0:T(8,128)(2,1)S(1)} %maximum_select_fusion.3), channel_id=1, source_target_pairs={{0,64},{64,0},{1,65},{65,1},{2,66},{66,2},{3,67},{67,3},{4,68},{68... | collective-permute-start | bytes 221192 | tf_op jit(solution)/shard_map/ppermute | solution.py:59
  29.1 8.5 %collective-permute-start.2 = (bf16[64,1152]{1,0:T(8,128)(2,1)S(1)}, bf16[64,1152]{1,0:T(8,128)(2,1)S(1)}, u32[]{:S(2)}, u32[]{:S(2)}) collective-permute-start(bf16[64,1152]{1,0:T(8,128)(2,1)S(1)} %maximum_select_fusion.2), channel_id=1, source_target_pairs={{0,128},{128,0},{1,129},{129,1},{2,130},{130,2},{3,131},{131,3},{4... | collective-permute-start | bytes 442376 | tf_op jit(solution)/shard_map/ppermute | solution.py:59
  44.7 16.1 %copy-start.2 = (bf16[16,112,128]{2,1,0:T(8,128)(2,1)}, bf16[16,112,128]{2,1,0:T(8,128)(2,1)S(1)}, u32[]{:S(2)}) copy-start(bf16[16,112,128]{2,1,0:T(8,128)(2,1)S(1)} %all-to-all-done.own_ref) | copy-start | bytes 1376260
  72.3 23.7 %collective-permute-start.3 = (bf16[128,1152]{1,0:T(8,128)(2,1)S(1)}, bf16[128,1152]{1,0:T(8,128)(2,1)S(1)}, u32[]{:S(2)}, u32[]{:S(2)}) collective-permute-start(bf16[128,1152]{1,0:T(8,128)(2,1)S(1)} %maximum_select_fusion.1), channel_id=1, source_target_pairs={{0,256},{256,0},{1,257},{257,1},{2,258},{258,2},{3,259},{259,3},{4... | collective-permute-start | bytes 884744 | tf_op jit(solution)/shard_map/ppermute | solution.py:59
  77.1 28.7 %all-to-all-start.2 = ((f32[32,8,128]{2,1,0:T(8,128)}), f32[32,8,128]{2,1,0:T(8,128)S(1)}, u32[]{:S(2)}, u32[]{:S(2)}) async-start(f32[32,8,128]{2,1,0:T(8,128)} %get-tuple-element.53), calls=%async_computation.2 | async-start | bytes 262144 | tf_op jit(solution)/shard_map/all_to_all | solution.py:511
  86.7 14.8 %collective-permute-start.6 = (bf16[1056,128]{1,0:T(8,128)(2,1)}, bf16[1056,128]{1,0:T(8,128)(2,1)S(1)}, u32[]{:S(2)}, u32[]{:S(2)}) collective-permute-start(bf16[1056,128]{1,0:T(8,128)(2,1)} %get-tuple-element.55.y_ref), channel_id=1, source_target_pairs={{0,17},{1,16},{16,1},{17,0},{2,19},{3,18},{18,3},{19,2},{4,21},{5,... | collective-permute-start | bytes 811016 | tf_op jit(solution)/shard_map/ppermute | solution.py:59
  91.0 13.4 %collective-permute-start.5 = (bf16[1056,128]{1,0:T(8,128)(2,1)}, bf16[1056,128]{1,0:T(8,128)(2,1)S(1)}, u32[]{:S(2)}, u32[]{:S(2)}) collective-permute-start(bf16[1056,128]{1,0:T(8,128)(2,1)} %get-tuple-element.55.y_ref), channel_id=1, source_target_pairs={{0,16},{1,17},{16,0},{17,1},{2,18},{3,19},{18,2},{19,3},{4,20},{5,... | collective-permute-start | bytes 811016 | tf_op jit(solution)/shard_map/ppermute | solution.py:59
  93.5 12.3 %collective-permute-start.4 = (bf16[1056,128]{1,0:T(8,128)(2,1)}, bf16[1056,128]{1,0:T(8,128)(2,1)S(1)}, u32[]{:S(2)}, u32[]{:S(2)}) collective-permute-start(bf16[1056,128]{1,0:T(8,128)(2,1)} %get-tuple-element.55.y_ref), channel_id=1, source_target_pairs={{0,1},{1,0},{16,17},{17,16},{2,3},{3,2},{18,19},{19,18},{4,5},{5,4... | collective-permute-start | bytes 811016 | tf_op jit(solution)/shard_map/ppermute | solution.py:59
  105.8 2.7 %copy-start.6 = (f32[32,8,128]{2,1,0:T(8,128)}, f32[32,8,128]{2,1,0:T(8,128)S(1)}, u32[]{:S(2)}) copy-start(f32[32,8,128]{2,1,0:T(8,128)S(1)} %all-to-all-done.2.means_ref) | copy-start | bytes 393220
  110.9 8.3 %copy-start.7 = (bf16[1056,128]{1,0:T(8,128)(2,1)S(1)}, bf16[1056,128]{1,0:T(8,128)(2,1)}, u32[]{:S(2)}) copy-start(bf16[1056,128]{1,0:T(8,128)(2,1)} %get-tuple-element.55.y_ref) | copy-start | bytes 811012
  110.9 17.6 %all-to-all-start.3 = ((f32[16,8,1024]{2,1,0:T(8,128)}), f32[16,8,1024]{2,1,0:T(8,128)S(1)}, u32[]{:S(2)}, u32[]{:S(2)}) async-start(f32[16,8,1024]{2,1,0:T(8,128)} %get-tuple-element.57), calls=%async_computation.3 | async-start | bytes 1048576 | tf_op jit(solution)/shard_map/all_to_all | solution.py:524
  128.6 0.8 copy-start.1
  133.5 29.2 %all-to-all-start.4 = ((f32[32,16,128]{2,1,0:T(8,128)}), f32[32,16,128]{2,1,0:T(8,128)S(1)}, u32[]{:S(2)}, u32[]{:S(2)}) async-start(f32[32,16,128]{2,1,0:T(8,128)} %loss.1), calls=%async_computation.4 | async-start | bytes 524288 | tf_op jit(solution)/shard_map/all_to_all | solution.py:544
  162.7 0.7 copy-start.4
  165.3 17.6 %all-to-all-start.5 = ((f32[16,8,128]{2,1,0:T(8,128)}), f32[16,8,128]{2,1,0:T(8,128)S(1)}, u32[]{:S(2)}, u32[]{:S(2)}) async-start(f32[16,8,128]{2,1,0:T(8,128)} %get-tuple-element.75), calls=%async_computation.5 | async-start | bytes 131072 | tf_op jit(solution)/shard_map/all_to_all | solution.py:568
  182.8 0.6 copy-start.5
  185.4 18.8 %all-to-all-start.7 = ((f32[16,8,1536]{2,1,0:T(8,128)}), f32[16,8,1536]{2,1,0:T(8,128)S(1)}, u32[]{:S(2)}, u32[]{:S(2)}) async-start(f32[16,8,1536]{2,1,0:T(8,128)} %get-tuple-element.87), calls=%async_computation.7 | async-start | bytes 1572864 | tf_op jit(solution)/shard_map/all_to_all | solution.py:580
  204.2 13.6 %copy-start = (f32[16,8,1536]{2,1,0:T(8,128)}, f32[16,8,1536]{2,1,0:T(8,128)S(1)}, u32[]{:S(2)}) copy-start(f32[16,8,1536]{2,1,0:T(8,128)S(1)} %all-to-all-done.7) | copy-start | bytes 2359300
  204.2 27.9 %all-to-all-start.6 = ((bf16[16,64,128]{2,1,0:T(8,128)(2,1)}), bf16[16,64,128]{2,1,0:T(8,128)(2,1)S(1)}, u32[]{:S(2)}, u32[]{:S(2)}) async-start(bf16[16,64,128]{2,1,0:T(8,128)(2,1)} %columns.1), calls=%async_computation.6 | async-start | bytes 524288 | tf_op jit(solution)/shard_map/all_to_all | solution.py:592
  232.0 0.7 copy-start.3

commit v4 on v3

v4 whole, which is shorter than its diff:
```python
import functools

import jax
import jax.numpy as jnp
from jax import lax
from jax.experimental import pallas as pl
from jax.experimental.pallas import tpu as pltpu
from jax.sharding import Mesh, PartitionSpec as P

HEAD_COUNT = 8
HEAD_DIM = 64
GROUPS = 8
DOCS = 16
MODEL = 1024
WIDTH = 512
ROWS = 128
HALF = 64
QUARTER = 1024
PLANE = 16
SCALE = HEAD_DIM ** (-0.5)

RECIPROCAL_TEMP = 20.0
GRADIENT_FACTOR = 64.0
NORM_EPS = 1e-06
QUERY_COUNT = 8192
EXACT = lax.Precision.HIGHEST

BF16 = jnp.bfloat16
F32 = jnp.float32

GRP = ("yh", "xa", "xb", "co")
SEQ = ("yl", "za", "zb", "zc", "zd")
ZED = ("za", "zb", "zc", "zd")
SQUARE = ("yl", "zd")
HEADS = ("za", "zb", "zc")
NT = (((1,), (1,)), ((), ()))
TN = (((0,), (0,)), ((), ()))

VMEM_BYTES = 56 << 20


def params():
    return pltpu.CompilerParams(vmem_limit_bytes=VMEM_BYTES)


def cost(flops, moved, exps=0):
    return pl.CostEstimate(flops=int(flops), bytes_accessed=int(moved), transcendentals=int(exps))


def share(value, axes):
    count = 2 ** len(axes)
    return lax.all_to_all(
        jnp.broadcast_to(value[None], (count,) + value.shape), axes, split_axis=0, concat_axis=0
    )


def swap(value, axes, flip):
    count = 2 ** len(axes)
    return lax.ppermute(value, axes, [(i, i ^ flip) for i in range(count)])


def gather_grp(value):
    for axis in GRP:
        other = swap(value, (axis,), 1)
        first = lax.axis_index(axis) == 0
        value = jnp.where(
            first,
            jnp.concatenate([value, other], axis=0),
            jnp.concatenate([other, value], axis=0),
        )
    return value


def three(value):
    high = value.astype(BF16)
    rest = value - high.astype(F32)
    middle = rest.astype(BF16)
    low = (rest - middle.astype(F32)).astype(BF16)
    return high, middle, low


def stacked(value):
    parts = [part.astype(F32) for part in three(value)]
    parts.append(jnp.zeros_like(value))
    return jnp.concatenate(parts, axis=0).astype(BF16)


def folded(product):
    return (product[16:24] + product[8:16]) + product[0:8]


def column_of(values):
    row = lax.broadcasted_iota(jnp.int32, (GROUPS, 128), 0)
    out = jnp.full((GROUPS, 128), values[0])
    for n in range(1, GROUPS):
        out = jnp.where(row == n, values[n], out)
    return out


def member_of(position, lens_ref):
    ends = [lens_ref[0]]
    for n in range(1, GROUPS):
        ends.append(ends[-1] + lens_ref[n])
    last = column_of(ends)
    first = last - column_of([lens_ref[n] for n in range(GROUPS)])
    return ((position >= first[:, 0:1]) & (position < last[:, 0:1])).astype(F32)


def lengths_of(lens_ref):
    return column_of([lens_ref[n] for n in range(GROUPS)]).astype(F32)


def quarter_member(lens_ref, plane, half):
    row = lax.broadcasted_iota(jnp.int32, (GROUPS, QUARTER), 1)
    position = plane * (PLANE * ROWS) + (row >> 6) * ROWS + half * HALF + (row & 63)
    return member_of(position, lens_ref)


def local_member(lens_ref, first):
    return member_of(first + lax.broadcasted_iota(jnp.int32, (GROUPS, ROWS), 1), lens_ref)


def halves(packed):
    return jnp.concatenate([packed[:, :, 0:64], packed[:, :, 64:128]], axis=1)


def lanes(rows):
    return lax.broadcasted_iota(jnp.int32, (rows, 128), 1)


def pack_kernel(place_ref, lens_ref, q_ref, k_ref, v_ref, inputs_ref, out_ref):
    mine = local_member(lens_ref, place_ref[3]).astype(BF16)
    sums = jnp.dot(mine, inputs_ref[...], preferred_element_type=F32)
    high, middle, low = [part.astype(F32) for part in three(sums)]
    zero = jnp.zeros((GROUPS, HALF), F32)
    for head in range(HEAD_COUNT):
        cols = slice(head * HEAD_DIM, (head + 1) * HEAD_DIM)
        for half in range(2):
            rows = slice(half * HALF, (half + 1) * HALF)
            place = 2 * head + half
            out_ref[place, 0:64, :] = jnp.concatenate([k_ref[rows, cols], v_ref[rows, cols]], axis=1)
            query = q_ref[rows, cols] * jnp.asarray(SCALE, BF16)
            out_ref[place, 64:96, :] = jnp.concatenate([query[0:32], query[32:64]], axis=1)
            part = slice(place * HALF, (place + 1) * HALF)
            upper = jnp.concatenate([high[:, part], middle[:, part]], axis=1)
            lower = jnp.concatenate([low[:, part], zero], axis=1)
            out_ref[place, 96:112, :] = jnp.concatenate([upper, lower], axis=0).astype(BF16)


def unpack_kernel(in_ref, q_ref, k_ref):
    for pair in range(HEAD_COUNT // 2):
        cols = slice(pair * 128, (pair + 1) * 128)
        for half in range(2):
            rows = slice(half * HALF, (half + 1) * HALF)
            first, second = in_ref[4 * pair + half], in_ref[4 * pair + 2 + half]
            k_ref[rows, cols] = jnp.concatenate([first[:, 0:64], second[:, 0:64]], axis=1)
            q_ref[rows, cols] = jnp.concatenate([first[:, 64:128], second[:, 64:128]], axis=1)


BLOCK = 256
PARTS = BLOCK // 128


KEYS = 4 * QUARTER


def forward_kernel(
    place_ref, lens_ref, own_ref, x_ref, y_ref, lse_ref, means_ref, q_s
):
    queries = halves(own_ref[:, 64:96, :]).reshape(QUARTER, HEAD_DIM)
    q_s[...] = jnp.concatenate([queries, jnp.zeros_like(queries)], axis=1)

    def block(i, carry):
        rows = pl.ds(pl.multiple_of(i * BLOCK, BLOCK), BLOCK)
        scores = lax.dot_general(q_s[rows, :], x_ref[...], NT, preferred_element_type=F32)
        top = jnp.max(scores, axis=1, keepdims=True)
        grown = jnp.exp(scores - top)
        total = jnp.sum(grown, axis=1, keepdims=True)
        prob = (grown * (1.0 / total)).astype(BF16)
        mixed = jnp.dot(prob, x_ref[...], preferred_element_type=F32).astype(BF16)
        y_ref[rows, :] = jnp.where(lanes(BLOCK) < 64, q_s[rows, :], mixed)
        log_total = top + jnp.log(total)
        for part in range(PARTS):
            square = jnp.broadcast_to(log_total[part * 128 : (part + 1) * 128], (128, 128))
            lse_ref[pl.ds(i * PARTS + part, 1), :] = jnp.transpose(square)[0:1, :]
        return carry

    lax.fori_loop(0, QUARTER // BLOCK, block, 0)
    y_ref[QUARTER : QUARTER + 32, :] = stacked(lse_ref[...])
    member = quarter_member(lens_ref, place_ref[0], place_ref[1]).astype(BF16)
    attn_sums = jnp.dot(member, y_ref[0:QUARTER, :], preferred_element_type=F32)
    sums = jnp.sum(own_ref[:, 96:112, :].astype(F32), axis=0)
    input_sums = (sums[0:8] + pltpu.roll(sums[0:8], 64, 1)) + sums[8:16]
    means = jnp.where(lanes(GROUPS) < 64, input_sums, attn_sums) / lengths_of(lens_ref)
    means_ref[...] = jnp.broadcast_to(means[None], (2 * PLANE, GROUPS, 128))


def pool_kernel(doc_ref, means_ref, w_ref, query_ref, row_ref, own_ref, means_out_ref, logits_ref, out_ref):
    columns, heads = [], []
    for z in range(PLANE):
        both = means_ref[z] + means_ref[PLANE + z]
        columns.append(both[:, 0:64])
        if z % 2 == 0:
            heads.append(both[:, 64:128])
        else:
            heads[-1] = heads[-1] + both[:, 64:128]
    means = jnp.concatenate(heads, axis=1)
    projected = jnp.dot(stacked(means), w_ref[...], preferred_element_type=F32)
    pooled = jnp.concatenate(columns, axis=1) + folded(projected)
    own_ref[...] = pooled
    means_out_ref[...] = means
    unit = pooled / jnp.sqrt(jnp.sum(pooled * pooled, axis=1, keepdims=True) + NORM_EPS)
    logits = folded(
        lax.dot_general(stacked(unit), query_ref[:, :MODEL], NT, preferred_element_type=F32)
    )
    logits = logits * (RECIPROCAL_TEMP / row_ref[0:1, :])
    logits_ref[...] = logits
    group = doc_ref[0] * GROUPS + lax.broadcasted_iota(jnp.int32, logits.shape, 0)
    target = (group == row_ref[8:9, :].astype(jnp.int32)).astype(F32)
    total = jnp.sum(jnp.exp(logits), axis=0, keepdims=True)
    chosen = jnp.sum(target * logits, axis=0, keepdims=True)
    zero = jnp.zeros((4, 128), F32)
    sums = jnp.concatenate(
        [total[:, 0:128], total[:, 128:256], chosen[:, 0:128], chosen[:, 128:256], zero], axis=0
    )
    out_ref[...] = jnp.broadcast_to(sums[None], (DOCS, 8, 128))


def prepare_kernel(place_ref, pooled_ref, w_ref, out_ref):
    head = place_ref[2]
    pooled = pooled_ref[...]
    norms = jnp.sqrt(jnp.sum(pooled * pooled, axis=1, keepdims=True) + NORM_EPS)
    unit = pooled / norms
    w_head = w_ref[pl.ds(pl.multiple_of(head * HEAD_DIM, HEAD_DIM), HEAD_DIM), :]
    w_twice = jnp.concatenate([w_head, w_head], axis=0)
    out_ref[0:8, :] = folded(
        lax.dot_general(stacked(unit), w_twice, NT, preferred_element_type=F32)
    )
    z = 2 * head + place_ref[1]
    part = unit[:, 0:64]
    for n in range(1, PLANE):
        part = jnp.where(z == n, unit[:, n * HALF : (n + 1) * HALF], part)
    out_ref[8:16, :] = jnp.concatenate([part, part], axis=1)
    out_ref[16:24, :] = jnp.broadcast_to(norms, (GROUPS, 128))


def query_kernel(query_ref, out_ref):
    query = query_ref[:, :MODEL].astype(F32)
    squares = lax.dot_general(
        jnp.ones((8, MODEL), F32), query * query, NT, precision=EXACT, preferred_element_type=F32
    )
    out_ref[0:8, :] = jnp.sqrt(squares + NORM_EPS)
    out_ref[8:16, :] = lax.dot_general(
        jnp.ones((8, 128), BF16), query_ref[:, MODEL:], NT, preferred_element_type=F32
    )


def loss_kernel(doc_ref, sums_ref, logits_ref, own_ref, query_ref, row_ref, w_ref, out_ref):
    sums = sums_ref[0]
    for n in range(1, DOCS):
        sums = sums + sums_ref[n]
    total = jnp.concatenate([sums[0:1], sums[1:2]], axis=1)
    losses = jnp.log(sums[0:2]) - sums[2:4]
    loss = jnp.sum(jnp.sum(losses, axis=1, keepdims=True), axis=0, keepdims=True)
    query = query_ref[:, :MODEL]
    scale = RECIPROCAL_TEMP / row_ref[0:1, :]
    logits = logits_ref[...]
    group = doc_ref[0] * GROUPS + lax.broadcasted_iota(jnp.int32, logits.shape, 0)
    target = (group == row_ref[8:9, :].astype(jnp.int32)).astype(F32)
    weight = (jnp.exp(logits) / total - target) * (GRADIENT_FACTOR * scale)
    grad = folded(jnp.dot(stacked(weight), query, preferred_element_type=F32))
    own = own_ref[...]
    own_unit = own / jnp.sqrt(jnp.sum(own * own, axis=1, keepdims=True) + NORM_EPS)
    along = jnp.sum(own_unit * grad, axis=1, keepdims=True)
    spread = folded(
        lax.dot_general(stacked(grad), w_ref[...], NT, preferred_element_type=F32)
    )
    extra = jnp.where(lanes(GROUPS) < 64, along, loss)
    for z in range(PLANE):
        head = z // 2
        chunk = jnp.concatenate(
            [
                spread[:, head * HEAD_DIM : (head + 1) * HEAD_DIM],
                grad[:, z * HALF : (z + 1) * HALF],
            ],
            axis=1,
        )
        for plane in range(2):
            out_ref[plane * PLANE + z, 0:8, :] = chunk
            out_ref[plane * PLANE + z, 8:16, :] = extra


def mass_kernel(lens_ref, own_ref, y_ref, mass_ref, lse_ref, k_s, member_s):
    mine = own_ref[:, 0:64, :].reshape(QUARTER, 128)
    k_s[...] = jnp.where(lanes(QUARTER) < 64, mine, jnp.zeros_like(mine))
    for n in range(4):
        lse = y_ref[n * (QUARTER + 32) + QUARTER : (n + 1) * (QUARTER + 32), :].astype(F32)
        lse = (lse[16:24] + lse[8:16]) + lse[0:8]
        for part in range(8):
            at = n * QUARTER + part * 128
            lse_ref[:, at : at + 128] = jnp.broadcast_to(lse[part : part + 1, :], (8, 128))
        member = quarter_member(lens_ref, n // 2, n % 2)
        padded = jnp.concatenate([member, jnp.zeros((120, QUARTER), F32)], axis=0)
        member_s[:, n * QUARTER : (n + 1) * QUARTER] = padded.astype(BF16)

    def block(i, carry):
        rows = pl.ds(pl.multiple_of(i * BLOCK, BLOCK), BLOCK)
        sums = jnp.zeros((BLOCK, 128), F32)
        for n in range(4):
            cols = slice(n * QUARTER, (n + 1) * QUARTER)
            other = y_ref[n * (QUARTER + 32) : n * (QUARTER + 32) + QUARTER, :]
            scores = lax.dot_general(k_s[rows, :], other, NT, preferred_element_type=F32)
            prob = jnp.exp(scores - lse_ref[0:1, cols]).astype(BF16)
            sums = sums + lax.dot_general(
                prob, member_s[:, cols], NT, preferred_element_type=F32
            )
        for part in range(PARTS):
            mass_ref[i * PARTS + part] = jnp.transpose(sums[part * 128 : (part + 1) * 128])[0:8, :]
        return carry

    lax.fori_loop(0, QUARTER // BLOCK, block, 0)


def group_kernel(lens_ref, terms_ref, ready_ref, mass_ref, dattn_ref, grad_ref, loss_ref):
    sums = terms_ref[0]
    for n in range(1, 2 * PLANE):
        sums = sums + terms_ref[n]
    along = sums[8:16, 0:1]
    loss_ref[...] = sums[8:16, :] / QUERY_COUNT
    norms = ready_ref[16:24, :]
    raw = jnp.concatenate([sums[0:8, 0:64], sums[0:8, 0:64]], axis=1)
    dattn_ref[...] = (raw - ready_ref[0:8, :] * along) / norms / lengths_of(lens_ref)
    grad = (sums[0:8, 64:128] - ready_ref[8:16, 0:64] * along) / norms[:, 0:64]
    for z in range(PLANE):
        half = (z % 2) * HALF
        grad_ref[z] = jnp.concatenate([grad, mass_ref[z // 2, :, half : half + HALF]], axis=1)


def inputs_kernel(place_ref, lens_ref, parts_ref, means_ref, grad_inputs_ref, out_ref):
    grad = jnp.concatenate([parts_ref[z, :, 0:64] for z in range(PLANE)], axis=1)
    mine = local_member(lens_ref, place_ref[3])
    members = jnp.concatenate([mine, mine, mine, mine], axis=0).astype(BF16)
    grad_inputs_ref[...] = lax.dot_general(
        members, stacked(grad / lengths_of(lens_ref)[:, 0:1]), TN, preferred_element_type=F32
    ).astype(BF16)
    both = jnp.concatenate([grad, means_ref[...]], axis=1)
    out_ref[...] = jnp.concatenate([both, jnp.zeros_like(both)], axis=0).astype(BF16)


def value_kernel(lens_ref, parts_ref, w_ref, grad_v_ref):
    grad = jnp.concatenate([parts_ref[z, :, 0:64] for z in range(PLANE)], axis=1)
    grad = grad / lengths_of(lens_ref)[:, 0:1]
    dattn = folded(lax.dot_general(stacked(grad), w_ref[...], NT, preferred_element_type=F32))
    dattn = dattn.astype(BF16).astype(F32)
    dattn = jnp.concatenate([dattn, dattn, dattn, jnp.zeros_like(dattn)], axis=0).astype(BF16)
    for pair in range(HEAD_COUNT // 2):
        cols = slice(pair * 128, (pair + 1) * 128)
        both = []
        for head in (2 * pair, 2 * pair + 1):
            mass = jnp.concatenate(
                [parts_ref[2 * head, :, 64:128], parts_ref[2 * head + 1, :, 64:128]], axis=1
            )
            both.append(
                lax.dot_general(stacked(mass), dattn[:, cols], TN, preferred_element_type=F32)
            )
        grad_v_ref[:, cols] = jnp.where(lanes(ROWS) < 64, both[0], both[1]).astype(BF16)


def weight_kernel(in_ref, out_ref):
    out_ref[...] = lax.dot_general(
        in_ref[:, MODEL:], in_ref[:, :MODEL], TN, preferred_element_type=F32
    )


CHUNK = 512
TALL = 512


def row_kernel(place_ref, lens_ref, y_ref, lse_ref, x_ref, dattn_ref, out_ref, q_s, d_s, delta_s):
    lane = lanes(QUARTER)
    member = quarter_member(lens_ref, place_ref[0], place_ref[1]).astype(BF16)
    spread = lax.dot_general(
        member, dattn_ref[...].astype(BF16), TN, preferred_element_type=F32
    )
    spread = jnp.where(lane < 64, 0.0, spread)
    mine = y_ref[0:QUARTER, :]
    q_s[...] = jnp.where(lane < 64, mine, jnp.zeros_like(mine))
    d_s[...] = spread.astype(BF16)
    delta_s[...] = jnp.broadcast_to(
        jnp.sum(spread * mine.astype(F32), axis=1, keepdims=True), (QUARTER, 128)
    )

    def block(i, carry):
        rows = pl.ds(pl.multiple_of(i * TALL, TALL), TALL)
        columns = []
        for part in range(TALL // 128):
            line = lse_ref[pl.ds(i * (TALL // 128) + part, 1), :]
            columns.append(jnp.transpose(jnp.broadcast_to(line, (128, 128))))
        log_total = jnp.concatenate(columns, axis=0)[:, 0:1]
        delta = delta_s[rows, 0:1]
        total = jnp.zeros((TALL, 128), F32)
        for n in range(KEYS // CHUNK):
            part = x_ref[n * CHUNK : (n + 1) * CHUNK, :]
            scores = lax.dot_general(q_s[rows, :], part, NT, preferred_element_type=F32)
            prob_grad = lax.dot_general(d_s[rows, :], part, NT, preferred_element_type=F32)
            score_grad = (jnp.exp(scores - log_total) * (prob_grad - delta)).astype(BF16)
            total = total + jnp.dot(score_grad, part, preferred_element_type=F32)
        total = total * SCALE
        out_ref[rows, :] = jnp.concatenate([total[:, 0:64]] * 2, axis=1).astype(BF16)
        return carry

    lax.fori_loop(0, QUARTER // TALL, block, 0)


def column_kernel(
    lens_ref, own_ref, y_ref, lse_ref, dattn_ref, grad_q_ref, out_ref, y_s, k_s, v_s, delta_s
):
    lane = lanes(QUARTER)
    mine = own_ref[:, 0:64, :].reshape(QUARTER, 128)
    zero = jnp.zeros_like(mine)
    k_s[...] = jnp.where(lane < 64, mine, zero)
    v_s[...] = jnp.where(lane < 64, zero, mine)
    dattn = jnp.where(lanes(GROUPS) < 64, 0.0, dattn_ref[...]).astype(BF16)
    for n in range(4):
        rows = slice(n * QUARTER, (n + 1) * QUARTER)
        member = quarter_member(lens_ref, n // 2, n % 2)
        spread = lax.dot_general(member.astype(BF16), dattn, TN, preferred_element_type=F32)
        other = y_ref[n * (QUARTER + 32) : n * (QUARTER + 32) + QUARTER, :]
        y_s[rows, :] = jnp.where(lane < 64, other, spread.astype(BF16))
        products = lax.dot_general(dattn, other, NT, preferred_element_type=F32)
        delta_s[:, rows] = jnp.broadcast_to(
            jnp.sum(products * member, axis=0, keepdims=True), (8, QUARTER)
        )

    def block(i, carry):
        rows = pl.ds(pl.multiple_of(i * BLOCK, BLOCK), BLOCK)
        total = jnp.zeros((BLOCK, 128), F32)
        for n in range(KEYS // CHUNK):
            cols = slice(n * CHUNK, (n + 1) * CHUNK)
            part = y_s[cols, :]
            scores = lax.dot_general(k_s[rows, :], part, NT, preferred_element_type=F32)
            prob_grad = lax.dot_general(v_s[rows, :], part, NT, preferred_element_type=F32)
            score_grad = (
                jnp.exp(scores - lse_ref[0:1, cols]) * (prob_grad - delta_s[0:1, cols])
            ).astype(BF16)
            total = total + jnp.dot(score_grad, part, preferred_element_type=F32)
        both = jnp.where(lanes(BLOCK) < 64, total.astype(BF16), grad_q_ref[rows, :])
        count = BLOCK // HALF
        out_ref[pl.ds(i * count, count), :, :] = both.reshape(count, HALF, 128)
        return carry

    lax.fori_loop(0, QUARTER // BLOCK, block, 0)


SMEM = pl.BlockSpec(memory_space=pltpu.SMEM)
VMEM = pl.BlockSpec(memory_space=pltpu.VMEM)


def call(kernel, outs, scalars, arrays, scratch, estimate, name):
    return pl.pallas_call(
        kernel,
        out_shape=outs,
        in_specs=[SMEM] * len(scalars) + [VMEM] * len(arrays),
        out_specs=jax.tree.map(lambda _: VMEM, outs),
        scratch_shapes=scratch,
        compiler_params=params(),
        cost_estimate=estimate,
        name=name,
    )(*scalars, *arrays)


def shape(dims, dtype):
    return jax.ShapeDtypeStruct(dims, dtype)


def body(inputs, q_heads, k_heads, v_heads, w_out, group_lens, query_emb, positive):
    plane = lax.axis_index("yl")
    half = lax.axis_index("zd")
    head = lax.axis_index(HEADS)
    first = lax.axis_index(SEQ) * ROWS
    doc = lax.axis_index(GRP).reshape(1).astype(jnp.int32)
    place = jnp.stack([plane, half, head, first]).astype(jnp.int32)
    lengths = group_lens[0]
    exchange = functools.partial(lax.all_to_all, split_axis=0, concat_axis=0)
    barrier = lax.optimization_barrier
    pairs = QUARTER * KEYS

    packed = call(
        pack_kernel, shape((PLANE, 112, 128), BF16), (place, lengths),
        (q_heads[0], k_heads[0], v_heads[0], inputs[0]), (), cost(0, 1000000), "pack",
    )
    tagged = jnp.concatenate(
        [query_emb, jnp.pad(positive.astype(BF16)[:, None], ((0, 0), (0, 127)))], axis=1
    )
    packed, tagged = barrier((packed, tagged))
    own = exchange(packed, ZED)
    queries = gather_grp(tagged)
    own, queries = barrier((own, queries))
    keys = share(own[:, 0:64, :], SQUARE).reshape(KEYS, 128)

    mine, lse, means = call(
        forward_kernel,
        (
            shape((QUARTER + 32, 128), BF16),
            shape((8, 128), F32),
            shape((2 * PLANE, GROUPS, 128), F32),
        ),
        (place, lengths), (own, keys), [pltpu.VMEM((QUARTER, 128), BF16)],
        cost(pairs * 256 * 4, 3000000, pairs), "forward",
    )
    mine, means, queries = barrier((mine, means, queries))
    means = exchange(means, SEQ)
    around = [swap(mine, SQUARE, flip) for flip in (1, 2, 3)]
    query_rows = call(
        query_kernel, shape((16, 256), F32), (), (queries,), (), cost(6 * 2 * 8 * 256 * 1024, 600000),
        "queries",
    )
    means, query_rows, around = barrier((means, query_rows, around))
    pooled_own, doc_means, logits, sums = call(
        pool_kernel,
        (
            shape((GROUPS, MODEL), F32),
            shape((GROUPS, WIDTH), F32),
            shape((GROUPS, 256), F32),
            shape((DOCS, 8, 128), F32),
        ),
        (doc,), (means, w_out, queries, query_rows), (), cost(2 * 32 * 768 * 1024, 1800000), "pool",
    )
    sums = exchange(sums, GRP)
    square = [mine] + around
    rotated = [jnp.where(half == 0, square[n], square[n ^ 1]) for n in range(4)]
    ordered = [jnp.where(plane == 0, rotated[n], rotated[n ^ 2]) for n in range(4)]
    others = jnp.concatenate(ordered, axis=0)
    ready = call(
        prepare_kernel, shape((24, 128), F32), (place,), (pooled_own, w_out), (),
        cost(2 * 32 * 128 * 1024, 1200000), "prepare",
    )
    sums, others, ready = barrier((sums, others, ready))
    terms = call(
        loss_kernel, shape((2 * PLANE, 16, 128), F32), (doc,),
        (sums, logits, pooled_own, queries, query_rows, w_out), (),
        cost(2 * 32 * 768 * 1024, 1800000, 2000), "loss",
    )
    terms, own, others = barrier((terms, own, others))
    terms = exchange(terms, SEQ)
    mass, lse_rows = call(
        mass_kernel,
        (shape((GROUPS, 8, 128), F32), shape((8, KEYS), F32)),
        (lengths,), (own, others),
        [pltpu.VMEM((QUARTER, 128), BF16), pltpu.VMEM((128, KEYS), BF16)],
        cost(pairs * 256 * 4, 2500000, pairs), "mass",
    )
    terms, mass, lse_rows = barrier((terms, mass, lse_rows))

    dattn, grad_part, loss = call(
        group_kernel,
        (
            shape((GROUPS, 128), F32),
            shape((PLANE, GROUPS, 128), F32),
            shape((GROUPS, 128), F32),
        ),
        (lengths,), (terms, ready, mass), (), cost(0, 100000), "group",
    )
    mean_loss = loss[0, 64]
    grad_parts = exchange(grad_part, ZED)
    grad_rows = call(
        row_kernel, shape((QUARTER, 128), BF16), (place, lengths), (mine, lse, keys, dattn),
        [
            pltpu.VMEM((QUARTER, 128), BF16),
            pltpu.VMEM((QUARTER, 128), BF16),
            pltpu.VMEM((QUARTER, 128), F32),
        ],
        cost(pairs * 256 * 6, 2000000, pairs), "rows",
    )
    packed_grads = call(
        column_kernel, shape((PLANE, HALF, 128), BF16), (lengths,),
        (own, others, lse_rows, dattn, grad_rows),
        [
            pltpu.VMEM((KEYS, 128), BF16),
            pltpu.VMEM((QUARTER, 128), BF16),
            pltpu.VMEM((QUARTER, 128), BF16),
            pltpu.VMEM((8, KEYS), F32),
        ],
        cost(pairs * 256 * 6, 2500000, pairs), "columns",
    )
    packed_grads, grad_parts = barrier((packed_grads, grad_parts))
    grad_inputs, grads = call(
        inputs_kernel,
        (shape((ROWS, MODEL), BF16), shape((2 * GROUPS, MODEL + WIDTH), BF16)),
        (place, lengths), (grad_parts, doc_means), (), cost(2 * 32 * 128 * 1024, 1200000), "inputs",
    )
    home = exchange(packed_grads, ZED)
    all_grads = gather_grp(grads[0:GROUPS])
    out = shape((ROWS, WIDTH), BF16)
    grad_v = call(
        value_kernel, out, (lengths,), (grad_parts, w_out), (), cost(2 * 32 * 512 * 1024, 1300000),
        "values",
    )
    grad_w_out = call(
        weight_kernel, shape((WIDTH, MODEL), F32), (), (all_grads,), (),
        cost(2 * 128 * 512 * 1024, 2500000), "weights",
    )
    grad_q, grad_k = call(
        unpack_kernel, (out, out), (), (home,), (), cost(0, 500000), "unpack"
    )
    return (mean_loss, grad_inputs[None], grad_q[None], grad_k[None], grad_v[None], grad_w_out)


def solution(mesh):
    fine = Mesh(mesh.devices.reshape((2,) * 9), GRP + SEQ)
    rows = P(GRP, SEQ, None)
    return jax.shard_map(
        body,
        mesh=fine,
        in_specs=(
            rows,
            rows,
            rows,
            rows,
            P(),
            P(GRP, None),
            P(GRP + SEQ, None),
            P(GRP + SEQ),
        ),
        out_specs=(P(), rows, rows, rows, rows, P()),
        check_vma=False,
    )
```

time: 236 us -> 238 us (level)
  the two profiles are of different devices: /device:TPU:64 before, /device:TPU:1 now
where the time goes in v4:
time: 238 us; the launch traced here: 236 us
  starting transfers between devices  103 us (43%)
  Pallas kernels  65.7 us (28%)
  waiting for transfers between devices  38.6 us (16%)
  blocking collectives  16.8 us (7%)
  local copies, waits for them, and re-layouts  5.67 us (2%)
  other arithmetic  5.15 us (2%)
    pallas_call x14, Pallas kernels, call(): pl.pallas_call(kernel, out_shape=outs, in_specs=[SMEM] * len(scalars) + [...  65.7 us
    ppermute x11, starting transfers between devices, swap(): return lax.ppermute(value, axes, [(i, i ^ flip) for i in range(count)])  41.2 us
    ppermute x11, waiting for transfers between devices, swap(): return lax.ppermute(value, axes, [(i, i ^ flip) for i in range(count)])  24 us
    all_to_all x1, blocking collectives, share(): lax.all_to_all(jnp.broadcast_to(value[None], (count,) + value.shape), axe...  16.8 us
    all_to_all x1, starting transfers between devices, body(): own = exchange(packed, ZED)  15.7 us
    all_to_all x1, starting transfers between devices, body(): means = exchange(means, SEQ)  12.6 us
    all_to_all x1, starting transfers between devices, body(): home = exchange(packed_grads, ZED)  11.5 us
    all_to_all x1, waiting for transfers between devices, body(): terms = exchange(terms, SEQ)  11.5 us
  transfers between devices with their start and end apart: 17, of which 10 were waited for; matrix products, arithmetic and copies ran while one was open for 2% of the time, Pallas kernels for 18%

profile of v4, /device:TPU:1, one launch (start us, length us, event | category | flops | bytes accessed | tf_op | source)
XLA Modules:
  0.0 236.3 jit_solution(8080228059910691928)
XLA Ops:
  5.0 15.7 %all-to-all-start = ((bf16[16,112,128]{2,1,0:T(8,128)(2,1)}), bf16[16,112,128]{2,1,0:T(8,128)(2,1)S(1)}, u32[]{:S(2)}, u32[]{:S(2)}) async-start(bf16[16,112,128]{2,1,0:T(8,128)(2,1)} %pack.1), calls=%async_computation | async-start | bytes 917504 | tf_op jit(solution)/shard_map/all_to_all | solution.py:496
  20.7 4.8 %collective-permute-start = (bf16[16,1152]{1,0:T(8,128)(2,1)S(1)}, bf16[16,1152]{1,0:T(8,128)(2,1)S(1)}, u32[]{:S(2)}, u32[]{:S(2)}) collective-permute-start(bf16[16,1152]{1,0:T(8,128)(2,1)S(1)} %fusion.1), channel_id=1, source_target_pairs={{0,256},{256,0},{1,257},{257,1},{2,258},{258,2},{3,259},{259,3},{4... | collective-permute-start | bytes 110600 | tf_op jit(solution)/shard_map/ppermute | solution.py:59
  27.0 4.7 %collective-permute-start.1 = (bf16[32,1152]{1,0:T(8,128)(2,1)S(1)}, bf16[32,1152]{1,0:T(8,128)(2,1)S(1)}, u32[]{:S(2)}, u32[]{:S(2)}) collective-permute-start(bf16[32,1152]{1,0:T(8,128)(2,1)S(1)} %maximum_select_fusion.6), channel_id=1, source_target_pairs={{0,128},{128,0},{1,129},{129,1},{2,130},{130,2},{3,131},{131,3},{4... | collective-permute-start | bytes 221192 | tf_op jit(solution)/shard_map/ppermute | solution.py:59
  33.9 3.1 %collective-permute-start.2 = (bf16[64,1152]{1,0:T(8,128)(2,1)S(1)}, bf16[64,1152]{1,0:T(8,128)(2,1)S(1)}, u32[]{:S(2)}, u32[]{:S(2)}) collective-permute-start(bf16[64,1152]{1,0:T(8,128)(2,1)S(1)} %maximum_select_fusion.4), channel_id=1, source_target_pairs={{0,64},{64,0},{1,65},{65,1},{2,66},{66,2},{3,67},{67,3},{4,68},{68... | collective-permute-start | bytes 442376 | tf_op jit(solution)/shard_map/ppermute | solution.py:59
  37.0 3.0 %collective-permute-done.2 = bf16[64,1152]{1,0:T(8,128)(2,1)S(1)} collective-permute-done((bf16[64,1152]{1,0:T(8,128)(2,1)S(1)}, bf16[64,1152]{1,0:T(8,128)(2,1)S(1)}, u32[]{:S(2)}, u32[]{:S(2)}) %collective-permute-start.2) | collective-permute-done | bytes 147488 | tf_op jit(solution)/shard_map/ppermute | solution.py:59
  40.1 5.7 %collective-permute-start.3 = (bf16[128,1152]{1,0:T(8,128)(2,1)S(1)}, bf16[128,1152]{1,0:T(8,128)(2,1)S(1)}, u32[]{:S(2)}, u32[]{:S(2)}) collective-permute-start(bf16[128,1152]{1,0:T(8,128)(2,1)S(1)} %maximum_select_fusion.2), channel_id=1, source_target_pairs={{0,32},{32,0},{1,33},{33,1},{2,34},{34,2},{3,35},{35,3},{4,36},{36... | collective-permute-start | bytes 884744 | tf_op jit(solution)/shard_map/ppermute | solution.py:59
  48.3 16.8 %all_to_all.35 = bf16[4,16,64,128]{3,2,1,0:T(8,128)(2,1)} all-to-all(bf16[4,16,64,128]{3,2,1,0:T(8,128)(2,1)S(1)} %broadcast_in_dim.22), channel_id=1, replica_groups=mesh['yh'=2,'xa'=2,'xb'=2,'co'=2,'yl'=2,'za'=2,'zb'=2,'zc'=2,'zd'=2] {'y..., dimensions={0} | all-to-all | bytes 2097152 | tf_op jit(solution)/shard_map/all_to_all | solution.py:52
  65.1 10.3 %forward.1 = (bf16[1056,128]{1,0:T(8,128)(2,1)}, f32[8,128]{1,0:T(8,128)}, f32[32,8,128]{2,1,0:T(8,128)}) custom-call(s32[4]{0:T(128)} %pad_add_fusion.place_ref, s32[8]{0:T(128)} %bitcast.26, bf16[16,112,128]{2,1,0:T(8,128)(2,1)} %copy-done, bf16[4096,128]{1,0:T(8,128)(2,1)} %bitcast.18), custom_call_target="tpu_custom_call" | custom-call | flops 4294967296 | bytes 3000000 | tf_op jit(solution)/shard_map/forward/pallas_call | solution.py:460
  75.4 12.6 %all-to-all-start.2 = ((f32[32,8,128]{2,1,0:T(8,128)}), f32[32,8,128]{2,1,0:T(8,128)S(1)}, u32[]{:S(2)}, u32[]{:S(2)}) async-start(f32[32,8,128]{2,1,0:T(8,128)} %get-tuple-element.51), calls=%async_computation.2 | async-start | bytes 262144 | tf_op jit(solution)/shard_map/all_to_all | solution.py:512
  88.0 3.1 %collective-permute-start.4 = (bf16[1056,128]{1,0:T(8,128)(2,1)}, bf16[1056,128]{1,0:T(8,128)(2,1)S(1)}, u32[]{:S(2)}, u32[]{:S(2)}) collective-permute-start(bf16[1056,128]{1,0:T(8,128)(2,1)} %get-tuple-element.53.y_ref), channel_id=1, source_target_pairs={{0,1},{1,0},{16,17},{17,16},{2,3},{3,2},{18,19},{19,18},{4,5},{5,4... | collective-permute-start | bytes 811016 | tf_op jit(solution)/shard_map/ppermute | solution.py:59
  91.1 3.1 %collective-permute-start.5 = (bf16[1056,128]{1,0:T(8,128)(2,1)}, bf16[1056,128]{1,0:T(8,128)(2,1)S(1)}, u32[]{:S(2)}, u32[]{:S(2)}) collective-permute-start(bf16[1056,128]{1,0:T(8,128)(2,1)} %get-tuple-element.53.y_ref), channel_id=1, source_target_pairs={{0,16},{1,17},{16,0},{17,1},{2,18},{3,19},{18,2},{19,3},{4,20},{5,... | collective-permute-start | bytes 811016 | tf_op jit(solution)/shard_map/ppermute | solution.py:59
  96.4 2.7 %queries.1.row_ref = f32[16,256]{1,0:T(8,128)} custom-call(bf16[256,1152]{1,0:T(8,128)(2,1)} %maximum_select_fusion.query_ref), custom_call_target="tpu_custom_call" | custom-call | flops 25165824 | bytes 600000 | tf_op jit(solution)/shard_map/queries/pallas_call | solution.py:460
  99.1 2.8 %collective-permute-done.4 = bf16[1056,128]{1,0:T(8,128)(2,1)S(1)} collective-permute-done((bf16[1056,128]{1,0:T(8,128)(2,1)}, bf16[1056,128]{1,0:T(8,128)(2,1)S(1)}, u32[]{:S(2)}, u32[]{:S(2)}) %collective-permute-start.4) | collective-permute-done | bytes 270368 | tf_op jit(solution)/shard_map/ppermute | solution.py:59
  101.9 6.7 %collective-permute-done.6 = bf16[1056,128]{1,0:T(8,128)(2,1)S(1)} collective-permute-done((bf16[1056,128]{1,0:T(8,128)(2,1)}, bf16[1056,128]{1,0:T(8,128)(2,1)S(1)}, u32[]{:S(2)}, u32[]{:S(2)}) %collective-permute-start.6) | collective-permute-done | bytes 270368 | tf_op jit(solution)/shard_map/ppermute | solution.py:59
  109.3 2.7 %pool.1 = (f32[8,1024]{1,0:T(8,128)}, f32[8,512]{1,0:T(8,128)}, f32[8,256]{1,0:T(8,128)}, f32[16,8,128]{2,1,0:T(8,128)}) custom-call(s32[1]{0:T(128)} %bitcast.1.doc_ref, f32[32,8,128]{2,1,0:T(8,128)} %copy-done.4, bf16[512,1024]{1,0:T(8,128)(2,1)} %w_ref.7, bf16[256,1152]{1,0:T(8,128)(2,1)} %maximum_select_fusion.query_ref, f32[16,256]{1,0:T(8,128)} %queries.1.row_ref), custom_call_target="tpu_custom_call" | custom-call | flops 50331648 | bytes 1800000 | tf_op jit(solution)/shard_map/pool/pallas_call | solution.py:460
  112.0 8.0 %all-to-all-start.3 = ((f32[16,8,128]{2,1,0:T(8,128)}), f32[16,8,128]{2,1,0:T(8,128)S(1)}, u32[]{:S(2)}, u32[]{:S(2)}) async-start(f32[16,8,128]{2,1,0:T(8,128)} %get-tuple-element.56), calls=%async_computation.3 | async-start | bytes 131072 | tf_op jit(solution)/shard_map/all_to_all | solution.py:529
  121.2 3.0 %prepare.1.ready_ref = f32[24,128]{1,0:T(8,128)} custom-call(s32[4]{0:T(128)} %pad_add_fusion.place_ref, f32[8,1024]{1,0:T(8,128)} %get-tuple-element.60.pooled_ref.own_ref, bf16[512,1024]{1,0:T(8,128)(2,1)} %w_ref.7), custom_call_target="tpu_custom_call" | custom-call | flops 8388608 | bytes 1200000 | tf_op jit(solution)/shard_map/prepare/pallas_call | solution.py:460
  124.2 3.1 %all-to-all-done.3.sums_ref = f32[16,8,128]{2,1,0:T(8,128)S(1)} async-done(((f32[16,8,128]{2,1,0:T(8,128)}), f32[16,8,128]{2,1,0:T(8,128)S(1)}, u32[]{:S(2)}, u32[]{:S(2)}) %all-to-all-start.3) | async-done | bytes 65568 | tf_op jit(solution)/shard_map/all_to_all | solution.py:529
  128.0 2.8 %loss.1 = f32[32,16,128]{2,1,0:T(8,128)} custom-call(s32[1]{0:T(128)} %bitcast.1.doc_ref, f32[16,8,128]{2,1,0:T(8,128)} %copy-done.6, f32[8,256]{1,0:T(8,128)} %get-tuple-element.62.logits_ref, f32[8,1024]{1,0:T(8,128)} %get-tuple-element.60.pooled_ref.own_ref, bf16[256,1152]{1,0:T(8,128)(2,1)} %maximum_select_fusion.query_ref, f32[16,256]{1,0:T(8,128)} %queries.1.row_ref, ...), custom_call_target="tpu_custom_call" | custom-call | flops 50331648 | bytes 1800000 | tf_op jit(solution)/shard_map/loss/pallas_call | solution.py:460
  130.7 10.1 %all-to-all-start.4 = ((f32[32,16,128]{2,1,0:T(8,128)}), f32[32,16,128]{2,1,0:T(8,128)S(1)}, u32[]{:S(2)}, u32[]{:S(2)}) async-start(f32[32,16,128]{2,1,0:T(8,128)} %loss.1), calls=%async_computation.4 | async-start | bytes 524288 | tf_op jit(solution)/shard_map/all_to_all | solution.py:545
  140.8 8.9 %mass.1 = (f32[8,8,128]{2,1,0:T(8,128)}, f32[8,4096]{1,0:T(8,128)}) custom-call(s32[8]{0:T(128)} %bitcast.27, bf16[16,112,128]{2,1,0:T(8,128)(2,1)} %copy-done, bf16[4224,128]{1,0:T(8,128)(2,1)} %pad_maximum_fusion.y_ref), custom_call_target="tpu_custom_call" | custom-call | flops 4294967296 | bytes 2500000 | tf_op jit(solution)/shard_map/mass/pallas_call | solution.py:460
  149.7 11.5 %all-to-all-done.4.terms_ref = f32[32,16,128]{2,1,0:T(8,128)S(1)} async-done(((f32[32,16,128]{2,1,0:T(8,128)}), f32[32,16,128]{2,1,0:T(8,128)S(1)}, u32[]{:S(2)}, u32[]{:S(2)}) %all-to-all-start.4) | async-done | bytes 262176 | tf_op jit(solution)/shard_map/all_to_all | solution.py:545
  163.7 4.4 %all-to-all-start.5 = ((f32[16,8,128]{2,1,0:T(8,128)}), f32[16,8,128]{2,1,0:T(8,128)S(1)}, u32[]{:S(2)}, u32[]{:S(2)}) async-start(f32[16,8,128]{2,1,0:T(8,128)} %get-tuple-element.76), calls=%async_computation.5 | async-start | bytes 131072 | tf_op jit(solution)/shard_map/all_to_all | solution.py:565
  168.1 9.8 %rows.1.grad_q_ref = bf16[1024,128]{1,0:T(8,128)(2,1)} custom-call(s32[4]{0:T(128)} %pad_add_fusion.place_ref, s32[8]{0:T(128)} %bitcast.29, bf16[1056,128]{1,0:T(8,128)(2,1)} %get-tuple-element.53.y_ref, f32[8,128]{1,0:T(8,128)} %get-tuple-element.75.lse_ref, bf16[4096,128]{1,0:T(8,128)(2,1)} %bitcast.19, f32[8,128]{1,0:T(8,128)} %get-tuple-element.74.dattn_ref), custom_call_target="tpu_custom_call" | custom-call | flops 6442450944 | bytes 2000000 | tf_op jit(solution)/shard_map/rows/pallas_call | solution.py:460
  177.9 12.6 %columns.1 = bf16[16,64,128]{2,1,0:T(8,128)(2,1)} custom-call(s32[8]{0:T(128)} %bitcast.30, bf16[16,112,128]{2,1,0:T(8,128)(2,1)} %copy-done, bf16[4224,128]{1,0:T(8,128)(2,1)} %pad_maximum_fusion.y_ref, f32[8,4096]{1,0:T(8,128)} %get-tuple-element.73.lse_ref, f32[8,128]{1,0:T(8,128)} %get-tuple-element.74.dattn_ref, bf16[1024,128]{1,0:T(8,128)(2,1)} %rows.1.grad_q_ref), custom_call_target="tpu_custom_call" | custom-call | flops 6442450944 | bytes 2500000 | tf_op jit(solution)/shard_map/columns/pallas_call | solution.py:460
  196.0 3.8 %collective-permute-done.7 = bf16[8,1536]{1,0:T(8,128)(2,1)S(1)} collective-permute-done((bf16[8,1536]{1,0:T(8,128)(2,1)S(1)}, bf16[8,1536]{1,0:T(8,128)(2,1)S(1)}, u32[]{:S(2)}, u32[]{:S(2)}) %collective-permute-start.7) | collective-permute-done | bytes 24608 | tf_op jit(solution)/shard_map/ppermute | solution.py:59
  199.8 2.8 %collective-permute-start.8 = (bf16[16,1536]{1,0:T(8,128)(2,1)S(1)}, bf16[16,1536]{1,0:T(8,128)(2,1)S(1)}, u32[]{:S(2)}, u32[]{:S(2)}) collective-permute-start(bf16[16,1536]{1,0:T(8,128)(2,1)S(1)} %maximum_select_fusion.7), channel_id=1, source_target_pairs={{0,128},{128,0},{1,129},{129,1},{2,130},{130,2},{3,131},{131,3},{4... | collective-permute-start | bytes 147464 | tf_op jit(solution)/shard_map/ppermute | solution.py:59
  202.7 11.5 %all-to-all-start.6 = ((bf16[16,64,128]{2,1,0:T(8,128)(2,1)}), bf16[16,64,128]{2,1,0:T(8,128)(2,1)S(1)}, u32[]{:S(2)}, u32[]{:S(2)}) async-start(bf16[16,64,128]{2,1,0:T(8,128)(2,1)} %columns.1), calls=%async_computation.6 | async-start | bytes 524288 | tf_op jit(solution)/shard_map/all_to_all | solution.py:592
  216.7 2.8 %collective-permute-done.9 = bf16[32,1536]{1,0:T(8,128)(2,1)S(1)} collective-permute-done((bf16[32,1536]{1,0:T(8,128)(2,1)S(1)}, bf16[32,1536]{1,0:T(8,128)(2,1)S(1)}, u32[]{:S(2)}, u32[]{:S(2)}) %collective-permute-start.9) | collective-permute-done | bytes 98336 | tf_op jit(solution)/shard_map/ppermute | solution.py:59
  219.6 6.8 %collective-permute-start.10 = (bf16[64,1536]{1,0:T(8,128)(2,1)S(1)}, bf16[64,1536]{1,0:T(8,128)(2,1)S(1)}, u32[]{:S(2)}, u32[]{:S(2)}) collective-permute-start(bf16[64,1536]{1,0:T(8,128)(2,1)S(1)} %maximum_select_fusion.3), channel_id=1, source_target_pairs={{0,32},{32,0},{1,33},{33,1},{2,34},{34,2},{3,35},{35,3},{4,36},{36... | collective-permute-start | bytes 589832 | tf_op jit(solution)/shard_map/ppermute | solution.py:59
  227.7 2.6 %values.1 = bf16[128,512]{1,0:T(8,128)(2,1)} custom-call(s32[8]{0:T(128)} %bitcast.32, f32[16,8,128]{2,1,0:T(8,128)} %copy-done.3, bf16[512,1024]{1,0:T(8,128)(2,1)} %w_ref.7), custom_call_target="tpu_custom_call" | custom-call | flops 33554432 | bytes 1300000 | tf_op jit(solution)/shard_map/values/pallas_call | solution.py:460
  231.0 2.8 %weights.1 = f32[512,1024]{1,0:T(8,128)} custom-call(bf16[128,1536]{1,0:T(8,128)(2,1)} %maximum_select_fusion.1.in_ref), custom_call_target="tpu_custom_call" | custom-call | flops 134217728 | bytes 2500000 | tf_op jit(solution)/shard_map/weights/pallas_call | solution.py:460
  (49 shorter events, 30.2 us)
Async XLA Ops:
  5.0 43.0 %all-to-all-start = ((bf16[16,112,128]{2,1,0:T(8,128)(2,1)}), bf16[16,112,128]{2,1,0:T(8,128)(2,1)S(1)}, u32[]{:S(2)}, u32[]{:S(2)}) async-start(bf16[16,112,128]{2,1,0:T(8,128)(2,1)} %pack.1), calls=%async_computation | async-start | bytes 917504 | tf_op jit(solution)/shard_map/all_to_all | solution.py:496
  20.7 6.2 %collective-permute-start = (bf16[16,1152]{1,0:T(8,128)(2,1)S(1)}, bf16[16,1152]{1,0:T(8,128)(2,1)S(1)}, u32[]{:S(2)}, u32[]{:S(2)}) collective-permute-start(bf16[16,1152]{1,0:T(8,128)(2,1)S(1)} %fusion.1), channel_id=1, source_target_pairs={{0,256},{256,0},{1,257},{257,1},{2,258},{258,2},{3,259},{259,3},{4... | collective-permute-start | bytes 110600 | tf_op jit(solution)/shard_map/ppermute | solution.py:59
  27.0 6.9 %collective-permute-start.1 = (bf16[32,1152]{1,0:T(8,128)(2,1)S(1)}, bf16[32,1152]{1,0:T(8,128)(2,1)S(1)}, u32[]{:S(2)}, u32[]{:S(2)}) collective-permute-start(bf16[32,1152]{1,0:T(8,128)(2,1)S(1)} %maximum_select_fusion.6), channel_id=1, source_target_pairs={{0,128},{128,0},{1,129},{129,1},{2,130},{130,2},{3,131},{131,3},{4... | collective-permute-start | bytes 221192 | tf_op jit(solution)/shard_map/ppermute | solution.py:59
  33.9 6.2 %collective-permute-start.2 = (bf16[64,1152]{1,0:T(8,128)(2,1)S(1)}, bf16[64,1152]{1,0:T(8,128)(2,1)S(1)}, u32[]{:S(2)}, u32[]{:S(2)}) collective-permute-start(bf16[64,1152]{1,0:T(8,128)(2,1)S(1)} %maximum_select_fusion.4), channel_id=1, source_target_pairs={{0,64},{64,0},{1,65},{65,1},{2,66},{66,2},{3,67},{67,3},{4,68},{68... | collective-permute-start | bytes 442376 | tf_op jit(solution)/shard_map/ppermute | solution.py:59
  40.1 6.9 %collective-permute-start.3 = (bf16[128,1152]{1,0:T(8,128)(2,1)S(1)}, bf16[128,1152]{1,0:T(8,128)(2,1)S(1)}, u32[]{:S(2)}, u32[]{:S(2)}) collective-permute-start(bf16[128,1152]{1,0:T(8,128)(2,1)S(1)} %maximum_select_fusion.2), channel_id=1, source_target_pairs={{0,32},{32,0},{1,33},{33,1},{2,34},{34,2},{3,35},{35,3},{4,36},{36... | collective-permute-start | bytes 884744 | tf_op jit(solution)/shard_map/ppermute | solution.py:59
  48.0 17.1 %copy-start = (bf16[16,112,128]{2,1,0:T(8,128)(2,1)}, bf16[16,112,128]{2,1,0:T(8,128)(2,1)S(1)}, u32[]{:S(2)}) copy-start(bf16[16,112,128]{2,1,0:T(8,128)(2,1)S(1)} %all-to-all-done.own_ref) | copy-start | bytes 1376260
  75.4 33.3 %all-to-all-start.2 = ((f32[32,8,128]{2,1,0:T(8,128)}), f32[32,8,128]{2,1,0:T(8,128)S(1)}, u32[]{:S(2)}, u32[]{:S(2)}) async-start(f32[32,8,128]{2,1,0:T(8,128)} %get-tuple-element.51), calls=%async_computation.2 | async-start | bytes 262144 | tf_op jit(solution)/shard_map/all_to_all | solution.py:512
  88.0 13.9 %collective-permute-start.4 = (bf16[1056,128]{1,0:T(8,128)(2,1)}, bf16[1056,128]{1,0:T(8,128)(2,1)S(1)}, u32[]{:S(2)}, u32[]{:S(2)}) collective-permute-start(bf16[1056,128]{1,0:T(8,128)(2,1)} %get-tuple-element.53.y_ref), channel_id=1, source_target_pairs={{0,1},{1,0},{16,17},{17,16},{2,3},{3,2},{18,19},{19,18},{4,5},{5,4... | collective-permute-start | bytes 811016 | tf_op jit(solution)/shard_map/ppermute | solution.py:59
  91.1 10.8 %collective-permute-start.5 = (bf16[1056,128]{1,0:T(8,128)(2,1)}, bf16[1056,128]{1,0:T(8,128)(2,1)S(1)}, u32[]{:S(2)}, u32[]{:S(2)}) collective-permute-start(bf16[1056,128]{1,0:T(8,128)(2,1)} %get-tuple-element.53.y_ref), channel_id=1, source_target_pairs={{0,16},{1,17},{16,0},{17,1},{2,18},{3,19},{18,2},{19,3},{4,20},{5,... | collective-permute-start | bytes 811016 | tf_op jit(solution)/shard_map/ppermute | solution.py:59
  94.2 14.4 %collective-permute-start.6 = (bf16[1056,128]{1,0:T(8,128)(2,1)}, bf16[1056,128]{1,0:T(8,128)(2,1)S(1)}, u32[]{:S(2)}, u32[]{:S(2)}) collective-permute-start(bf16[1056,128]{1,0:T(8,128)(2,1)} %get-tuple-element.53.y_ref), channel_id=1, source_target_pairs={{0,17},{1,16},{16,1},{17,0},{2,19},{3,18},{18,3},{19,2},{4,21},{5,... | collective-permute-start | bytes 811016 | tf_op jit(solution)/shard_map/ppermute | solution.py:59
  96.4 23.6 %copy-start.5 = (bf16[1056,128]{1,0:T(8,128)(2,1)S(1)}, bf16[1056,128]{1,0:T(8,128)(2,1)}, u32[]{:S(2)}) copy-start(bf16[1056,128]{1,0:T(8,128)(2,1)} %get-tuple-element.53.y_ref) | copy-start | bytes 811012
  108.7 0.7 copy-start.4
  112.0 15.3 %all-to-all-start.3 = ((f32[16,8,128]{2,1,0:T(8,128)}), f32[16,8,128]{2,1,0:T(8,128)S(1)}, u32[]{:S(2)}, u32[]{:S(2)}) async-start(f32[16,8,128]{2,1,0:T(8,128)} %get-tuple-element.56), calls=%async_computation.3 | async-start | bytes 131072 | tf_op jit(solution)/shard_map/all_to_all | solution.py:529
  127.3 0.6 copy-start.6
  130.7 30.4 %all-to-all-start.4 = ((f32[32,16,128]{2,1,0:T(8,128)}), f32[32,16,128]{2,1,0:T(8,128)S(1)}, u32[]{:S(2)}, u32[]{:S(2)}) async-start(f32[32,16,128]{2,1,0:T(8,128)} %loss.1), calls=%async_computation.4 | async-start | bytes 524288 | tf_op jit(solution)/shard_map/all_to_all | solution.py:545
  161.2 0.7 copy-start.2
  163.7 26.8 %all-to-all-start.5 = ((f32[16,8,128]{2,1,0:T(8,128)}), f32[16,8,128]{2,1,0:T(8,128)S(1)}, u32[]{:S(2)}, u32[]{:S(2)}) async-start(f32[16,8,128]{2,1,0:T(8,128)} %get-tuple-element.76), calls=%async_computation.5 | async-start | bytes 131072 | tf_op jit(solution)/shard_map/all_to_all | solution.py:565
  190.5 0.6 copy-start.3
  193.7 6.1 %collective-permute-start.7 = (bf16[8,1536]{1,0:T(8,128)(2,1)S(1)}, bf16[8,1536]{1,0:T(8,128)(2,1)S(1)}, u32[]{:S(2)}, u32[]{:S(2)}) collective-permute-start(bf16[8,1536]{1,0:T(8,128)(2,1)S(1)} %slice.11), channel_id=1, source_target_pairs={{0,256},{256,0},{1,257},{257,1},{2,258},{258,2},{3,259},{259,3},{4... | collective-permute-start | bytes 73736 | tf_op jit(solution)/shard_map/ppermute | solution.py:59
  199.8 14.3 %collective-permute-start.8 = (bf16[16,1536]{1,0:T(8,128)(2,1)S(1)}, bf16[16,1536]{1,0:T(8,128)(2,1)S(1)}, u32[]{:S(2)}, u32[]{:S(2)}) collective-permute-start(bf16[16,1536]{1,0:T(8,128)(2,1)S(1)} %maximum_select_fusion.7), channel_id=1, source_target_pairs={{0,128},{128,0},{1,129},{129,1},{2,130},{130,2},{3,131},{131,3},{4... | collective-permute-start | bytes 147464 | tf_op jit(solution)/shard_map/ppermute | solution.py:59
  202.7 31.2 %all-to-all-start.6 = ((bf16[16,64,128]{2,1,0:T(8,128)(2,1)}), bf16[16,64,128]{2,1,0:T(8,128)(2,1)S(1)}, u32[]{:S(2)}, u32[]{:S(2)}) async-start(bf16[16,64,128]{2,1,0:T(8,128)(2,1)} %columns.1), calls=%async_computation.6 | async-start | bytes 524288 | tf_op jit(solution)/shard_map/all_to_all | solution.py:592
  214.2 5.4 %collective-permute-start.9 = (bf16[32,1536]{1,0:T(8,128)(2,1)S(1)}, bf16[32,1536]{1,0:T(8,128)(2,1)S(1)}, u32[]{:S(2)}, u32[]{:S(2)}) collective-permute-start(bf16[32,1536]{1,0:T(8,128)(2,1)S(1)} %maximum_select_fusion.5), channel_id=1, source_target_pairs={{0,64},{64,0},{1,65},{65,1},{2,66},{66,2},{3,67},{67,3},{4,68},{68... | collective-permute-start | bytes 294920 | tf_op jit(solution)/shard_map/ppermute | solution.py:59
  219.6 10.7 %collective-permute-start.10 = (bf16[64,1536]{1,0:T(8,128)(2,1)S(1)}, bf16[64,1536]{1,0:T(8,128)(2,1)S(1)}, u32[]{:S(2)}, u32[]{:S(2)}) collective-permute-start(bf16[64,1536]{1,0:T(8,128)(2,1)S(1)} %maximum_select_fusion.3), channel_id=1, source_target_pairs={{0,32},{32,0},{1,33},{33,1},{2,34},{34,2},{3,35},{35,3},{4,36},{36... | collective-permute-start | bytes 589832 | tf_op jit(solution)/shard_map/ppermute | solution.py:59
  233.8 0.7 copy-start.1

commit v5 on v4

--- a/solution.py
+++ b/solution.py
@@ -36,11 +36,11 @@
 NT = (((1,), (1,)), ((), ()))
 TN = (((0,), (0,)), ((), ()))
 
-VMEM_BYTES = 56 << 20
-
-
-def params():
-    return pltpu.CompilerParams(vmem_limit_bytes=VMEM_BYTES)
+HELD = 512
+
+
+def params(large):
+    return pltpu.CompilerParams(vmem_limit_bytes=(40 if large else 12) << 20)
 
 
 def cost(flops, moved, exps=0):
@@ -59,8 +59,8 @@
     return lax.ppermute(value, axes, [(i, i ^ flip) for i in range(count)])
 
 
-def gather_grp(value):
-    for axis in GRP:
+def gather(value, axes):
+    for axis in axes:
         other = swap(value, (axis,), 1)
         first = lax.axis_index(axis) == 0
         value = jnp.where(
@@ -69,6 +69,13 @@
             jnp.concatenate([other, value], axis=0),
         )
     return value
+
+
+def gather_pair(value, axes):
+    square = [value] + [swap(value, axes, flip) for flip in (1, 2, 3)]
+    low, high = lax.axis_index(axes[1]) == 0, lax.axis_index(axes[0]) == 0
+    turned = [jnp.where(low, square[n], square[n ^ 1]) for n in range(4)]
+    return jnp.concatenate([jnp.where(high, turned[n], turned[n ^ 2]) for n in range(4)], axis=0)
 
 
 def three(value):
@@ -191,19 +198,14 @@
     attn_sums = jnp.dot(member, y_ref[0:QUARTER, :], preferred_element_type=F32)
     sums = jnp.sum(own_ref[:, 96:112, :].astype(F32), axis=0)
     input_sums = (sums[0:8] + pltpu.roll(sums[0:8], 64, 1)) + sums[8:16]
-    means = jnp.where(lanes(GROUPS) < 64, input_sums, attn_sums) / lengths_of(lens_ref)
-    means_ref[...] = jnp.broadcast_to(means[None], (2 * PLANE, GROUPS, 128))
+    means_ref[...] = jnp.where(lanes(GROUPS) < 64, input_sums, attn_sums) / lengths_of(lens_ref)
 
 
 def pool_kernel(doc_ref, means_ref, w_ref, query_ref, row_ref, own_ref, means_out_ref, logits_ref, out_ref):
-    columns, heads = [], []
-    for z in range(PLANE):
-        both = means_ref[z] + means_ref[PLANE + z]
-        columns.append(both[:, 0:64])
-        if z % 2 == 0:
-            heads.append(both[:, 64:128])
-        else:
-            heads[-1] = heads[-1] + both[:, 64:128]
+    columns = [means_ref[z, :, 0:64] for z in range(PLANE)]
+    heads = [
+        means_ref[z, :, 64:128] + means_ref[z + 1, :, 64:128] for z in range(0, PLANE, 2)
+    ]
     means = jnp.concatenate(heads, axis=1)
     projected = jnp.dot(stacked(means), w_ref[...], preferred_element_type=F32)
     pooled = jnp.concatenate(columns, axis=1) + folded(projected)
@@ -219,9 +221,8 @@
     target = (group == row_ref[8:9, :].astype(jnp.int32)).astype(F32)
     total = jnp.sum(jnp.exp(logits), axis=0, keepdims=True)
     chosen = jnp.sum(target * logits, axis=0, keepdims=True)
-    zero = jnp.zeros((4, 128), F32)
     sums = jnp.concatenate(
-        [total[:, 0:128], total[:, 128:256], chosen[:, 0:128], chosen[:, 128:256], zero], axis=0
+        [row[:, n : n + 128] for row in (total, chosen) for n in range(0, HELD, 128)], axis=0
     )
     out_ref[...] = jnp.broadcast_to(sums[None], (DOCS, 8, 128))
 
@@ -259,8 +260,8 @@
     sums = sums_ref[0]
     for n in range(1, DOCS):
         sums = sums + sums_ref[n]
-    total = jnp.concatenate([sums[0:1], sums[1:2]], axis=1)
-    losses = jnp.log(sums[0:2]) - sums[2:4]
+    total = jnp.concatenate([sums[n : n + 1] for n in range(4)], axis=1)
+    losses = jnp.log(sums[0:4]) - sums[4:8]
     loss = jnp.sum(jnp.sum(losses, axis=1, keepdims=True), axis=0, keepdims=True)
     query = query_ref[:, :MODEL]
     scale = RECIPROCAL_TEMP / row_ref[0:1, :]
@@ -285,9 +286,8 @@
             ],
             axis=1,
         )
-        for plane in range(2):
-            out_ref[plane * PLANE + z, 0:8, :] = chunk
-            out_ref[plane * PLANE + z, 8:16, :] = extra
+        out_ref[z, 0:8, :] = chunk
+        out_ref[z, 8:16, :] = extra
 
 
 def mass_kernel(lens_ref, own_ref, y_ref, mass_ref, lse_ref, k_s, member_s):
@@ -323,7 +323,7 @@
 
 def group_kernel(lens_ref, terms_ref, ready_ref, mass_ref, dattn_ref, grad_ref, loss_ref):
     sums = terms_ref[0]
-    for n in range(1, 2 * PLANE):
+    for n in range(1, PLANE):
         sums = sums + terms_ref[n]
     along = sums[8:16, 0:1]
     loss_ref[...] = sums[8:16, :] / QUERY_COUNT
@@ -463,7 +463,7 @@
         in_specs=[SMEM] * len(scalars) + [VMEM] * len(arrays),
         out_specs=jax.tree.map(lambda _: VMEM, outs),
         scratch_shapes=scratch,
-        compiler_params=params(),
+        compiler_params=params(bool(scratch)),
         cost_estimate=estimate,
         name=name,
     )(*scalars, *arrays)
@@ -494,25 +494,29 @@
     )
     packed, tagged = barrier((packed, tagged))
     own = exchange(packed, ZED)
-    queries = gather_grp(tagged)
+    queries = gather(tagged, ("yh", "yl", "xa", "xb"))
     own, queries = barrier((own, queries))
     keys = share(own[:, 0:64, :], SQUARE).reshape(KEYS, 128)
+    queries = gather(queries, ("co",))
+    own, keys, queries = barrier((own, keys, queries))
 
     mine, lse, means = call(
         forward_kernel,
         (
             shape((QUARTER + 32, 128), BF16),
             shape((8, 128), F32),
-            shape((2 * PLANE, GROUPS, 128), F32),
+            shape((GROUPS, 128), F32),
         ),
         (place, lengths), (own, keys), [pltpu.VMEM((QUARTER, 128), BF16)],
         cost(pairs * 256 * 4, 3000000, pairs), "forward",
     )
+    means = means + swap(means, ("yl",), 1)
+    means = jnp.broadcast_to(means[None], (PLANE, GROUPS, 128))
     mine, means, queries = barrier((mine, means, queries))
-    means = exchange(means, SEQ)
+    means = exchange(means, ZED)
     around = [swap(mine, SQUARE, flip) for flip in (1, 2, 3)]
     query_rows = call(
-        query_kernel, shape((16, 256), F32), (), (queries,), (), cost(6 * 2 * 8 * 256 * 1024, 600000),
+        query_kernel, shape((16, HELD), F32), (), (queries,), (), cost(6 * 2 * 8 * HELD * 1024, 1200000),
         "queries",
     )
     means, query_rows, around = barrier((means, query_rows, around))
@@ -521,7 +525,7 @@
         (
             shape((GROUPS, MODEL), F32),
             shape((GROUPS, WIDTH), F32),
-            shape((GROUPS, 256), F32),
+            shape((GROUPS, HELD), F32),
             shape((DOCS, 8, 128), F32),
         ),
         (doc,), (means, w_out, queries, query_rows), (), cost(2 * 32 * 768 * 1024, 1800000), "pool",
@@ -537,12 +541,12 @@
     )
     sums, others, ready = barrier((sums, others, ready))
     terms = call(
-        loss_kernel, shape((2 * PLANE, 16, 128), F32), (doc,),
+        loss_kernel, shape((PLANE, 16, 128), F32), (doc,),
         (sums, logits, pooled_own, queries, query_rows, w_out), (),
         cost(2 * 32 * 768 * 1024, 1800000, 2000), "loss",
     )
     terms, own, others = barrier((terms, own, others))
-    terms = exchange(terms, SEQ)
+    terms = exchange(terms, ZED)
     mass, lse_rows = call(
         mass_kernel,
         (shape((GROUPS, 8, 128), F32), shape((8, KEYS), F32)),
@@ -590,18 +594,18 @@
         (place, lengths), (grad_parts, doc_means), (), cost(2 * 32 * 128 * 1024, 1200000), "inputs",
     )
     home = exchange(packed_grads, ZED)
-    all_grads = gather_grp(grads[0:GROUPS])
+    all_grads = gather_pair(gather_pair(grads[0:GROUPS], ("yh", "xa")), ("xb", "co"))
     out = shape((ROWS, WIDTH), BF16)
     grad_v = call(
-        value_kernel, out, (lengths,), (grad_parts, w_out), (), cost(2 * 32 * 512 * 1024, 1300000),
+        value_kernel, out, (lengths,), (grad_parts, w_out), (), cost(0, 0),
         "values",
     )
     grad_w_out = call(
         weight_kernel, shape((WIDTH, MODEL), F32), (), (all_grads,), (),
-        cost(2 * 128 * 512 * 1024, 2500000), "weights",
+        cost(0, 0), "weights",
     )
     grad_q, grad_k = call(
-        unpack_kernel, (out, out), (), (home,), (), cost(0, 500000), "unpack"
+        unpack_kernel, (out, out), (), (home,), (), cost(0, 0), "unpack"
     )
     return (mean_loss, grad_inputs[None], grad_q[None], grad_k[None], grad_v[None], grad_w_out)
 

time: 238 us -> 241 us (1.013)
  the two profiles are of different devices: /device:TPU:1 before, /device:TPU:32 now
where the time goes in v5:
time: 241 us; the launch traced here: 240 us
  starting transfers between devices  112 us (46%)
  waiting for transfers between devices  60.8 us (25%)
  Pallas kernels  51.3 us (21%)
  local copies, waits for them, and re-layouts  9.14 us (4%)
  other arithmetic  6.04 us (3%)
    pallas_call x14, Pallas kernels, call(): pl.pallas_call(kernel, out_shape=outs, in_specs=[SMEM] * len(scalars) + [...  51.3 us
    ppermute x15, starting transfers between devices, swap(): return lax.ppermute(value, axes, [(i, i ^ flip) for i in range(count)])  50.4 us
    ppermute x15, waiting for transfers between devices, swap(): return lax.ppermute(value, axes, [(i, i ^ flip) for i in range(count)])  21.9 us
    all_to_all x1, waiting for transfers between devices, body(): home = exchange(packed_grads, ZED)  16.5 us
    all_to_all x1, starting transfers between devices, body(): own = exchange(packed, ZED)  15.2 us
    all_to_all x1, starting transfers between devices, body(): home = exchange(packed_grads, ZED)  12 us
    all_to_all x1, starting transfers between devices, body(): means = exchange(means, ZED)  11.9 us
    all_to_all x1, waiting for transfers between devices, body(): means = exchange(means, ZED)  10.1 us
  transfers between devices with their start and end apart: 22, of which 12 were waited for; matrix products, arithmetic and copies ran while one was open for 2% of the time, Pallas kernels for 14%

profile of v5, /device:TPU:32, one launch (start us, length us, event | category | flops | bytes accessed | tf_op | source)
XLA Modules:
  0.0 240.1 jit_solution(18188886245121500478)
XLA Ops:
  8.1 15.2 %all-to-all-start = ((bf16[16,112,128]{2,1,0:T(8,128)(2,1)}), bf16[16,112,128]{2,1,0:T(8,128)(2,1)S(1)}, u32[]{:S(2)}, u32[]{:S(2)}) async-start(bf16[16,112,128]{2,1,0:T(8,128)(2,1)} %pack.1), calls=%async_computation | async-start | bytes 917504 | tf_op jit(solution)/shard_map/all_to_all | solution.py:496
  23.3 5.1 %collective-permute-start = (bf16[16,1152]{1,0:T(8,128)(2,1)S(1)}, bf16[16,1152]{1,0:T(8,128)(2,1)S(1)}, u32[]{:S(2)}, u32[]{:S(2)}) collective-permute-start(bf16[16,1152]{1,0:T(8,128)(2,1)S(1)} %fusion.1), channel_id=1, source_target_pairs={{0,256},{256,0},{1,257},{257,1},{2,258},{258,2},{3,259},{259,3},{4... | collective-permute-start | bytes 110600 | tf_op jit(solution)/shard_map/ppermute | solution.py:59
  30.7 3.5 %collective-permute-start.1 = (bf16[32,1152]{1,0:T(8,128)(2,1)S(1)}, bf16[32,1152]{1,0:T(8,128)(2,1)S(1)}, u32[]{:S(2)}, u32[]{:S(2)}) collective-permute-start(bf16[32,1152]{1,0:T(8,128)(2,1)S(1)} %maximum_select_fusion.4), channel_id=1, source_target_pairs={{0,16},{16,0},{1,17},{17,1},{2,18},{18,2},{3,19},{19,3},{4,20},{20... | collective-permute-start | bytes 221192 | tf_op jit(solution)/shard_map/ppermute | solution.py:59
  34.2 2.7 %collective-permute-done.1 = bf16[32,1152]{1,0:T(8,128)(2,1)S(1)} collective-permute-done((bf16[32,1152]{1,0:T(8,128)(2,1)S(1)}, bf16[32,1152]{1,0:T(8,128)(2,1)S(1)}, u32[]{:S(2)}, u32[]{:S(2)}) %collective-permute-start.1) | collective-permute-done | bytes 73760 | tf_op jit(solution)/shard_map/ppermute | solution.py:59
  37.0 4.9 %collective-permute-start.2 = (bf16[64,1152]{1,0:T(8,128)(2,1)S(1)}, bf16[64,1152]{1,0:T(8,128)(2,1)S(1)}, u32[]{:S(2)}, u32[]{:S(2)}) collective-permute-start(bf16[64,1152]{1,0:T(8,128)(2,1)S(1)} %maximum_select_fusion.3), channel_id=1, source_target_pairs={{0,128},{128,0},{1,129},{129,1},{2,130},{130,2},{3,131},{131,3},{4... | collective-permute-start | bytes 442376 | tf_op jit(solution)/shard_map/ppermute | solution.py:59
  41.9 3.6 %collective-permute-done.2 = bf16[64,1152]{1,0:T(8,128)(2,1)S(1)} collective-permute-done((bf16[64,1152]{1,0:T(8,128)(2,1)S(1)}, bf16[64,1152]{1,0:T(8,128)(2,1)S(1)}, u32[]{:S(2)}, u32[]{:S(2)}) %collective-permute-start.2) | collective-permute-done | bytes 147488 | tf_op jit(solution)/shard_map/ppermute | solution.py:59
  45.6 3.4 %collective-permute-start.3 = (bf16[128,1152]{1,0:T(8,128)(2,1)S(1)}, bf16[128,1152]{1,0:T(8,128)(2,1)S(1)}, u32[]{:S(2)}, u32[]{:S(2)}) collective-permute-start(bf16[128,1152]{1,0:T(8,128)(2,1)S(1)} %maximum_select_fusion.2), channel_id=1, source_target_pairs={{0,64},{64,0},{1,65},{65,1},{2,66},{66,2},{3,67},{67,3},{4,68},{68... | collective-permute-start | bytes 884744 | tf_op jit(solution)/shard_map/ppermute | solution.py:59
  49.0 5.2 %collective-permute-done.3 = bf16[128,1152]{1,0:T(8,128)(2,1)S(1)} collective-permute-done((bf16[128,1152]{1,0:T(8,128)(2,1)S(1)}, bf16[128,1152]{1,0:T(8,128)(2,1)S(1)}, u32[]{:S(2)}, u32[]{:S(2)}) %collective-permute-start.3) | collective-permute-done | bytes 294944 | tf_op jit(solution)/shard_map/ppermute | solution.py:59
  55.6 4.3 %all-to-all-start.1 = ((bf16[4,16,64,128]{3,2,1,0:T(8,128)(2,1)}), bf16[4,16,64,128]{3,2,1,0:T(8,128)(2,1)S(1)}, u32[]{:S(2)}, u32[]{:S(2)}) async-start(bf16[4,16,64,128]{3,2,1,0:T(8,128)(2,1)} %broadcast_in_dim.28), calls=%async_computation.1 | async-start | bytes 2097152 | tf_op jit(solution)/shard_map/all_to_all | solution.py:52
  65.8 2.9 %all-to-all-done.1 = bf16[4,16,64,128]{3,2,1,0:T(8,128)(2,1)S(1)} async-done(((bf16[4,16,64,128]{3,2,1,0:T(8,128)(2,1)}), bf16[4,16,64,128]{3,2,1,0:T(8,128)(2,1)S(1)}, u32[]{:S(2)}, u32[]{:S(2)}) %all-to-all-start.1) | async-done | bytes 1048608 | tf_op jit(solution)/shard_map/all_to_all | solution.py:52
  68.7 8.8 %forward.1 = (bf16[1056,128]{1,0:T(8,128)(2,1)S(1)}, f32[8,128]{1,0:T(8,128)S(1)}, f32[8,128]{1,0:T(8,128)S(1)}) custom-call(s32[4]{0:T(128)S(1)} %pad_add_fusion.place_ref, s32[8]{0:T(128)S(1)} %bitcast.25, bf16[16,112,128]{2,1,0:T(8,128)(2,1)S(1)} %all-to-all-done.own_ref, bf16[4096,128]{1,0:T(8,128)(2,1)S(1)} %bitcast.18), custom_call_target="tpu_custom_call" | custom-call | flops 4294967296 | bytes 3000000 | tf_op jit(solution)/shard_map/forward/pallas_call | solution.py:460
  78.5 2.6 %collective-permute-start.5 = (f32[8,128]{1,0:T(8,128)S(1)}, f32[8,128]{1,0:T(8,128)S(1)}, u32[]{:S(2)}, u32[]{:S(2)}) collective-permute-start(f32[8,128]{1,0:T(8,128)S(1)} %get-tuple-element.55), channel_id=1, source_target_pairs={{0,16},{16,0},{1,17},{17,1},{2,18},{18,2},{3,19},{19,3},{4,20},{20... | collective-permute-start | bytes 12296 | tf_op jit(solution)/shard_map/ppermute | solution.py:59
  81.1 3.0 %collective-permute-done.5 = f32[8,128]{1,0:T(8,128)S(1)} collective-permute-done((f32[8,128]{1,0:T(8,128)S(1)}, f32[8,128]{1,0:T(8,128)S(1)}, u32[]{:S(2)}, u32[]{:S(2)}) %collective-permute-start.5) | collective-permute-done | bytes 4128 | tf_op jit(solution)/shard_map/ppermute | solution.py:59
  87.3 3.4 %collective-permute-start.7 = (bf16[1056,128]{1,0:T(8,128)(2,1)S(1)}, bf16[1056,128]{1,0:T(8,128)(2,1)}, u32[]{:S(2)}, u32[]{:S(2)}) collective-permute-start(bf16[1056,128]{1,0:T(8,128)(2,1)S(1)} %get-tuple-element.59.y_ref), channel_id=1, source_target_pairs={{0,16},{1,17},{16,0},{17,1},{2,18},{3,19},{18,2},{19,3},{4,20},{5,... | collective-permute-start | bytes 811016 | tf_op jit(solution)/shard_map/ppermute | solution.py:59
  90.7 3.3 %collective-permute-start.8 = (bf16[1056,128]{1,0:T(8,128)(2,1)S(1)}, bf16[1056,128]{1,0:T(8,128)(2,1)}, u32[]{:S(2)}, u32[]{:S(2)}) collective-permute-start(bf16[1056,128]{1,0:T(8,128)(2,1)S(1)} %get-tuple-element.59.y_ref), channel_id=1, source_target_pairs={{0,17},{1,16},{16,1},{17,0},{2,19},{3,18},{18,3},{19,2},{4,21},{5,... | collective-permute-start | bytes 811016 | tf_op jit(solution)/shard_map/ppermute | solution.py:59
  94.0 11.9 %all-to-all-start.2 = ((f32[16,8,128]{2,1,0:T(8,128)}), f32[16,8,128]{2,1,0:T(8,128)S(1)}, u32[]{:S(2)}, u32[]{:S(2)}) async-start(f32[16,8,128]{2,1,0:T(8,128)} %broadcast_in_dim.29), calls=%async_computation.2 | async-start | bytes 131072 | tf_op jit(solution)/shard_map/all_to_all | solution.py:516
  107.7 10.1 %all-to-all-done.2.means_ref = f32[16,8,128]{2,1,0:T(8,128)S(1)} async-done(((f32[16,8,128]{2,1,0:T(8,128)}), f32[16,8,128]{2,1,0:T(8,128)S(1)}, u32[]{:S(2)}, u32[]{:S(2)}) %all-to-all-start.2) | async-done | bytes 65568 | tf_op jit(solution)/shard_map/all_to_all | solution.py:516
  119.2 7.2 %all-to-all-start.3 = ((f32[16,8,128]{2,1,0:T(8,128)}), f32[16,8,128]{2,1,0:T(8,128)S(1)}, u32[]{:S(2)}, u32[]{:S(2)}) async-start(f32[16,8,128]{2,1,0:T(8,128)} %get-tuple-element.62), calls=%async_computation.3 | async-start | bytes 131072 | tf_op jit(solution)/shard_map/all_to_all | solution.py:533
  130.3 3.8 %all-to-all-done.3.sums_ref = f32[16,8,128]{2,1,0:T(8,128)S(1)} async-done(((f32[16,8,128]{2,1,0:T(8,128)}), f32[16,8,128]{2,1,0:T(8,128)S(1)}, u32[]{:S(2)}, u32[]{:S(2)}) %all-to-all-start.3) | async-done | bytes 65568 | tf_op jit(solution)/shard_map/all_to_all | solution.py:533
  135.4 4.4 %all-to-all-start.4 = ((f32[16,16,128]{2,1,0:T(8,128)}), f32[16,16,128]{2,1,0:T(8,128)S(1)}, u32[]{:S(2)}, u32[]{:S(2)}) async-start(f32[16,16,128]{2,1,0:T(8,128)} %loss.1), calls=%async_computation.4 | async-start | bytes 262144 | tf_op jit(solution)/shard_map/all_to_all | solution.py:549
  141.0 7.4 %mass.1 = (f32[8,8,128]{2,1,0:T(8,128)S(1)}, f32[8,4096]{1,0:T(8,128)S(1)}) custom-call(s32[8]{0:T(128)S(1)} %bitcast.26, bf16[16,112,128]{2,1,0:T(8,128)(2,1)S(1)} %all-to-all-done.own_ref, bf16[4224,128]{1,0:T(8,128)(2,1)S(1)} %copy-done.1), custom_call_target="tpu_custom_call" | custom-call | flops 4294967296 | bytes 2500000 | tf_op jit(solution)/shard_map/mass/pallas_call | solution.py:460
  148.5 5.8 %all-to-all-done.4.terms_ref = f32[16,16,128]{2,1,0:T(8,128)S(1)} async-done(((f32[16,16,128]{2,1,0:T(8,128)}), f32[16,16,128]{2,1,0:T(8,128)S(1)}, u32[]{:S(2)}, u32[]{:S(2)}) %all-to-all-start.4) | async-done | bytes 131104 | tf_op jit(solution)/shard_map/all_to_all | solution.py:549
  155.7 6.3 %all-to-all-start.5 = ((f32[16,8,128]{2,1,0:T(8,128)}), f32[16,8,128]{2,1,0:T(8,128)S(1)}, u32[]{:S(2)}, u32[]{:S(2)}) async-start(f32[16,8,128]{2,1,0:T(8,128)} %get-tuple-element.82), calls=%async_computation.5 | async-start | bytes 131072 | tf_op jit(solution)/shard_map/all_to_all | solution.py:569
  162.0 8.3 %rows.1.grad_q_ref = bf16[1024,128]{1,0:T(8,128)(2,1)S(1)} custom-call(s32[4]{0:T(128)S(1)} %pad_add_fusion.place_ref, s32[8]{0:T(128)S(1)} %bitcast.28, bf16[1056,128]{1,0:T(8,128)(2,1)S(1)} %get-tuple-element.59.y_ref, f32[8,128]{1,0:T(8,128)S(1)} %get-tuple-element.81.lse_ref, bf16[4096,128]{1,0:T(8,128)(2,1)S(1)} %bitcast.19, ...), custom_call_target="tpu_custom_call" | custom-call | flops 6442450944 | bytes 2000000 | tf_op jit(solution)/shard_map/rows/pallas_call | solution.py:460
  170.3 11.7 %columns.1 = bf16[16,64,128]{2,1,0:T(8,128)(2,1)} custom-call(s32[8]{0:T(128)S(1)} %bitcast.29, bf16[16,112,128]{2,1,0:T(8,128)(2,1)S(1)} %all-to-all-done.own_ref, bf16[4224,128]{1,0:T(8,128)(2,1)S(1)} %copy-done.2, f32[8,4096]{1,0:T(8,128)S(1)} %get-tuple-element.79.lse_ref, f32[8,128]{1,0:T(8,128)S(1)} %get-tuple-element.80.dattn_ref, ...), custom_call_target="tpu_custom_call" | custom-call | flops 6442450944 | bytes 2500000 | tf_op jit(solution)/shard_map/columns/pallas_call | solution.py:460
  186.0 5.4 %collective-permute-start.11 = (bf16[8,1536]{1,0:T(8,128)(2,1)S(1)}, bf16[8,1536]{1,0:T(8,128)(2,1)S(1)}, u32[]{:S(2)}, u32[]{:S(2)}) collective-permute-start(bf16[8,1536]{1,0:T(8,128)(2,1)S(1)} %slice.11), channel_id=1, source_target_pairs={{0,384},{128,256},{256,128},{384,0},{1,385},{129,257},{257,129},{3... | collective-permute-start | bytes 73736 | tf_op jit(solution)/shard_map/ppermute | solution.py:59
  191.5 4.2 %collective-permute-start.9 = (bf16[8,1536]{1,0:T(8,128)(2,1)S(1)}, bf16[8,1536]{1,0:T(8,128)(2,1)S(1)}, u32[]{:S(2)}, u32[]{:S(2)}) collective-permute-start(bf16[8,1536]{1,0:T(8,128)(2,1)S(1)} %slice.11), channel_id=1, source_target_pairs={{0,128},{128,0},{256,384},{384,256},{1,129},{129,1},{257,385},{385... | collective-permute-start | bytes 73736 | tf_op jit(solution)/shard_map/ppermute | solution.py:59
  195.7 3.0 %collective-permute-done.9 = bf16[8,1536]{1,0:T(8,128)(2,1)S(1)} collective-permute-done((bf16[8,1536]{1,0:T(8,128)(2,1)S(1)}, bf16[8,1536]{1,0:T(8,128)(2,1)S(1)}, u32[]{:S(2)}, u32[]{:S(2)}) %collective-permute-start.9) | collective-permute-done | bytes 24608 | tf_op jit(solution)/shard_map/ppermute | solution.py:59
  200.7 2.8 %collective-permute-start.13 = (bf16[32,1536]{1,0:T(8,128)(2,1)S(1)}, bf16[32,1536]{1,0:T(8,128)(2,1)S(1)}, u32[]{:S(2)}, u32[]{:S(2)}) collective-permute-start(bf16[32,1536]{1,0:T(8,128)(2,1)S(1)} %pad_maximum_fusion.2), channel_id=1, source_target_pairs={{0,64},{32,96},{64,0},{96,32},{1,65},{33,97},{65,1},{97,33},{2,66}... | collective-permute-start | bytes 294920 | tf_op jit(solution)/shard_map/ppermute | solution.py:59
  203.5 2.9 %collective-permute-start.14 = (bf16[32,1536]{1,0:T(8,128)(2,1)S(1)}, bf16[32,1536]{1,0:T(8,128)(2,1)S(1)}, u32[]{:S(2)}, u32[]{:S(2)}) collective-permute-start(bf16[32,1536]{1,0:T(8,128)(2,1)S(1)} %pad_maximum_fusion.2), channel_id=1, source_target_pairs={{0,96},{32,64},{64,32},{96,0},{1,97},{33,65},{65,33},{97,1},{2,98}... | collective-permute-start | bytes 294920 | tf_op jit(solution)/shard_map/ppermute | solution.py:59
  208.8 12.0 %all-to-all-start.6 = ((bf16[16,64,128]{2,1,0:T(8,128)(2,1)}), bf16[16,64,128]{2,1,0:T(8,128)(2,1)S(1)}, u32[]{:S(2)}, u32[]{:S(2)}) async-start(bf16[16,64,128]{2,1,0:T(8,128)(2,1)} %columns.1), calls=%async_computation.6 | async-start | bytes 524288 | tf_op jit(solution)/shard_map/all_to_all | solution.py:596
  222.8 16.5 %all-to-all-done.6.in_ref = bf16[16,64,128]{2,1,0:T(8,128)(2,1)S(1)} async-done(((bf16[16,64,128]{2,1,0:T(8,128)(2,1)}), bf16[16,64,128]{2,1,0:T(8,128)(2,1)S(1)}, u32[]{:S(2)}, u32[]{:S(2)}) %all-to-all-start.6) | async-done | bytes 262176 | tf_op jit(solution)/shard_map/all_to_all | solution.py:596
  (72 shorter events, 43.5 us)
Async XLA Ops:
  2.2 1.0 copy-start.5
  3.2 0.9 copy-start.6
  4.1 0.9 copy-start.7
  8.1 46.2 %all-to-all-start = ((bf16[16,112,128]{2,1,0:T(8,128)(2,1)}), bf16[16,112,128]{2,1,0:T(8,128)(2,1)S(1)}, u32[]{:S(2)}, u32[]{:S(2)}) async-start(bf16[16,112,128]{2,1,0:T(8,128)(2,1)} %pack.1), calls=%async_computation | async-start | bytes 917504 | tf_op jit(solution)/shard_map/all_to_all | solution.py:496
  23.3 7.3 %collective-permute-start = (bf16[16,1152]{1,0:T(8,128)(2,1)S(1)}, bf16[16,1152]{1,0:T(8,128)(2,1)S(1)}, u32[]{:S(2)}, u32[]{:S(2)}) collective-permute-start(bf16[16,1152]{1,0:T(8,128)(2,1)S(1)} %fusion.1), channel_id=1, source_target_pairs={{0,256},{256,0},{1,257},{257,1},{2,258},{258,2},{3,259},{259,3},{4... | collective-permute-start | bytes 110600 | tf_op jit(solution)/shard_map/ppermute | solution.py:59
  30.7 6.2 %collective-permute-start.1 = (bf16[32,1152]{1,0:T(8,128)(2,1)S(1)}, bf16[32,1152]{1,0:T(8,128)(2,1)S(1)}, u32[]{:S(2)}, u32[]{:S(2)}) collective-permute-start(bf16[32,1152]{1,0:T(8,128)(2,1)S(1)} %maximum_select_fusion.4), channel_id=1, source_target_pairs={{0,16},{16,0},{1,17},{17,1},{2,18},{18,2},{3,19},{19,3},{4,20},{20... | collective-permute-start | bytes 221192 | tf_op jit(solution)/shard_map/ppermute | solution.py:59
  37.0 8.5 %collective-permute-start.2 = (bf16[64,1152]{1,0:T(8,128)(2,1)S(1)}, bf16[64,1152]{1,0:T(8,128)(2,1)S(1)}, u32[]{:S(2)}, u32[]{:S(2)}) collective-permute-start(bf16[64,1152]{1,0:T(8,128)(2,1)S(1)} %maximum_select_fusion.3), channel_id=1, source_target_pairs={{0,128},{128,0},{1,129},{129,1},{2,130},{130,2},{3,131},{131,3},{4... | collective-permute-start | bytes 442376 | tf_op jit(solution)/shard_map/ppermute | solution.py:59
  45.6 8.6 %collective-permute-start.3 = (bf16[128,1152]{1,0:T(8,128)(2,1)S(1)}, bf16[128,1152]{1,0:T(8,128)(2,1)S(1)}, u32[]{:S(2)}, u32[]{:S(2)}) collective-permute-start(bf16[128,1152]{1,0:T(8,128)(2,1)S(1)} %maximum_select_fusion.2), channel_id=1, source_target_pairs={{0,64},{64,0},{1,65},{65,1},{2,66},{66,2},{3,67},{67,3},{4,68},{68... | collective-permute-start | bytes 884744 | tf_op jit(solution)/shard_map/ppermute | solution.py:59
  54.3 7.5 %copy-start.11 = (bf16[256,1152]{1,0:T(8,128)(2,1)}, bf16[256,1152]{1,0:T(8,128)(2,1)S(1)}, u32[]{:S(2)}) copy-start(bf16[256,1152]{1,0:T(8,128)(2,1)S(1)} %maximum_select_fusion.1) | copy-start | bytes 1769476
  55.6 13.1 %all-to-all-start.1 = ((bf16[4,16,64,128]{3,2,1,0:T(8,128)(2,1)}), bf16[4,16,64,128]{3,2,1,0:T(8,128)(2,1)S(1)}, u32[]{:S(2)}, u32[]{:S(2)}) async-start(bf16[4,16,64,128]{3,2,1,0:T(8,128)(2,1)} %broadcast_in_dim.28), calls=%async_computation.1 | async-start | bytes 2097152 | tf_op jit(solution)/shard_map/all_to_all | solution.py:52
  59.9 4.0 %collective-permute-start.4 = (bf16[256,1152]{1,0:T(8,128)(2,1)S(1)}, bf16[256,1152]{1,0:T(8,128)(2,1)}, u32[]{:S(2)}, u32[]{:S(2)}) collective-permute-start(bf16[256,1152]{1,0:T(8,128)(2,1)S(1)} %maximum_select_fusion.1), channel_id=1, source_target_pairs={{0,32},{32,0},{1,33},{33,1},{2,34},{34,2},{3,35},{35,3},{4,36},{36... | collective-permute-start | bytes 1769480 | tf_op jit(solution)/shard_map/ppermute | solution.py:59
  61.8 6.9 %copy-start.10 = (s32[1,8]{1,0:T(1,128)S(1)}, s32[1,8]{1,0:T(1,128)}, u32[]{:S(2)}) copy-start(s32[1,8]{1,0:T(1,128)} %param.13) | copy-start | bytes 100
  77.5 1.0 copy-start.3
  78.5 39.3 %copy-start = (bf16[512,1024]{1,0:T(8,128)(2,1)S(1)}, bf16[512,1024]{1,0:T(8,128)(2,1)}, u32[]{:S(2)}) copy-start(bf16[512,1024]{1,0:T(8,128)(2,1)} %w_ref.7) | copy-start | bytes 3145732
  78.5 5.6 %collective-permute-start.5 = (f32[8,128]{1,0:T(8,128)S(1)}, f32[8,128]{1,0:T(8,128)S(1)}, u32[]{:S(2)}, u32[]{:S(2)}) collective-permute-start(f32[8,128]{1,0:T(8,128)S(1)} %get-tuple-element.55), channel_id=1, source_target_pairs={{0,16},{16,0},{1,17},{17,1},{2,18},{18,2},{3,19},{19,3},{4,20},{20... | collective-permute-start | bytes 12296 | tf_op jit(solution)/shard_map/ppermute | solution.py:59
  84.8 33.0 %collective-permute-start.6 = (bf16[1056,128]{1,0:T(8,128)(2,1)S(1)}, bf16[1056,128]{1,0:T(8,128)(2,1)S(1)}, u32[]{:S(2)}, u32[]{:S(2)}) collective-permute-start(bf16[1056,128]{1,0:T(8,128)(2,1)S(1)} %get-tuple-element.59.y_ref), channel_id=1, source_target_pairs={{0,1},{1,0},{16,17},{17,16},{2,3},{3,2},{18,19},{19,18},{4,5},{5,4... | collective-permute-start | bytes 811016 | tf_op jit(solution)/shard_map/ppermute | solution.py:59
  87.3 30.5 %collective-permute-start.7 = (bf16[1056,128]{1,0:T(8,128)(2,1)S(1)}, bf16[1056,128]{1,0:T(8,128)(2,1)}, u32[]{:S(2)}, u32[]{:S(2)}) collective-permute-start(bf16[1056,128]{1,0:T(8,128)(2,1)S(1)} %get-tuple-element.59.y_ref), channel_id=1, source_target_pairs={{0,16},{1,17},{16,0},{17,1},{2,18},{3,19},{18,2},{19,3},{4,20},{5,... | collective-permute-start | bytes 811016 | tf_op jit(solution)/shard_map/ppermute | solution.py:59
  90.7 27.1 %collective-permute-start.8 = (bf16[1056,128]{1,0:T(8,128)(2,1)S(1)}, bf16[1056,128]{1,0:T(8,128)(2,1)}, u32[]{:S(2)}, u32[]{:S(2)}) collective-permute-start(bf16[1056,128]{1,0:T(8,128)(2,1)S(1)} %get-tuple-element.59.y_ref), channel_id=1, source_target_pairs={{0,17},{1,16},{16,1},{17,0},{2,19},{3,18},{18,3},{19,2},{4,21},{5,... | collective-permute-start | bytes 811016 | tf_op jit(solution)/shard_map/ppermute | solution.py:59
  94.0 23.8 %all-to-all-start.2 = ((f32[16,8,128]{2,1,0:T(8,128)}), f32[16,8,128]{2,1,0:T(8,128)S(1)}, u32[]{:S(2)}, u32[]{:S(2)}) async-start(f32[16,8,128]{2,1,0:T(8,128)} %broadcast_in_dim.29), calls=%async_computation.2 | async-start | bytes 131072 | tf_op jit(solution)/shard_map/all_to_all | solution.py:516
  119.2 14.8 %all-to-all-start.3 = ((f32[16,8,128]{2,1,0:T(8,128)}), f32[16,8,128]{2,1,0:T(8,128)S(1)}, u32[]{:S(2)}, u32[]{:S(2)}) async-start(f32[16,8,128]{2,1,0:T(8,128)} %get-tuple-element.62), calls=%async_computation.3 | async-start | bytes 131072 | tf_op jit(solution)/shard_map/all_to_all | solution.py:533
  135.4 18.9 %all-to-all-start.4 = ((f32[16,16,128]{2,1,0:T(8,128)}), f32[16,16,128]{2,1,0:T(8,128)S(1)}, u32[]{:S(2)}, u32[]{:S(2)}) async-start(f32[16,16,128]{2,1,0:T(8,128)} %loss.1), calls=%async_computation.4 | async-start | bytes 262144 | tf_op jit(solution)/shard_map/all_to_all | solution.py:549
  139.8 1.2 copy-start.1
  141.0 20.9 %copy-start.4 = (bf16[4,16,64,128]{3,2,1,0:T(8,128)(2,1)S(1)}, bf16[4,16,64,128]{3,2,1,0:T(8,128)(2,1)}, u32[]{:S(2)}) copy-start(bf16[4,16,64,128]{3,2,1,0:T(8,128)(2,1)} %copy-done.3) | copy-start | bytes 3145732
  155.7 26.3 %all-to-all-start.5 = ((f32[16,8,128]{2,1,0:T(8,128)}), f32[16,8,128]{2,1,0:T(8,128)S(1)}, u32[]{:S(2)}, u32[]{:S(2)}) async-start(f32[16,8,128]{2,1,0:T(8,128)} %get-tuple-element.82), calls=%async_computation.5 | async-start | bytes 131072 | tf_op jit(solution)/shard_map/all_to_all | solution.py:569
  162.0 8.3 %copy-start.2 = (bf16[4224,128]{1,0:T(8,128)(2,1)S(1)}, bf16[4224,128]{1,0:T(8,128)(2,1)}, u32[]{:S(2)}) copy-start(bf16[4224,128]{1,0:T(8,128)(2,1)} %pad_maximum_fusion.y_ref) | copy-start | bytes 3244036
  183.5 12.2 %collective-permute-start.10 = (bf16[8,1536]{1,0:T(8,128)(2,1)S(1)}, bf16[8,1536]{1,0:T(8,128)(2,1)S(1)}, u32[]{:S(2)}, u32[]{:S(2)}) collective-permute-start(bf16[8,1536]{1,0:T(8,128)(2,1)S(1)} %slice.11), channel_id=1, source_target_pairs={{0,256},{128,384},{256,0},{384,128},{1,257},{129,385},{257,1},{385... | collective-permute-start | bytes 73736 | tf_op jit(solution)/shard_map/ppermute | solution.py:59
  186.0 9.7 %collective-permute-start.11 = (bf16[8,1536]{1,0:T(8,128)(2,1)S(1)}, bf16[8,1536]{1,0:T(8,128)(2,1)S(1)}, u32[]{:S(2)}, u32[]{:S(2)}) collective-permute-start(bf16[8,1536]{1,0:T(8,128)(2,1)S(1)} %slice.11), channel_id=1, source_target_pairs={{0,384},{128,256},{256,128},{384,0},{1,385},{129,257},{257,129},{3... | collective-permute-start | bytes 73736 | tf_op jit(solution)/shard_map/ppermute | solution.py:59
  191.5 7.2 %collective-permute-start.9 = (bf16[8,1536]{1,0:T(8,128)(2,1)S(1)}, bf16[8,1536]{1,0:T(8,128)(2,1)S(1)}, u32[]{:S(2)}, u32[]{:S(2)}) collective-permute-start(bf16[8,1536]{1,0:T(8,128)(2,1)S(1)} %slice.11), channel_id=1, source_target_pairs={{0,128},{128,0},{256,384},{384,256},{1,129},{129,1},{257,385},{385... | collective-permute-start | bytes 73736 | tf_op jit(solution)/shard_map/ppermute | solution.py:59
  198.7 22.1 %collective-permute-start.12 = (bf16[32,1536]{1,0:T(8,128)(2,1)S(1)}, bf16[32,1536]{1,0:T(8,128)(2,1)S(1)}, u32[]{:S(2)}, u32[]{:S(2)}) collective-permute-start(bf16[32,1536]{1,0:T(8,128)(2,1)S(1)} %pad_maximum_fusion.2), channel_id=1, source_target_pairs={{0,32},{32,0},{64,96},{96,64},{1,33},{33,1},{65,97},{97,65},{2,34}... | collective-permute-start | bytes 294920 | tf_op jit(solution)/shard_map/ppermute | solution.py:59
  200.7 20.1 %collective-permute-start.13 = (bf16[32,1536]{1,0:T(8,128)(2,1)S(1)}, bf16[32,1536]{1,0:T(8,128)(2,1)S(1)}, u32[]{:S(2)}, u32[]{:S(2)}) collective-permute-start(bf16[32,1536]{1,0:T(8,128)(2,1)S(1)} %pad_maximum_fusion.2), channel_id=1, source_target_pairs={{0,64},{32,96},{64,0},{96,32},{1,65},{33,97},{65,1},{97,33},{2,66}... | collective-permute-start | bytes 294920 | tf_op jit(solution)/shard_map/ppermute | solution.py:59
  203.5 17.3 %collective-permute-start.14 = (bf16[32,1536]{1,0:T(8,128)(2,1)S(1)}, bf16[32,1536]{1,0:T(8,128)(2,1)S(1)}, u32[]{:S(2)}, u32[]{:S(2)}) collective-permute-start(bf16[32,1536]{1,0:T(8,128)(2,1)S(1)} %pad_maximum_fusion.2), channel_id=1, source_target_pairs={{0,96},{32,64},{64,32},{96,0},{1,97},{33,65},{65,33},{97,1},{2,98}... | collective-permute-start | bytes 294920 | tf_op jit(solution)/shard_map/ppermute | solution.py:59
  208.8 30.5 %all-to-all-start.6 = ((bf16[16,64,128]{2,1,0:T(8,128)(2,1)}), bf16[16,64,128]{2,1,0:T(8,128)(2,1)S(1)}, u32[]{:S(2)}, u32[]{:S(2)}) async-start(bf16[16,64,128]{2,1,0:T(8,128)(2,1)} %columns.1), calls=%async_computation.6 | async-start | bytes 524288 | tf_op jit(solution)/shard_map/all_to_all | solution.py:596
  (2 other events, 1.6 us)

commit v6 on v5

--- a/solution.py
+++ b/solution.py
@@ -69,13 +69,6 @@
             jnp.concatenate([other, value], axis=0),
         )
     return value
-
-
-def gather_pair(value, axes):
-    square = [value] + [swap(value, axes, flip) for flip in (1, 2, 3)]
-    low, high = lax.axis_index(axes[1]) == 0, lax.axis_index(axes[0]) == 0
-    turned = [jnp.where(low, square[n], square[n ^ 1]) for n in range(4)]
-    return jnp.concatenate([jnp.where(high, turned[n], turned[n ^ 2]) for n in range(4)], axis=0)
 
 
 def three(value):
@@ -198,13 +191,14 @@
     attn_sums = jnp.dot(member, y_ref[0:QUARTER, :], preferred_element_type=F32)
     sums = jnp.sum(own_ref[:, 96:112, :].astype(F32), axis=0)
     input_sums = (sums[0:8] + pltpu.roll(sums[0:8], 64, 1)) + sums[8:16]
-    means_ref[...] = jnp.where(lanes(GROUPS) < 64, input_sums, attn_sums) / lengths_of(lens_ref)
+    means = jnp.where(lanes(GROUPS) < 64, input_sums, attn_sums) / lengths_of(lens_ref)
+    means_ref[...] = jnp.concatenate([means, means], axis=0)
 
 
 def pool_kernel(doc_ref, means_ref, w_ref, query_ref, row_ref, own_ref, means_out_ref, logits_ref, out_ref):
-    columns = [means_ref[z, :, 0:64] for z in range(PLANE)]
+    columns = [means_ref[z, 0:8, 0:64] for z in range(PLANE)]
     heads = [
-        means_ref[z, :, 64:128] + means_ref[z + 1, :, 64:128] for z in range(0, PLANE, 2)
+        means_ref[z, 0:8, 64:128] + means_ref[z + 1, 0:8, 64:128] for z in range(0, PLANE, 2)
     ]
     means = jnp.concatenate(heads, axis=1)
     projected = jnp.dot(stacked(means), w_ref[...], preferred_element_type=F32)
@@ -344,7 +338,9 @@
         members, stacked(grad / lengths_of(lens_ref)[:, 0:1]), TN, preferred_element_type=F32
     ).astype(BF16)
     both = jnp.concatenate([grad, means_ref[...]], axis=1)
-    out_ref[...] = jnp.concatenate([both, jnp.zeros_like(both)], axis=0).astype(BF16)
+    wide = (MODEL + WIDTH) // 2
+    both = jnp.concatenate([both[:, :wide], both[:, wide:]], axis=0)
+    out_ref[...] = jnp.broadcast_to(both.astype(BF16)[None], (DOCS, 2 * GROUPS, wide))
 
 
 def value_kernel(lens_ref, parts_ref, w_ref, grad_v_ref):
@@ -367,8 +363,12 @@
 
 
 def weight_kernel(in_ref, out_ref):
+    wide = (MODEL + WIDTH) // 2
+    both = in_ref[...].astype(F32)
+    both = [both[:, n : n + 8].reshape(DOCS * GROUPS, wide) for n in (0, 8)]
+    both = jnp.concatenate(both, axis=1).astype(BF16)
     out_ref[...] = lax.dot_general(
-        in_ref[:, MODEL:], in_ref[:, :MODEL], TN, preferred_element_type=F32
+        both[:, MODEL:], both[:, :MODEL], TN, preferred_element_type=F32
     )
 
 
@@ -376,7 +376,9 @@
 TALL = 512
 
 
-def row_kernel(place_ref, lens_ref, y_ref, lse_ref, x_ref, dattn_ref, out_ref, q_s, d_s, delta_s):
+def row_kernel(
+    place_ref, lens_ref, y_ref, lse_ref, x_ref, dattn_ref, grad_k_ref, out_ref, q_s, d_s, delta_s
+):
     lane = lanes(QUARTER)
     member = quarter_member(lens_ref, place_ref[0], place_ref[1]).astype(BF16)
     spread = lax.dot_general(
@@ -406,14 +408,17 @@
             score_grad = (jnp.exp(scores - log_total) * (prob_grad - delta)).astype(BF16)
             total = total + jnp.dot(score_grad, part, preferred_element_type=F32)
         total = total * SCALE
-        out_ref[rows, :] = jnp.concatenate([total[:, 0:64]] * 2, axis=1).astype(BF16)
+        total = jnp.concatenate([total[:, 0:64]] * 2, axis=1).astype(BF16)
+        both = jnp.where(lanes(TALL) < 64, grad_k_ref[rows, :], total)
+        count = TALL // HALF
+        out_ref[pl.ds(i * count, count), :, :] = both.reshape(count, HALF, 128)
         return carry
 
     lax.fori_loop(0, QUARTER // TALL, block, 0)
 
 
 def column_kernel(
-    lens_ref, own_ref, y_ref, lse_ref, dattn_ref, grad_q_ref, out_ref, y_s, k_s, v_s, delta_s
+    lens_ref, own_ref, y_ref, lse_ref, dattn_ref, out_ref, y_s, k_s, v_s, delta_s
 ):
     lane = lanes(QUARTER)
     mine = own_ref[:, 0:64, :].reshape(QUARTER, 128)
@@ -444,9 +449,7 @@
                 jnp.exp(scores - lse_ref[0:1, cols]) * (prob_grad - delta_s[0:1, cols])
             ).astype(BF16)
             total = total + jnp.dot(score_grad, part, preferred_element_type=F32)
-        both = jnp.where(lanes(BLOCK) < 64, total.astype(BF16), grad_q_ref[rows, :])
-        count = BLOCK // HALF
-        out_ref[pl.ds(i * count, count), :, :] = both.reshape(count, HALF, 128)
+        out_ref[rows, :] = total.astype(BF16)
         return carry
 
     lax.fori_loop(0, QUARTER // BLOCK, block, 0)
@@ -463,7 +466,7 @@
         in_specs=[SMEM] * len(scalars) + [VMEM] * len(arrays),
         out_specs=jax.tree.map(lambda _: VMEM, outs),
         scratch_shapes=scratch,
-        compiler_params=params(bool(scratch)),
+        compiler_params=params(bool(scratch) or name == "pack"),
         cost_estimate=estimate,
         name=name,
     )(*scalars, *arrays)
@@ -494,10 +497,10 @@
     )
     packed, tagged = barrier((packed, tagged))
     own = exchange(packed, ZED)
-    queries = gather(tagged, ("yh", "yl", "xa", "xb"))
+    queries = gather(tagged, ("yh", "yl", "xa"))
     own, queries = barrier((own, queries))
     keys = share(own[:, 0:64, :], SQUARE).reshape(KEYS, 128)
-    queries = gather(queries, ("co",))
+    queries = gather(queries, ("xb", "co"))
     own, keys, queries = barrier((own, keys, queries))
 
     mine, lse, means = call(
@@ -505,13 +508,13 @@
         (
             shape((QUARTER + 32, 128), BF16),
             shape((8, 128), F32),
-            shape((GROUPS, 128), F32),
+            shape((2 * GROUPS, 128), F32),
         ),
         (place, lengths), (own, keys), [pltpu.VMEM((QUARTER, 128), BF16)],
         cost(pairs * 256 * 4, 3000000, pairs), "forward",
     )
     means = means + swap(means, ("yl",), 1)
-    means = jnp.broadcast_to(means[None], (PLANE, GROUPS, 128))
+    means = jnp.broadcast_to(means[None], (PLANE, 2 * GROUPS, 128))
     mine, means, queries = barrier((mine, means, queries))
     means = exchange(means, ZED)
     around = [swap(mine, SQUARE, flip) for flip in (1, 2, 3)]
@@ -567,18 +570,9 @@
     )
     mean_loss = loss[0, 64]
     grad_parts = exchange(grad_part, ZED)
-    grad_rows = call(
-        row_kernel, shape((QUARTER, 128), BF16), (place, lengths), (mine, lse, keys, dattn),
-        [
-            pltpu.VMEM((QUARTER, 128), BF16),
-            pltpu.VMEM((QUARTER, 128), BF16),
-            pltpu.VMEM((QUARTER, 128), F32),
-        ],
-        cost(pairs * 256 * 6, 2000000, pairs), "rows",
-    )
-    packed_grads = call(
-        column_kernel, shape((PLANE, HALF, 128), BF16), (lengths,),
-        (own, others, lse_rows, dattn, grad_rows),
+    grad_columns = call(
+        column_kernel, shape((QUARTER, 128), BF16), (lengths,),
+        (own, others, lse_rows, dattn),
         [
             pltpu.VMEM((KEYS, 128), BF16),
             pltpu.VMEM((QUARTER, 128), BF16),
@@ -587,25 +581,36 @@
         ],
         cost(pairs * 256 * 6, 2500000, pairs), "columns",
     )
-    packed_grads, grad_parts = barrier((packed_grads, grad_parts))
     grad_inputs, grads = call(
         inputs_kernel,
-        (shape((ROWS, MODEL), BF16), shape((2 * GROUPS, MODEL + WIDTH), BF16)),
+        (shape((ROWS, MODEL), BF16), shape((DOCS, 2 * GROUPS, (MODEL + WIDTH) // 2), BF16)),
         (place, lengths), (grad_parts, doc_means), (), cost(2 * 32 * 128 * 1024, 1200000), "inputs",
     )
+    grad_columns, grads = barrier((grad_columns, grads))
+    all_grads = exchange(grads, GRP)
+    packed_grads = call(
+        row_kernel, shape((PLANE, HALF, 128), BF16), (place, lengths),
+        (mine, lse, keys, dattn, grad_columns),
+        [
+            pltpu.VMEM((QUARTER, 128), BF16),
+            pltpu.VMEM((QUARTER, 128), BF16),
+            pltpu.VMEM((QUARTER, 128), F32),
+        ],
+        cost(pairs * 256 * 6, 2000000, pairs), "rows",
+    )
+    packed_grads, grad_parts = barrier((packed_grads, grad_parts))
     home = exchange(packed_grads, ZED)
-    all_grads = gather_pair(gather_pair(grads[0:GROUPS], ("yh", "xa")), ("xb", "co"))
     out = shape((ROWS, WIDTH), BF16)
     grad_v = call(
-        value_kernel, out, (lengths,), (grad_parts, w_out), (), cost(0, 0),
+        value_kernel, out, (lengths,), (grad_parts, w_out), (), cost(2 * 32 * 512 * 1024, 1300000),
         "values",
     )
     grad_w_out = call(
         weight_kernel, shape((WIDTH, MODEL), F32), (), (all_grads,), (),
-        cost(0, 0), "weights",
+        cost(2 * 384 * 512 * 1024, 3000000), "weights",
     )
     grad_q, grad_k = call(
-        unpack_kernel, (out, out), (), (home,), (), cost(0, 0), "unpack"
+        unpack_kernel, (out, out), (), (home,), (), cost(0, 500000), "unpack"
     )
     return (mean_loss, grad_inputs[None], grad_q[None], grad_k[None], grad_v[None], grad_w_out)
 

time: 241 us -> 225 us (0.934)
  the two profiles are of different devices: /device:TPU:32 before, /device:TPU:2 now
where the time goes in v6:
time: 225 us; the launch traced here: 224 us
  starting transfers between devices  96.4 us (43%)
  waiting for transfers between devices  56.8 us (25%)
  Pallas kernels  51.7 us (23%)
  local copies, waits for them, and re-layouts  12 us (5%)
  other arithmetic  5.85 us (3%)
    pallas_call x14, Pallas kernels, call(): pl.pallas_call(kernel, out_shape=outs, in_specs=[SMEM] * len(scalars) + [...  51.7 us
    ppermute x9, starting transfers between devices, swap(): return lax.ppermute(value, axes, [(i, i ^ flip) for i in range(count)])  30.2 us
    ppermute x9, waiting for transfers between devices, swap(): return lax.ppermute(value, axes, [(i, i ^ flip) for i in range(count)])  28.5 us
    all_to_all x1, starting transfers between devices, body(): own = exchange(packed, ZED)  15.2 us
    all_to_all x1, waiting for transfers between devices, body(): home = exchange(packed_grads, ZED)  14.3 us
    all_to_all x1, starting transfers between devices, body(): home = exchange(packed_grads, ZED)  11.1 us
    all_to_all x1, starting transfers between devices, body(): terms = exchange(terms, ZED)  10.1 us
    unnamed x28, local copies, waits for them, and re-layouts  9.44 us
  transfers between devices with their start and end apart: 17, of which 13 were waited for; matrix products, arithmetic and copies ran while one was open for 2% of the time, Pallas kernels for 15%

profile of v6, /device:TPU:2, one launch (start us, length us, event | category | flops | bytes accessed | tf_op | source)
XLA Modules:
  0.0 223.8 jit_solution(10424144226946861498)
XLA Ops:
  8.1 15.2 %all-to-all-start = ((bf16[16,112,128]{2,1,0:T(8,128)(2,1)}), bf16[16,112,128]{2,1,0:T(8,128)(2,1)S(1)}, u32[]{:S(2)}, u32[]{:S(2)}) async-start(bf16[16,112,128]{2,1,0:T(8,128)(2,1)} %pack.1), calls=%async_computation | async-start | bytes 917504 | tf_op jit(solution)/shard_map/all_to_all | solution.py:499
  23.3 5.1 %collective-permute-start = (bf16[16,1152]{1,0:T(8,128)(2,1)S(1)}, bf16[16,1152]{1,0:T(8,128)(2,1)S(1)}, u32[]{:S(2)}, u32[]{:S(2)}) collective-permute-start(bf16[16,1152]{1,0:T(8,128)(2,1)S(1)} %fusion.1), channel_id=1, source_target_pairs={{0,256},{256,0},{1,257},{257,1},{2,258},{258,2},{3,259},{259,3},{4... | collective-permute-start | bytes 110600 | tf_op jit(solution)/shard_map/ppermute | solution.py:59
  28.4 2.2 %collective-permute-done = bf16[16,1152]{1,0:T(8,128)(2,1)S(1)} collective-permute-done((bf16[16,1152]{1,0:T(8,128)(2,1)S(1)}, bf16[16,1152]{1,0:T(8,128)(2,1)S(1)}, u32[]{:S(2)}, u32[]{:S(2)}) %collective-permute-start) | collective-permute-done | bytes 36896 | tf_op jit(solution)/shard_map/ppermute | solution.py:59
  30.7 3.5 %collective-permute-start.1 = (bf16[32,1152]{1,0:T(8,128)(2,1)S(1)}, bf16[32,1152]{1,0:T(8,128)(2,1)S(1)}, u32[]{:S(2)}, u32[]{:S(2)}) collective-permute-start(bf16[32,1152]{1,0:T(8,128)(2,1)S(1)} %maximum_select_fusion.4), channel_id=1, source_target_pairs={{0,16},{16,0},{1,17},{17,1},{2,18},{18,2},{3,19},{19,3},{4,20},{20... | collective-permute-start | bytes 221192 | tf_op jit(solution)/shard_map/ppermute | solution.py:59
  34.2 2.7 %collective-permute-done.1 = bf16[32,1152]{1,0:T(8,128)(2,1)S(1)} collective-permute-done((bf16[32,1152]{1,0:T(8,128)(2,1)S(1)}, bf16[32,1152]{1,0:T(8,128)(2,1)S(1)}, u32[]{:S(2)}, u32[]{:S(2)}) %collective-permute-start.1) | collective-permute-done | bytes 73760 | tf_op jit(solution)/shard_map/ppermute | solution.py:59
  37.0 4.0 %collective-permute-start.2 = (bf16[64,1152]{1,0:T(8,128)(2,1)S(1)}, bf16[64,1152]{1,0:T(8,128)(2,1)S(1)}, u32[]{:S(2)}, u32[]{:S(2)}) collective-permute-start(bf16[64,1152]{1,0:T(8,128)(2,1)S(1)} %maximum_select_fusion.3), channel_id=1, source_target_pairs={{0,128},{128,0},{1,129},{129,1},{2,130},{130,2},{3,131},{131,3},{4... | collective-permute-start | bytes 442376 | tf_op jit(solution)/shard_map/ppermute | solution.py:59
  41.0 4.5 %collective-permute-done.2 = bf16[64,1152]{1,0:T(8,128)(2,1)S(1)} collective-permute-done((bf16[64,1152]{1,0:T(8,128)(2,1)S(1)}, bf16[64,1152]{1,0:T(8,128)(2,1)S(1)}, u32[]{:S(2)}, u32[]{:S(2)}) %collective-permute-start.2) | collective-permute-done | bytes 147488 | tf_op jit(solution)/shard_map/ppermute | solution.py:59
  45.6 4.5 %all-to-all-done.own_ref = bf16[16,112,128]{2,1,0:T(8,128)(2,1)S(1)} async-done(((bf16[16,112,128]{2,1,0:T(8,128)(2,1)}), bf16[16,112,128]{2,1,0:T(8,128)(2,1)S(1)}, u32[]{:S(2)}, u32[]{:S(2)}) %all-to-all-start) | async-done | bytes 458784 | tf_op jit(solution)/shard_map/all_to_all | solution.py:499
  51.3 3.5 %all-to-all-start.1 = ((bf16[4,16,64,128]{3,2,1,0:T(8,128)(2,1)}), bf16[4,16,64,128]{3,2,1,0:T(8,128)(2,1)S(1)}, u32[]{:S(2)}, u32[]{:S(2)}) async-start(bf16[4,16,64,128]{3,2,1,0:T(8,128)(2,1)} %broadcast_in_dim.28), calls=%async_computation.1 | async-start | bytes 2097152 | tf_op jit(solution)/shard_map/all_to_all | solution.py:52
  54.9 2.4 %collective-permute-start.3 = (bf16[128,1152]{1,0:T(8,128)(2,1)S(1)}, bf16[128,1152]{1,0:T(8,128)(2,1)S(1)}, u32[]{:S(2)}, u32[]{:S(2)}) collective-permute-start(bf16[128,1152]{1,0:T(8,128)(2,1)S(1)} %maximum_select_fusion.2), channel_id=1, source_target_pairs={{0,64},{64,0},{1,65},{65,1},{2,66},{66,2},{3,67},{67,3},{4,68},{68... | collective-permute-start | bytes 884744 | tf_op jit(solution)/shard_map/ppermute | solution.py:59
  57.3 6.2 %collective-permute-done.3 = bf16[128,1152]{1,0:T(8,128)(2,1)S(1)} collective-permute-done((bf16[128,1152]{1,0:T(8,128)(2,1)S(1)}, bf16[128,1152]{1,0:T(8,128)(2,1)S(1)}, u32[]{:S(2)}, u32[]{:S(2)}) %collective-permute-start.3) | collective-permute-done | bytes 294944 | tf_op jit(solution)/shard_map/ppermute | solution.py:59
  65.6 2.1 collective-permute-done.4
  67.7 1.9 maximum_select_fusion.query_ref
  69.6 9.0 %forward.1 = (bf16[1056,128]{1,0:T(8,128)(2,1)S(1)}, f32[8,128]{1,0:T(8,128)S(1)}, f32[16,128]{1,0:T(8,128)S(1)}) custom-call(s32[4]{0:T(128)S(1)} %pad_add_fusion.place_ref, s32[8]{0:T(128)S(1)} %bitcast.25, bf16[16,112,128]{2,1,0:T(8,128)(2,1)S(1)} %all-to-all-done.own_ref, bf16[4096,128]{1,0:T(8,128)(2,1)S(1)} %bitcast.18), custom_call_target="tpu_custom_call" | custom-call | flops 4294967296 | bytes 3000000 | tf_op jit(solution)/shard_map/forward/pallas_call | solution.py:463
  79.6 4.0 %collective-permute-start.5 = (f32[16,128]{1,0:T(8,128)S(1)}, f32[16,128]{1,0:T(8,128)S(1)}, u32[]{:S(2)}, u32[]{:S(2)}) collective-permute-start(f32[16,128]{1,0:T(8,128)S(1)} %get-tuple-element.57), channel_id=1, source_target_pairs={{0,16},{16,0},{1,17},{17,1},{2,18},{18,2},{3,19},{19,3},{4,20},{20... | collective-permute-start | bytes 24584 | tf_op jit(solution)/shard_map/ppermute | solution.py:59
  85.9 8.0 %all-to-all-start.2 = ((f32[16,16,128]{2,1,0:T(8,128)}), f32[16,16,128]{2,1,0:T(8,128)S(1)}, u32[]{:S(2)}, u32[]{:S(2)}) async-start(f32[16,16,128]{2,1,0:T(8,128)} %broadcast_in_dim.29), calls=%async_computation.2 | async-start | bytes 262144 | tf_op jit(solution)/shard_map/all_to_all | solution.py:519
  94.0 3.8 %collective-permute-start.6 = (bf16[1056,128]{1,0:T(8,128)(2,1)S(1)}, bf16[1056,128]{1,0:T(8,128)(2,1)S(1)}, u32[]{:S(2)}, u32[]{:S(2)}) collective-permute-start(bf16[1056,128]{1,0:T(8,128)(2,1)S(1)} %get-tuple-element.61.y_ref), channel_id=1, source_target_pairs={{0,1},{1,0},{16,17},{17,16},{2,3},{3,2},{18,19},{19,18},{4,5},{5,4... | collective-permute-start | bytes 811016 | tf_op jit(solution)/shard_map/ppermute | solution.py:59
  97.8 3.4 %collective-permute-start.7 = (bf16[1056,128]{1,0:T(8,128)(2,1)S(1)}, bf16[1056,128]{1,0:T(8,128)(2,1)}, u32[]{:S(2)}, u32[]{:S(2)}) collective-permute-start(bf16[1056,128]{1,0:T(8,128)(2,1)S(1)} %get-tuple-element.61.y_ref), channel_id=1, source_target_pairs={{0,16},{1,17},{16,0},{17,1},{2,18},{3,19},{18,2},{19,3},{4,20},{5,... | collective-permute-start | bytes 811016 | tf_op jit(solution)/shard_map/ppermute | solution.py:59
  101.2 2.0 collective-permute-start.8
  105.0 3.2 %collective-permute-done.6 = bf16[1056,128]{1,0:T(8,128)(2,1)S(1)} collective-permute-done((bf16[1056,128]{1,0:T(8,128)(2,1)S(1)}, bf16[1056,128]{1,0:T(8,128)(2,1)S(1)}, u32[]{:S(2)}, u32[]{:S(2)}) %collective-permute-start.6) | collective-permute-done | bytes 270368 | tf_op jit(solution)/shard_map/ppermute | solution.py:59
  108.2 6.0 %collective-permute-done.8 = bf16[1056,128]{1,0:T(8,128)(2,1)} collective-permute-done((bf16[1056,128]{1,0:T(8,128)(2,1)S(1)}, bf16[1056,128]{1,0:T(8,128)(2,1)}, u32[]{:S(2)}, u32[]{:S(2)}) %collective-permute-start.8) | collective-permute-done | bytes 270368 | tf_op jit(solution)/shard_map/ppermute | solution.py:59
  115.6 7.5 %all-to-all-start.3 = ((f32[16,8,128]{2,1,0:T(8,128)}), f32[16,8,128]{2,1,0:T(8,128)S(1)}, u32[]{:S(2)}, u32[]{:S(2)}) async-start(f32[16,8,128]{2,1,0:T(8,128)} %get-tuple-element.64), calls=%async_computation.3 | async-start | bytes 131072 | tf_op jit(solution)/shard_map/all_to_all | solution.py:536
  127.0 2.4 %all-to-all-done.3.sums_ref = f32[16,8,128]{2,1,0:T(8,128)S(1)} async-done(((f32[16,8,128]{2,1,0:T(8,128)}), f32[16,8,128]{2,1,0:T(8,128)S(1)}, u32[]{:S(2)}, u32[]{:S(2)}) %all-to-all-start.3) | async-done | bytes 65568 | tf_op jit(solution)/shard_map/all_to_all | solution.py:536
  130.7 10.1 %all-to-all-start.4 = ((f32[16,16,128]{2,1,0:T(8,128)}), f32[16,16,128]{2,1,0:T(8,128)S(1)}, u32[]{:S(2)}, u32[]{:S(2)}) async-start(f32[16,16,128]{2,1,0:T(8,128)} %loss.1), calls=%async_computation.4 | async-start | bytes 262144 | tf_op jit(solution)/shard_map/all_to_all | solution.py:552
  142.0 7.4 %mass.1 = (f32[8,8,128]{2,1,0:T(8,128)S(1)}, f32[8,4096]{1,0:T(8,128)S(1)}) custom-call(s32[8]{0:T(128)S(1)} %bitcast.26, bf16[16,112,128]{2,1,0:T(8,128)(2,1)S(1)} %all-to-all-done.own_ref, bf16[4224,128]{1,0:T(8,128)(2,1)S(1)} %copy-done.1), custom_call_target="tpu_custom_call" | custom-call | flops 4294967296 | bytes 2500000 | tf_op jit(solution)/shard_map/mass/pallas_call | solution.py:463
  149.4 6.1 %all-to-all-done.4.terms_ref = f32[16,16,128]{2,1,0:T(8,128)S(1)} async-done(((f32[16,16,128]{2,1,0:T(8,128)}), f32[16,16,128]{2,1,0:T(8,128)S(1)}, u32[]{:S(2)}, u32[]{:S(2)}) %all-to-all-start.4) | async-done | bytes 131104 | tf_op jit(solution)/shard_map/all_to_all | solution.py:552
  156.9 6.0 %all-to-all-start.5 = ((f32[16,8,128]{2,1,0:T(8,128)}), f32[16,8,128]{2,1,0:T(8,128)S(1)}, u32[]{:S(2)}, u32[]{:S(2)}) async-start(f32[16,8,128]{2,1,0:T(8,128)} %get-tuple-element.81), calls=%async_computation.5 | async-start | bytes 131072 | tf_op jit(solution)/shard_map/all_to_all | solution.py:572
  162.9 11.0 %columns.1.grad_k_ref = bf16[1024,128]{1,0:T(8,128)(2,1)S(1)} custom-call(s32[8]{0:T(128)S(1)} %bitcast.28, bf16[16,112,128]{2,1,0:T(8,128)(2,1)S(1)} %all-to-all-done.own_ref, bf16[4224,128]{1,0:T(8,128)(2,1)S(1)} %copy-done.2, f32[8,4096]{1,0:T(8,128)S(1)} %get-tuple-element.86.lse_ref, f32[8,128]{1,0:T(8,128)S(1)} %get-tuple-element.85.dattn_ref), custom_call_target="tpu_custom_call" | custom-call | flops 6442450944 | bytes 2500000 | tf_op jit(solution)/shard_map/columns/pallas_call | solution.py:463
  177.1 4.9 %all-to-all-start.7 = ((bf16[16,16,768]{2,1,0:T(8,128)(2,1)}), bf16[16,16,768]{2,1,0:T(8,128)(2,1)S(1)}, u32[]{:S(2)}, u32[]{:S(2)}) async-start(bf16[16,16,768]{2,1,0:T(8,128)(2,1)} %get-tuple-element.93), calls=%async_computation.7 | async-start | bytes 786432 | tf_op jit(solution)/shard_map/all_to_all | solution.py:590
  184.2 9.1 %rows.1 = bf16[16,64,128]{2,1,0:T(8,128)(2,1)} custom-call(s32[4]{0:T(128)S(1)} %pad_add_fusion.place_ref, s32[8]{0:T(128)S(1)} %bitcast.30, bf16[1056,128]{1,0:T(8,128)(2,1)S(1)} %get-tuple-element.61.y_ref, f32[8,128]{1,0:T(8,128)S(1)} %get-tuple-element.84.lse_ref, bf16[4096,128]{1,0:T(8,128)(2,1)S(1)} %bitcast.19, ...), custom_call_target="tpu_custom_call" | custom-call | flops 6442450944 | bytes 2000000 | tf_op jit(solution)/shard_map/rows/pallas_call | solution.py:463
  193.4 11.1 %all-to-all-start.6 = ((bf16[16,64,128]{2,1,0:T(8,128)(2,1)}), bf16[16,64,128]{2,1,0:T(8,128)(2,1)S(1)}, u32[]{:S(2)}, u32[]{:S(2)}) async-start(bf16[16,64,128]{2,1,0:T(8,128)(2,1)} %rows.1), calls=%async_computation.6 | async-start | bytes 524288 | tf_op jit(solution)/shard_map/all_to_all | solution.py:602
  208.6 14.3 %all-to-all-done.6.in_ref = bf16[16,64,128]{2,1,0:T(8,128)(2,1)S(1)} async-done(((bf16[16,64,128]{2,1,0:T(8,128)(2,1)}), bf16[16,64,128]{2,1,0:T(8,128)(2,1)S(1)}, u32[]{:S(2)}, u32[]{:S(2)}) %all-to-all-start.6) | async-done | bytes 262176 | tf_op jit(solution)/shard_map/all_to_all | solution.py:602
  (60 shorter events, 35.6 us)
Async XLA Ops:
  2.2 1.0 copy-start.5
  3.2 0.9 copy-start.6
  4.1 0.9 copy-start.7
  5.0 0.9 copy-start.8
  5.9 0.7 copy-start.9
  8.1 42.0 %all-to-all-start = ((bf16[16,112,128]{2,1,0:T(8,128)(2,1)}), bf16[16,112,128]{2,1,0:T(8,128)(2,1)S(1)}, u32[]{:S(2)}, u32[]{:S(2)}) async-start(bf16[16,112,128]{2,1,0:T(8,128)(2,1)} %pack.1), calls=%async_computation | async-start | bytes 917504 | tf_op jit(solution)/shard_map/all_to_all | solution.py:499
  23.3 7.4 %collective-permute-start = (bf16[16,1152]{1,0:T(8,128)(2,1)S(1)}, bf16[16,1152]{1,0:T(8,128)(2,1)S(1)}, u32[]{:S(2)}, u32[]{:S(2)}) collective-permute-start(bf16[16,1152]{1,0:T(8,128)(2,1)S(1)} %fusion.1), channel_id=1, source_target_pairs={{0,256},{256,0},{1,257},{257,1},{2,258},{258,2},{3,259},{259,3},{4... | collective-permute-start | bytes 110600 | tf_op jit(solution)/shard_map/ppermute | solution.py:59
  30.7 6.2 %collective-permute-start.1 = (bf16[32,1152]{1,0:T(8,128)(2,1)S(1)}, bf16[32,1152]{1,0:T(8,128)(2,1)S(1)}, u32[]{:S(2)}, u32[]{:S(2)}) collective-permute-start(bf16[32,1152]{1,0:T(8,128)(2,1)S(1)} %maximum_select_fusion.4), channel_id=1, source_target_pairs={{0,16},{16,0},{1,17},{17,1},{2,18},{18,2},{3,19},{19,3},{4,20},{20... | collective-permute-start | bytes 221192 | tf_op jit(solution)/shard_map/ppermute | solution.py:59
  37.0 8.5 %collective-permute-start.2 = (bf16[64,1152]{1,0:T(8,128)(2,1)S(1)}, bf16[64,1152]{1,0:T(8,128)(2,1)S(1)}, u32[]{:S(2)}, u32[]{:S(2)}) collective-permute-start(bf16[64,1152]{1,0:T(8,128)(2,1)S(1)} %maximum_select_fusion.3), channel_id=1, source_target_pairs={{0,128},{128,0},{1,129},{129,1},{2,130},{130,2},{3,131},{131,3},{4... | collective-permute-start | bytes 442376 | tf_op jit(solution)/shard_map/ppermute | solution.py:59
  51.3 18.2 %all-to-all-start.1 = ((bf16[4,16,64,128]{3,2,1,0:T(8,128)(2,1)}), bf16[4,16,64,128]{3,2,1,0:T(8,128)(2,1)S(1)}, u32[]{:S(2)}, u32[]{:S(2)}) async-start(bf16[4,16,64,128]{3,2,1,0:T(8,128)(2,1)} %broadcast_in_dim.28), calls=%async_computation.1 | async-start | bytes 2097152 | tf_op jit(solution)/shard_map/all_to_all | solution.py:52
  54.9 8.6 %collective-permute-start.3 = (bf16[128,1152]{1,0:T(8,128)(2,1)S(1)}, bf16[128,1152]{1,0:T(8,128)(2,1)S(1)}, u32[]{:S(2)}, u32[]{:S(2)}) collective-permute-start(bf16[128,1152]{1,0:T(8,128)(2,1)S(1)} %maximum_select_fusion.2), channel_id=1, source_target_pairs={{0,64},{64,0},{1,65},{65,1},{2,66},{66,2},{3,67},{67,3},{4,68},{68... | collective-permute-start | bytes 884744 | tf_op jit(solution)/shard_map/ppermute | solution.py:59
  63.6 1.9 copy-start.13
  63.6 4.0 %collective-permute-start.4 = (bf16[256,1152]{1,0:T(8,128)(2,1)S(1)}, bf16[256,1152]{1,0:T(8,128)(2,1)}, u32[]{:S(2)}, u32[]{:S(2)}) collective-permute-start(bf16[256,1152]{1,0:T(8,128)(2,1)S(1)} %maximum_select_fusion.1), channel_id=1, source_target_pairs={{0,32},{32,0},{1,33},{33,1},{2,34},{34,2},{3,35},{35,3},{4,36},{36... | collective-permute-start | bytes 1769480 | tf_op jit(solution)/shard_map/ppermute | solution.py:59
  65.6 4.0 %copy-start.10 = (s32[1,8]{1,0:T(1,128)S(1)}, s32[1,8]{1,0:T(1,128)}, u32[]{:S(2)}) copy-start(s32[1,8]{1,0:T(1,128)} %param.13) | copy-start | bytes 100
  78.6 1.0 copy-start.3
  79.6 34.6 %copy-start = (bf16[512,1024]{1,0:T(8,128)(2,1)S(1)}, bf16[512,1024]{1,0:T(8,128)(2,1)}, u32[]{:S(2)}) copy-start(bf16[512,1024]{1,0:T(8,128)(2,1)} %w_ref.7) | copy-start | bytes 3145732
  79.6 5.7 %collective-permute-start.5 = (f32[16,128]{1,0:T(8,128)S(1)}, f32[16,128]{1,0:T(8,128)S(1)}, u32[]{:S(2)}, u32[]{:S(2)}) collective-permute-start(f32[16,128]{1,0:T(8,128)S(1)} %get-tuple-element.57), channel_id=1, source_target_pairs={{0,16},{16,0},{1,17},{17,1},{2,18},{18,2},{3,19},{19,3},{4,20},{20... | collective-permute-start | bytes 24584 | tf_op jit(solution)/shard_map/ppermute | solution.py:59
  85.9 28.2 %all-to-all-start.2 = ((f32[16,16,128]{2,1,0:T(8,128)}), f32[16,16,128]{2,1,0:T(8,128)S(1)}, u32[]{:S(2)}, u32[]{:S(2)}) async-start(f32[16,16,128]{2,1,0:T(8,128)} %broadcast_in_dim.29), calls=%async_computation.2 | async-start | bytes 262144 | tf_op jit(solution)/shard_map/all_to_all | solution.py:519
  94.0 14.2 %collective-permute-start.6 = (bf16[1056,128]{1,0:T(8,128)(2,1)S(1)}, bf16[1056,128]{1,0:T(8,128)(2,1)S(1)}, u32[]{:S(2)}, u32[]{:S(2)}) collective-permute-start(bf16[1056,128]{1,0:T(8,128)(2,1)S(1)} %get-tuple-element.61.y_ref), channel_id=1, source_target_pairs={{0,1},{1,0},{16,17},{17,16},{2,3},{3,2},{18,19},{19,18},{4,5},{5,4... | collective-permute-start | bytes 811016 | tf_op jit(solution)/shard_map/ppermute | solution.py:59
  97.8 10.4 %collective-permute-start.7 = (bf16[1056,128]{1,0:T(8,128)(2,1)S(1)}, bf16[1056,128]{1,0:T(8,128)(2,1)}, u32[]{:S(2)}, u32[]{:S(2)}) collective-permute-start(bf16[1056,128]{1,0:T(8,128)(2,1)S(1)} %get-tuple-element.61.y_ref), channel_id=1, source_target_pairs={{0,16},{1,17},{16,0},{17,1},{2,18},{3,19},{18,2},{19,3},{4,20},{5,... | collective-permute-start | bytes 811016 | tf_op jit(solution)/shard_map/ppermute | solution.py:59
  101.2 13.0 %collective-permute-start.8 = (bf16[1056,128]{1,0:T(8,128)(2,1)S(1)}, bf16[1056,128]{1,0:T(8,128)(2,1)}, u32[]{:S(2)}, u32[]{:S(2)}) collective-permute-start(bf16[1056,128]{1,0:T(8,128)(2,1)S(1)} %get-tuple-element.61.y_ref), channel_id=1, source_target_pairs={{0,17},{1,16},{16,1},{17,0},{2,19},{3,18},{18,3},{19,2},{4,21},{5,... | collective-permute-start | bytes 811016 | tf_op jit(solution)/shard_map/ppermute | solution.py:59
  115.6 13.7 %all-to-all-start.3 = ((f32[16,8,128]{2,1,0:T(8,128)}), f32[16,8,128]{2,1,0:T(8,128)S(1)}, u32[]{:S(2)}, u32[]{:S(2)}) async-start(f32[16,8,128]{2,1,0:T(8,128)} %get-tuple-element.64), calls=%async_computation.3 | async-start | bytes 131072 | tf_op jit(solution)/shard_map/all_to_all | solution.py:536
  130.7 24.8 %all-to-all-start.4 = ((f32[16,16,128]{2,1,0:T(8,128)}), f32[16,16,128]{2,1,0:T(8,128)S(1)}, u32[]{:S(2)}, u32[]{:S(2)}) async-start(f32[16,16,128]{2,1,0:T(8,128)} %loss.1), calls=%async_computation.4 | async-start | bytes 262144 | tf_op jit(solution)/shard_map/all_to_all | solution.py:552
  140.8 1.2 copy-start.1
  142.0 20.9 %copy-start.2 = (bf16[4224,128]{1,0:T(8,128)(2,1)S(1)}, bf16[4224,128]{1,0:T(8,128)(2,1)}, u32[]{:S(2)}) copy-start(bf16[4224,128]{1,0:T(8,128)(2,1)} %pad_maximum_fusion.y_ref) | copy-start | bytes 3244036
  156.9 18.7 %all-to-all-start.5 = ((f32[16,8,128]{2,1,0:T(8,128)}), f32[16,8,128]{2,1,0:T(8,128)S(1)}, u32[]{:S(2)}, u32[]{:S(2)}) async-start(f32[16,8,128]{2,1,0:T(8,128)} %get-tuple-element.81), calls=%async_computation.5 | async-start | bytes 131072 | tf_op jit(solution)/shard_map/all_to_all | solution.py:572
  174.0 0.7 copy-start.11
  177.1 16.2 %all-to-all-start.7 = ((bf16[16,16,768]{2,1,0:T(8,128)(2,1)}), bf16[16,16,768]{2,1,0:T(8,128)(2,1)S(1)}, u32[]{:S(2)}, u32[]{:S(2)}) async-start(bf16[16,16,768]{2,1,0:T(8,128)(2,1)} %get-tuple-element.93), calls=%async_computation.7 | async-start | bytes 786432 | tf_op jit(solution)/shard_map/all_to_all | solution.py:590
  182.0 1.2 copy-start.4
  183.3 0.9 copy-start.12
  193.4 29.6 %all-to-all-start.6 = ((bf16[16,64,128]{2,1,0:T(8,128)(2,1)}), bf16[16,64,128]{2,1,0:T(8,128)(2,1)S(1)}, u32[]{:S(2)}, u32[]{:S(2)}) async-start(bf16[16,64,128]{2,1,0:T(8,128)(2,1)} %rows.1), calls=%async_computation.6 | async-start | bytes 524288 | tf_op jit(solution)/shard_map/all_to_all | solution.py:602

commit v7 on v6

--- a/solution.py
+++ b/solution.py
@@ -39,8 +39,8 @@
 HELD = 512
 
 
-def params(large):
-    return pltpu.CompilerParams(vmem_limit_bytes=(40 if large else 12) << 20)
+def params(mebibytes):
+    return pltpu.CompilerParams(vmem_limit_bytes=mebibytes << 20)
 
 
 def cost(flops, moved, exps=0):
@@ -162,11 +162,14 @@
 
 
 KEYS = 4 * QUARTER
+SPARE = 544
 
 
 def forward_kernel(
-    place_ref, lens_ref, own_ref, x_ref, y_ref, lse_ref, means_ref, q_s
+    place_ref, lens_ref, own_ref, all_ref, x_ref, y_ref, spare_ref, lse_ref, means_ref, q_s
 ):
+    for n in range(4):
+        x_ref[n * QUARTER : (n + 1) * QUARTER, :] = all_ref[n, :, 0:64, :].reshape(QUARTER, 128)
     queries = halves(own_ref[:, 64:96, :]).reshape(QUARTER, HEAD_DIM)
     q_s[...] = jnp.concatenate([queries, jnp.zeros_like(queries)], axis=1)
 
@@ -186,7 +189,10 @@
         return carry
 
     lax.fori_loop(0, QUARTER // BLOCK, block, 0)
-    y_ref[QUARTER : QUARTER + 32, :] = stacked(lse_ref[...])
+    spare_ref[0:512, :] = jnp.concatenate(
+        [y_ref[0:512, :][:, 64:128], y_ref[512:1024, :][:, 64:128]], axis=1
+    )
+    spare_ref[512:SPARE, :] = stacked(lse_ref[...])
     member = quarter_member(lens_ref, place_ref[0], place_ref[1]).astype(BF16)
     attn_sums = jnp.dot(member, y_ref[0:QUARTER, :], preferred_element_type=F32)
     sums = jnp.sum(own_ref[:, 96:112, :].astype(F32), axis=0)
@@ -284,11 +290,15 @@
         out_ref[z, 8:16, :] = extra
 
 
-def mass_kernel(lens_ref, own_ref, y_ref, mass_ref, lse_ref, k_s, member_s):
+def mass_kernel(lens_ref, own_ref, all_ref, spare_ref, mass_ref, lse_ref, y_ref, k_s, member_s):
     mine = own_ref[:, 0:64, :].reshape(QUARTER, 128)
     k_s[...] = jnp.where(lanes(QUARTER) < 64, mine, jnp.zeros_like(mine))
     for n in range(4):
-        lse = y_ref[n * (QUARTER + 32) + QUARTER : (n + 1) * (QUARTER + 32), :].astype(F32)
+        queries = halves(all_ref[n, :, 64:96, :]).reshape(QUARTER, HEAD_DIM)
+        y_ref[n * QUARTER : (n + 1) * QUARTER, :] = jnp.concatenate(
+            [queries, jnp.zeros_like(queries)], axis=1
+        )
+        lse = spare_ref[n * SPARE + 512 : (n + 1) * SPARE, :].astype(F32)
         lse = (lse[16:24] + lse[8:16]) + lse[0:8]
         for part in range(8):
             at = n * QUARTER + part * 128
@@ -302,8 +312,7 @@
         sums = jnp.zeros((BLOCK, 128), F32)
         for n in range(4):
             cols = slice(n * QUARTER, (n + 1) * QUARTER)
-            other = y_ref[n * (QUARTER + 32) : n * (QUARTER + 32) + QUARTER, :]
-            scores = lax.dot_general(k_s[rows, :], other, NT, preferred_element_type=F32)
+            scores = lax.dot_general(k_s[rows, :], y_ref[cols, :], NT, preferred_element_type=F32)
             prob = jnp.exp(scores - lse_ref[0:1, cols]).astype(BF16)
             sums = sums + lax.dot_general(
                 prob, member_s[:, cols], NT, preferred_element_type=F32
@@ -418,21 +427,28 @@
 
 
 def column_kernel(
-    lens_ref, own_ref, y_ref, lse_ref, dattn_ref, out_ref, y_s, k_s, v_s, delta_s
+    lens_ref, own_ref, y_ref, spare_ref, lse_ref, dattn_ref, out_ref, y_s, k_s, v_s, delta_s
 ):
     lane = lanes(QUARTER)
     mine = own_ref[:, 0:64, :].reshape(QUARTER, 128)
     zero = jnp.zeros_like(mine)
     k_s[...] = jnp.where(lane < 64, mine, zero)
     v_s[...] = jnp.where(lane < 64, zero, mine)
+    early = jnp.where(lanes(GROUPS) < 64, dattn_ref[...], 0.0).astype(BF16)
     dattn = jnp.where(lanes(GROUPS) < 64, 0.0, dattn_ref[...]).astype(BF16)
     for n in range(4):
         rows = slice(n * QUARTER, (n + 1) * QUARTER)
         member = quarter_member(lens_ref, n // 2, n % 2)
         spread = lax.dot_general(member.astype(BF16), dattn, TN, preferred_element_type=F32)
-        other = y_ref[n * (QUARTER + 32) : n * (QUARTER + 32) + QUARTER, :]
-        y_s[rows, :] = jnp.where(lane < 64, other, spread.astype(BF16))
-        products = lax.dot_general(dattn, other, NT, preferred_element_type=F32)
+        y_s[rows, :] = jnp.where(lane < 64, y_ref[rows, :], spread.astype(BF16))
+        attn = spare_ref[n * SPARE : n * SPARE + 512, :]
+        products = jnp.concatenate(
+            [
+                lax.dot_general(part, attn, NT, preferred_element_type=F32)
+                for part in (early, dattn)
+            ],
+            axis=1,
+        )
         delta_s[:, rows] = jnp.broadcast_to(
             jnp.sum(products * member, axis=0, keepdims=True), (8, QUARTER)
         )
@@ -466,7 +482,7 @@
         in_specs=[SMEM] * len(scalars) + [VMEM] * len(arrays),
         out_specs=jax.tree.map(lambda _: VMEM, outs),
         scratch_shapes=scratch,
-        compiler_params=params(bool(scratch) or name == "pack"),
+        compiler_params=params(56 if name == "pack" else 40 if scratch else 12),
         cost_estimate=estimate,
         name=name,
     )(*scalars, *arrays)
@@ -499,14 +515,16 @@
     own = exchange(packed, ZED)
     queries = gather(tagged, ("yh", "yl", "xa"))
     own, queries = barrier((own, queries))
-    keys = share(own[:, 0:64, :], SQUARE).reshape(KEYS, 128)
+    keys = share(own[:, 0:96, :], SQUARE)
     queries = gather(queries, ("xb", "co"))
     own, keys, queries = barrier((own, keys, queries))
 
-    mine, lse, means = call(
+    rows, mine, spare, lse, means = call(
         forward_kernel,
         (
-            shape((QUARTER + 32, 128), BF16),
+            shape((KEYS, 128), BF16),
+            shape((QUARTER, 128), BF16),
+            shape((SPARE, 128), BF16),
             shape((8, 128), F32),
             shape((2 * GROUPS, 128), F32),
         ),
@@ -515,9 +533,9 @@
     )
     means = means + swap(means, ("yl",), 1)
     means = jnp.broadcast_to(means[None], (PLANE, 2 * GROUPS, 128))
-    mine, means, queries = barrier((mine, means, queries))
+    spare, means, queries = barrier((spare, means, queries))
     means = exchange(means, ZED)
-    around = [swap(mine, SQUARE, flip) for flip in (1, 2, 3)]
+    around = [swap(spare, SQUARE, flip) for flip in (1, 2, 3)]
     query_rows = call(
         query_kernel, shape((16, HELD), F32), (), (queries,), (), cost(6 * 2 * 8 * HELD * 1024, 1200000),
         "queries",
@@ -534,7 +552,7 @@
         (doc,), (means, w_out, queries, query_rows), (), cost(2 * 32 * 768 * 1024, 1800000), "pool",
     )
     sums = exchange(sums, GRP)
-    square = [mine] + around
+    square = [spare] + around
     rotated = [jnp.where(half == 0, square[n], square[n ^ 1]) for n in range(4)]
     ordered = [jnp.where(plane == 0, rotated[n], rotated[n ^ 2]) for n in range(4)]
     others = jnp.concatenate(ordered, axis=0)
@@ -548,12 +566,12 @@
         (sums, logits, pooled_own, queries, query_rows, w_out), (),
         cost(2 * 32 * 768 * 1024, 1800000, 2000), "loss",
     )
-    terms, own, others = barrier((terms, own, others))
+    terms, own, keys, others = barrier((terms, own, keys, others))
     terms = exchange(terms, ZED)
-    mass, lse_rows = call(
+    mass, lse_rows, columns = call(
         mass_kernel,
-        (shape((GROUPS, 8, 128), F32), shape((8, KEYS), F32)),
-        (lengths,), (own, others),
+        (shape((GROUPS, 8, 128), F32), shape((8, KEYS), F32), shape((KEYS, 128), BF16)),
+        (lengths,), (own, keys, others),
         [pltpu.VMEM((QUARTER, 128), BF16), pltpu.VMEM((128, KEYS), BF16)],
         cost(pairs * 256 * 4, 2500000, pairs), "mass",
     )
@@ -572,7 +590,7 @@
     grad_parts = exchange(grad_part, ZED)
     grad_columns = call(
         column_kernel, shape((QUARTER, 128), BF16), (lengths,),
-        (own, others, lse_rows, dattn),
+        (own, columns, others, lse_rows, dattn),
         [
             pltpu.VMEM((KEYS, 128), BF16),
             pltpu.VMEM((QUARTER, 128), BF16),
@@ -590,7 +608,7 @@
     all_grads = exchange(grads, GRP)
     packed_grads = call(
         row_kernel, shape((PLANE, HALF, 128), BF16), (place, lengths),
-        (mine, lse, keys, dattn, grad_columns),
+        (mine, lse, rows, dattn, grad_columns),
         [
             pltpu.VMEM((QUARTER, 128), BF16),
             pltpu.VMEM((QUARTER, 128), BF16),

time: 225 us -> 224 us (level)
  starting transfers between devices: 96.4 us -> 102 us
  waiting for transfers between devices: 56.8 us -> 53 us
  local copies, waits for them, and re-layouts: 12 us -> 9.45 us
  Pallas kernels: 51.7 us -> 54 us
    ppermute x9, waiting for transfers between devices: 28.5 us -> 23.7 us  [swap(): return lax.ppermute(value, axes, [(i, i ^ flip) for i in range(count)])]
    unnamed x28 -> x22, local copies, waits for them, and re-layouts: 9.44 us -> 6.69 us
    pallas_call x14, Pallas kernels: 51.7 us -> 54 us  [call(): pl.pallas_call(kernel, out_shape=outs, in_specs=[SMEM] * len(scalars) + [...]
  transfers between devices with their start and end apart: 17 -> 17, of which waited for: 13 -> 13; matrix products, arithmetic and copies ran while one was open for 2% -> 1% of each run, Pallas kernels for 15% -> 16%
where the time goes in v7:
time: 224 us; the launch traced here: 223 us
  starting transfers between devices  102 us (46%)
  Pallas kernels  54 us (24%)
  waiting for transfers between devices  53 us (24%)
  local copies, waits for them, and re-layouts  9.45 us (4%)
  other arithmetic  3.66 us (2%)
    pallas_call x14, Pallas kernels, call(): pl.pallas_call(kernel, out_shape=outs, in_specs=[SMEM] * len(scalars) + [...  54 us
    ppermute x9, starting transfers between devices, swap(): return lax.ppermute(value, axes, [(i, i ^ flip) for i in range(count)])  29.8 us
    ppermute x9, waiting for transfers between devices, swap(): return lax.ppermute(value, axes, [(i, i ^ flip) for i in range(count)])  23.7 us
    all_to_all x1, starting transfers between devices, body(): own = exchange(packed, ZED)  15.2 us
    all_to_all x1, waiting for transfers between devices, body(): home = exchange(packed_grads, ZED)  14.3 us
    all_to_all x1, starting transfers between devices, body(): home = exchange(packed_grads, ZED)  12 us
    all_to_all x1, starting transfers between devices, body(): terms = exchange(terms, ZED)  10.7 us
    all_to_all x1, starting transfers between devices, body(): means = exchange(means, ZED)  9.96 us
  transfers between devices with their start and end apart: 17, of which 13 were waited for; matrix products, arithmetic and copies ran while one was open for 1% of the time, Pallas kernels for 16%

profile of v7, /device:TPU:2, one launch (start us, length us, event | category | flops | bytes accessed | tf_op | source)
XLA Modules:
  0.0 222.7 jit_solution(13161985927783156359)
XLA Ops:
  2.8 2.2 pack.1
  4.9 15.2 %all-to-all-start = ((bf16[16,112,128]{2,1,0:T(8,128)(2,1)}), bf16[16,112,128]{2,1,0:T(8,128)(2,1)S(1)}, u32[]{:S(2)}, u32[]{:S(2)}) async-start(bf16[16,112,128]{2,1,0:T(8,128)(2,1)} %pack.1), calls=%async_computation | async-start | bytes 917504 | tf_op jit(solution)/shard_map/all_to_all | solution.py:515
  20.1 5.1 %collective-permute-start = (bf16[16,1152]{1,0:T(8,128)(2,1)S(1)}, bf16[16,1152]{1,0:T(8,128)(2,1)S(1)}, u32[]{:S(2)}, u32[]{:S(2)}) collective-permute-start(bf16[16,1152]{1,0:T(8,128)(2,1)S(1)} %fusion.1), channel_id=1, source_target_pairs={{0,256},{256,0},{1,257},{257,1},{2,258},{258,2},{3,259},{259,3},{4... | collective-permute-start | bytes 110600 | tf_op jit(solution)/shard_map/ppermute | solution.py:59
  25.2 2.2 %collective-permute-done = bf16[16,1152]{1,0:T(8,128)(2,1)S(1)} collective-permute-done((bf16[16,1152]{1,0:T(8,128)(2,1)S(1)}, bf16[16,1152]{1,0:T(8,128)(2,1)S(1)}, u32[]{:S(2)}, u32[]{:S(2)}) %collective-permute-start) | collective-permute-done | bytes 36896 | tf_op jit(solution)/shard_map/ppermute | solution.py:59
  27.5 3.5 %collective-permute-start.1 = (bf16[32,1152]{1,0:T(8,128)(2,1)S(1)}, bf16[32,1152]{1,0:T(8,128)(2,1)S(1)}, u32[]{:S(2)}, u32[]{:S(2)}) collective-permute-start(bf16[32,1152]{1,0:T(8,128)(2,1)S(1)} %maximum_select_fusion.4), channel_id=1, source_target_pairs={{0,16},{16,0},{1,17},{17,1},{2,18},{18,2},{3,19},{19,3},{4,20},{20... | collective-permute-start | bytes 221192 | tf_op jit(solution)/shard_map/ppermute | solution.py:59
  31.0 2.7 %collective-permute-done.1 = bf16[32,1152]{1,0:T(8,128)(2,1)S(1)} collective-permute-done((bf16[32,1152]{1,0:T(8,128)(2,1)S(1)}, bf16[32,1152]{1,0:T(8,128)(2,1)S(1)}, u32[]{:S(2)}, u32[]{:S(2)}) %collective-permute-start.1) | collective-permute-done | bytes 73760 | tf_op jit(solution)/shard_map/ppermute | solution.py:59
  33.8 4.0 %collective-permute-start.2 = (bf16[64,1152]{1,0:T(8,128)(2,1)S(1)}, bf16[64,1152]{1,0:T(8,128)(2,1)S(1)}, u32[]{:S(2)}, u32[]{:S(2)}) collective-permute-start(bf16[64,1152]{1,0:T(8,128)(2,1)S(1)} %maximum_select_fusion.3), channel_id=1, source_target_pairs={{0,128},{128,0},{1,129},{129,1},{2,130},{130,2},{3,131},{131,3},{4... | collective-permute-start | bytes 442376 | tf_op jit(solution)/shard_map/ppermute | solution.py:59
  37.8 4.5 %collective-permute-done.2 = bf16[64,1152]{1,0:T(8,128)(2,1)S(1)} collective-permute-done((bf16[64,1152]{1,0:T(8,128)(2,1)S(1)}, bf16[64,1152]{1,0:T(8,128)(2,1)S(1)}, u32[]{:S(2)}, u32[]{:S(2)}) %collective-permute-start.2) | collective-permute-done | bytes 147488 | tf_op jit(solution)/shard_map/ppermute | solution.py:59
  42.4 4.5 %all-to-all-done.own_ref = bf16[16,112,128]{2,1,0:T(8,128)(2,1)S(1)} async-done(((bf16[16,112,128]{2,1,0:T(8,128)(2,1)}), bf16[16,112,128]{2,1,0:T(8,128)(2,1)S(1)}, u32[]{:S(2)}, u32[]{:S(2)}) %all-to-all-start) | async-done | bytes 458784 | tf_op jit(solution)/shard_map/all_to_all | solution.py:515
  48.3 4.3 %all-to-all-start.1 = ((bf16[4,16,96,128]{3,2,1,0:T(8,128)(2,1)}), bf16[4,16,96,128]{3,2,1,0:T(8,128)(2,1)}, u32[]{:S(2)}, u32[]{:S(2)}) async-start(bf16[4,16,96,128]{3,2,1,0:T(8,128)(2,1)} %broadcast_in_dim.28), calls=%async_computation.1 | async-start | bytes 3145728 | tf_op jit(solution)/shard_map/all_to_all | solution.py:52
  52.7 2.4 %collective-permute-start.3 = (bf16[128,1152]{1,0:T(8,128)(2,1)S(1)}, bf16[128,1152]{1,0:T(8,128)(2,1)S(1)}, u32[]{:S(2)}, u32[]{:S(2)}) collective-permute-start(bf16[128,1152]{1,0:T(8,128)(2,1)S(1)} %maximum_select_fusion.2), channel_id=1, source_target_pairs={{0,64},{64,0},{1,65},{65,1},{2,66},{66,2},{3,67},{67,3},{4,68},{68... | collective-permute-start | bytes 884744 | tf_op jit(solution)/shard_map/ppermute | solution.py:59
  55.1 6.2 %collective-permute-done.3 = bf16[128,1152]{1,0:T(8,128)(2,1)S(1)} collective-permute-done((bf16[128,1152]{1,0:T(8,128)(2,1)S(1)}, bf16[128,1152]{1,0:T(8,128)(2,1)S(1)}, u32[]{:S(2)}, u32[]{:S(2)}) %collective-permute-start.3) | collective-permute-done | bytes 294944 | tf_op jit(solution)/shard_map/ppermute | solution.py:59
  65.7 2.2 %all-to-all-done.1.all_ref = bf16[4,16,96,128]{3,2,1,0:T(8,128)(2,1)} async-done(((bf16[4,16,96,128]{3,2,1,0:T(8,128)(2,1)}), bf16[4,16,96,128]{3,2,1,0:T(8,128)(2,1)}, u32[]{:S(2)}, u32[]{:S(2)}) %all-to-all-start.1) | async-done | bytes 1572896 | tf_op jit(solution)/shard_map/all_to_all | solution.py:52
  68.0 9.8 %forward.1 = (bf16[4096,128]{1,0:T(8,128)(2,1)S(1)}, bf16[1024,128]{1,0:T(8,128)(2,1)S(1)}, bf16[544,128]{1,0:T(8,128)(2,1)S(1)}, f32[8,128]{1,0:T(8,128)S(1)}, f32[16,128]{1,0:T(8,128)S(1)}) custom-call(s32[4]{0:T(128)S(1)} %copy-done.2, s32[8]{0:T(128)S(1)} %bitcast.18, bf16[16,112,128]{2,1,0:T(8,128)(2,1)S(1)} %all-to-all-done.own_ref, ...), custom_call_target="tpu_custom_call" | custom-call | flops 4294967296 | bytes 3000000 | tf_op jit(solution)/shard_map/forward/pallas_call | solution.py:479
  79.5 3.6 %collective-permute-start.5 = (f32[16,128]{1,0:T(8,128)S(1)}, f32[16,128]{1,0:T(8,128)S(1)}, u32[]{:S(2)}, u32[]{:S(2)}) collective-permute-start(f32[16,128]{1,0:T(8,128)S(1)} %get-tuple-element.61), channel_id=1, source_target_pairs={{0,16},{16,0},{1,17},{17,1},{2,18},{18,2},{3,19},{19,3},{4,20},{20... | collective-permute-start | bytes 24584 | tf_op jit(solution)/shard_map/ppermute | solution.py:59
  83.1 2.0 collective-permute-done.5
  85.8 10.0 %all-to-all-start.2 = ((f32[16,16,128]{2,1,0:T(8,128)}), f32[16,16,128]{2,1,0:T(8,128)S(1)}, u32[]{:S(2)}, u32[]{:S(2)}) async-start(f32[16,16,128]{2,1,0:T(8,128)} %broadcast_in_dim.29), calls=%async_computation.2 | async-start | bytes 262144 | tf_op jit(solution)/shard_map/all_to_all | solution.py:537
  95.8 3.8 %collective-permute-start.6 = (bf16[544,128]{1,0:T(8,128)(2,1)S(1)}, bf16[544,128]{1,0:T(8,128)(2,1)S(1)}, u32[]{:S(2)}, u32[]{:S(2)}) collective-permute-start(bf16[544,128]{1,0:T(8,128)(2,1)S(1)} %get-tuple-element.65), channel_id=1, source_target_pairs={{0,1},{1,0},{16,17},{17,16},{2,3},{3,2},{18,19},{19,18},{4,5},{5,4... | collective-permute-start | bytes 417800 | tf_op jit(solution)/shard_map/ppermute | solution.py:59
  99.6 3.3 %collective-permute-start.7 = (bf16[544,128]{1,0:T(8,128)(2,1)S(1)}, bf16[544,128]{1,0:T(8,128)(2,1)S(1)}, u32[]{:S(2)}, u32[]{:S(2)}) collective-permute-start(bf16[544,128]{1,0:T(8,128)(2,1)S(1)} %get-tuple-element.65), channel_id=1, source_target_pairs={{0,16},{1,17},{16,0},{17,1},{2,18},{3,19},{18,2},{19,3},{4,20},{5,... | collective-permute-start | bytes 417800 | tf_op jit(solution)/shard_map/ppermute | solution.py:59
  103.0 2.0 collective-permute-start.8
  107.7 3.3 %collective-permute-done.8 = bf16[544,128]{1,0:T(8,128)(2,1)} collective-permute-done((bf16[544,128]{1,0:T(8,128)(2,1)S(1)}, bf16[544,128]{1,0:T(8,128)(2,1)}, u32[]{:S(2)}, u32[]{:S(2)}) %collective-permute-start.8) | collective-permute-done | bytes 139296 | tf_op jit(solution)/shard_map/ppermute | solution.py:59
  112.4 7.5 %all-to-all-start.3 = ((f32[16,8,128]{2,1,0:T(8,128)}), f32[16,8,128]{2,1,0:T(8,128)S(1)}, u32[]{:S(2)}, u32[]{:S(2)}) async-start(f32[16,8,128]{2,1,0:T(8,128)} %get-tuple-element.68), calls=%async_computation.3 | async-start | bytes 131072 | tf_op jit(solution)/shard_map/all_to_all | solution.py:554
  122.5 3.6 %all-to-all-done.3.sums_ref = f32[16,8,128]{2,1,0:T(8,128)S(1)} async-done(((f32[16,8,128]{2,1,0:T(8,128)}), f32[16,8,128]{2,1,0:T(8,128)S(1)}, u32[]{:S(2)}, u32[]{:S(2)}) %all-to-all-start.3) | async-done | bytes 65568 | tf_op jit(solution)/shard_map/all_to_all | solution.py:554
  127.4 10.7 %all-to-all-start.4 = ((f32[16,16,128]{2,1,0:T(8,128)}), f32[16,16,128]{2,1,0:T(8,128)S(1)}, u32[]{:S(2)}, u32[]{:S(2)}) async-start(f32[16,16,128]{2,1,0:T(8,128)} %loss.1), calls=%async_computation.4 | async-start | bytes 262144 | tf_op jit(solution)/shard_map/all_to_all | solution.py:570
  138.1 8.4 %mass.1 = (f32[8,8,128]{2,1,0:T(8,128)S(1)}, f32[8,4096]{1,0:T(8,128)S(1)}, bf16[4096,128]{1,0:T(8,128)(2,1)S(1)}) custom-call(s32[8]{0:T(128)S(1)} %bitcast.19, bf16[16,112,128]{2,1,0:T(8,128)(2,1)S(1)} %all-to-all-done.own_ref, bf16[4,16,96,128]{3,2,1,0:T(8,128)(2,1)} %all-to-all-done.1.all_ref, bf16[2176,128]{1,0:T(8,128)(2,1)S(1)} %pad_maximum_fusion.spare_ref), custom_call_target="tpu_custom_call" | custom-call | flops 4294967296 | bytes 2500000 | tf_op jit(solution)/shard_map/mass/pallas_call | solution.py:479
  148.2 4.6 %all-to-all-done.4.terms_ref = f32[16,16,128]{2,1,0:T(8,128)S(1)} async-done(((f32[16,16,128]{2,1,0:T(8,128)}), f32[16,16,128]{2,1,0:T(8,128)S(1)}, u32[]{:S(2)}, u32[]{:S(2)}) %all-to-all-start.4) | async-done | bytes 131104 | tf_op jit(solution)/shard_map/all_to_all | solution.py:570
  154.2 7.4 %all-to-all-start.5 = ((f32[16,8,128]{2,1,0:T(8,128)}), f32[16,8,128]{2,1,0:T(8,128)S(1)}, u32[]{:S(2)}, u32[]{:S(2)}) async-start(f32[16,8,128]{2,1,0:T(8,128)} %get-tuple-element.86), calls=%async_computation.5 | async-start | bytes 131072 | tf_op jit(solution)/shard_map/all_to_all | solution.py:590
  163.8 11.0 %columns.1.grad_k_ref = bf16[1024,128]{1,0:T(8,128)(2,1)S(1)} custom-call(s32[8]{0:T(128)S(1)} %bitcast.21, bf16[16,112,128]{2,1,0:T(8,128)(2,1)S(1)} %all-to-all-done.own_ref, bf16[4096,128]{1,0:T(8,128)(2,1)S(1)} %copy-done.4, bf16[2176,128]{1,0:T(8,128)(2,1)S(1)} %pad_maximum_fusion.spare_ref, f32[8,4096]{1,0:T(8,128)S(1)} %copy-done.10, ...), custom_call_target="tpu_custom_call" | custom-call | flops 6442450944 | bytes 2500000 | tf_op jit(solution)/shard_map/columns/pallas_call | solution.py:479
  176.3 4.8 %all-to-all-start.7 = ((bf16[16,16,768]{2,1,0:T(8,128)(2,1)}), bf16[16,16,768]{2,1,0:T(8,128)(2,1)S(1)}, u32[]{:S(2)}, u32[]{:S(2)}) async-start(bf16[16,16,768]{2,1,0:T(8,128)(2,1)} %get-tuple-element.101), calls=%async_computation.7 | async-start | bytes 786432 | tf_op jit(solution)/shard_map/all_to_all | solution.py:608
  182.3 9.0 %rows.1 = bf16[16,64,128]{2,1,0:T(8,128)(2,1)} custom-call(s32[4]{0:T(128)S(1)} %copy-done.2, s32[8]{0:T(128)S(1)} %bitcast.23, bf16[1024,128]{1,0:T(8,128)(2,1)S(1)} %copy-done.8, f32[8,128]{1,0:T(8,128)S(1)} %get-tuple-element.90.lse_ref, bf16[4096,128]{1,0:T(8,128)(2,1)S(1)} %copy-done.6, f32[8,128]{1,0:T(8,128)S(1)} %get-tuple-element.92.dattn_ref, ...), custom_call_target="tpu_custom_call" | custom-call | flops 6442450944 | bytes 2000000 | tf_op jit(solution)/shard_map/rows/pallas_call | solution.py:479
  191.3 12.0 %all-to-all-start.6 = ((bf16[16,64,128]{2,1,0:T(8,128)(2,1)}), bf16[16,64,128]{2,1,0:T(8,128)(2,1)S(1)}, u32[]{:S(2)}, u32[]{:S(2)}) async-start(bf16[16,64,128]{2,1,0:T(8,128)(2,1)} %rows.1), calls=%async_computation.6 | async-start | bytes 524288 | tf_op jit(solution)/shard_map/all_to_all | solution.py:620
  207.6 14.3 %all-to-all-done.6.in_ref = bf16[16,64,128]{2,1,0:T(8,128)(2,1)S(1)} async-done(((bf16[16,64,128]{2,1,0:T(8,128)(2,1)}), bf16[16,64,128]{2,1,0:T(8,128)(2,1)S(1)}, u32[]{:S(2)}, u32[]{:S(2)}) %all-to-all-start.6) | async-done | bytes 262176 | tf_op jit(solution)/shard_map/all_to_all | solution.py:620
  (54 shorter events, 31.4 us)
Async XLA Ops:
  4.9 42.0 %all-to-all-start = ((bf16[16,112,128]{2,1,0:T(8,128)(2,1)}), bf16[16,112,128]{2,1,0:T(8,128)(2,1)S(1)}, u32[]{:S(2)}, u32[]{:S(2)}) async-start(bf16[16,112,128]{2,1,0:T(8,128)(2,1)} %pack.1), calls=%async_computation | async-start | bytes 917504 | tf_op jit(solution)/shard_map/all_to_all | solution.py:515
  20.1 7.4 %collective-permute-start = (bf16[16,1152]{1,0:T(8,128)(2,1)S(1)}, bf16[16,1152]{1,0:T(8,128)(2,1)S(1)}, u32[]{:S(2)}, u32[]{:S(2)}) collective-permute-start(bf16[16,1152]{1,0:T(8,128)(2,1)S(1)} %fusion.1), channel_id=1, source_target_pairs={{0,256},{256,0},{1,257},{257,1},{2,258},{258,2},{3,259},{259,3},{4... | collective-permute-start | bytes 110600 | tf_op jit(solution)/shard_map/ppermute | solution.py:59
  27.5 6.2 %collective-permute-start.1 = (bf16[32,1152]{1,0:T(8,128)(2,1)S(1)}, bf16[32,1152]{1,0:T(8,128)(2,1)S(1)}, u32[]{:S(2)}, u32[]{:S(2)}) collective-permute-start(bf16[32,1152]{1,0:T(8,128)(2,1)S(1)} %maximum_select_fusion.4), channel_id=1, source_target_pairs={{0,16},{16,0},{1,17},{17,1},{2,18},{18,2},{3,19},{19,3},{4,20},{20... | collective-permute-start | bytes 221192 | tf_op jit(solution)/shard_map/ppermute | solution.py:59
  33.8 8.5 %collective-permute-start.2 = (bf16[64,1152]{1,0:T(8,128)(2,1)S(1)}, bf16[64,1152]{1,0:T(8,128)(2,1)S(1)}, u32[]{:S(2)}, u32[]{:S(2)}) collective-permute-start(bf16[64,1152]{1,0:T(8,128)(2,1)S(1)} %maximum_select_fusion.3), channel_id=1, source_target_pairs={{0,128},{128,0},{1,129},{129,1},{2,130},{130,2},{3,131},{131,3},{4... | collective-permute-start | bytes 442376 | tf_op jit(solution)/shard_map/ppermute | solution.py:59
  48.3 19.7 %all-to-all-start.1 = ((bf16[4,16,96,128]{3,2,1,0:T(8,128)(2,1)}), bf16[4,16,96,128]{3,2,1,0:T(8,128)(2,1)}, u32[]{:S(2)}, u32[]{:S(2)}) async-start(bf16[4,16,96,128]{3,2,1,0:T(8,128)(2,1)} %broadcast_in_dim.28), calls=%async_computation.1 | async-start | bytes 3145728 | tf_op jit(solution)/shard_map/all_to_all | solution.py:52
  52.7 8.6 %collective-permute-start.3 = (bf16[128,1152]{1,0:T(8,128)(2,1)S(1)}, bf16[128,1152]{1,0:T(8,128)(2,1)S(1)}, u32[]{:S(2)}, u32[]{:S(2)}) collective-permute-start(bf16[128,1152]{1,0:T(8,128)(2,1)S(1)} %maximum_select_fusion.2), channel_id=1, source_target_pairs={{0,64},{64,0},{1,65},{65,1},{2,66},{66,2},{3,67},{67,3},{4,68},{68... | collective-permute-start | bytes 884744 | tf_op jit(solution)/shard_map/ppermute | solution.py:59
  61.4 3.9 %collective-permute-start.4 = (bf16[256,1152]{1,0:T(8,128)(2,1)S(1)}, bf16[256,1152]{1,0:T(8,128)(2,1)S(1)}, u32[]{:S(2)}, u32[]{:S(2)}) collective-permute-start(bf16[256,1152]{1,0:T(8,128)(2,1)S(1)} %maximum_select_fusion.1), channel_id=1, source_target_pairs={{0,32},{32,0},{1,33},{33,1},{2,34},{34,2},{3,35},{35,3},{4,36},{36... | collective-permute-start | bytes 1769480 | tf_op jit(solution)/shard_map/ppermute | solution.py:59
  63.3 4.6 %copy-start.1 = (s32[1,8]{1,0:T(1,128)S(1)}, s32[1,8]{1,0:T(1,128)}, u32[]{:S(2)}) copy-start(s32[1,8]{1,0:T(1,128)} %param.13) | copy-start | bytes 100
  63.3 4.6 %copy-start.2 = (s32[4]{0:T(128)S(1)}, s32[4]{0:T(128)}, u32[]{:S(2)}) copy-start(s32[4]{0:T(128)} %pad_add_fusion.place_ref) | copy-start | bytes 52
  77.8 1.0 copy-start.5
  78.8 0.7 copy-start.7
  79.5 31.5 %copy-start = (bf16[512,1024]{1,0:T(8,128)(2,1)S(1)}, bf16[512,1024]{1,0:T(8,128)(2,1)}, u32[]{:S(2)}) copy-start(bf16[512,1024]{1,0:T(8,128)(2,1)} %w_ref.7) | copy-start | bytes 3145732
  79.5 5.7 %collective-permute-start.5 = (f32[16,128]{1,0:T(8,128)S(1)}, f32[16,128]{1,0:T(8,128)S(1)}, u32[]{:S(2)}, u32[]{:S(2)}) collective-permute-start(f32[16,128]{1,0:T(8,128)S(1)} %get-tuple-element.61), channel_id=1, source_target_pairs={{0,16},{16,0},{1,17},{17,1},{2,18},{18,2},{3,19},{19,3},{4,20},{20... | collective-permute-start | bytes 24584 | tf_op jit(solution)/shard_map/ppermute | solution.py:59
  85.8 25.1 %all-to-all-start.2 = ((f32[16,16,128]{2,1,0:T(8,128)}), f32[16,16,128]{2,1,0:T(8,128)S(1)}, u32[]{:S(2)}, u32[]{:S(2)}) async-start(f32[16,16,128]{2,1,0:T(8,128)} %broadcast_in_dim.29), calls=%async_computation.2 | async-start | bytes 262144 | tf_op jit(solution)/shard_map/all_to_all | solution.py:537
  95.8 11.0 %collective-permute-start.6 = (bf16[544,128]{1,0:T(8,128)(2,1)S(1)}, bf16[544,128]{1,0:T(8,128)(2,1)S(1)}, u32[]{:S(2)}, u32[]{:S(2)}) collective-permute-start(bf16[544,128]{1,0:T(8,128)(2,1)S(1)} %get-tuple-element.65), channel_id=1, source_target_pairs={{0,1},{1,0},{16,17},{17,16},{2,3},{3,2},{18,19},{19,18},{4,5},{5,4... | collective-permute-start | bytes 417800 | tf_op jit(solution)/shard_map/ppermute | solution.py:59
  99.6 8.0 %collective-permute-start.7 = (bf16[544,128]{1,0:T(8,128)(2,1)S(1)}, bf16[544,128]{1,0:T(8,128)(2,1)S(1)}, u32[]{:S(2)}, u32[]{:S(2)}) collective-permute-start(bf16[544,128]{1,0:T(8,128)(2,1)S(1)} %get-tuple-element.65), channel_id=1, source_target_pairs={{0,16},{1,17},{16,0},{17,1},{2,18},{3,19},{18,2},{19,3},{4,20},{5,... | collective-permute-start | bytes 417800 | tf_op jit(solution)/shard_map/ppermute | solution.py:59
  103.0 8.0 %collective-permute-start.8 = (bf16[544,128]{1,0:T(8,128)(2,1)S(1)}, bf16[544,128]{1,0:T(8,128)(2,1)}, u32[]{:S(2)}, u32[]{:S(2)}) collective-permute-start(bf16[544,128]{1,0:T(8,128)(2,1)S(1)} %get-tuple-element.65), channel_id=1, source_target_pairs={{0,17},{1,16},{16,1},{17,0},{2,19},{3,18},{18,3},{19,2},{4,21},{5,... | collective-permute-start | bytes 417800 | tf_op jit(solution)/shard_map/ppermute | solution.py:59
  112.4 13.7 %all-to-all-start.3 = ((f32[16,8,128]{2,1,0:T(8,128)}), f32[16,8,128]{2,1,0:T(8,128)S(1)}, u32[]{:S(2)}, u32[]{:S(2)}) async-start(f32[16,8,128]{2,1,0:T(8,128)} %get-tuple-element.68), calls=%async_computation.3 | async-start | bytes 131072 | tf_op jit(solution)/shard_map/all_to_all | solution.py:554
  127.4 25.4 %all-to-all-start.4 = ((f32[16,16,128]{2,1,0:T(8,128)}), f32[16,16,128]{2,1,0:T(8,128)S(1)}, u32[]{:S(2)}, u32[]{:S(2)}) async-start(f32[16,16,128]{2,1,0:T(8,128)} %loss.1), calls=%async_computation.4 | async-start | bytes 262144 | tf_op jit(solution)/shard_map/all_to_all | solution.py:570
  146.5 1.0 copy-start.3
  147.5 0.7 copy-start.9
  154.2 20.6 %all-to-all-start.5 = ((f32[16,8,128]{2,1,0:T(8,128)}), f32[16,8,128]{2,1,0:T(8,128)S(1)}, u32[]{:S(2)}, u32[]{:S(2)}) async-start(f32[16,8,128]{2,1,0:T(8,128)} %get-tuple-element.86), calls=%async_computation.5 | async-start | bytes 131072 | tf_op jit(solution)/shard_map/all_to_all | solution.py:590
  161.6 1.2 copy-start.4
  162.9 0.9 copy-start.10
  163.8 17.3 %copy-start.8 = (bf16[1024,128]{1,0:T(8,128)(2,1)S(1)}, bf16[1024,128]{1,0:T(8,128)(2,1)}, u32[]{:S(2)}) copy-start(bf16[1024,128]{1,0:T(8,128)(2,1)} %copy-done.7) | copy-start | bytes 786436
  176.3 15.0 %all-to-all-start.7 = ((bf16[16,16,768]{2,1,0:T(8,128)(2,1)}), bf16[16,16,768]{2,1,0:T(8,128)(2,1)S(1)}, u32[]{:S(2)}, u32[]{:S(2)}) async-start(bf16[16,16,768]{2,1,0:T(8,128)(2,1)} %get-tuple-element.101), calls=%async_computation.7 | async-start | bytes 786432 | tf_op jit(solution)/shard_map/all_to_all | solution.py:608
  181.1 1.2 copy-start.6
  191.3 30.5 %all-to-all-start.6 = ((bf16[16,64,128]{2,1,0:T(8,128)(2,1)}), bf16[16,64,128]{2,1,0:T(8,128)(2,1)S(1)}, u32[]{:S(2)}, u32[]{:S(2)}) async-start(bf16[16,64,128]{2,1,0:T(8,128)(2,1)} %rows.1), calls=%async_computation.6 | async-start | bytes 524288 | tf_op jit(solution)/shard_map/all_to_all | solution.py:620

commit v8 on v7

--- a/solution.py
+++ b/solution.py
@@ -162,7 +162,7 @@
 
 
 KEYS = 4 * QUARTER
-SPARE = 544
+SPARE = 512
 
 
 def forward_kernel(
@@ -189,16 +189,21 @@
         return carry
 
     lax.fori_loop(0, QUARTER // BLOCK, block, 0)
-    spare_ref[0:512, :] = jnp.concatenate(
+    spare_ref[...] = jnp.concatenate(
         [y_ref[0:512, :][:, 64:128], y_ref[512:1024, :][:, 64:128]], axis=1
     )
-    spare_ref[512:SPARE, :] = stacked(lse_ref[...])
     member = quarter_member(lens_ref, place_ref[0], place_ref[1]).astype(BF16)
     attn_sums = jnp.dot(member, y_ref[0:QUARTER, :], preferred_element_type=F32)
     sums = jnp.sum(own_ref[:, 96:112, :].astype(F32), axis=0)
     input_sums = (sums[0:8] + pltpu.roll(sums[0:8], 64, 1)) + sums[8:16]
     means = jnp.where(lanes(GROUPS) < 64, input_sums, attn_sums) / lengths_of(lens_ref)
-    means_ref[...] = jnp.concatenate([means, means], axis=0)
+    means_ref[...] = jnp.concatenate([means, lse_ref[...]], axis=0)
+
+
+def plane_kernel(mine_ref, other_ref, out_ref):
+    mine, other = mine_ref[...], other_ref[...]
+    both = jnp.concatenate([mine[0:8] + other[0:8], mine[8:16], other[8:16]], axis=0)
+    out_ref[...] = jnp.broadcast_to(both[None], (PLANE, 3 * GROUPS, 128))
 
 
 def pool_kernel(doc_ref, means_ref, w_ref, query_ref, row_ref, own_ref, means_out_ref, logits_ref, out_ref):
@@ -290,7 +295,9 @@
         out_ref[z, 8:16, :] = extra
 
 
-def mass_kernel(lens_ref, own_ref, all_ref, spare_ref, mass_ref, lse_ref, y_ref, k_s, member_s):
+def mass_kernel(
+    place_ref, lens_ref, own_ref, all_ref, means_ref, mass_ref, lse_ref, y_ref, k_s, member_s
+):
     mine = own_ref[:, 0:64, :].reshape(QUARTER, 128)
     k_s[...] = jnp.where(lanes(QUARTER) < 64, mine, jnp.zeros_like(mine))
     for n in range(4):
@@ -298,8 +305,8 @@
         y_ref[n * QUARTER : (n + 1) * QUARTER, :] = jnp.concatenate(
             [queries, jnp.zeros_like(queries)], axis=1
         )
-        lse = spare_ref[n * SPARE + 512 : (n + 1) * SPARE, :].astype(F32)
-        lse = (lse[16:24] + lse[8:16]) + lse[0:8]
+        both = means_ref[2 * place_ref[2] + n % 2]
+        lse = jnp.where(place_ref[0] == n // 2, both[8:16], both[16:24])
         for part in range(8):
             at = n * QUARTER + part * 128
             lse_ref[:, at : at + 128] = jnp.broadcast_to(lse[part : part + 1, :], (8, 128))
@@ -324,7 +331,14 @@
     lax.fori_loop(0, QUARTER // BLOCK, block, 0)
 
 
-def group_kernel(lens_ref, terms_ref, ready_ref, mass_ref, dattn_ref, grad_ref, loss_ref):
+def rows_of(line):
+    return jnp.concatenate([line[:, n : n + 128] for n in range(0, QUARTER, 128)], axis=0)
+
+
+def group_kernel(
+    place_ref, lens_ref, terms_ref, ready_ref, mass_ref, spare_ref, other_ref,
+    dattn_ref, grad_ref, loss_ref, delta_ref,
+):
     sums = terms_ref[0]
     for n in range(1, PLANE):
         sums = sums + terms_ref[n]
@@ -332,7 +346,24 @@
     loss_ref[...] = sums[8:16, :] / QUERY_COUNT
     norms = ready_ref[16:24, :]
     raw = jnp.concatenate([sums[0:8, 0:64], sums[0:8, 0:64]], axis=1)
-    dattn_ref[...] = (raw - ready_ref[0:8, :] * along) / norms / lengths_of(lens_ref)
+    dattn = (raw - ready_ref[0:8, :] * along) / norms / lengths_of(lens_ref)
+    dattn_ref[...] = dattn
+    lane = lanes(GROUPS)
+    ends = [
+        jnp.where(lane < 64, dattn, 0.0).astype(BF16),
+        jnp.where(lane < 64, 0.0, dattn).astype(BF16),
+    ]
+    for n, (attn, plane) in enumerate(
+        ((spare_ref, place_ref[0]), (other_ref, 1 - place_ref[0]))
+    ):
+        products = jnp.concatenate(
+            [lax.dot_general(part, attn[...], NT, preferred_element_type=F32) for part in ends],
+            axis=1,
+        )
+        member = quarter_member(lens_ref, plane, place_ref[1])
+        delta_ref[n * 8 : (n + 1) * 8, :] = rows_of(
+            jnp.sum(products * member, axis=0, keepdims=True)
+        )
     grad = (sums[0:8, 64:128] - ready_ref[8:16, 0:64] * along) / norms[:, 0:64]
     for z in range(PLANE):
         half = (z % 2) * HALF
@@ -386,7 +417,7 @@
 
 
 def row_kernel(
-    place_ref, lens_ref, y_ref, lse_ref, x_ref, dattn_ref, grad_k_ref, out_ref, q_s, d_s, delta_s
+    place_ref, lens_ref, y_ref, lse_ref, x_ref, dattn_ref, out_ref, q_s, d_s, delta_s
 ):
     lane = lanes(QUARTER)
     member = quarter_member(lens_ref, place_ref[0], place_ref[1]).astype(BF16)
@@ -417,45 +448,36 @@
             score_grad = (jnp.exp(scores - log_total) * (prob_grad - delta)).astype(BF16)
             total = total + jnp.dot(score_grad, part, preferred_element_type=F32)
         total = total * SCALE
-        total = jnp.concatenate([total[:, 0:64]] * 2, axis=1).astype(BF16)
-        both = jnp.where(lanes(TALL) < 64, grad_k_ref[rows, :], total)
-        count = TALL // HALF
-        out_ref[pl.ds(i * count, count), :, :] = both.reshape(count, HALF, 128)
+        out_ref[rows, :] = jnp.concatenate([total[:, 0:64]] * 2, axis=1).astype(BF16)
         return carry
 
     lax.fori_loop(0, QUARTER // TALL, block, 0)
 
 
 def column_kernel(
-    lens_ref, own_ref, y_ref, spare_ref, lse_ref, dattn_ref, out_ref, y_s, k_s, v_s, delta_s
+    place_ref, lens_ref, own_ref, y_ref, mine_ref, other_ref, lse_ref, dattn_ref, grad_q_ref,
+    out_ref, y_s, k_s, v_s, delta_s,
 ):
     lane = lanes(QUARTER)
     mine = own_ref[:, 0:64, :].reshape(QUARTER, 128)
     zero = jnp.zeros_like(mine)
     k_s[...] = jnp.where(lane < 64, mine, zero)
     v_s[...] = jnp.where(lane < 64, zero, mine)
-    early = jnp.where(lanes(GROUPS) < 64, dattn_ref[...], 0.0).astype(BF16)
     dattn = jnp.where(lanes(GROUPS) < 64, 0.0, dattn_ref[...]).astype(BF16)
     for n in range(4):
         rows = slice(n * QUARTER, (n + 1) * QUARTER)
         member = quarter_member(lens_ref, n // 2, n % 2)
         spread = lax.dot_general(member.astype(BF16), dattn, TN, preferred_element_type=F32)
         y_s[rows, :] = jnp.where(lane < 64, y_ref[rows, :], spread.astype(BF16))
-        attn = spare_ref[n * SPARE : n * SPARE + 512, :]
-        products = jnp.concatenate(
-            [
-                lax.dot_general(part, attn, NT, preferred_element_type=F32)
-                for part in (early, dattn)
-            ],
-            axis=1,
-        )
-        delta_s[:, rows] = jnp.broadcast_to(
-            jnp.sum(products * member, axis=0, keepdims=True), (8, QUARTER)
-        )
+        delta = jnp.where(place_ref[1] == n % 2, mine_ref[...], other_ref[...])
+        delta = jnp.where(place_ref[0] == n // 2, delta[0:8], delta[8:16])
+        for part in range(8):
+            at = n * QUARTER + part * 128
+            delta_s[:, at : at + 128] = jnp.broadcast_to(delta[part : part + 1, :], (8, 128))
 
     def block(i, carry):
-        rows = pl.ds(pl.multiple_of(i * BLOCK, BLOCK), BLOCK)
-        total = jnp.zeros((BLOCK, 128), F32)
+        rows = pl.ds(pl.multiple_of(i * TALL, TALL), TALL)
+        total = jnp.zeros((TALL, 128), F32)
         for n in range(KEYS // CHUNK):
             cols = slice(n * CHUNK, (n + 1) * CHUNK)
             part = y_s[cols, :]
@@ -465,10 +487,12 @@
                 jnp.exp(scores - lse_ref[0:1, cols]) * (prob_grad - delta_s[0:1, cols])
             ).astype(BF16)
             total = total + jnp.dot(score_grad, part, preferred_element_type=F32)
-        out_ref[rows, :] = total.astype(BF16)
+        both = jnp.where(lanes(TALL) < 64, total.astype(BF16), grad_q_ref[rows, :])
+        count = TALL // HALF
+        out_ref[pl.ds(i * count, count), :, :] = both.reshape(count, HALF, 128)
         return carry
 
-    lax.fori_loop(0, QUARTER // BLOCK, block, 0)
+    lax.fori_loop(0, QUARTER // TALL, block, 0)
 
 
 SMEM = pl.BlockSpec(memory_space=pltpu.SMEM)
@@ -508,16 +532,20 @@
         pack_kernel, shape((PLANE, 112, 128), BF16), (place, lengths),
         (q_heads[0], k_heads[0], v_heads[0], inputs[0]), (), cost(0, 1000000), "pack",
     )
+    packed, query_emb, positive = barrier((packed, query_emb, positive))
     tagged = jnp.concatenate(
         [query_emb, jnp.pad(positive.astype(BF16)[:, None], ((0, 0), (0, 127)))], axis=1
     )
-    packed, tagged = barrier((packed, tagged))
     own = exchange(packed, ZED)
     queries = gather(tagged, ("yh", "yl", "xa"))
     own, queries = barrier((own, queries))
     keys = share(own[:, 0:96, :], SQUARE)
     queries = gather(queries, ("xb", "co"))
-    own, keys, queries = barrier((own, keys, queries))
+    query_rows = call(
+        query_kernel, shape((16, HELD), F32), (), (queries,), (), cost(6 * 2 * 8 * HELD * 1024, 1200000),
+        "queries",
+    )
+    own, keys, queries, query_rows = barrier((own, keys, queries, query_rows))
 
     rows, mine, spare, lse, means = call(
         forward_kernel,
@@ -531,16 +559,15 @@
         (place, lengths), (own, keys), [pltpu.VMEM((QUARTER, 128), BF16)],
         cost(pairs * 256 * 4, 3000000, pairs), "forward",
     )
-    means = means + swap(means, ("yl",), 1)
-    means = jnp.broadcast_to(means[None], (PLANE, 2 * GROUPS, 128))
-    spare, means, queries = barrier((spare, means, queries))
+    other_means = swap(means, ("yl",), 1)
+    means = call(
+        plane_kernel, shape((PLANE, 3 * GROUPS, 128), F32), (), (means, other_means), (),
+        cost(0, 200000), "plane",
+    )
+    spare, means = barrier((spare, means))
     means = exchange(means, ZED)
-    around = [swap(spare, SQUARE, flip) for flip in (1, 2, 3)]
-    query_rows = call(
-        query_kernel, shape((16, HELD), F32), (), (queries,), (), cost(6 * 2 * 8 * HELD * 1024, 1200000),
-        "queries",
-    )
-    means, query_rows, around = barrier((means, query_rows, around))
+    other_spare = swap(spare, ("yl",), 1)
+    means, other_spare = barrier((means, other_spare))
     pooled_own, doc_means, logits, sums = call(
         pool_kernel,
         (
@@ -552,45 +579,59 @@
         (doc,), (means, w_out, queries, query_rows), (), cost(2 * 32 * 768 * 1024, 1800000), "pool",
     )
     sums = exchange(sums, GRP)
-    square = [spare] + around
-    rotated = [jnp.where(half == 0, square[n], square[n ^ 1]) for n in range(4)]
-    ordered = [jnp.where(plane == 0, rotated[n], rotated[n ^ 2]) for n in range(4)]
-    others = jnp.concatenate(ordered, axis=0)
     ready = call(
         prepare_kernel, shape((24, 128), F32), (place,), (pooled_own, w_out), (),
         cost(2 * 32 * 128 * 1024, 1200000), "prepare",
     )
-    sums, others, ready = barrier((sums, others, ready))
+    sums, ready = barrier((sums, ready))
     terms = call(
         loss_kernel, shape((PLANE, 16, 128), F32), (doc,),
         (sums, logits, pooled_own, queries, query_rows, w_out), (),
         cost(2 * 32 * 768 * 1024, 1800000, 2000), "loss",
     )
-    terms, own, keys, others = barrier((terms, own, keys, others))
+    terms, own, keys = barrier((terms, own, keys))
     terms = exchange(terms, ZED)
     mass, lse_rows, columns = call(
         mass_kernel,
         (shape((GROUPS, 8, 128), F32), shape((8, KEYS), F32), shape((KEYS, 128), BF16)),
-        (lengths,), (own, keys, others),
+        (place, lengths), (own, keys, means),
         [pltpu.VMEM((QUARTER, 128), BF16), pltpu.VMEM((128, KEYS), BF16)],
         cost(pairs * 256 * 4, 2500000, pairs), "mass",
     )
     terms, mass, lse_rows = barrier((terms, mass, lse_rows))
 
-    dattn, grad_part, loss = call(
+    dattn, grad_part, loss, delta = call(
         group_kernel,
         (
             shape((GROUPS, 128), F32),
             shape((PLANE, GROUPS, 128), F32),
             shape((GROUPS, 128), F32),
+            shape((2 * GROUPS, 128), F32),
         ),
-        (lengths,), (terms, ready, mass), (), cost(0, 100000), "group",
+        (place, lengths), (terms, ready, mass, spare, other_spare), (), cost(0, 100000), "group",
     )
     mean_loss = loss[0, 64]
     grad_parts = exchange(grad_part, ZED)
-    grad_columns = call(
-        column_kernel, shape((QUARTER, 128), BF16), (lengths,),
-        (own, columns, others, lse_rows, dattn),
+    other_delta = swap(delta, ("zd",), 1)
+    grad_rows = call(
+        row_kernel, shape((QUARTER, 128), BF16), (place, lengths), (mine, lse, rows, dattn),
+        [
+            pltpu.VMEM((QUARTER, 128), BF16),
+            pltpu.VMEM((QUARTER, 128), BF16),
+            pltpu.VMEM((QUARTER, 128), F32),
+        ],
+        cost(pairs * 256 * 6, 2000000, pairs), "rows",
+    )
+    grad_inputs, grads = call(
+        inputs_kernel,
+        (shape((ROWS, MODEL), BF16), shape((DOCS, 2 * GROUPS, (MODEL + WIDTH) // 2), BF16)),
+        (place, lengths), (grad_parts, doc_means), (), cost(2 * 32 * 128 * 1024, 1200000), "inputs",
+    )
+    grad_rows, grads, other_delta = barrier((grad_rows, grads, other_delta))
+    all_grads = exchange(grads, GRP)
+    packed_grads = call(
+        column_kernel, shape((PLANE, HALF, 128), BF16), (place, lengths),
+        (own, columns, delta, other_delta, lse_rows, dattn, grad_rows),
         [
             pltpu.VMEM((KEYS, 128), BF16),
             pltpu.VMEM((QUARTER, 128), BF16),
@@ -598,23 +639,6 @@
             pltpu.VMEM((8, KEYS), F32),
         ],
         cost(pairs * 256 * 6, 2500000, pairs), "columns",
-    )
-    grad_inputs, grads = call(
-        inputs_kernel,
-        (shape((ROWS, MODEL), BF16), shape((DOCS, 2 * GROUPS, (MODEL + WIDTH) // 2), BF16)),
-        (place, lengths), (grad_parts, doc_means), (), cost(2 * 32 * 128 * 1024, 1200000), "inputs",
-    )
-    grad_columns, grads = barrier((grad_columns, grads))
-    all_grads = exchange(grads, GRP)
-    packed_grads = call(
-        row_kernel, shape((PLANE, HALF, 128), BF16), (place, lengths),
-        (mine, lse, rows, dattn, grad_columns),
-        [
-            pltpu.VMEM((QUARTER, 128), BF16),
-            pltpu.VMEM((QUARTER, 128), BF16),
-            pltpu.VMEM((QUARTER, 128), F32),
-        ],
-        cost(pairs * 256 * 6, 2000000, pairs), "rows",
     )
     packed_grads, grad_parts = barrier((packed_grads, grad_parts))
     home = exchange(packed_grads, ZED)

time: 224 us -> 215 us (0.960)
  starting transfers between devices: 102 us -> 91.4 us
  waiting for transfers between devices: 53 us -> 60.2 us
  other arithmetic: 3.66 us -> 1.25 us
    all_to_all x1, waiting for transfers between devices: 0.01 us -> 8.09 us  [body(): means = exchange(means, ZED)]
    all_to_all x1, starting transfers between devices: 10.7 us -> 4.4 us  [body(): terms = exchange(terms, ZED)]
    pallas_call x14 -> x15, Pallas kernels: 54 us -> 51.9 us  [call(): pl.pallas_call(kernel, out_shape=outs, in_specs=[SMEM] * len(scalars) + [...]
    ppermute x9 -> x8, starting transfers between devices: 29.8 us -> 27.8 us  [swap(): return lax.ppermute(value, axes, [(i, i ^ flip) for i in range(count)])]
    ppermute x9 -> x8, waiting for transfers between devices: 23.7 us -> 23.1 us  [swap(): return lax.ppermute(value, axes, [(i, i ^ flip) for i in range(count)])]
  transfers between devices with their start and end apart: 17 -> 16, of which waited for: 13 -> 13; matrix products, arithmetic and copies ran while one was open for 1% -> 1% of each run, Pallas kernels for 16% -> 16%
where the time goes in v8:
time: 215 us; the launch traced here: 214 us
  starting transfers between devices  91.4 us (43%)
  waiting for transfers between devices  60.2 us (28%)
  Pallas kernels  51.9 us (24%)
  local copies, waits for them, and re-layouts  8.17 us (4%)
    pallas_call x15, Pallas kernels, call(): pl.pallas_call(kernel, out_shape=outs, in_specs=[SMEM] * len(scalars) + [...  51.9 us
    ppermute x8, starting transfers between devices, swap(): return lax.ppermute(value, axes, [(i, i ^ flip) for i in range(count)])  27.8 us
    ppermute x8, waiting for transfers between devices, swap(): return lax.ppermute(value, axes, [(i, i ^ flip) for i in range(count)])  23.1 us
    all_to_all x1, starting transfers between devices, body(): own = exchange(packed, ZED)  15.2 us
    all_to_all x1, waiting for transfers between devices, body(): home = exchange(packed_grads, ZED)  14.3 us
    all_to_all x1, starting transfers between devices, body(): home = exchange(packed_grads, ZED)  10.7 us
    all_to_all x1, starting transfers between devices, body(): means = exchange(means, ZED)  9.94 us
    all_to_all x1, waiting for transfers between devices, body(): means = exchange(means, ZED)  8.09 us
  transfers between devices with their start and end apart: 16, of which 13 were waited for; matrix products, arithmetic and copies ran while one was open for 1% of the time, Pallas kernels for 16%

profile of v8, /device:TPU:2, one launch (start us, length us, event | category | flops | bytes accessed | tf_op | source)
XLA Modules:
  0.0 213.9 jit_solution(16139131120446098242)
XLA Ops:
  1.3 2.2 %pack.1 = bf16[16,112,128]{2,1,0:T(8,128)(2,1)} custom-call(s32[4]{0:T(128)} %pad_add_fusion.place_ref, s32[8]{0:T(128)} %bitcast.17, bf16[128,512]{1,0:T(8,128)(2,1)} %bitcast.26, bf16[128,512]{1,0:T(8,128)(2,1)} %bitcast.27, bf16[128,512]{1,0:T(8,128)(2,1)} %bitcast.28, bf16[128,1024]{1,0:T(8,128)(2,1)} %bitcast.25), custom_call_target="tpu_custom_call" | custom-call | bytes 1000000 | tf_op jit(solution)/shard_map/pack/pallas_call | solution.py:503
  3.4 15.2 %all-to-all-start = ((bf16[16,112,128]{2,1,0:T(8,128)(2,1)}), bf16[16,112,128]{2,1,0:T(8,128)(2,1)S(1)}, u32[]{:S(2)}, u32[]{:S(2)}) async-start(bf16[16,112,128]{2,1,0:T(8,128)(2,1)} %pack.1), calls=%async_computation | async-start | bytes 917504 | tf_op jit(solution)/shard_map/all_to_all | solution.py:539
  18.8 5.1 %collective-permute-start = (bf16[16,1152]{1,0:T(8,128)(2,1)S(1)}, bf16[16,1152]{1,0:T(8,128)(2,1)S(1)}, u32[]{:S(2)}, u32[]{:S(2)}) collective-permute-start(bf16[16,1152]{1,0:T(8,128)(2,1)S(1)} %pad_maximum_fusion), channel_id=1, source_target_pairs={{0,256},{256,0},{1,257},{257,1},{2,258},{258,2},{3,259},{259,3},{4... | collective-permute-start | bytes 110600 | tf_op jit(solution)/shard_map/ppermute | solution.py:59
  23.9 2.2 %collective-permute-done = bf16[16,1152]{1,0:T(8,128)(2,1)S(1)} collective-permute-done((bf16[16,1152]{1,0:T(8,128)(2,1)S(1)}, bf16[16,1152]{1,0:T(8,128)(2,1)S(1)}, u32[]{:S(2)}, u32[]{:S(2)}) %collective-permute-start) | collective-permute-done | bytes 36896 | tf_op jit(solution)/shard_map/ppermute | solution.py:59
  26.1 3.5 %collective-permute-start.1 = (bf16[32,1152]{1,0:T(8,128)(2,1)S(1)}, bf16[32,1152]{1,0:T(8,128)(2,1)S(1)}, u32[]{:S(2)}, u32[]{:S(2)}) collective-permute-start(bf16[32,1152]{1,0:T(8,128)(2,1)S(1)} %maximum_select_fusion.4), channel_id=1, source_target_pairs={{0,16},{16,0},{1,17},{17,1},{2,18},{18,2},{3,19},{19,3},{4,20},{20... | collective-permute-start | bytes 221192 | tf_op jit(solution)/shard_map/ppermute | solution.py:59
  29.6 2.7 %collective-permute-done.1 = bf16[32,1152]{1,0:T(8,128)(2,1)S(1)} collective-permute-done((bf16[32,1152]{1,0:T(8,128)(2,1)S(1)}, bf16[32,1152]{1,0:T(8,128)(2,1)S(1)}, u32[]{:S(2)}, u32[]{:S(2)}) %collective-permute-start.1) | collective-permute-done | bytes 73760 | tf_op jit(solution)/shard_map/ppermute | solution.py:59
  32.4 4.0 %collective-permute-start.2 = (bf16[64,1152]{1,0:T(8,128)(2,1)S(1)}, bf16[64,1152]{1,0:T(8,128)(2,1)S(1)}, u32[]{:S(2)}, u32[]{:S(2)}) collective-permute-start(bf16[64,1152]{1,0:T(8,128)(2,1)S(1)} %maximum_select_fusion.3), channel_id=1, source_target_pairs={{0,128},{128,0},{1,129},{129,1},{2,130},{130,2},{3,131},{131,3},{4... | collective-permute-start | bytes 442376 | tf_op jit(solution)/shard_map/ppermute | solution.py:59
  36.5 4.5 %collective-permute-done.2 = bf16[64,1152]{1,0:T(8,128)(2,1)S(1)} collective-permute-done((bf16[64,1152]{1,0:T(8,128)(2,1)S(1)}, bf16[64,1152]{1,0:T(8,128)(2,1)S(1)}, u32[]{:S(2)}, u32[]{:S(2)}) %collective-permute-start.2) | collective-permute-done | bytes 147488 | tf_op jit(solution)/shard_map/ppermute | solution.py:59
  41.0 4.4 %all-to-all-done.own_ref = bf16[16,112,128]{2,1,0:T(8,128)(2,1)S(1)} async-done(((bf16[16,112,128]{2,1,0:T(8,128)(2,1)}), bf16[16,112,128]{2,1,0:T(8,128)(2,1)S(1)}, u32[]{:S(2)}, u32[]{:S(2)}) %all-to-all-start) | async-done | bytes 458784 | tf_op jit(solution)/shard_map/all_to_all | solution.py:539
  46.8 4.3 %all-to-all-start.1 = ((bf16[4,16,96,128]{3,2,1,0:T(8,128)(2,1)}), bf16[4,16,96,128]{3,2,1,0:T(8,128)(2,1)}, u32[]{:S(2)}, u32[]{:S(2)}) async-start(bf16[4,16,96,128]{3,2,1,0:T(8,128)(2,1)} %broadcast_in_dim.22), calls=%async_computation.1 | async-start | bytes 3145728 | tf_op jit(solution)/shard_map/all_to_all | solution.py:52
  51.2 2.4 %collective-permute-start.3 = (bf16[128,1152]{1,0:T(8,128)(2,1)S(1)}, bf16[128,1152]{1,0:T(8,128)(2,1)S(1)}, u32[]{:S(2)}, u32[]{:S(2)}) collective-permute-start(bf16[128,1152]{1,0:T(8,128)(2,1)S(1)} %maximum_select_fusion.2), channel_id=1, source_target_pairs={{0,64},{64,0},{1,65},{65,1},{2,66},{66,2},{3,67},{67,3},{4,68},{68... | collective-permute-start | bytes 884744 | tf_op jit(solution)/shard_map/ppermute | solution.py:59
  53.6 6.2 %collective-permute-done.3 = bf16[128,1152]{1,0:T(8,128)(2,1)S(1)} collective-permute-done((bf16[128,1152]{1,0:T(8,128)(2,1)S(1)}, bf16[128,1152]{1,0:T(8,128)(2,1)S(1)}, u32[]{:S(2)}, u32[]{:S(2)}) %collective-permute-start.3) | collective-permute-done | bytes 294944 | tf_op jit(solution)/shard_map/ppermute | solution.py:59
  61.8 2.0 collective-permute-done.4
  66.5 9.8 %forward.1 = (bf16[4096,128]{1,0:T(8,128)(2,1)S(1)}, bf16[1024,128]{1,0:T(8,128)(2,1)S(1)}, bf16[512,128]{1,0:T(8,128)(2,1)S(1)}, f32[8,128]{1,0:T(8,128)S(1)}, f32[16,128]{1,0:T(8,128)S(1)}) custom-call(s32[4]{0:T(128)S(1)} %copy-done.1, s32[8]{0:T(128)S(1)} %bitcast.18, bf16[16,112,128]{2,1,0:T(8,128)(2,1)S(1)} %all-to-all-done.own_ref, ...), custom_call_target="tpu_custom_call" | custom-call | flops 4294967296 | bytes 3000000 | tf_op jit(solution)/shard_map/forward/pallas_call | solution.py:503
  78.0 3.5 %collective-permute-start.5 = (f32[16,128]{1,0:T(8,128)S(1)}, f32[16,128]{1,0:T(8,128)S(1)}, u32[]{:S(2)}, u32[]{:S(2)}) collective-permute-start(f32[16,128]{1,0:T(8,128)S(1)} %get-tuple-element.60.mine_ref), channel_id=1, source_target_pairs={{0,16},{16,0},{1,17},{17,1},{2,18},{18,2},{3,19},{19,3},{4,20},{20... | collective-permute-start | bytes 24584 | tf_op jit(solution)/shard_map/ppermute | solution.py:59
  81.4 2.0 collective-permute-done.5.other_ref
  84.2 9.9 %all-to-all-start.2 = ((f32[16,24,128]{2,1,0:T(8,128)}), f32[16,24,128]{2,1,0:T(8,128)S(1)}, u32[]{:S(2)}, u32[]{:S(2)}) async-start(f32[16,24,128]{2,1,0:T(8,128)} %plane.1), calls=%async_computation.2 | async-start | bytes 393216 | tf_op jit(solution)/shard_map/all_to_all | solution.py:568
  94.1 3.4 %collective-permute-start.6 = (bf16[512,128]{1,0:T(8,128)(2,1)S(1)}, bf16[512,128]{1,0:T(8,128)(2,1)S(1)}, u32[]{:S(2)}, u32[]{:S(2)}) collective-permute-start(bf16[512,128]{1,0:T(8,128)(2,1)S(1)} %get-tuple-element.62.spare_ref), channel_id=1, source_target_pairs={{0,16},{16,0},{1,17},{17,1},{2,18},{18,2},{3,19},{19,3},{4,20},{20... | collective-permute-start | bytes 393224 | tf_op jit(solution)/shard_map/ppermute | solution.py:59
  97.5 3.5 %collective-permute-done.6.other_ref = bf16[512,128]{1,0:T(8,128)(2,1)S(1)} collective-permute-done((bf16[512,128]{1,0:T(8,128)(2,1)S(1)}, bf16[512,128]{1,0:T(8,128)(2,1)S(1)}, u32[]{:S(2)}, u32[]{:S(2)}) %collective-permute-start.6) | collective-permute-done | bytes 131104 | tf_op jit(solution)/shard_map/ppermute | solution.py:59
  101.0 8.1 %all-to-all-done.2.means_ref = f32[16,24,128]{2,1,0:T(8,128)S(1)} async-done(((f32[16,24,128]{2,1,0:T(8,128)}), f32[16,24,128]{2,1,0:T(8,128)S(1)}, u32[]{:S(2)}, u32[]{:S(2)}) %all-to-all-start.2) | async-done | bytes 196640 | tf_op jit(solution)/shard_map/all_to_all | solution.py:568
  110.5 7.5 %all-to-all-start.3 = ((f32[16,8,128]{2,1,0:T(8,128)}), f32[16,8,128]{2,1,0:T(8,128)S(1)}, u32[]{:S(2)}, u32[]{:S(2)}) async-start(f32[16,8,128]{2,1,0:T(8,128)} %get-tuple-element.66), calls=%async_computation.3 | async-start | bytes 131072 | tf_op jit(solution)/shard_map/all_to_all | solution.py:581
  119.7 4.6 %all-to-all-done.3.sums_ref = f32[16,8,128]{2,1,0:T(8,128)S(1)} async-done(((f32[16,8,128]{2,1,0:T(8,128)}), f32[16,8,128]{2,1,0:T(8,128)S(1)}, u32[]{:S(2)}, u32[]{:S(2)}) %all-to-all-start.3) | async-done | bytes 65568 | tf_op jit(solution)/shard_map/all_to_all | solution.py:581
  125.6 4.4 %all-to-all-start.4 = ((f32[16,16,128]{2,1,0:T(8,128)}), f32[16,16,128]{2,1,0:T(8,128)S(1)}, u32[]{:S(2)}, u32[]{:S(2)}) async-start(f32[16,16,128]{2,1,0:T(8,128)} %loss.1), calls=%async_computation.4 | async-start | bytes 262144 | tf_op jit(solution)/shard_map/all_to_all | solution.py:593
  130.0 8.4 %mass.1 = (f32[8,8,128]{2,1,0:T(8,128)S(1)}, f32[8,4096]{1,0:T(8,128)S(1)}, bf16[4096,128]{1,0:T(8,128)(2,1)S(1)}) custom-call(s32[4]{0:T(128)S(1)} %copy-done.1, s32[8]{0:T(128)S(1)} %bitcast.19, bf16[16,112,128]{2,1,0:T(8,128)(2,1)S(1)} %all-to-all-done.own_ref, bf16[4,16,96,128]{3,2,1,0:T(8,128)(2,1)} %all-to-all-done.1.all_ref, ...), custom_call_target="tpu_custom_call" | custom-call | flops 4294967296 | bytes 2500000 | tf_op jit(solution)/shard_map/mass/pallas_call | solution.py:503
  139.4 5.3 %all-to-all-done.4.terms_ref = f32[16,16,128]{2,1,0:T(8,128)S(1)} async-done(((f32[16,16,128]{2,1,0:T(8,128)}), f32[16,16,128]{2,1,0:T(8,128)S(1)}, u32[]{:S(2)}, u32[]{:S(2)}) %all-to-all-start.4) | async-done | bytes 131104 | tf_op jit(solution)/shard_map/all_to_all | solution.py:593
  146.1 6.7 %all-to-all-start.5 = ((f32[16,8,128]{2,1,0:T(8,128)}), f32[16,8,128]{2,1,0:T(8,128)S(1)}, u32[]{:S(2)}, u32[]{:S(2)}) async-start(f32[16,8,128]{2,1,0:T(8,128)} %get-tuple-element.80), calls=%async_computation.5 | async-start | bytes 131072 | tf_op jit(solution)/shard_map/all_to_all | solution.py:614
  152.9 4.0 %collective-permute-start.7 = (f32[16,128]{1,0:T(8,128)S(1)}, f32[16,128]{1,0:T(8,128)S(1)}, u32[]{:S(2)}, u32[]{:S(2)}) collective-permute-start(f32[16,128]{1,0:T(8,128)S(1)} %get-tuple-element.84.mine_ref), channel_id=1, source_target_pairs={{0,1},{1,0},{2,3},{3,2},{4,5},{5,4},{6,7},{7,6},{8,9},{9,8},{10,11... | collective-permute-start | bytes 24584 | tf_op jit(solution)/shard_map/ppermute | solution.py:59
  159.0 8.3 %rows.1.grad_q_ref = bf16[1024,128]{1,0:T(8,128)(2,1)S(1)} custom-call(s32[4]{0:T(128)S(1)} %copy-done.1, s32[8]{0:T(128)S(1)} %bitcast.21, bf16[1024,128]{1,0:T(8,128)(2,1)S(1)} %copy-done.8, f32[8,128]{1,0:T(8,128)S(1)} %get-tuple-element.86.lse_ref, bf16[4096,128]{1,0:T(8,128)(2,1)S(1)} %copy-done.6, f32[8,128]{1,0:T(8,128)S(1)} %get-tuple-element.88.dattn_ref), custom_call_target="tpu_custom_call" | custom-call | flops 6442450944 | bytes 2000000 | tf_op jit(solution)/shard_map/rows/pallas_call | solution.py:503
  168.9 4.8 %all-to-all-start.7 = ((bf16[16,16,768]{2,1,0:T(8,128)(2,1)}), bf16[16,16,768]{2,1,0:T(8,128)(2,1)S(1)}, u32[]{:S(2)}, u32[]{:S(2)}) async-start(bf16[16,16,768]{2,1,0:T(8,128)(2,1)} %get-tuple-element.97), calls=%async_computation.7 | async-start | bytes 786432 | tf_op jit(solution)/shard_map/all_to_all | solution.py:631
  174.9 8.9 %columns.1 = bf16[16,64,128]{2,1,0:T(8,128)(2,1)} custom-call(s32[4]{0:T(128)S(1)} %copy-done.1, s32[8]{0:T(128)S(1)} %bitcast.23, bf16[16,112,128]{2,1,0:T(8,128)(2,1)S(1)} %all-to-all-done.own_ref, bf16[4096,128]{1,0:T(8,128)(2,1)S(1)} %copy-done.4, f32[16,128]{1,0:T(8,128)S(1)} %get-tuple-element.84.mine_ref, ...), custom_call_target="tpu_custom_call" | custom-call | flops 6442450944 | bytes 2500000 | tf_op jit(solution)/shard_map/columns/pallas_call | solution.py:503
  183.9 10.7 %all-to-all-start.6 = ((bf16[16,64,128]{2,1,0:T(8,128)(2,1)}), bf16[16,64,128]{2,1,0:T(8,128)(2,1)S(1)}, u32[]{:S(2)}, u32[]{:S(2)}) async-start(bf16[16,64,128]{2,1,0:T(8,128)(2,1)} %columns.1), calls=%async_computation.6 | async-start | bytes 524288 | tf_op jit(solution)/shard_map/all_to_all | solution.py:644
  198.7 14.3 %all-to-all-done.6.in_ref = bf16[16,64,128]{2,1,0:T(8,128)(2,1)S(1)} async-done(((bf16[16,64,128]{2,1,0:T(8,128)(2,1)}), bf16[16,64,128]{2,1,0:T(8,128)(2,1)S(1)}, u32[]{:S(2)}, u32[]{:S(2)}) %all-to-all-start.6) | async-done | bytes 262176 | tf_op jit(solution)/shard_map/all_to_all | solution.py:644
  (50 shorter events, 26.1 us)
Async XLA Ops:
  0.6 18.0 %copy-start.10 = (s32[16]{0:T(128)S(1)}, s32[16]{0:T(128)}, u32[]{:S(2)}) copy-start(s32[16]{0:T(128)} %param.15) | copy-start | bytes 196
  0.6 18.1 %copy-start.9 = (bf16[16,1024]{1,0:T(8,128)(2,1)S(1)}, bf16[16,1024]{1,0:T(8,128)(2,1)}, u32[]{:S(2)}) copy-start(bf16[16,1024]{1,0:T(8,128)(2,1)} %param.14) | copy-start | bytes 98308
  3.4 42.0 %all-to-all-start = ((bf16[16,112,128]{2,1,0:T(8,128)(2,1)}), bf16[16,112,128]{2,1,0:T(8,128)(2,1)S(1)}, u32[]{:S(2)}, u32[]{:S(2)}) async-start(bf16[16,112,128]{2,1,0:T(8,128)(2,1)} %pack.1), calls=%async_computation | async-start | bytes 917504 | tf_op jit(solution)/shard_map/all_to_all | solution.py:539
  18.8 7.4 %collective-permute-start = (bf16[16,1152]{1,0:T(8,128)(2,1)S(1)}, bf16[16,1152]{1,0:T(8,128)(2,1)S(1)}, u32[]{:S(2)}, u32[]{:S(2)}) collective-permute-start(bf16[16,1152]{1,0:T(8,128)(2,1)S(1)} %pad_maximum_fusion), channel_id=1, source_target_pairs={{0,256},{256,0},{1,257},{257,1},{2,258},{258,2},{3,259},{259,3},{4... | collective-permute-start | bytes 110600 | tf_op jit(solution)/shard_map/ppermute | solution.py:59
  26.1 6.2 %collective-permute-start.1 = (bf16[32,1152]{1,0:T(8,128)(2,1)S(1)}, bf16[32,1152]{1,0:T(8,128)(2,1)S(1)}, u32[]{:S(2)}, u32[]{:S(2)}) collective-permute-start(bf16[32,1152]{1,0:T(8,128)(2,1)S(1)} %maximum_select_fusion.4), channel_id=1, source_target_pairs={{0,16},{16,0},{1,17},{17,1},{2,18},{18,2},{3,19},{19,3},{4,20},{20... | collective-permute-start | bytes 221192 | tf_op jit(solution)/shard_map/ppermute | solution.py:59
  32.4 8.5 %collective-permute-start.2 = (bf16[64,1152]{1,0:T(8,128)(2,1)S(1)}, bf16[64,1152]{1,0:T(8,128)(2,1)S(1)}, u32[]{:S(2)}, u32[]{:S(2)}) collective-permute-start(bf16[64,1152]{1,0:T(8,128)(2,1)S(1)} %maximum_select_fusion.3), channel_id=1, source_target_pairs={{0,128},{128,0},{1,129},{129,1},{2,130},{130,2},{3,131},{131,3},{4... | collective-permute-start | bytes 442376 | tf_op jit(solution)/shard_map/ppermute | solution.py:59
  46.8 19.7 %all-to-all-start.1 = ((bf16[4,16,96,128]{3,2,1,0:T(8,128)(2,1)}), bf16[4,16,96,128]{3,2,1,0:T(8,128)(2,1)}, u32[]{:S(2)}, u32[]{:S(2)}) async-start(bf16[4,16,96,128]{3,2,1,0:T(8,128)(2,1)} %broadcast_in_dim.22), calls=%async_computation.1 | async-start | bytes 3145728 | tf_op jit(solution)/shard_map/all_to_all | solution.py:52
  51.2 8.6 %collective-permute-start.3 = (bf16[128,1152]{1,0:T(8,128)(2,1)S(1)}, bf16[128,1152]{1,0:T(8,128)(2,1)S(1)}, u32[]{:S(2)}, u32[]{:S(2)}) collective-permute-start(bf16[128,1152]{1,0:T(8,128)(2,1)S(1)} %maximum_select_fusion.2), channel_id=1, source_target_pairs={{0,64},{64,0},{1,65},{65,1},{2,66},{66,2},{3,67},{67,3},{4,68},{68... | collective-permute-start | bytes 884744 | tf_op jit(solution)/shard_map/ppermute | solution.py:59
  59.9 3.9 %collective-permute-start.4 = (bf16[256,1152]{1,0:T(8,128)(2,1)S(1)}, bf16[256,1152]{1,0:T(8,128)(2,1)S(1)}, u32[]{:S(2)}, u32[]{:S(2)}) collective-permute-start(bf16[256,1152]{1,0:T(8,128)(2,1)S(1)} %maximum_select_fusion.1), channel_id=1, source_target_pairs={{0,32},{32,0},{1,33},{33,1},{2,34},{34,2},{3,35},{35,3},{4,36},{36... | collective-permute-start | bytes 1769480 | tf_op jit(solution)/shard_map/ppermute | solution.py:59
  64.2 2.2 %copy-start.1 = (s32[4]{0:T(128)S(1)}, s32[4]{0:T(128)}, u32[]{:S(2)}) copy-start(s32[4]{0:T(128)} %pad_add_fusion.place_ref) | copy-start | bytes 52
  64.3 2.2 %copy-start.2 = (s32[1,8]{1,0:T(1,128)S(1)}, s32[1,8]{1,0:T(1,128)}, u32[]{:S(2)}) copy-start(s32[1,8]{1,0:T(1,128)} %param.13) | copy-start | bytes 100
  66.5 42.6 %copy-start = (bf16[512,1024]{1,0:T(8,128)(2,1)S(1)}, bf16[512,1024]{1,0:T(8,128)(2,1)}, u32[]{:S(2)}) copy-start(bf16[512,1024]{1,0:T(8,128)(2,1)} %w_ref.7) | copy-start | bytes 3145732
  76.3 1.0 copy-start.5
  77.2 0.7 copy-start.7
  78.0 5.5 %collective-permute-start.5 = (f32[16,128]{1,0:T(8,128)S(1)}, f32[16,128]{1,0:T(8,128)S(1)}, u32[]{:S(2)}, u32[]{:S(2)}) collective-permute-start(f32[16,128]{1,0:T(8,128)S(1)} %get-tuple-element.60.mine_ref), channel_id=1, source_target_pairs={{0,16},{16,0},{1,17},{17,1},{2,18},{18,2},{3,19},{19,3},{4,20},{20... | collective-permute-start | bytes 24584 | tf_op jit(solution)/shard_map/ppermute | solution.py:59
  84.2 24.9 %all-to-all-start.2 = ((f32[16,24,128]{2,1,0:T(8,128)}), f32[16,24,128]{2,1,0:T(8,128)S(1)}, u32[]{:S(2)}, u32[]{:S(2)}) async-start(f32[16,24,128]{2,1,0:T(8,128)} %plane.1), calls=%async_computation.2 | async-start | bytes 393216 | tf_op jit(solution)/shard_map/all_to_all | solution.py:568
  94.1 6.9 %collective-permute-start.6 = (bf16[512,128]{1,0:T(8,128)(2,1)S(1)}, bf16[512,128]{1,0:T(8,128)(2,1)S(1)}, u32[]{:S(2)}, u32[]{:S(2)}) collective-permute-start(bf16[512,128]{1,0:T(8,128)(2,1)S(1)} %get-tuple-element.62.spare_ref), channel_id=1, source_target_pairs={{0,16},{16,0},{1,17},{17,1},{2,18},{18,2},{3,19},{19,3},{4,20},{20... | collective-permute-start | bytes 393224 | tf_op jit(solution)/shard_map/ppermute | solution.py:59
  110.5 13.7 %all-to-all-start.3 = ((f32[16,8,128]{2,1,0:T(8,128)}), f32[16,8,128]{2,1,0:T(8,128)S(1)}, u32[]{:S(2)}, u32[]{:S(2)}) async-start(f32[16,8,128]{2,1,0:T(8,128)} %get-tuple-element.66), calls=%async_computation.3 | async-start | bytes 131072 | tf_op jit(solution)/shard_map/all_to_all | solution.py:581
  125.6 19.1 %all-to-all-start.4 = ((f32[16,16,128]{2,1,0:T(8,128)}), f32[16,16,128]{2,1,0:T(8,128)S(1)}, u32[]{:S(2)}, u32[]{:S(2)}) async-start(f32[16,16,128]{2,1,0:T(8,128)} %loss.1), calls=%async_computation.4 | async-start | bytes 262144 | tf_op jit(solution)/shard_map/all_to_all | solution.py:593
  138.4 1.0 copy-start.3
  146.1 21.2 %all-to-all-start.5 = ((f32[16,8,128]{2,1,0:T(8,128)}), f32[16,8,128]{2,1,0:T(8,128)S(1)}, u32[]{:S(2)}, u32[]{:S(2)}) async-start(f32[16,8,128]{2,1,0:T(8,128)} %get-tuple-element.80), calls=%async_computation.5 | async-start | bytes 131072 | tf_op jit(solution)/shard_map/all_to_all | solution.py:614
  152.9 16.0 %collective-permute-start.7 = (f32[16,128]{1,0:T(8,128)S(1)}, f32[16,128]{1,0:T(8,128)S(1)}, u32[]{:S(2)}, u32[]{:S(2)}) collective-permute-start(f32[16,128]{1,0:T(8,128)S(1)} %get-tuple-element.84.mine_ref), channel_id=1, source_target_pairs={{0,1},{1,0},{2,3},{3,2},{4,5},{5,4},{6,7},{7,6},{8,9},{9,8},{10,11... | collective-permute-start | bytes 24584 | tf_op jit(solution)/shard_map/ppermute | solution.py:59
  156.9 1.2 copy-start.6
  158.1 0.9 copy-start.8
  168.9 15.0 %all-to-all-start.7 = ((bf16[16,16,768]{2,1,0:T(8,128)(2,1)}), bf16[16,16,768]{2,1,0:T(8,128)(2,1)S(1)}, u32[]{:S(2)}, u32[]{:S(2)}) async-start(bf16[16,16,768]{2,1,0:T(8,128)(2,1)} %get-tuple-element.97), calls=%async_computation.7 | async-start | bytes 786432 | tf_op jit(solution)/shard_map/all_to_all | solution.py:631
  173.7 1.2 copy-start.4
  183.9 29.2 %all-to-all-start.6 = ((bf16[16,64,128]{2,1,0:T(8,128)(2,1)}), bf16[16,64,128]{2,1,0:T(8,128)(2,1)S(1)}, u32[]{:S(2)}, u32[]{:S(2)}) async-start(bf16[16,64,128]{2,1,0:T(8,128)(2,1)} %columns.1), calls=%async_computation.6 | async-start | bytes 524288 | tf_op jit(solution)/shard_map/all_to_all | solution.py:644

commit v9 on v8

--- a/solution.py
+++ b/solution.py
@@ -157,7 +157,7 @@
             q_ref[rows, cols] = jnp.concatenate([first[:, 64:128], second[:, 64:128]], axis=1)
 
 
-BLOCK = 256
+BLOCK = 512
 PARTS = BLOCK // 128
 
 
@@ -165,13 +165,29 @@
 SPARE = 512
 
 
-def forward_kernel(
-    place_ref, lens_ref, own_ref, all_ref, x_ref, y_ref, spare_ref, lse_ref, means_ref, q_s
-):
+def fill(all_ref, x_ref):
     for n in range(4):
         x_ref[n * QUARTER : (n + 1) * QUARTER, :] = all_ref[n, :, 0:64, :].reshape(QUARTER, 128)
+
+
+def own_queries(own_ref):
     queries = halves(own_ref[:, 64:96, :]).reshape(QUARTER, HEAD_DIM)
-    q_s[...] = jnp.concatenate([queries, jnp.zeros_like(queries)], axis=1)
+    return jnp.concatenate([queries, jnp.zeros_like(queries)], axis=1)
+
+
+def turned(lines):
+    columns = []
+    for part in range(8):
+        line = jnp.broadcast_to(lines[part : part + 1, :], (128, 128))
+        columns.append(jnp.transpose(line))
+    return jnp.concatenate(columns, axis=0)
+
+
+def forward_kernel(
+    place_ref, lens_ref, own_ref, all_ref, spare_ref, lse_ref, means_ref, x_ref, y_ref, q_s
+):
+    fill(all_ref, x_ref)
+    q_s[...] = own_queries(own_ref)
 
     def block(i, carry):
         rows = pl.ds(pl.multiple_of(i * BLOCK, BLOCK), BLOCK)
@@ -413,33 +429,26 @@
 
 
 CHUNK = 512
-TALL = 512
+TALL = 1024
 
 
 def row_kernel(
-    place_ref, lens_ref, y_ref, lse_ref, x_ref, dattn_ref, out_ref, q_s, d_s, delta_s
+    place_ref, lens_ref, own_ref, all_ref, lse_ref, delta_ref, dattn_ref,
+    out_ref, x_ref, q_s, d_s, delta_s, lse_s,
 ):
-    lane = lanes(QUARTER)
+    fill(all_ref, x_ref)
+    q_s[...] = own_queries(own_ref)
     member = quarter_member(lens_ref, place_ref[0], place_ref[1]).astype(BF16)
     spread = lax.dot_general(
         member, dattn_ref[...].astype(BF16), TN, preferred_element_type=F32
     )
-    spread = jnp.where(lane < 64, 0.0, spread)
-    mine = y_ref[0:QUARTER, :]
-    q_s[...] = jnp.where(lane < 64, mine, jnp.zeros_like(mine))
-    d_s[...] = spread.astype(BF16)
-    delta_s[...] = jnp.broadcast_to(
-        jnp.sum(spread * mine.astype(F32), axis=1, keepdims=True), (QUARTER, 128)
-    )
+    d_s[...] = jnp.where(lanes(QUARTER) < 64, 0.0, spread).astype(BF16)
+    delta_s[...] = turned(delta_ref[0:8, :])
+    lse_s[...] = turned(lse_ref[...])
 
     def block(i, carry):
         rows = pl.ds(pl.multiple_of(i * TALL, TALL), TALL)
-        columns = []
-        for part in range(TALL // 128):
-            line = lse_ref[pl.ds(i * (TALL // 128) + part, 1), :]
-            columns.append(jnp.transpose(jnp.broadcast_to(line, (128, 128))))
-        log_total = jnp.concatenate(columns, axis=0)[:, 0:1]
-        delta = delta_s[rows, 0:1]
+        log_total, delta = lse_s[rows, 0:1], delta_s[rows, 0:1]
         total = jnp.zeros((TALL, 128), F32)
         for n in range(KEYS // CHUNK):
             part = x_ref[n * CHUNK : (n + 1) * CHUNK, :]
@@ -547,16 +556,19 @@
     )
     own, keys, queries, query_rows = barrier((own, keys, queries, query_rows))
 
-    rows, mine, spare, lse, means = call(
+    spare, lse, means = call(
         forward_kernel,
         (
-            shape((KEYS, 128), BF16),
-            shape((QUARTER, 128), BF16),
             shape((SPARE, 128), BF16),
             shape((8, 128), F32),
             shape((2 * GROUPS, 128), F32),
         ),
-        (place, lengths), (own, keys), [pltpu.VMEM((QUARTER, 128), BF16)],
+        (place, lengths), (own, keys),
+        [
+            pltpu.VMEM((KEYS, 128), BF16),
+            pltpu.VMEM((QUARTER, 128), BF16),
+            pltpu.VMEM((QUARTER, 128), BF16),
+        ],
         cost(pairs * 256 * 4, 3000000, pairs), "forward",
     )
     other_means = swap(means, ("yl",), 1)
@@ -614,10 +626,12 @@
     grad_parts = exchange(grad_part, ZED)
     other_delta = swap(delta, ("zd",), 1)
     grad_rows = call(
-        row_kernel, shape((QUARTER, 128), BF16), (place, lengths), (mine, lse, rows, dattn),
+        row_kernel, shape((QUARTER, 128), BF16), (place, lengths), (own, keys, lse, delta, dattn),
         [
+            pltpu.VMEM((KEYS, 128), BF16),
             pltpu.VMEM((QUARTER, 128), BF16),
             pltpu.VMEM((QUARTER, 128), BF16),
+            pltpu.VMEM((QUARTER, 128), F32),
             pltpu.VMEM((QUARTER, 128), F32),
         ],
         cost(pairs * 256 * 6, 2000000, pairs), "rows",

time: 215 us -> 214 us (level)
  the two profiles are of different devices: /device:TPU:2 before, /device:TPU:64 now
where the time goes in v9:
time: 214 us; the launch traced here: 212 us
  starting transfers between devices  92.6 us (43%)
  waiting for transfers between devices  58.9 us (28%)
  Pallas kernels  54.4 us (25%)
  local copies, waits for them, and re-layouts  4.32 us (2%)
    pallas_call x15, Pallas kernels, call(): pl.pallas_call(kernel, out_shape=outs, in_specs=[SMEM] * len(scalars) + [...  54.4 us
    ppermute x8, starting transfers between devices, swap(): return lax.ppermute(value, axes, [(i, i ^ flip) for i in range(count)])  29 us
    ppermute x8, waiting for transfers between devices, swap(): return lax.ppermute(value, axes, [(i, i ^ flip) for i in range(count)])  21.3 us
    all_to_all x1, starting transfers between devices, body(): own = exchange(packed, ZED)  14.8 us
    all_to_all x1, waiting for transfers between devices, body(): home = exchange(packed_grads, ZED)  14.2 us
    all_to_all x1, starting transfers between devices, body(): home = exchange(packed_grads, ZED)  11.1 us
    all_to_all x1, starting transfers between devices, body(): means = exchange(means, ZED)  9.63 us
    all_to_all x1, starting transfers between devices, body(): sums = exchange(sums, GRP)  7.04 us
  transfers between devices with their start and end apart: 16, of which 14 were waited for; matrix products, arithmetic and copies ran while one was open for 1% of the time, Pallas kernels for 16%

profile of v9, /device:TPU:64, one launch (start us, length us, event | category | flops | bytes accessed | tf_op | source)
XLA Modules:
  0.0 212.4 jit_solution(4146801065005662899)
XLA Ops:
  1.3 2.2 %pack.1 = bf16[16,112,128]{2,1,0:T(8,128)(2,1)} custom-call(s32[4]{0:T(128)} %pad_add_fusion.place_ref, s32[8]{0:T(128)} %bitcast.17, bf16[128,512]{1,0:T(8,128)(2,1)} %bitcast.26, bf16[128,512]{1,0:T(8,128)(2,1)} %bitcast.27, bf16[128,512]{1,0:T(8,128)(2,1)} %bitcast.28, bf16[128,1024]{1,0:T(8,128)(2,1)} %bitcast.25), custom_call_target="tpu_custom_call" | custom-call | bytes 1000000 | tf_op jit(solution)/shard_map/pack/pallas_call | solution.py:512
  3.4 14.8 %all-to-all-start = ((bf16[16,112,128]{2,1,0:T(8,128)(2,1)}), bf16[16,112,128]{2,1,0:T(8,128)(2,1)S(1)}, u32[]{:S(2)}, u32[]{:S(2)}) async-start(bf16[16,112,128]{2,1,0:T(8,128)(2,1)} %pack.1), calls=%async_computation | async-start | bytes 917504 | tf_op jit(solution)/shard_map/all_to_all | solution.py:548
  18.3 5.1 %collective-permute-start = (bf16[16,1152]{1,0:T(8,128)(2,1)S(1)}, bf16[16,1152]{1,0:T(8,128)(2,1)S(1)}, u32[]{:S(2)}, u32[]{:S(2)}) collective-permute-start(bf16[16,1152]{1,0:T(8,128)(2,1)S(1)} %pad_maximum_fusion), channel_id=1, source_target_pairs={{0,256},{256,0},{1,257},{257,1},{2,258},{258,2},{3,259},{259,3},{4... | collective-permute-start | bytes 110600 | tf_op jit(solution)/shard_map/ppermute | solution.py:59
  23.4 2.2 %collective-permute-done = bf16[16,1152]{1,0:T(8,128)(2,1)S(1)} collective-permute-done((bf16[16,1152]{1,0:T(8,128)(2,1)S(1)}, bf16[16,1152]{1,0:T(8,128)(2,1)S(1)}, u32[]{:S(2)}, u32[]{:S(2)}) %collective-permute-start) | collective-permute-done | bytes 36896 | tf_op jit(solution)/shard_map/ppermute | solution.py:59
  25.7 3.5 %collective-permute-start.1 = (bf16[32,1152]{1,0:T(8,128)(2,1)S(1)}, bf16[32,1152]{1,0:T(8,128)(2,1)S(1)}, u32[]{:S(2)}, u32[]{:S(2)}) collective-permute-start(bf16[32,1152]{1,0:T(8,128)(2,1)S(1)} %maximum_select_fusion.4), channel_id=1, source_target_pairs={{0,16},{16,0},{1,17},{17,1},{2,18},{18,2},{3,19},{19,3},{4,20},{20... | collective-permute-start | bytes 221192 | tf_op jit(solution)/shard_map/ppermute | solution.py:59
  29.2 2.7 %collective-permute-done.1 = bf16[32,1152]{1,0:T(8,128)(2,1)S(1)} collective-permute-done((bf16[32,1152]{1,0:T(8,128)(2,1)S(1)}, bf16[32,1152]{1,0:T(8,128)(2,1)S(1)}, u32[]{:S(2)}, u32[]{:S(2)}) %collective-permute-start.1) | collective-permute-done | bytes 73760 | tf_op jit(solution)/shard_map/ppermute | solution.py:59
  32.0 4.9 %collective-permute-start.2 = (bf16[64,1152]{1,0:T(8,128)(2,1)S(1)}, bf16[64,1152]{1,0:T(8,128)(2,1)S(1)}, u32[]{:S(2)}, u32[]{:S(2)}) collective-permute-start(bf16[64,1152]{1,0:T(8,128)(2,1)S(1)} %maximum_select_fusion.3), channel_id=1, source_target_pairs={{0,128},{128,0},{1,129},{129,1},{2,130},{130,2},{3,131},{131,3},{4... | collective-permute-start | bytes 442376 | tf_op jit(solution)/shard_map/ppermute | solution.py:59
  36.9 3.6 %collective-permute-done.2 = bf16[64,1152]{1,0:T(8,128)(2,1)S(1)} collective-permute-done((bf16[64,1152]{1,0:T(8,128)(2,1)S(1)}, bf16[64,1152]{1,0:T(8,128)(2,1)S(1)}, u32[]{:S(2)}, u32[]{:S(2)}) %collective-permute-start.2) | collective-permute-done | bytes 147488 | tf_op jit(solution)/shard_map/ppermute | solution.py:59
  40.6 2.7 %all-to-all-done.own_ref = bf16[16,112,128]{2,1,0:T(8,128)(2,1)S(1)} async-done(((bf16[16,112,128]{2,1,0:T(8,128)(2,1)}), bf16[16,112,128]{2,1,0:T(8,128)(2,1)S(1)}, u32[]{:S(2)}, u32[]{:S(2)}) %all-to-all-start) | async-done | bytes 458784 | tf_op jit(solution)/shard_map/all_to_all | solution.py:548
  44.6 4.3 %all-to-all-start.1 = ((bf16[4,16,96,128]{3,2,1,0:T(8,128)(2,1)}), bf16[4,16,96,128]{3,2,1,0:T(8,128)(2,1)}, u32[]{:S(2)}, u32[]{:S(2)}) async-start(bf16[4,16,96,128]{3,2,1,0:T(8,128)(2,1)} %broadcast_in_dim.22), calls=%async_computation.1 | async-start | bytes 3145728 | tf_op jit(solution)/shard_map/all_to_all | solution.py:52
  49.0 3.4 %collective-permute-start.3 = (bf16[128,1152]{1,0:T(8,128)(2,1)S(1)}, bf16[128,1152]{1,0:T(8,128)(2,1)S(1)}, u32[]{:S(2)}, u32[]{:S(2)}) collective-permute-start(bf16[128,1152]{1,0:T(8,128)(2,1)S(1)} %maximum_select_fusion.2), channel_id=1, source_target_pairs={{0,64},{64,0},{1,65},{65,1},{2,66},{66,2},{3,67},{67,3},{4,68},{68... | collective-permute-start | bytes 884744 | tf_op jit(solution)/shard_map/ppermute | solution.py:59
  52.4 5.2 %collective-permute-done.3 = bf16[128,1152]{1,0:T(8,128)(2,1)S(1)} collective-permute-done((bf16[128,1152]{1,0:T(8,128)(2,1)S(1)}, bf16[128,1152]{1,0:T(8,128)(2,1)S(1)}, u32[]{:S(2)}, u32[]{:S(2)}) %collective-permute-start.3) | collective-permute-done | bytes 294944 | tf_op jit(solution)/shard_map/ppermute | solution.py:59
  63.9 2.5 %all-to-all-done.1.all_ref = bf16[4,16,96,128]{3,2,1,0:T(8,128)(2,1)} async-done(((bf16[4,16,96,128]{3,2,1,0:T(8,128)(2,1)}), bf16[4,16,96,128]{3,2,1,0:T(8,128)(2,1)}, u32[]{:S(2)}, u32[]{:S(2)}) %all-to-all-start.1) | async-done | bytes 1572896 | tf_op jit(solution)/shard_map/all_to_all | solution.py:52
  66.3 13.1 %forward.1 = (bf16[512,128]{1,0:T(8,128)(2,1)S(1)}, f32[8,128]{1,0:T(8,128)S(1)}, f32[16,128]{1,0:T(8,128)S(1)}) custom-call(s32[4]{0:T(128)S(1)} %copy-done.1, s32[8]{0:T(128)S(1)} %bitcast.18, bf16[16,112,128]{2,1,0:T(8,128)(2,1)S(1)} %all-to-all-done.own_ref, bf16[4,16,96,128]{3,2,1,0:T(8,128)(2,1)} %all-to-all-done.1.all_ref), custom_call_target="tpu_custom_call" | custom-call | flops 4294967296 | bytes 3000000 | tf_op jit(solution)/shard_map/forward/pallas_call | solution.py:512
  79.4 3.5 %collective-permute-start.5 = (f32[16,128]{1,0:T(8,128)S(1)}, f32[16,128]{1,0:T(8,128)S(1)}, u32[]{:S(2)}, u32[]{:S(2)}) collective-permute-start(f32[16,128]{1,0:T(8,128)S(1)} %get-tuple-element.58.mine_ref), channel_id=1, source_target_pairs={{0,16},{16,0},{1,17},{17,1},{2,18},{18,2},{3,19},{19,3},{4,20},{20... | collective-permute-start | bytes 24584 | tf_op jit(solution)/shard_map/ppermute | solution.py:59
  82.9 2.1 collective-permute-done.5.other_ref
  85.6 9.6 %all-to-all-start.2 = ((f32[16,24,128]{2,1,0:T(8,128)}), f32[16,24,128]{2,1,0:T(8,128)S(1)}, u32[]{:S(2)}, u32[]{:S(2)}) async-start(f32[16,24,128]{2,1,0:T(8,128)} %plane.1), calls=%async_computation.2 | async-start | bytes 393216 | tf_op jit(solution)/shard_map/all_to_all | solution.py:580
  95.3 3.4 %collective-permute-start.6 = (bf16[512,128]{1,0:T(8,128)(2,1)S(1)}, bf16[512,128]{1,0:T(8,128)(2,1)S(1)}, u32[]{:S(2)}, u32[]{:S(2)}) collective-permute-start(bf16[512,128]{1,0:T(8,128)(2,1)S(1)} %get-tuple-element.60.spare_ref), channel_id=1, source_target_pairs={{0,16},{16,0},{1,17},{17,1},{2,18},{18,2},{3,19},{19,3},{4,20},{20... | collective-permute-start | bytes 393224 | tf_op jit(solution)/shard_map/ppermute | solution.py:59
  98.7 3.5 %collective-permute-done.6.other_ref = bf16[512,128]{1,0:T(8,128)(2,1)S(1)} collective-permute-done((bf16[512,128]{1,0:T(8,128)(2,1)S(1)}, bf16[512,128]{1,0:T(8,128)(2,1)S(1)}, u32[]{:S(2)}, u32[]{:S(2)}) %collective-permute-start.6) | collective-permute-done | bytes 131104 | tf_op jit(solution)/shard_map/ppermute | solution.py:59
  102.1 6.6 %all-to-all-done.2.means_ref = f32[16,24,128]{2,1,0:T(8,128)S(1)} async-done(((f32[16,24,128]{2,1,0:T(8,128)}), f32[16,24,128]{2,1,0:T(8,128)S(1)}, u32[]{:S(2)}, u32[]{:S(2)}) %all-to-all-start.2) | async-done | bytes 196640 | tf_op jit(solution)/shard_map/all_to_all | solution.py:580
  110.1 7.0 %all-to-all-start.3 = ((f32[16,8,128]{2,1,0:T(8,128)}), f32[16,8,128]{2,1,0:T(8,128)S(1)}, u32[]{:S(2)}, u32[]{:S(2)}) async-start(f32[16,8,128]{2,1,0:T(8,128)} %get-tuple-element.64), calls=%async_computation.3 | async-start | bytes 131072 | tf_op jit(solution)/shard_map/all_to_all | solution.py:593
  118.8 5.9 %all-to-all-done.3.sums_ref = f32[16,8,128]{2,1,0:T(8,128)S(1)} async-done(((f32[16,8,128]{2,1,0:T(8,128)}), f32[16,8,128]{2,1,0:T(8,128)S(1)}, u32[]{:S(2)}, u32[]{:S(2)}) %all-to-all-start.3) | async-done | bytes 65568 | tf_op jit(solution)/shard_map/all_to_all | solution.py:593
  126.1 6.0 %all-to-all-start.4 = ((f32[16,16,128]{2,1,0:T(8,128)}), f32[16,16,128]{2,1,0:T(8,128)S(1)}, u32[]{:S(2)}, u32[]{:S(2)}) async-start(f32[16,16,128]{2,1,0:T(8,128)} %loss.1), calls=%async_computation.4 | async-start | bytes 262144 | tf_op jit(solution)/shard_map/all_to_all | solution.py:605
  132.1 7.8 %mass.1 = (f32[8,8,128]{2,1,0:T(8,128)S(1)}, f32[8,4096]{1,0:T(8,128)S(1)}, bf16[4096,128]{1,0:T(8,128)(2,1)S(1)}) custom-call(s32[4]{0:T(128)S(1)} %copy-done.1, s32[8]{0:T(128)S(1)} %bitcast.19, bf16[16,112,128]{2,1,0:T(8,128)(2,1)S(1)} %all-to-all-done.own_ref, bf16[4,16,96,128]{3,2,1,0:T(8,128)(2,1)} %all-to-all-done.1.all_ref, ...), custom_call_target="tpu_custom_call" | custom-call | flops 4294967296 | bytes 2500000 | tf_op jit(solution)/shard_map/mass/pallas_call | solution.py:512
  140.8 5.1 %all-to-all-done.4.terms_ref = f32[16,16,128]{2,1,0:T(8,128)S(1)} async-done(((f32[16,16,128]{2,1,0:T(8,128)}), f32[16,16,128]{2,1,0:T(8,128)S(1)}, u32[]{:S(2)}, u32[]{:S(2)}) %all-to-all-start.4) | async-done | bytes 131104 | tf_op jit(solution)/shard_map/all_to_all | solution.py:605
  147.3 7.0 %all-to-all-start.5 = ((f32[16,8,128]{2,1,0:T(8,128)}), f32[16,8,128]{2,1,0:T(8,128)S(1)}, u32[]{:S(2)}, u32[]{:S(2)}) async-start(f32[16,8,128]{2,1,0:T(8,128)} %get-tuple-element.78), calls=%async_computation.5 | async-start | bytes 131072 | tf_op jit(solution)/shard_map/all_to_all | solution.py:626
  154.3 3.4 %collective-permute-start.7 = (f32[16,128]{1,0:T(8,128)S(1)}, f32[16,128]{1,0:T(8,128)S(1)}, u32[]{:S(2)}, u32[]{:S(2)}) collective-permute-start(f32[16,128]{1,0:T(8,128)S(1)} %get-tuple-element.82.delta_ref.mine_ref), channel_id=1, source_target_pairs={{0,1},{1,0},{2,3},{3,2},{4,5},{5,4},{6,7},{7,6},{8,9},{9,8},{10,11... | collective-permute-start | bytes 24584 | tf_op jit(solution)/shard_map/ppermute | solution.py:59
  157.6 8.6 %rows.1.grad_q_ref = bf16[1024,128]{1,0:T(8,128)(2,1)S(1)} custom-call(s32[4]{0:T(128)S(1)} %copy-done.1, s32[8]{0:T(128)S(1)} %bitcast.21, bf16[16,112,128]{2,1,0:T(8,128)(2,1)S(1)} %all-to-all-done.own_ref, bf16[4,16,96,128]{3,2,1,0:T(8,128)(2,1)} %all-to-all-done.1.all_ref, f32[8,128]{1,0:T(8,128)S(1)} %get-tuple-element.83.lse_ref, ...), custom_call_target="tpu_custom_call" | custom-call | flops 6442450944 | bytes 2000000 | tf_op jit(solution)/shard_map/rows/pallas_call | solution.py:512
  167.8 3.8 %all-to-all-start.7 = ((bf16[16,16,768]{2,1,0:T(8,128)(2,1)}), bf16[16,16,768]{2,1,0:T(8,128)(2,1)S(1)}, u32[]{:S(2)}, u32[]{:S(2)}) async-start(bf16[16,16,768]{2,1,0:T(8,128)(2,1)} %get-tuple-element.93), calls=%async_computation.7 | async-start | bytes 786432 | tf_op jit(solution)/shard_map/all_to_all | solution.py:645
  172.8 8.5 %columns.1 = bf16[16,64,128]{2,1,0:T(8,128)(2,1)} custom-call(s32[4]{0:T(128)S(1)} %copy-done.1, s32[8]{0:T(128)S(1)} %bitcast.23, bf16[16,112,128]{2,1,0:T(8,128)(2,1)S(1)} %all-to-all-done.own_ref, bf16[4096,128]{1,0:T(8,128)(2,1)S(1)} %copy-done.4, f32[16,128]{1,0:T(8,128)S(1)} %get-tuple-element.82.delta_ref.mine_ref, ...), custom_call_target="tpu_custom_call" | custom-call | flops 6442450944 | bytes 2500000 | tf_op jit(solution)/shard_map/columns/pallas_call | solution.py:512
  182.1 11.1 %all-to-all-start.6 = ((bf16[16,64,128]{2,1,0:T(8,128)(2,1)}), bf16[16,64,128]{2,1,0:T(8,128)(2,1)S(1)}, u32[]{:S(2)}, u32[]{:S(2)}) async-start(bf16[16,64,128]{2,1,0:T(8,128)(2,1)} %columns.1), calls=%async_computation.6 | async-start | bytes 524288 | tf_op jit(solution)/shard_map/all_to_all | solution.py:658
  197.4 14.2 %all-to-all-done.6.in_ref = bf16[16,64,128]{2,1,0:T(8,128)(2,1)S(1)} async-done(((bf16[16,64,128]{2,1,0:T(8,128)(2,1)}), bf16[16,64,128]{2,1,0:T(8,128)(2,1)S(1)}, u32[]{:S(2)}, u32[]{:S(2)}) %all-to-all-start.6) | async-done | bytes 262176 | tf_op jit(solution)/shard_map/all_to_all | solution.py:658
  (42 shorter events, 24.5 us)
Async XLA Ops:
  0.6 17.7 %copy-start.5 = (bf16[16,1024]{1,0:T(8,128)(2,1)S(1)}, bf16[16,1024]{1,0:T(8,128)(2,1)}, u32[]{:S(2)}) copy-start(bf16[16,1024]{1,0:T(8,128)(2,1)} %param.14) | copy-start | bytes 98308
  0.6 17.5 %copy-start.6 = (s32[16]{0:T(128)S(1)}, s32[16]{0:T(128)}, u32[]{:S(2)}) copy-start(s32[16]{0:T(128)} %param.15) | copy-start | bytes 196
  3.4 39.8 %all-to-all-start = ((bf16[16,112,128]{2,1,0:T(8,128)(2,1)}), bf16[16,112,128]{2,1,0:T(8,128)(2,1)S(1)}, u32[]{:S(2)}, u32[]{:S(2)}) async-start(bf16[16,112,128]{2,1,0:T(8,128)(2,1)} %pack.1), calls=%async_computation | async-start | bytes 917504 | tf_op jit(solution)/shard_map/all_to_all | solution.py:548
  18.3 7.4 %collective-permute-start = (bf16[16,1152]{1,0:T(8,128)(2,1)S(1)}, bf16[16,1152]{1,0:T(8,128)(2,1)S(1)}, u32[]{:S(2)}, u32[]{:S(2)}) collective-permute-start(bf16[16,1152]{1,0:T(8,128)(2,1)S(1)} %pad_maximum_fusion), channel_id=1, source_target_pairs={{0,256},{256,0},{1,257},{257,1},{2,258},{258,2},{3,259},{259,3},{4... | collective-permute-start | bytes 110600 | tf_op jit(solution)/shard_map/ppermute | solution.py:59
  25.7 6.2 %collective-permute-start.1 = (bf16[32,1152]{1,0:T(8,128)(2,1)S(1)}, bf16[32,1152]{1,0:T(8,128)(2,1)S(1)}, u32[]{:S(2)}, u32[]{:S(2)}) collective-permute-start(bf16[32,1152]{1,0:T(8,128)(2,1)S(1)} %maximum_select_fusion.4), channel_id=1, source_target_pairs={{0,16},{16,0},{1,17},{17,1},{2,18},{18,2},{3,19},{19,3},{4,20},{20... | collective-permute-start | bytes 221192 | tf_op jit(solution)/shard_map/ppermute | solution.py:59
  32.0 8.5 %collective-permute-start.2 = (bf16[64,1152]{1,0:T(8,128)(2,1)S(1)}, bf16[64,1152]{1,0:T(8,128)(2,1)S(1)}, u32[]{:S(2)}, u32[]{:S(2)}) collective-permute-start(bf16[64,1152]{1,0:T(8,128)(2,1)S(1)} %maximum_select_fusion.3), channel_id=1, source_target_pairs={{0,128},{128,0},{1,129},{129,1},{2,130},{130,2},{3,131},{131,3},{4... | collective-permute-start | bytes 442376 | tf_op jit(solution)/shard_map/ppermute | solution.py:59
  44.6 21.7 %all-to-all-start.1 = ((bf16[4,16,96,128]{3,2,1,0:T(8,128)(2,1)}), bf16[4,16,96,128]{3,2,1,0:T(8,128)(2,1)}, u32[]{:S(2)}, u32[]{:S(2)}) async-start(bf16[4,16,96,128]{3,2,1,0:T(8,128)(2,1)} %broadcast_in_dim.22), calls=%async_computation.1 | async-start | bytes 3145728 | tf_op jit(solution)/shard_map/all_to_all | solution.py:52
  49.0 8.6 %collective-permute-start.3 = (bf16[128,1152]{1,0:T(8,128)(2,1)S(1)}, bf16[128,1152]{1,0:T(8,128)(2,1)S(1)}, u32[]{:S(2)}, u32[]{:S(2)}) collective-permute-start(bf16[128,1152]{1,0:T(8,128)(2,1)S(1)} %maximum_select_fusion.2), channel_id=1, source_target_pairs={{0,64},{64,0},{1,65},{65,1},{2,66},{66,2},{3,67},{67,3},{4,68},{68... | collective-permute-start | bytes 884744 | tf_op jit(solution)/shard_map/ppermute | solution.py:59
  57.7 3.9 %collective-permute-start.4 = (bf16[256,1152]{1,0:T(8,128)(2,1)S(1)}, bf16[256,1152]{1,0:T(8,128)(2,1)S(1)}, u32[]{:S(2)}, u32[]{:S(2)}) collective-permute-start(bf16[256,1152]{1,0:T(8,128)(2,1)S(1)} %maximum_select_fusion.1), channel_id=1, source_target_pairs={{0,32},{32,0},{1,33},{33,1},{2,34},{34,2},{3,35},{35,3},{4,36},{36... | collective-permute-start | bytes 1769480 | tf_op jit(solution)/shard_map/ppermute | solution.py:59
  62.1 4.3 %copy-start.1 = (s32[4]{0:T(128)S(1)}, s32[4]{0:T(128)}, u32[]{:S(2)}) copy-start(s32[4]{0:T(128)} %pad_add_fusion.place_ref) | copy-start | bytes 52
  62.1 4.3 %copy-start.2 = (s32[1,8]{1,0:T(1,128)S(1)}, s32[1,8]{1,0:T(1,128)}, u32[]{:S(2)}) copy-start(s32[1,8]{1,0:T(1,128)} %param.13) | copy-start | bytes 100
  66.3 42.3 %copy-start = (bf16[512,1024]{1,0:T(8,128)(2,1)S(1)}, bf16[512,1024]{1,0:T(8,128)(2,1)}, u32[]{:S(2)}) copy-start(bf16[512,1024]{1,0:T(8,128)(2,1)} %w_ref.7) | copy-start | bytes 3145732
  79.4 5.5 %collective-permute-start.5 = (f32[16,128]{1,0:T(8,128)S(1)}, f32[16,128]{1,0:T(8,128)S(1)}, u32[]{:S(2)}, u32[]{:S(2)}) collective-permute-start(f32[16,128]{1,0:T(8,128)S(1)} %get-tuple-element.58.mine_ref), channel_id=1, source_target_pairs={{0,16},{16,0},{1,17},{17,1},{2,18},{18,2},{3,19},{19,3},{4,20},{20... | collective-permute-start | bytes 24584 | tf_op jit(solution)/shard_map/ppermute | solution.py:59
  85.6 23.0 %all-to-all-start.2 = ((f32[16,24,128]{2,1,0:T(8,128)}), f32[16,24,128]{2,1,0:T(8,128)S(1)}, u32[]{:S(2)}, u32[]{:S(2)}) async-start(f32[16,24,128]{2,1,0:T(8,128)} %plane.1), calls=%async_computation.2 | async-start | bytes 393216 | tf_op jit(solution)/shard_map/all_to_all | solution.py:580
  95.3 6.8 %collective-permute-start.6 = (bf16[512,128]{1,0:T(8,128)(2,1)S(1)}, bf16[512,128]{1,0:T(8,128)(2,1)S(1)}, u32[]{:S(2)}, u32[]{:S(2)}) collective-permute-start(bf16[512,128]{1,0:T(8,128)(2,1)S(1)} %get-tuple-element.60.spare_ref), channel_id=1, source_target_pairs={{0,16},{16,0},{1,17},{17,1},{2,18},{18,2},{3,19},{19,3},{4,20},{20... | collective-permute-start | bytes 393224 | tf_op jit(solution)/shard_map/ppermute | solution.py:59
  110.1 14.7 %all-to-all-start.3 = ((f32[16,8,128]{2,1,0:T(8,128)}), f32[16,8,128]{2,1,0:T(8,128)S(1)}, u32[]{:S(2)}, u32[]{:S(2)}) async-start(f32[16,8,128]{2,1,0:T(8,128)} %get-tuple-element.64), calls=%async_computation.3 | async-start | bytes 131072 | tf_op jit(solution)/shard_map/all_to_all | solution.py:593
  126.1 19.8 %all-to-all-start.4 = ((f32[16,16,128]{2,1,0:T(8,128)}), f32[16,16,128]{2,1,0:T(8,128)S(1)}, u32[]{:S(2)}, u32[]{:S(2)}) async-start(f32[16,16,128]{2,1,0:T(8,128)} %loss.1), calls=%async_computation.4 | async-start | bytes 262144 | tf_op jit(solution)/shard_map/all_to_all | solution.py:605
  139.9 1.0 copy-start.3
  147.3 19.0 %all-to-all-start.5 = ((f32[16,8,128]{2,1,0:T(8,128)}), f32[16,8,128]{2,1,0:T(8,128)S(1)}, u32[]{:S(2)}, u32[]{:S(2)}) async-start(f32[16,8,128]{2,1,0:T(8,128)} %get-tuple-element.78), calls=%async_computation.5 | async-start | bytes 131072 | tf_op jit(solution)/shard_map/all_to_all | solution.py:626
  154.3 13.5 %collective-permute-start.7 = (f32[16,128]{1,0:T(8,128)S(1)}, f32[16,128]{1,0:T(8,128)S(1)}, u32[]{:S(2)}, u32[]{:S(2)}) collective-permute-start(f32[16,128]{1,0:T(8,128)S(1)} %get-tuple-element.82.delta_ref.mine_ref), channel_id=1, source_target_pairs={{0,1},{1,0},{2,3},{3,2},{4,5},{5,4},{6,7},{7,6},{8,9},{9,8},{10,11... | collective-permute-start | bytes 24584 | tf_op jit(solution)/shard_map/ppermute | solution.py:59
  167.8 14.3 %all-to-all-start.7 = ((bf16[16,16,768]{2,1,0:T(8,128)(2,1)}), bf16[16,16,768]{2,1,0:T(8,128)(2,1)S(1)}, u32[]{:S(2)}, u32[]{:S(2)}) async-start(bf16[16,16,768]{2,1,0:T(8,128)(2,1)} %get-tuple-element.93), calls=%async_computation.7 | async-start | bytes 786432 | tf_op jit(solution)/shard_map/all_to_all | solution.py:645
  171.6 1.2 copy-start.4
  182.1 29.5 %all-to-all-start.6 = ((bf16[16,64,128]{2,1,0:T(8,128)(2,1)}), bf16[16,64,128]{2,1,0:T(8,128)(2,1)S(1)}, u32[]{:S(2)}, u32[]{:S(2)}) async-start(bf16[16,64,128]{2,1,0:T(8,128)(2,1)} %columns.1), calls=%async_computation.6 | async-start | bytes 524288 | tf_op jit(solution)/shard_map/all_to_all | solution.py:658

commit v10 on v9

--- a/solution.py
+++ b/solution.py
@@ -27,6 +27,8 @@
 
 BF16 = jnp.bfloat16
 F32 = jnp.float32
+
+NEG_LARGE = -1e30
 
 GRP = ("yh", "xa", "xb", "co")
 SEQ = ("yl", "za", "zb", "zc", "zd")
@@ -163,6 +165,8 @@
 
 KEYS = 4 * QUARTER
 SPARE = 512
+CHUNK = 512
+TALL = 1024
 
 
 def fill(all_ref, x_ref):
@@ -189,22 +193,29 @@
     fill(all_ref, x_ref)
     q_s[...] = own_queries(own_ref)
 
-    def block(i, carry):
-        rows = pl.ds(pl.multiple_of(i * BLOCK, BLOCK), BLOCK)
-        scores = lax.dot_general(q_s[rows, :], x_ref[...], NT, preferred_element_type=F32)
-        top = jnp.max(scores, axis=1, keepdims=True)
+    top = jnp.full((QUARTER, 128), NEG_LARGE, F32)
+    for n in range(KEYS // CHUNK):
+        part = x_ref[n * CHUNK : (n + 1) * CHUNK, :]
+        scores = lax.dot_general(q_s[...], part, NT, preferred_element_type=F32)
+        for m in range(0, CHUNK, 128):
+            top = jnp.maximum(top, scores[:, m : m + 128])
+    top = jnp.max(top, axis=1, keepdims=True)
+    sums = jnp.zeros((QUARTER, 128), F32)
+    mixed = jnp.zeros((QUARTER, 128), F32)
+    for n in range(KEYS // CHUNK):
+        part = x_ref[n * CHUNK : (n + 1) * CHUNK, :]
+        scores = lax.dot_general(q_s[...], part, NT, preferred_element_type=F32)
         grown = jnp.exp(scores - top)
-        total = jnp.sum(grown, axis=1, keepdims=True)
-        prob = (grown * (1.0 / total)).astype(BF16)
-        mixed = jnp.dot(prob, x_ref[...], preferred_element_type=F32).astype(BF16)
-        y_ref[rows, :] = jnp.where(lanes(BLOCK) < 64, q_s[rows, :], mixed)
-        log_total = top + jnp.log(total)
-        for part in range(PARTS):
-            square = jnp.broadcast_to(log_total[part * 128 : (part + 1) * 128], (128, 128))
-            lse_ref[pl.ds(i * PARTS + part, 1), :] = jnp.transpose(square)[0:1, :]
-        return carry
-
-    lax.fori_loop(0, QUARTER // BLOCK, block, 0)
+        for m in range(0, CHUNK, 128):
+            sums = sums + grown[:, m : m + 128]
+        mixed = mixed + jnp.dot(grown.astype(BF16), part, preferred_element_type=F32)
+    total = jnp.sum(sums, axis=1, keepdims=True)
+    y_ref[...] = (mixed * (1.0 / total)).astype(BF16)
+    log_total = top + jnp.log(total)
+    for part in range(8):
+        square = jnp.broadcast_to(log_total[part * 128 : (part + 1) * 128], (128, 128))
+        lse_ref[part : part + 1, :] = jnp.transpose(square)[0:1, :]
+
     spare_ref[...] = jnp.concatenate(
         [y_ref[0:512, :][:, 64:128], y_ref[512:1024, :][:, 64:128]], axis=1
     )
@@ -428,10 +439,6 @@
     )
 
 
-CHUNK = 512
-TALL = 1024
-
-
 def row_kernel(
     place_ref, lens_ref, own_ref, all_ref, lse_ref, delta_ref, dattn_ref,
     out_ref, x_ref, q_s, d_s, delta_s, lse_s,

time: 214 us -> 212 us (level)
  no operation moved by 1% of the time
where the time goes in v10:
time: 212 us; the launch traced here: 211 us
  starting transfers between devices  92.3 us (44%)
  waiting for transfers between devices  59.2 us (28%)
  Pallas kernels  53.2 us (25%)
  local copies, waits for them, and re-layouts  4.32 us (2%)
    pallas_call x15, Pallas kernels, call(): pl.pallas_call(kernel, out_shape=outs, in_specs=[SMEM] * len(scalars) + [...  53.2 us
    ppermute x8, starting transfers between devices, swap(): return lax.ppermute(value, axes, [(i, i ^ flip) for i in range(count)])  29 us
    ppermute x8, waiting for transfers between devices, swap(): return lax.ppermute(value, axes, [(i, i ^ flip) for i in range(count)])  21.3 us
    all_to_all x1, starting transfers between devices, body(): own = exchange(packed, ZED)  14.8 us
    all_to_all x1, waiting for transfers between devices, body(): home = exchange(packed_grads, ZED)  14.2 us
    all_to_all x1, starting transfers between devices, body(): home = exchange(packed_grads, ZED)  11.1 us
    all_to_all x1, starting transfers between devices, body(): means = exchange(means, ZED)  9.63 us
    all_to_all x1, starting transfers between devices, body(): sums = exchange(sums, GRP)  7.04 us
  transfers between devices with their start and end apart: 16, of which 14 were waited for; matrix products, arithmetic and copies ran while one was open for 1% of the time, Pallas kernels for 16%

profile of v10, /device:TPU:64, one launch (start us, length us, event | category | flops | bytes accessed | tf_op | source)
XLA Modules:
  0.0 211.2 jit_solution(193791482853147360)
XLA Ops:
  1.3 2.2 %pack.1 = bf16[16,112,128]{2,1,0:T(8,128)(2,1)} custom-call(s32[4]{0:T(128)} %pad_add_fusion.place_ref, s32[8]{0:T(128)} %bitcast.17, bf16[128,512]{1,0:T(8,128)(2,1)} %bitcast.26, bf16[128,512]{1,0:T(8,128)(2,1)} %bitcast.27, bf16[128,512]{1,0:T(8,128)(2,1)} %bitcast.28, bf16[128,1024]{1,0:T(8,128)(2,1)} %bitcast.25), custom_call_target="tpu_custom_call" | custom-call | bytes 1000000 | tf_op jit(solution)/shard_map/pack/pallas_call | solution.py:519
  3.4 14.8 %all-to-all-start = ((bf16[16,112,128]{2,1,0:T(8,128)(2,1)}), bf16[16,112,128]{2,1,0:T(8,128)(2,1)S(1)}, u32[]{:S(2)}, u32[]{:S(2)}) async-start(bf16[16,112,128]{2,1,0:T(8,128)(2,1)} %pack.1), calls=%async_computation | async-start | bytes 917504 | tf_op jit(solution)/shard_map/all_to_all | solution.py:555
  18.3 5.1 %collective-permute-start = (bf16[16,1152]{1,0:T(8,128)(2,1)S(1)}, bf16[16,1152]{1,0:T(8,128)(2,1)S(1)}, u32[]{:S(2)}, u32[]{:S(2)}) collective-permute-start(bf16[16,1152]{1,0:T(8,128)(2,1)S(1)} %pad_maximum_fusion), channel_id=1, source_target_pairs={{0,256},{256,0},{1,257},{257,1},{2,258},{258,2},{3,259},{259,3},{4... | collective-permute-start | bytes 110600 | tf_op jit(solution)/shard_map/ppermute | solution.py:61
  23.4 2.2 %collective-permute-done = bf16[16,1152]{1,0:T(8,128)(2,1)S(1)} collective-permute-done((bf16[16,1152]{1,0:T(8,128)(2,1)S(1)}, bf16[16,1152]{1,0:T(8,128)(2,1)S(1)}, u32[]{:S(2)}, u32[]{:S(2)}) %collective-permute-start) | collective-permute-done | bytes 36896 | tf_op jit(solution)/shard_map/ppermute | solution.py:61
  25.7 3.5 %collective-permute-start.1 = (bf16[32,1152]{1,0:T(8,128)(2,1)S(1)}, bf16[32,1152]{1,0:T(8,128)(2,1)S(1)}, u32[]{:S(2)}, u32[]{:S(2)}) collective-permute-start(bf16[32,1152]{1,0:T(8,128)(2,1)S(1)} %maximum_select_fusion.4), channel_id=1, source_target_pairs={{0,16},{16,0},{1,17},{17,1},{2,18},{18,2},{3,19},{19,3},{4,20},{20... | collective-permute-start | bytes 221192 | tf_op jit(solution)/shard_map/ppermute | solution.py:61
  29.2 2.7 %collective-permute-done.1 = bf16[32,1152]{1,0:T(8,128)(2,1)S(1)} collective-permute-done((bf16[32,1152]{1,0:T(8,128)(2,1)S(1)}, bf16[32,1152]{1,0:T(8,128)(2,1)S(1)}, u32[]{:S(2)}, u32[]{:S(2)}) %collective-permute-start.1) | collective-permute-done | bytes 73760 | tf_op jit(solution)/shard_map/ppermute | solution.py:61
  32.0 4.9 %collective-permute-start.2 = (bf16[64,1152]{1,0:T(8,128)(2,1)S(1)}, bf16[64,1152]{1,0:T(8,128)(2,1)S(1)}, u32[]{:S(2)}, u32[]{:S(2)}) collective-permute-start(bf16[64,1152]{1,0:T(8,128)(2,1)S(1)} %maximum_select_fusion.3), channel_id=1, source_target_pairs={{0,128},{128,0},{1,129},{129,1},{2,130},{130,2},{3,131},{131,3},{4... | collective-permute-start | bytes 442376 | tf_op jit(solution)/shard_map/ppermute | solution.py:61
  36.9 3.6 %collective-permute-done.2 = bf16[64,1152]{1,0:T(8,128)(2,1)S(1)} collective-permute-done((bf16[64,1152]{1,0:T(8,128)(2,1)S(1)}, bf16[64,1152]{1,0:T(8,128)(2,1)S(1)}, u32[]{:S(2)}, u32[]{:S(2)}) %collective-permute-start.2) | collective-permute-done | bytes 147488 | tf_op jit(solution)/shard_map/ppermute | solution.py:61
  40.6 2.7 %all-to-all-done.own_ref = bf16[16,112,128]{2,1,0:T(8,128)(2,1)S(1)} async-done(((bf16[16,112,128]{2,1,0:T(8,128)(2,1)}), bf16[16,112,128]{2,1,0:T(8,128)(2,1)S(1)}, u32[]{:S(2)}, u32[]{:S(2)}) %all-to-all-start) | async-done | bytes 458784 | tf_op jit(solution)/shard_map/all_to_all | solution.py:555
  44.6 4.3 %all-to-all-start.1 = ((bf16[4,16,96,128]{3,2,1,0:T(8,128)(2,1)}), bf16[4,16,96,128]{3,2,1,0:T(8,128)(2,1)}, u32[]{:S(2)}, u32[]{:S(2)}) async-start(bf16[4,16,96,128]{3,2,1,0:T(8,128)(2,1)} %broadcast_in_dim.22), calls=%async_computation.1 | async-start | bytes 3145728 | tf_op jit(solution)/shard_map/all_to_all | solution.py:54
  49.0 3.4 %collective-permute-start.3 = (bf16[128,1152]{1,0:T(8,128)(2,1)S(1)}, bf16[128,1152]{1,0:T(8,128)(2,1)S(1)}, u32[]{:S(2)}, u32[]{:S(2)}) collective-permute-start(bf16[128,1152]{1,0:T(8,128)(2,1)S(1)} %maximum_select_fusion.2), channel_id=1, source_target_pairs={{0,64},{64,0},{1,65},{65,1},{2,66},{66,2},{3,67},{67,3},{4,68},{68... | collective-permute-start | bytes 884744 | tf_op jit(solution)/shard_map/ppermute | solution.py:61
  52.4 5.2 %collective-permute-done.3 = bf16[128,1152]{1,0:T(8,128)(2,1)S(1)} collective-permute-done((bf16[128,1152]{1,0:T(8,128)(2,1)S(1)}, bf16[128,1152]{1,0:T(8,128)(2,1)S(1)}, u32[]{:S(2)}, u32[]{:S(2)}) %collective-permute-start.3) | collective-permute-done | bytes 294944 | tf_op jit(solution)/shard_map/ppermute | solution.py:61
  63.9 2.5 %all-to-all-done.1.all_ref = bf16[4,16,96,128]{3,2,1,0:T(8,128)(2,1)} async-done(((bf16[4,16,96,128]{3,2,1,0:T(8,128)(2,1)}), bf16[4,16,96,128]{3,2,1,0:T(8,128)(2,1)}, u32[]{:S(2)}, u32[]{:S(2)}) %all-to-all-start.1) | async-done | bytes 1572896 | tf_op jit(solution)/shard_map/all_to_all | solution.py:54
  66.3 11.9 %forward.1 = (bf16[512,128]{1,0:T(8,128)(2,1)S(1)}, f32[8,128]{1,0:T(8,128)S(1)}, f32[16,128]{1,0:T(8,128)S(1)}) custom-call(s32[4]{0:T(128)S(1)} %copy-done.1, s32[8]{0:T(128)S(1)} %bitcast.18, bf16[16,112,128]{2,1,0:T(8,128)(2,1)S(1)} %all-to-all-done.own_ref, bf16[4,16,96,128]{3,2,1,0:T(8,128)(2,1)} %all-to-all-done.1.all_ref), custom_call_target="tpu_custom_call" | custom-call | flops 4294967296 | bytes 3000000 | tf_op jit(solution)/shard_map/forward/pallas_call | solution.py:519
  78.2 3.5 %collective-permute-start.5 = (f32[16,128]{1,0:T(8,128)S(1)}, f32[16,128]{1,0:T(8,128)S(1)}, u32[]{:S(2)}, u32[]{:S(2)}) collective-permute-start(f32[16,128]{1,0:T(8,128)S(1)} %get-tuple-element.58.mine_ref), channel_id=1, source_target_pairs={{0,16},{16,0},{1,17},{17,1},{2,18},{18,2},{3,19},{19,3},{4,20},{20... | collective-permute-start | bytes 24584 | tf_op jit(solution)/shard_map/ppermute | solution.py:61
  81.7 2.1 collective-permute-done.5.other_ref
  84.5 9.6 %all-to-all-start.2 = ((f32[16,24,128]{2,1,0:T(8,128)}), f32[16,24,128]{2,1,0:T(8,128)S(1)}, u32[]{:S(2)}, u32[]{:S(2)}) async-start(f32[16,24,128]{2,1,0:T(8,128)} %plane.1), calls=%async_computation.2 | async-start | bytes 393216 | tf_op jit(solution)/shard_map/all_to_all | solution.py:587
  94.1 3.4 %collective-permute-start.6 = (bf16[512,128]{1,0:T(8,128)(2,1)S(1)}, bf16[512,128]{1,0:T(8,128)(2,1)S(1)}, u32[]{:S(2)}, u32[]{:S(2)}) collective-permute-start(bf16[512,128]{1,0:T(8,128)(2,1)S(1)} %get-tuple-element.60.spare_ref), channel_id=1, source_target_pairs={{0,16},{16,0},{1,17},{17,1},{2,18},{18,2},{3,19},{19,3},{4,20},{20... | collective-permute-start | bytes 393224 | tf_op jit(solution)/shard_map/ppermute | solution.py:61
  97.5 3.5 %collective-permute-done.6.other_ref = bf16[512,128]{1,0:T(8,128)(2,1)S(1)} collective-permute-done((bf16[512,128]{1,0:T(8,128)(2,1)S(1)}, bf16[512,128]{1,0:T(8,128)(2,1)S(1)}, u32[]{:S(2)}, u32[]{:S(2)}) %collective-permute-start.6) | collective-permute-done | bytes 131104 | tf_op jit(solution)/shard_map/ppermute | solution.py:61
  101.0 6.6 %all-to-all-done.2.means_ref = f32[16,24,128]{2,1,0:T(8,128)S(1)} async-done(((f32[16,24,128]{2,1,0:T(8,128)}), f32[16,24,128]{2,1,0:T(8,128)S(1)}, u32[]{:S(2)}, u32[]{:S(2)}) %all-to-all-start.2) | async-done | bytes 196640 | tf_op jit(solution)/shard_map/all_to_all | solution.py:587
  109.0 7.0 %all-to-all-start.3 = ((f32[16,8,128]{2,1,0:T(8,128)}), f32[16,8,128]{2,1,0:T(8,128)S(1)}, u32[]{:S(2)}, u32[]{:S(2)}) async-start(f32[16,8,128]{2,1,0:T(8,128)} %get-tuple-element.64), calls=%async_computation.3 | async-start | bytes 131072 | tf_op jit(solution)/shard_map/all_to_all | solution.py:600
  117.7 5.9 %all-to-all-done.3.sums_ref = f32[16,8,128]{2,1,0:T(8,128)S(1)} async-done(((f32[16,8,128]{2,1,0:T(8,128)}), f32[16,8,128]{2,1,0:T(8,128)S(1)}, u32[]{:S(2)}, u32[]{:S(2)}) %all-to-all-start.3) | async-done | bytes 65568 | tf_op jit(solution)/shard_map/all_to_all | solution.py:600
  125.0 6.0 %all-to-all-start.4 = ((f32[16,16,128]{2,1,0:T(8,128)}), f32[16,16,128]{2,1,0:T(8,128)S(1)}, u32[]{:S(2)}, u32[]{:S(2)}) async-start(f32[16,16,128]{2,1,0:T(8,128)} %loss.1), calls=%async_computation.4 | async-start | bytes 262144 | tf_op jit(solution)/shard_map/all_to_all | solution.py:612
  130.9 7.8 %mass.1 = (f32[8,8,128]{2,1,0:T(8,128)S(1)}, f32[8,4096]{1,0:T(8,128)S(1)}, bf16[4096,128]{1,0:T(8,128)(2,1)S(1)}) custom-call(s32[4]{0:T(128)S(1)} %copy-done.1, s32[8]{0:T(128)S(1)} %bitcast.19, bf16[16,112,128]{2,1,0:T(8,128)(2,1)S(1)} %all-to-all-done.own_ref, bf16[4,16,96,128]{3,2,1,0:T(8,128)(2,1)} %all-to-all-done.1.all_ref, ...), custom_call_target="tpu_custom_call" | custom-call | flops 4294967296 | bytes 2500000 | tf_op jit(solution)/shard_map/mass/pallas_call | solution.py:519
  139.7 5.4 %all-to-all-done.4.terms_ref = f32[16,16,128]{2,1,0:T(8,128)S(1)} async-done(((f32[16,16,128]{2,1,0:T(8,128)}), f32[16,16,128]{2,1,0:T(8,128)S(1)}, u32[]{:S(2)}, u32[]{:S(2)}) %all-to-all-start.4) | async-done | bytes 131104 | tf_op jit(solution)/shard_map/all_to_all | solution.py:612
  146.4 6.7 %all-to-all-start.5 = ((f32[16,8,128]{2,1,0:T(8,128)}), f32[16,8,128]{2,1,0:T(8,128)S(1)}, u32[]{:S(2)}, u32[]{:S(2)}) async-start(f32[16,8,128]{2,1,0:T(8,128)} %get-tuple-element.78), calls=%async_computation.5 | async-start | bytes 131072 | tf_op jit(solution)/shard_map/all_to_all | solution.py:633
  153.1 3.4 %collective-permute-start.7 = (f32[16,128]{1,0:T(8,128)S(1)}, f32[16,128]{1,0:T(8,128)S(1)}, u32[]{:S(2)}, u32[]{:S(2)}) collective-permute-start(f32[16,128]{1,0:T(8,128)S(1)} %get-tuple-element.82.delta_ref.mine_ref), channel_id=1, source_target_pairs={{0,1},{1,0},{2,3},{3,2},{4,5},{5,4},{6,7},{7,6},{8,9},{9,8},{10,11... | collective-permute-start | bytes 24584 | tf_op jit(solution)/shard_map/ppermute | solution.py:61
  156.5 8.6 %rows.1.grad_q_ref = bf16[1024,128]{1,0:T(8,128)(2,1)S(1)} custom-call(s32[4]{0:T(128)S(1)} %copy-done.1, s32[8]{0:T(128)S(1)} %bitcast.21, bf16[16,112,128]{2,1,0:T(8,128)(2,1)S(1)} %all-to-all-done.own_ref, bf16[4,16,96,128]{3,2,1,0:T(8,128)(2,1)} %all-to-all-done.1.all_ref, f32[8,128]{1,0:T(8,128)S(1)} %get-tuple-element.83.lse_ref, ...), custom_call_target="tpu_custom_call" | custom-call | flops 6442450944 | bytes 2000000 | tf_op jit(solution)/shard_map/rows/pallas_call | solution.py:519
  166.7 3.8 %all-to-all-start.7 = ((bf16[16,16,768]{2,1,0:T(8,128)(2,1)}), bf16[16,16,768]{2,1,0:T(8,128)(2,1)S(1)}, u32[]{:S(2)}, u32[]{:S(2)}) async-start(bf16[16,16,768]{2,1,0:T(8,128)(2,1)} %get-tuple-element.93), calls=%async_computation.7 | async-start | bytes 786432 | tf_op jit(solution)/shard_map/all_to_all | solution.py:652
  171.7 8.5 %columns.1 = bf16[16,64,128]{2,1,0:T(8,128)(2,1)} custom-call(s32[4]{0:T(128)S(1)} %copy-done.1, s32[8]{0:T(128)S(1)} %bitcast.23, bf16[16,112,128]{2,1,0:T(8,128)(2,1)S(1)} %all-to-all-done.own_ref, bf16[4096,128]{1,0:T(8,128)(2,1)S(1)} %copy-done.4, f32[16,128]{1,0:T(8,128)S(1)} %get-tuple-element.82.delta_ref.mine_ref, ...), custom_call_target="tpu_custom_call" | custom-call | flops 6442450944 | bytes 2500000 | tf_op jit(solution)/shard_map/columns/pallas_call | solution.py:519
  180.9 11.1 %all-to-all-start.6 = ((bf16[16,64,128]{2,1,0:T(8,128)(2,1)}), bf16[16,64,128]{2,1,0:T(8,128)(2,1)S(1)}, u32[]{:S(2)}, u32[]{:S(2)}) async-start(bf16[16,64,128]{2,1,0:T(8,128)(2,1)} %columns.1), calls=%async_computation.6 | async-start | bytes 524288 | tf_op jit(solution)/shard_map/all_to_all | solution.py:665
  196.2 14.2 %all-to-all-done.6.in_ref = bf16[16,64,128]{2,1,0:T(8,128)(2,1)S(1)} async-done(((bf16[16,64,128]{2,1,0:T(8,128)(2,1)}), bf16[16,64,128]{2,1,0:T(8,128)(2,1)S(1)}, u32[]{:S(2)}, u32[]{:S(2)}) %all-to-all-start.6) | async-done | bytes 262176 | tf_op jit(solution)/shard_map/all_to_all | solution.py:665
  (42 shorter events, 24.5 us)
Async XLA Ops:
  0.6 17.7 %copy-start.5 = (bf16[16,1024]{1,0:T(8,128)(2,1)S(1)}, bf16[16,1024]{1,0:T(8,128)(2,1)}, u32[]{:S(2)}) copy-start(bf16[16,1024]{1,0:T(8,128)(2,1)} %param.14) | copy-start | bytes 98308
  0.6 17.5 %copy-start.6 = (s32[16]{0:T(128)S(1)}, s32[16]{0:T(128)}, u32[]{:S(2)}) copy-start(s32[16]{0:T(128)} %param.15) | copy-start | bytes 196
  3.4 39.8 %all-to-all-start = ((bf16[16,112,128]{2,1,0:T(8,128)(2,1)}), bf16[16,112,128]{2,1,0:T(8,128)(2,1)S(1)}, u32[]{:S(2)}, u32[]{:S(2)}) async-start(bf16[16,112,128]{2,1,0:T(8,128)(2,1)} %pack.1), calls=%async_computation | async-start | bytes 917504 | tf_op jit(solution)/shard_map/all_to_all | solution.py:555
  18.3 7.4 %collective-permute-start = (bf16[16,1152]{1,0:T(8,128)(2,1)S(1)}, bf16[16,1152]{1,0:T(8,128)(2,1)S(1)}, u32[]{:S(2)}, u32[]{:S(2)}) collective-permute-start(bf16[16,1152]{1,0:T(8,128)(2,1)S(1)} %pad_maximum_fusion), channel_id=1, source_target_pairs={{0,256},{256,0},{1,257},{257,1},{2,258},{258,2},{3,259},{259,3},{4... | collective-permute-start | bytes 110600 | tf_op jit(solution)/shard_map/ppermute | solution.py:61
  25.7 6.2 %collective-permute-start.1 = (bf16[32,1152]{1,0:T(8,128)(2,1)S(1)}, bf16[32,1152]{1,0:T(8,128)(2,1)S(1)}, u32[]{:S(2)}, u32[]{:S(2)}) collective-permute-start(bf16[32,1152]{1,0:T(8,128)(2,1)S(1)} %maximum_select_fusion.4), channel_id=1, source_target_pairs={{0,16},{16,0},{1,17},{17,1},{2,18},{18,2},{3,19},{19,3},{4,20},{20... | collective-permute-start | bytes 221192 | tf_op jit(solution)/shard_map/ppermute | solution.py:61
  32.0 8.5 %collective-permute-start.2 = (bf16[64,1152]{1,0:T(8,128)(2,1)S(1)}, bf16[64,1152]{1,0:T(8,128)(2,1)S(1)}, u32[]{:S(2)}, u32[]{:S(2)}) collective-permute-start(bf16[64,1152]{1,0:T(8,128)(2,1)S(1)} %maximum_select_fusion.3), channel_id=1, source_target_pairs={{0,128},{128,0},{1,129},{129,1},{2,130},{130,2},{3,131},{131,3},{4... | collective-permute-start | bytes 442376 | tf_op jit(solution)/shard_map/ppermute | solution.py:61
  44.6 21.7 %all-to-all-start.1 = ((bf16[4,16,96,128]{3,2,1,0:T(8,128)(2,1)}), bf16[4,16,96,128]{3,2,1,0:T(8,128)(2,1)}, u32[]{:S(2)}, u32[]{:S(2)}) async-start(bf16[4,16,96,128]{3,2,1,0:T(8,128)(2,1)} %broadcast_in_dim.22), calls=%async_computation.1 | async-start | bytes 3145728 | tf_op jit(solution)/shard_map/all_to_all | solution.py:54
  49.0 8.6 %collective-permute-start.3 = (bf16[128,1152]{1,0:T(8,128)(2,1)S(1)}, bf16[128,1152]{1,0:T(8,128)(2,1)S(1)}, u32[]{:S(2)}, u32[]{:S(2)}) collective-permute-start(bf16[128,1152]{1,0:T(8,128)(2,1)S(1)} %maximum_select_fusion.2), channel_id=1, source_target_pairs={{0,64},{64,0},{1,65},{65,1},{2,66},{66,2},{3,67},{67,3},{4,68},{68... | collective-permute-start | bytes 884744 | tf_op jit(solution)/shard_map/ppermute | solution.py:61
  57.7 3.9 %collective-permute-start.4 = (bf16[256,1152]{1,0:T(8,128)(2,1)S(1)}, bf16[256,1152]{1,0:T(8,128)(2,1)S(1)}, u32[]{:S(2)}, u32[]{:S(2)}) collective-permute-start(bf16[256,1152]{1,0:T(8,128)(2,1)S(1)} %maximum_select_fusion.1), channel_id=1, source_target_pairs={{0,32},{32,0},{1,33},{33,1},{2,34},{34,2},{3,35},{35,3},{4,36},{36... | collective-permute-start | bytes 1769480 | tf_op jit(solution)/shard_map/ppermute | solution.py:61
  62.1 4.3 %copy-start.1 = (s32[4]{0:T(128)S(1)}, s32[4]{0:T(128)}, u32[]{:S(2)}) copy-start(s32[4]{0:T(128)} %pad_add_fusion.place_ref) | copy-start | bytes 52
  62.1 4.3 %copy-start.2 = (s32[1,8]{1,0:T(1,128)S(1)}, s32[1,8]{1,0:T(1,128)}, u32[]{:S(2)}) copy-start(s32[1,8]{1,0:T(1,128)} %param.13) | copy-start | bytes 100
  66.3 41.2 %copy-start = (bf16[512,1024]{1,0:T(8,128)(2,1)S(1)}, bf16[512,1024]{1,0:T(8,128)(2,1)}, u32[]{:S(2)}) copy-start(bf16[512,1024]{1,0:T(8,128)(2,1)} %w_ref.7) | copy-start | bytes 3145732
  78.2 5.5 %collective-permute-start.5 = (f32[16,128]{1,0:T(8,128)S(1)}, f32[16,128]{1,0:T(8,128)S(1)}, u32[]{:S(2)}, u32[]{:S(2)}) collective-permute-start(f32[16,128]{1,0:T(8,128)S(1)} %get-tuple-element.58.mine_ref), channel_id=1, source_target_pairs={{0,16},{16,0},{1,17},{17,1},{2,18},{18,2},{3,19},{19,3},{4,20},{20... | collective-permute-start | bytes 24584 | tf_op jit(solution)/shard_map/ppermute | solution.py:61
  84.5 23.0 %all-to-all-start.2 = ((f32[16,24,128]{2,1,0:T(8,128)}), f32[16,24,128]{2,1,0:T(8,128)S(1)}, u32[]{:S(2)}, u32[]{:S(2)}) async-start(f32[16,24,128]{2,1,0:T(8,128)} %plane.1), calls=%async_computation.2 | async-start | bytes 393216 | tf_op jit(solution)/shard_map/all_to_all | solution.py:587
  94.1 6.8 %collective-permute-start.6 = (bf16[512,128]{1,0:T(8,128)(2,1)S(1)}, bf16[512,128]{1,0:T(8,128)(2,1)S(1)}, u32[]{:S(2)}, u32[]{:S(2)}) collective-permute-start(bf16[512,128]{1,0:T(8,128)(2,1)S(1)} %get-tuple-element.60.spare_ref), channel_id=1, source_target_pairs={{0,16},{16,0},{1,17},{17,1},{2,18},{18,2},{3,19},{19,3},{4,20},{20... | collective-permute-start | bytes 393224 | tf_op jit(solution)/shard_map/ppermute | solution.py:61
  109.0 14.7 %all-to-all-start.3 = ((f32[16,8,128]{2,1,0:T(8,128)}), f32[16,8,128]{2,1,0:T(8,128)S(1)}, u32[]{:S(2)}, u32[]{:S(2)}) async-start(f32[16,8,128]{2,1,0:T(8,128)} %get-tuple-element.64), calls=%async_computation.3 | async-start | bytes 131072 | tf_op jit(solution)/shard_map/all_to_all | solution.py:600
  125.0 20.1 %all-to-all-start.4 = ((f32[16,16,128]{2,1,0:T(8,128)}), f32[16,16,128]{2,1,0:T(8,128)S(1)}, u32[]{:S(2)}, u32[]{:S(2)}) async-start(f32[16,16,128]{2,1,0:T(8,128)} %loss.1), calls=%async_computation.4 | async-start | bytes 262144 | tf_op jit(solution)/shard_map/all_to_all | solution.py:612
  138.7 1.0 copy-start.3
  146.4 18.7 %all-to-all-start.5 = ((f32[16,8,128]{2,1,0:T(8,128)}), f32[16,8,128]{2,1,0:T(8,128)S(1)}, u32[]{:S(2)}, u32[]{:S(2)}) async-start(f32[16,8,128]{2,1,0:T(8,128)} %get-tuple-element.78), calls=%async_computation.5 | async-start | bytes 131072 | tf_op jit(solution)/shard_map/all_to_all | solution.py:633
  153.1 13.5 %collective-permute-start.7 = (f32[16,128]{1,0:T(8,128)S(1)}, f32[16,128]{1,0:T(8,128)S(1)}, u32[]{:S(2)}, u32[]{:S(2)}) collective-permute-start(f32[16,128]{1,0:T(8,128)S(1)} %get-tuple-element.82.delta_ref.mine_ref), channel_id=1, source_target_pairs={{0,1},{1,0},{2,3},{3,2},{4,5},{5,4},{6,7},{7,6},{8,9},{9,8},{10,11... | collective-permute-start | bytes 24584 | tf_op jit(solution)/shard_map/ppermute | solution.py:61
  166.7 14.3 %all-to-all-start.7 = ((bf16[16,16,768]{2,1,0:T(8,128)(2,1)}), bf16[16,16,768]{2,1,0:T(8,128)(2,1)S(1)}, u32[]{:S(2)}, u32[]{:S(2)}) async-start(bf16[16,16,768]{2,1,0:T(8,128)(2,1)} %get-tuple-element.93), calls=%async_computation.7 | async-start | bytes 786432 | tf_op jit(solution)/shard_map/all_to_all | solution.py:652
  170.4 1.2 copy-start.4
  180.9 29.5 %all-to-all-start.6 = ((bf16[16,64,128]{2,1,0:T(8,128)(2,1)}), bf16[16,64,128]{2,1,0:T(8,128)(2,1)S(1)}, u32[]{:S(2)}, u32[]{:S(2)}) async-start(bf16[16,64,128]{2,1,0:T(8,128)(2,1)} %columns.1), calls=%async_computation.6 | async-start | bytes 524288 | tf_op jit(solution)/shard_map/all_to_all | solution.py:665

commit v11 on v9

--- a/solution.py
+++ b/solution.py
@@ -163,6 +163,9 @@
 
 KEYS = 4 * QUARTER
 SPARE = 512
+CHUNK = 512
+SHORT = 256
+TALL = 1024
 
 
 def fill(all_ref, x_ref):
@@ -190,21 +193,20 @@
     q_s[...] = own_queries(own_ref)
 
     def block(i, carry):
-        rows = pl.ds(pl.multiple_of(i * BLOCK, BLOCK), BLOCK)
+        rows = pl.ds(pl.multiple_of(i * SHORT, SHORT), SHORT)
         scores = lax.dot_general(q_s[rows, :], x_ref[...], NT, preferred_element_type=F32)
         top = jnp.max(scores, axis=1, keepdims=True)
         grown = jnp.exp(scores - top)
         total = jnp.sum(grown, axis=1, keepdims=True)
-        prob = (grown * (1.0 / total)).astype(BF16)
-        mixed = jnp.dot(prob, x_ref[...], preferred_element_type=F32).astype(BF16)
-        y_ref[rows, :] = jnp.where(lanes(BLOCK) < 64, q_s[rows, :], mixed)
+        mixed = jnp.dot(grown.astype(BF16), x_ref[...], preferred_element_type=F32)
+        y_ref[rows, :] = (mixed * (1.0 / total)).astype(BF16)
         log_total = top + jnp.log(total)
-        for part in range(PARTS):
+        for part in range(SHORT // 128):
             square = jnp.broadcast_to(log_total[part * 128 : (part + 1) * 128], (128, 128))
-            lse_ref[pl.ds(i * PARTS + part, 1), :] = jnp.transpose(square)[0:1, :]
+            lse_ref[pl.ds(i * (SHORT // 128) + part, 1), :] = jnp.transpose(square)[0:1, :]
         return carry
 
-    lax.fori_loop(0, QUARTER // BLOCK, block, 0)
+    lax.fori_loop(0, QUARTER // SHORT, block, 0)
     spare_ref[...] = jnp.concatenate(
         [y_ref[0:512, :][:, 64:128], y_ref[512:1024, :][:, 64:128]], axis=1
     )
@@ -428,10 +430,6 @@
     )
 
 
-CHUNK = 512
-TALL = 1024
-
-
 def row_kernel(
     place_ref, lens_ref, own_ref, all_ref, lse_ref, delta_ref, dattn_ref,
     out_ref, x_ref, q_s, d_s, delta_s, lse_s,

time: 214 us -> 210 us (0.981)
  Pallas kernels: 54.4 us -> 50.5 us
    pallas_call x15, Pallas kernels: 54.4 us -> 50.5 us  [call(): pl.pallas_call(kernel, out_shape=outs, in_specs=[SMEM] * len(scalars) + [...]
where the time goes in v11:
time: 210 us; the launch traced here: 209 us
  starting transfers between devices  92.5 us (44%)
  waiting for transfers between devices  59.2 us (28%)
  Pallas kernels  50.5 us (24%)
  local copies, waits for them, and re-layouts  4.32 us (2%)
    pallas_call x15, Pallas kernels, call(): pl.pallas_call(kernel, out_shape=outs, in_specs=[SMEM] * len(scalars) + [...  50.5 us
    ppermute x8, starting transfers between devices, swap(): return lax.ppermute(value, axes, [(i, i ^ flip) for i in range(count)])  29.2 us
    ppermute x8, waiting for transfers between devices, swap(): return lax.ppermute(value, axes, [(i, i ^ flip) for i in range(count)])  21.3 us
    all_to_all x1, starting transfers between devices, body(): own = exchange(packed, ZED)  14.8 us
    all_to_all x1, waiting for transfers between devices, body(): home = exchange(packed_grads, ZED)  14.2 us
    all_to_all x1, starting transfers between devices, body(): home = exchange(packed_grads, ZED)  11.1 us
    all_to_all x1, starting transfers between devices, body(): means = exchange(means, ZED)  9.62 us
    all_to_all x1, starting transfers between devices, body(): sums = exchange(sums, GRP)  7.03 us
  transfers between devices with their start and end apart: 16, of which 14 were waited for; matrix products, arithmetic and copies ran while one was open for 1% of the time, Pallas kernels for 16%

profile of v11, /device:TPU:64, one launch (start us, length us, event | category | flops | bytes accessed | tf_op | source)
XLA Modules:
  0.0 208.7 jit_solution(5532291620846335247)
XLA Ops:
  1.3 2.2 %pack.1 = bf16[16,112,128]{2,1,0:T(8,128)(2,1)} custom-call(s32[4]{0:T(128)} %pad_add_fusion.place_ref, s32[8]{0:T(128)} %bitcast.17, bf16[128,512]{1,0:T(8,128)(2,1)} %bitcast.26, bf16[128,512]{1,0:T(8,128)(2,1)} %bitcast.27, bf16[128,512]{1,0:T(8,128)(2,1)} %bitcast.28, bf16[128,1024]{1,0:T(8,128)(2,1)} %bitcast.25), custom_call_target="tpu_custom_call" | custom-call | bytes 1000000 | tf_op jit(solution)/shard_map/pack/pallas_call | solution.py:510
  3.4 14.8 %all-to-all-start = ((bf16[16,112,128]{2,1,0:T(8,128)(2,1)}), bf16[16,112,128]{2,1,0:T(8,128)(2,1)S(1)}, u32[]{:S(2)}, u32[]{:S(2)}) async-start(bf16[16,112,128]{2,1,0:T(8,128)(2,1)} %pack.1), calls=%async_computation | async-start | bytes 917504 | tf_op jit(solution)/shard_map/all_to_all | solution.py:546
  18.3 5.1 %collective-permute-start = (bf16[16,1152]{1,0:T(8,128)(2,1)S(1)}, bf16[16,1152]{1,0:T(8,128)(2,1)S(1)}, u32[]{:S(2)}, u32[]{:S(2)}) collective-permute-start(bf16[16,1152]{1,0:T(8,128)(2,1)S(1)} %pad_maximum_fusion), channel_id=1, source_target_pairs={{0,256},{256,0},{1,257},{257,1},{2,258},{258,2},{3,259},{259,3},{4... | collective-permute-start | bytes 110600 | tf_op jit(solution)/shard_map/ppermute | solution.py:59
  23.4 2.2 %collective-permute-done = bf16[16,1152]{1,0:T(8,128)(2,1)S(1)} collective-permute-done((bf16[16,1152]{1,0:T(8,128)(2,1)S(1)}, bf16[16,1152]{1,0:T(8,128)(2,1)S(1)}, u32[]{:S(2)}, u32[]{:S(2)}) %collective-permute-start) | collective-permute-done | bytes 36896 | tf_op jit(solution)/shard_map/ppermute | solution.py:59
  25.7 3.5 %collective-permute-start.1 = (bf16[32,1152]{1,0:T(8,128)(2,1)S(1)}, bf16[32,1152]{1,0:T(8,128)(2,1)S(1)}, u32[]{:S(2)}, u32[]{:S(2)}) collective-permute-start(bf16[32,1152]{1,0:T(8,128)(2,1)S(1)} %maximum_select_fusion.4), channel_id=1, source_target_pairs={{0,16},{16,0},{1,17},{17,1},{2,18},{18,2},{3,19},{19,3},{4,20},{20... | collective-permute-start | bytes 221192 | tf_op jit(solution)/shard_map/ppermute | solution.py:59
  29.2 2.7 %collective-permute-done.1 = bf16[32,1152]{1,0:T(8,128)(2,1)S(1)} collective-permute-done((bf16[32,1152]{1,0:T(8,128)(2,1)S(1)}, bf16[32,1152]{1,0:T(8,128)(2,1)S(1)}, u32[]{:S(2)}, u32[]{:S(2)}) %collective-permute-start.1) | collective-permute-done | bytes 73760 | tf_op jit(solution)/shard_map/ppermute | solution.py:59
  32.0 4.9 %collective-permute-start.2 = (bf16[64,1152]{1,0:T(8,128)(2,1)S(1)}, bf16[64,1152]{1,0:T(8,128)(2,1)S(1)}, u32[]{:S(2)}, u32[]{:S(2)}) collective-permute-start(bf16[64,1152]{1,0:T(8,128)(2,1)S(1)} %maximum_select_fusion.3), channel_id=1, source_target_pairs={{0,128},{128,0},{1,129},{129,1},{2,130},{130,2},{3,131},{131,3},{4... | collective-permute-start | bytes 442376 | tf_op jit(solution)/shard_map/ppermute | solution.py:59
  36.9 3.6 %collective-permute-done.2 = bf16[64,1152]{1,0:T(8,128)(2,1)S(1)} collective-permute-done((bf16[64,1152]{1,0:T(8,128)(2,1)S(1)}, bf16[64,1152]{1,0:T(8,128)(2,1)S(1)}, u32[]{:S(2)}, u32[]{:S(2)}) %collective-permute-start.2) | collective-permute-done | bytes 147488 | tf_op jit(solution)/shard_map/ppermute | solution.py:59
  40.6 2.7 %all-to-all-done.own_ref = bf16[16,112,128]{2,1,0:T(8,128)(2,1)S(1)} async-done(((bf16[16,112,128]{2,1,0:T(8,128)(2,1)}), bf16[16,112,128]{2,1,0:T(8,128)(2,1)S(1)}, u32[]{:S(2)}, u32[]{:S(2)}) %all-to-all-start) | async-done | bytes 458784 | tf_op jit(solution)/shard_map/all_to_all | solution.py:546
  44.6 4.3 %all-to-all-start.1 = ((bf16[4,16,96,128]{3,2,1,0:T(8,128)(2,1)}), bf16[4,16,96,128]{3,2,1,0:T(8,128)(2,1)}, u32[]{:S(2)}, u32[]{:S(2)}) async-start(bf16[4,16,96,128]{3,2,1,0:T(8,128)(2,1)} %broadcast_in_dim.22), calls=%async_computation.1 | async-start | bytes 3145728 | tf_op jit(solution)/shard_map/all_to_all | solution.py:52
  49.0 3.4 %collective-permute-start.3 = (bf16[128,1152]{1,0:T(8,128)(2,1)S(1)}, bf16[128,1152]{1,0:T(8,128)(2,1)S(1)}, u32[]{:S(2)}, u32[]{:S(2)}) collective-permute-start(bf16[128,1152]{1,0:T(8,128)(2,1)S(1)} %maximum_select_fusion.2), channel_id=1, source_target_pairs={{0,64},{64,0},{1,65},{65,1},{2,66},{66,2},{3,67},{67,3},{4,68},{68... | collective-permute-start | bytes 884744 | tf_op jit(solution)/shard_map/ppermute | solution.py:59
  52.4 5.2 %collective-permute-done.3 = bf16[128,1152]{1,0:T(8,128)(2,1)S(1)} collective-permute-done((bf16[128,1152]{1,0:T(8,128)(2,1)S(1)}, bf16[128,1152]{1,0:T(8,128)(2,1)S(1)}, u32[]{:S(2)}, u32[]{:S(2)}) %collective-permute-start.3) | collective-permute-done | bytes 294944 | tf_op jit(solution)/shard_map/ppermute | solution.py:59
  63.9 2.5 %all-to-all-done.1.all_ref = bf16[4,16,96,128]{3,2,1,0:T(8,128)(2,1)} async-done(((bf16[4,16,96,128]{3,2,1,0:T(8,128)(2,1)}), bf16[4,16,96,128]{3,2,1,0:T(8,128)(2,1)}, u32[]{:S(2)}, u32[]{:S(2)}) %all-to-all-start.1) | async-done | bytes 1572896 | tf_op jit(solution)/shard_map/all_to_all | solution.py:52
  66.3 9.2 %forward.1 = (bf16[512,128]{1,0:T(8,128)(2,1)S(1)}, f32[8,128]{1,0:T(8,128)S(1)}, f32[16,128]{1,0:T(8,128)S(1)}) custom-call(s32[4]{0:T(128)S(1)} %copy-done.1, s32[8]{0:T(128)S(1)} %bitcast.18, bf16[16,112,128]{2,1,0:T(8,128)(2,1)S(1)} %all-to-all-done.own_ref, bf16[4,16,96,128]{3,2,1,0:T(8,128)(2,1)} %all-to-all-done.1.all_ref), custom_call_target="tpu_custom_call" | custom-call | flops 4294967296 | bytes 3000000 | tf_op jit(solution)/shard_map/forward/pallas_call | solution.py:510
  75.5 3.5 %collective-permute-start.5 = (f32[16,128]{1,0:T(8,128)S(1)}, f32[16,128]{1,0:T(8,128)S(1)}, u32[]{:S(2)}, u32[]{:S(2)}) collective-permute-start(f32[16,128]{1,0:T(8,128)S(1)} %get-tuple-element.58.mine_ref), channel_id=1, source_target_pairs={{0,16},{16,0},{1,17},{17,1},{2,18},{18,2},{3,19},{19,3},{4,20},{20... | collective-permute-start | bytes 24584 | tf_op jit(solution)/shard_map/ppermute | solution.py:59
  79.0 2.1 collective-permute-done.5.other_ref
  81.7 9.6 %all-to-all-start.2 = ((f32[16,24,128]{2,1,0:T(8,128)}), f32[16,24,128]{2,1,0:T(8,128)S(1)}, u32[]{:S(2)}, u32[]{:S(2)}) async-start(f32[16,24,128]{2,1,0:T(8,128)} %plane.1), calls=%async_computation.2 | async-start | bytes 393216 | tf_op jit(solution)/shard_map/all_to_all | solution.py:578
  91.3 3.4 %collective-permute-start.6 = (bf16[512,128]{1,0:T(8,128)(2,1)S(1)}, bf16[512,128]{1,0:T(8,128)(2,1)S(1)}, u32[]{:S(2)}, u32[]{:S(2)}) collective-permute-start(bf16[512,128]{1,0:T(8,128)(2,1)S(1)} %get-tuple-element.60.spare_ref), channel_id=1, source_target_pairs={{0,16},{16,0},{1,17},{17,1},{2,18},{18,2},{3,19},{19,3},{4,20},{20... | collective-permute-start | bytes 393224 | tf_op jit(solution)/shard_map/ppermute | solution.py:59
  94.7 3.5 %collective-permute-done.6.other_ref = bf16[512,128]{1,0:T(8,128)(2,1)S(1)} collective-permute-done((bf16[512,128]{1,0:T(8,128)(2,1)S(1)}, bf16[512,128]{1,0:T(8,128)(2,1)S(1)}, u32[]{:S(2)}, u32[]{:S(2)}) %collective-permute-start.6) | collective-permute-done | bytes 131104 | tf_op jit(solution)/shard_map/ppermute | solution.py:59
  98.2 6.6 %all-to-all-done.2.means_ref = f32[16,24,128]{2,1,0:T(8,128)S(1)} async-done(((f32[16,24,128]{2,1,0:T(8,128)}), f32[16,24,128]{2,1,0:T(8,128)S(1)}, u32[]{:S(2)}, u32[]{:S(2)}) %all-to-all-start.2) | async-done | bytes 196640 | tf_op jit(solution)/shard_map/all_to_all | solution.py:578
  106.2 7.0 %all-to-all-start.3 = ((f32[16,8,128]{2,1,0:T(8,128)}), f32[16,8,128]{2,1,0:T(8,128)S(1)}, u32[]{:S(2)}, u32[]{:S(2)}) async-start(f32[16,8,128]{2,1,0:T(8,128)} %get-tuple-element.64), calls=%async_computation.3 | async-start | bytes 131072 | tf_op jit(solution)/shard_map/all_to_all | solution.py:591
  114.9 5.9 %all-to-all-done.3.sums_ref = f32[16,8,128]{2,1,0:T(8,128)S(1)} async-done(((f32[16,8,128]{2,1,0:T(8,128)}), f32[16,8,128]{2,1,0:T(8,128)S(1)}, u32[]{:S(2)}, u32[]{:S(2)}) %all-to-all-start.3) | async-done | bytes 65568 | tf_op jit(solution)/shard_map/all_to_all | solution.py:591
  122.2 6.0 %all-to-all-start.4 = ((f32[16,16,128]{2,1,0:T(8,128)}), f32[16,16,128]{2,1,0:T(8,128)S(1)}, u32[]{:S(2)}, u32[]{:S(2)}) async-start(f32[16,16,128]{2,1,0:T(8,128)} %loss.1), calls=%async_computation.4 | async-start | bytes 262144 | tf_op jit(solution)/shard_map/all_to_all | solution.py:603
  128.2 7.8 %mass.1 = (f32[8,8,128]{2,1,0:T(8,128)S(1)}, f32[8,4096]{1,0:T(8,128)S(1)}, bf16[4096,128]{1,0:T(8,128)(2,1)S(1)}) custom-call(s32[4]{0:T(128)S(1)} %copy-done.1, s32[8]{0:T(128)S(1)} %bitcast.19, bf16[16,112,128]{2,1,0:T(8,128)(2,1)S(1)} %all-to-all-done.own_ref, bf16[4,16,96,128]{3,2,1,0:T(8,128)(2,1)} %all-to-all-done.1.all_ref, ...), custom_call_target="tpu_custom_call" | custom-call | flops 4294967296 | bytes 2500000 | tf_op jit(solution)/shard_map/mass/pallas_call | solution.py:510
  136.9 5.4 %all-to-all-done.4.terms_ref = f32[16,16,128]{2,1,0:T(8,128)S(1)} async-done(((f32[16,16,128]{2,1,0:T(8,128)}), f32[16,16,128]{2,1,0:T(8,128)S(1)}, u32[]{:S(2)}, u32[]{:S(2)}) %all-to-all-start.4) | async-done | bytes 131104 | tf_op jit(solution)/shard_map/all_to_all | solution.py:603
  143.7 6.7 %all-to-all-start.5 = ((f32[16,8,128]{2,1,0:T(8,128)}), f32[16,8,128]{2,1,0:T(8,128)S(1)}, u32[]{:S(2)}, u32[]{:S(2)}) async-start(f32[16,8,128]{2,1,0:T(8,128)} %get-tuple-element.78), calls=%async_computation.5 | async-start | bytes 131072 | tf_op jit(solution)/shard_map/all_to_all | solution.py:624
  150.4 3.5 %collective-permute-start.7 = (f32[16,128]{1,0:T(8,128)S(1)}, f32[16,128]{1,0:T(8,128)S(1)}, u32[]{:S(2)}, u32[]{:S(2)}) collective-permute-start(f32[16,128]{1,0:T(8,128)S(1)} %get-tuple-element.82.delta_ref.mine_ref), channel_id=1, source_target_pairs={{0,1},{1,0},{2,3},{3,2},{4,5},{5,4},{6,7},{7,6},{8,9},{9,8},{10,11... | collective-permute-start | bytes 24584 | tf_op jit(solution)/shard_map/ppermute | solution.py:59
  153.9 8.6 %rows.1.grad_q_ref = bf16[1024,128]{1,0:T(8,128)(2,1)S(1)} custom-call(s32[4]{0:T(128)S(1)} %copy-done.1, s32[8]{0:T(128)S(1)} %bitcast.21, bf16[16,112,128]{2,1,0:T(8,128)(2,1)S(1)} %all-to-all-done.own_ref, bf16[4,16,96,128]{3,2,1,0:T(8,128)(2,1)} %all-to-all-done.1.all_ref, f32[8,128]{1,0:T(8,128)S(1)} %get-tuple-element.83.lse_ref, ...), custom_call_target="tpu_custom_call" | custom-call | flops 6442450944 | bytes 2000000 | tf_op jit(solution)/shard_map/rows/pallas_call | solution.py:510
  164.1 3.8 %all-to-all-start.7 = ((bf16[16,16,768]{2,1,0:T(8,128)(2,1)}), bf16[16,16,768]{2,1,0:T(8,128)(2,1)S(1)}, u32[]{:S(2)}, u32[]{:S(2)}) async-start(bf16[16,16,768]{2,1,0:T(8,128)(2,1)} %get-tuple-element.93), calls=%async_computation.7 | async-start | bytes 786432 | tf_op jit(solution)/shard_map/all_to_all | solution.py:643
  169.1 8.5 %columns.1 = bf16[16,64,128]{2,1,0:T(8,128)(2,1)} custom-call(s32[4]{0:T(128)S(1)} %copy-done.1, s32[8]{0:T(128)S(1)} %bitcast.23, bf16[16,112,128]{2,1,0:T(8,128)(2,1)S(1)} %all-to-all-done.own_ref, bf16[4096,128]{1,0:T(8,128)(2,1)S(1)} %copy-done.4, f32[16,128]{1,0:T(8,128)S(1)} %get-tuple-element.82.delta_ref.mine_ref, ...), custom_call_target="tpu_custom_call" | custom-call | flops 6442450944 | bytes 2500000 | tf_op jit(solution)/shard_map/columns/pallas_call | solution.py:510
  178.3 11.1 %all-to-all-start.6 = ((bf16[16,64,128]{2,1,0:T(8,128)(2,1)}), bf16[16,64,128]{2,1,0:T(8,128)(2,1)S(1)}, u32[]{:S(2)}, u32[]{:S(2)}) async-start(bf16[16,64,128]{2,1,0:T(8,128)(2,1)} %columns.1), calls=%async_computation.6 | async-start | bytes 524288 | tf_op jit(solution)/shard_map/all_to_all | solution.py:656
  193.6 14.2 %all-to-all-done.6.in_ref = bf16[16,64,128]{2,1,0:T(8,128)(2,1)S(1)} async-done(((bf16[16,64,128]{2,1,0:T(8,128)(2,1)}), bf16[16,64,128]{2,1,0:T(8,128)(2,1)S(1)}, u32[]{:S(2)}, u32[]{:S(2)}) %all-to-all-start.6) | async-done | bytes 262176 | tf_op jit(solution)/shard_map/all_to_all | solution.py:656
  (42 shorter events, 24.5 us)
Async XLA Ops:
  0.6 17.7 %copy-start.5 = (bf16[16,1024]{1,0:T(8,128)(2,1)S(1)}, bf16[16,1024]{1,0:T(8,128)(2,1)}, u32[]{:S(2)}) copy-start(bf16[16,1024]{1,0:T(8,128)(2,1)} %param.14) | copy-start | bytes 98308
  0.6 17.5 %copy-start.6 = (s32[16]{0:T(128)S(1)}, s32[16]{0:T(128)}, u32[]{:S(2)}) copy-start(s32[16]{0:T(128)} %param.15) | copy-start | bytes 196
  3.4 39.8 %all-to-all-start = ((bf16[16,112,128]{2,1,0:T(8,128)(2,1)}), bf16[16,112,128]{2,1,0:T(8,128)(2,1)S(1)}, u32[]{:S(2)}, u32[]{:S(2)}) async-start(bf16[16,112,128]{2,1,0:T(8,128)(2,1)} %pack.1), calls=%async_computation | async-start | bytes 917504 | tf_op jit(solution)/shard_map/all_to_all | solution.py:546
  18.3 7.4 %collective-permute-start = (bf16[16,1152]{1,0:T(8,128)(2,1)S(1)}, bf16[16,1152]{1,0:T(8,128)(2,1)S(1)}, u32[]{:S(2)}, u32[]{:S(2)}) collective-permute-start(bf16[16,1152]{1,0:T(8,128)(2,1)S(1)} %pad_maximum_fusion), channel_id=1, source_target_pairs={{0,256},{256,0},{1,257},{257,1},{2,258},{258,2},{3,259},{259,3},{4... | collective-permute-start | bytes 110600 | tf_op jit(solution)/shard_map/ppermute | solution.py:59
  25.7 6.2 %collective-permute-start.1 = (bf16[32,1152]{1,0:T(8,128)(2,1)S(1)}, bf16[32,1152]{1,0:T(8,128)(2,1)S(1)}, u32[]{:S(2)}, u32[]{:S(2)}) collective-permute-start(bf16[32,1152]{1,0:T(8,128)(2,1)S(1)} %maximum_select_fusion.4), channel_id=1, source_target_pairs={{0,16},{16,0},{1,17},{17,1},{2,18},{18,2},{3,19},{19,3},{4,20},{20... | collective-permute-start | bytes 221192 | tf_op jit(solution)/shard_map/ppermute | solution.py:59
  32.0 8.5 %collective-permute-start.2 = (bf16[64,1152]{1,0:T(8,128)(2,1)S(1)}, bf16[64,1152]{1,0:T(8,128)(2,1)S(1)}, u32[]{:S(2)}, u32[]{:S(2)}) collective-permute-start(bf16[64,1152]{1,0:T(8,128)(2,1)S(1)} %maximum_select_fusion.3), channel_id=1, source_target_pairs={{0,128},{128,0},{1,129},{129,1},{2,130},{130,2},{3,131},{131,3},{4... | collective-permute-start | bytes 442376 | tf_op jit(solution)/shard_map/ppermute | solution.py:59
  44.6 21.7 %all-to-all-start.1 = ((bf16[4,16,96,128]{3,2,1,0:T(8,128)(2,1)}), bf16[4,16,96,128]{3,2,1,0:T(8,128)(2,1)}, u32[]{:S(2)}, u32[]{:S(2)}) async-start(bf16[4,16,96,128]{3,2,1,0:T(8,128)(2,1)} %broadcast_in_dim.22), calls=%async_computation.1 | async-start | bytes 3145728 | tf_op jit(solution)/shard_map/all_to_all | solution.py:52
  49.0 8.6 %collective-permute-start.3 = (bf16[128,1152]{1,0:T(8,128)(2,1)S(1)}, bf16[128,1152]{1,0:T(8,128)(2,1)S(1)}, u32[]{:S(2)}, u32[]{:S(2)}) collective-permute-start(bf16[128,1152]{1,0:T(8,128)(2,1)S(1)} %maximum_select_fusion.2), channel_id=1, source_target_pairs={{0,64},{64,0},{1,65},{65,1},{2,66},{66,2},{3,67},{67,3},{4,68},{68... | collective-permute-start | bytes 884744 | tf_op jit(solution)/shard_map/ppermute | solution.py:59
  57.7 3.9 %collective-permute-start.4 = (bf16[256,1152]{1,0:T(8,128)(2,1)S(1)}, bf16[256,1152]{1,0:T(8,128)(2,1)S(1)}, u32[]{:S(2)}, u32[]{:S(2)}) collective-permute-start(bf16[256,1152]{1,0:T(8,128)(2,1)S(1)} %maximum_select_fusion.1), channel_id=1, source_target_pairs={{0,32},{32,0},{1,33},{33,1},{2,34},{34,2},{3,35},{35,3},{4,36},{36... | collective-permute-start | bytes 1769480 | tf_op jit(solution)/shard_map/ppermute | solution.py:59
  62.1 4.3 %copy-start.1 = (s32[4]{0:T(128)S(1)}, s32[4]{0:T(128)}, u32[]{:S(2)}) copy-start(s32[4]{0:T(128)} %pad_add_fusion.place_ref) | copy-start | bytes 52
  62.1 4.3 %copy-start.2 = (s32[1,8]{1,0:T(1,128)S(1)}, s32[1,8]{1,0:T(1,128)}, u32[]{:S(2)}) copy-start(s32[1,8]{1,0:T(1,128)} %param.13) | copy-start | bytes 100
  66.3 38.4 %copy-start = (bf16[512,1024]{1,0:T(8,128)(2,1)S(1)}, bf16[512,1024]{1,0:T(8,128)(2,1)}, u32[]{:S(2)}) copy-start(bf16[512,1024]{1,0:T(8,128)(2,1)} %w_ref.7) | copy-start | bytes 3145732
  75.5 5.5 %collective-permute-start.5 = (f32[16,128]{1,0:T(8,128)S(1)}, f32[16,128]{1,0:T(8,128)S(1)}, u32[]{:S(2)}, u32[]{:S(2)}) collective-permute-start(f32[16,128]{1,0:T(8,128)S(1)} %get-tuple-element.58.mine_ref), channel_id=1, source_target_pairs={{0,16},{16,0},{1,17},{17,1},{2,18},{18,2},{3,19},{19,3},{4,20},{20... | collective-permute-start | bytes 24584 | tf_op jit(solution)/shard_map/ppermute | solution.py:59
  81.7 23.0 %all-to-all-start.2 = ((f32[16,24,128]{2,1,0:T(8,128)}), f32[16,24,128]{2,1,0:T(8,128)S(1)}, u32[]{:S(2)}, u32[]{:S(2)}) async-start(f32[16,24,128]{2,1,0:T(8,128)} %plane.1), calls=%async_computation.2 | async-start | bytes 393216 | tf_op jit(solution)/shard_map/all_to_all | solution.py:578
  91.3 6.8 %collective-permute-start.6 = (bf16[512,128]{1,0:T(8,128)(2,1)S(1)}, bf16[512,128]{1,0:T(8,128)(2,1)S(1)}, u32[]{:S(2)}, u32[]{:S(2)}) collective-permute-start(bf16[512,128]{1,0:T(8,128)(2,1)S(1)} %get-tuple-element.60.spare_ref), channel_id=1, source_target_pairs={{0,16},{16,0},{1,17},{17,1},{2,18},{18,2},{3,19},{19,3},{4,20},{20... | collective-permute-start | bytes 393224 | tf_op jit(solution)/shard_map/ppermute | solution.py:59
  106.2 14.7 %all-to-all-start.3 = ((f32[16,8,128]{2,1,0:T(8,128)}), f32[16,8,128]{2,1,0:T(8,128)S(1)}, u32[]{:S(2)}, u32[]{:S(2)}) async-start(f32[16,8,128]{2,1,0:T(8,128)} %get-tuple-element.64), calls=%async_computation.3 | async-start | bytes 131072 | tf_op jit(solution)/shard_map/all_to_all | solution.py:591
  122.2 20.1 %all-to-all-start.4 = ((f32[16,16,128]{2,1,0:T(8,128)}), f32[16,16,128]{2,1,0:T(8,128)S(1)}, u32[]{:S(2)}, u32[]{:S(2)}) async-start(f32[16,16,128]{2,1,0:T(8,128)} %loss.1), calls=%async_computation.4 | async-start | bytes 262144 | tf_op jit(solution)/shard_map/all_to_all | solution.py:603
  135.9 1.0 copy-start.3
  143.7 18.8 %all-to-all-start.5 = ((f32[16,8,128]{2,1,0:T(8,128)}), f32[16,8,128]{2,1,0:T(8,128)S(1)}, u32[]{:S(2)}, u32[]{:S(2)}) async-start(f32[16,8,128]{2,1,0:T(8,128)} %get-tuple-element.78), calls=%async_computation.5 | async-start | bytes 131072 | tf_op jit(solution)/shard_map/all_to_all | solution.py:624
  150.4 13.7 %collective-permute-start.7 = (f32[16,128]{1,0:T(8,128)S(1)}, f32[16,128]{1,0:T(8,128)S(1)}, u32[]{:S(2)}, u32[]{:S(2)}) collective-permute-start(f32[16,128]{1,0:T(8,128)S(1)} %get-tuple-element.82.delta_ref.mine_ref), channel_id=1, source_target_pairs={{0,1},{1,0},{2,3},{3,2},{4,5},{5,4},{6,7},{7,6},{8,9},{9,8},{10,11... | collective-permute-start | bytes 24584 | tf_op jit(solution)/shard_map/ppermute | solution.py:59
  164.1 14.3 %all-to-all-start.7 = ((bf16[16,16,768]{2,1,0:T(8,128)(2,1)}), bf16[16,16,768]{2,1,0:T(8,128)(2,1)S(1)}, u32[]{:S(2)}, u32[]{:S(2)}) async-start(bf16[16,16,768]{2,1,0:T(8,128)(2,1)} %get-tuple-element.93), calls=%async_computation.7 | async-start | bytes 786432 | tf_op jit(solution)/shard_map/all_to_all | solution.py:643
  167.9 1.2 copy-start.4
  178.3 29.5 %all-to-all-start.6 = ((bf16[16,64,128]{2,1,0:T(8,128)(2,1)}), bf16[16,64,128]{2,1,0:T(8,128)(2,1)S(1)}, u32[]{:S(2)}, u32[]{:S(2)}) async-start(bf16[16,64,128]{2,1,0:T(8,128)(2,1)} %columns.1), calls=%async_computation.6 | async-start | bytes 524288 | tf_op jit(solution)/shard_map/all_to_all | solution.py:656

commit v12 on v11

--- a/solution.py
+++ b/solution.py
@@ -548,11 +548,7 @@
     own, queries = barrier((own, queries))
     keys = share(own[:, 0:96, :], SQUARE)
     queries = gather(queries, ("xb", "co"))
-    query_rows = call(
-        query_kernel, shape((16, HELD), F32), (), (queries,), (), cost(6 * 2 * 8 * HELD * 1024, 1200000),
-        "queries",
-    )
-    own, keys, queries, query_rows = barrier((own, keys, queries, query_rows))
+    own, keys, queries = barrier((own, keys, queries))
 
     spare, lse, means = call(
         forward_kernel,
@@ -574,10 +570,14 @@
         plane_kernel, shape((PLANE, 3 * GROUPS, 128), F32), (), (means, other_means), (),
         cost(0, 200000), "plane",
     )
-    spare, means = barrier((spare, means))
+    spare, means, queries = barrier((spare, means, queries))
     means = exchange(means, ZED)
     other_spare = swap(spare, ("yl",), 1)
-    means, other_spare = barrier((means, other_spare))
+    query_rows = call(
+        query_kernel, shape((16, HELD), F32), (), (queries,), (), cost(6 * 2 * 8 * HELD * 1024, 1200000),
+        "queries",
+    )
+    means, other_spare, query_rows = barrier((means, other_spare, query_rows))
     pooled_own, doc_means, logits, sums = call(
         pool_kernel,
         (

time: 210 us -> 210 us (level)
  no operation moved by 1% of the time
where the time goes in v12:
time: 210 us; the launch traced here: 209 us
  starting transfers between devices  92.6 us (44%)
  waiting for transfers between devices  59.2 us (28%)
  Pallas kernels  50.4 us (24%)
  local copies, waits for them, and re-layouts  4.32 us (2%)
    pallas_call x15, Pallas kernels, call(): pl.pallas_call(kernel, out_shape=outs, in_specs=[SMEM] * len(scalars) + [...  50.4 us
    ppermute x8, starting transfers between devices, swap(): return lax.ppermute(value, axes, [(i, i ^ flip) for i in range(count)])  29.3 us
    ppermute x8, waiting for transfers between devices, swap(): return lax.ppermute(value, axes, [(i, i ^ flip) for i in range(count)])  19.5 us
    all_to_all x1, starting transfers between devices, body(): own = exchange(packed, ZED)  14.8 us
    all_to_all x1, waiting for transfers between devices, body(): home = exchange(packed_grads, ZED)  14.2 us
    all_to_all x1, starting transfers between devices, body(): home = exchange(packed_grads, ZED)  11.1 us
    all_to_all x1, starting transfers between devices, body(): means = exchange(means, ZED)  9.64 us
    all_to_all x1, starting transfers between devices, body(): sums = exchange(sums, GRP)  7.03 us
  transfers between devices with their start and end apart: 16, of which 14 were waited for; matrix products, arithmetic and copies ran while one was open for 1% of the time, Pallas kernels for 16%

profile of v12, /device:TPU:64, one launch (start us, length us, event | category | flops | bytes accessed | tf_op | source)
XLA Modules:
  0.0 208.7 jit_solution(979135039248721050)
XLA Ops:
  1.3 2.2 %pack.1 = bf16[16,112,128]{2,1,0:T(8,128)(2,1)} custom-call(s32[4]{0:T(128)} %pad_add_fusion.place_ref, s32[8]{0:T(128)} %bitcast.17, bf16[128,512]{1,0:T(8,128)(2,1)} %bitcast.26, bf16[128,512]{1,0:T(8,128)(2,1)} %bitcast.27, bf16[128,512]{1,0:T(8,128)(2,1)} %bitcast.28, bf16[128,1024]{1,0:T(8,128)(2,1)} %bitcast.25), custom_call_target="tpu_custom_call" | custom-call | bytes 1000000 | tf_op jit(solution)/shard_map/pack/pallas_call | solution.py:510
  3.4 14.8 %all-to-all-start = ((bf16[16,112,128]{2,1,0:T(8,128)(2,1)}), bf16[16,112,128]{2,1,0:T(8,128)(2,1)S(1)}, u32[]{:S(2)}, u32[]{:S(2)}) async-start(bf16[16,112,128]{2,1,0:T(8,128)(2,1)} %pack.1), calls=%async_computation | async-start | bytes 917504 | tf_op jit(solution)/shard_map/all_to_all | solution.py:546
  18.3 5.1 %collective-permute-start = (bf16[16,1152]{1,0:T(8,128)(2,1)S(1)}, bf16[16,1152]{1,0:T(8,128)(2,1)S(1)}, u32[]{:S(2)}, u32[]{:S(2)}) collective-permute-start(bf16[16,1152]{1,0:T(8,128)(2,1)S(1)} %pad_maximum_fusion), channel_id=1, source_target_pairs={{0,256},{256,0},{1,257},{257,1},{2,258},{258,2},{3,259},{259,3},{4... | collective-permute-start | bytes 110600 | tf_op jit(solution)/shard_map/ppermute | solution.py:59
  23.4 2.2 %collective-permute-done = bf16[16,1152]{1,0:T(8,128)(2,1)S(1)} collective-permute-done((bf16[16,1152]{1,0:T(8,128)(2,1)S(1)}, bf16[16,1152]{1,0:T(8,128)(2,1)S(1)}, u32[]{:S(2)}, u32[]{:S(2)}) %collective-permute-start) | collective-permute-done | bytes 36896 | tf_op jit(solution)/shard_map/ppermute | solution.py:59
  25.7 3.5 %collective-permute-start.1 = (bf16[32,1152]{1,0:T(8,128)(2,1)S(1)}, bf16[32,1152]{1,0:T(8,128)(2,1)S(1)}, u32[]{:S(2)}, u32[]{:S(2)}) collective-permute-start(bf16[32,1152]{1,0:T(8,128)(2,1)S(1)} %maximum_select_fusion.4), channel_id=1, source_target_pairs={{0,16},{16,0},{1,17},{17,1},{2,18},{18,2},{3,19},{19,3},{4,20},{20... | collective-permute-start | bytes 221192 | tf_op jit(solution)/shard_map/ppermute | solution.py:59
  29.2 2.7 %collective-permute-done.1 = bf16[32,1152]{1,0:T(8,128)(2,1)S(1)} collective-permute-done((bf16[32,1152]{1,0:T(8,128)(2,1)S(1)}, bf16[32,1152]{1,0:T(8,128)(2,1)S(1)}, u32[]{:S(2)}, u32[]{:S(2)}) %collective-permute-start.1) | collective-permute-done | bytes 73760 | tf_op jit(solution)/shard_map/ppermute | solution.py:59
  32.0 4.9 %collective-permute-start.2 = (bf16[64,1152]{1,0:T(8,128)(2,1)S(1)}, bf16[64,1152]{1,0:T(8,128)(2,1)S(1)}, u32[]{:S(2)}, u32[]{:S(2)}) collective-permute-start(bf16[64,1152]{1,0:T(8,128)(2,1)S(1)} %maximum_select_fusion.3), channel_id=1, source_target_pairs={{0,128},{128,0},{1,129},{129,1},{2,130},{130,2},{3,131},{131,3},{4... | collective-permute-start | bytes 442376 | tf_op jit(solution)/shard_map/ppermute | solution.py:59
  36.9 3.6 %collective-permute-done.2 = bf16[64,1152]{1,0:T(8,128)(2,1)S(1)} collective-permute-done((bf16[64,1152]{1,0:T(8,128)(2,1)S(1)}, bf16[64,1152]{1,0:T(8,128)(2,1)S(1)}, u32[]{:S(2)}, u32[]{:S(2)}) %collective-permute-start.2) | collective-permute-done | bytes 147488 | tf_op jit(solution)/shard_map/ppermute | solution.py:59
  40.6 2.7 %all-to-all-done.own_ref = bf16[16,112,128]{2,1,0:T(8,128)(2,1)S(1)} async-done(((bf16[16,112,128]{2,1,0:T(8,128)(2,1)}), bf16[16,112,128]{2,1,0:T(8,128)(2,1)S(1)}, u32[]{:S(2)}, u32[]{:S(2)}) %all-to-all-start) | async-done | bytes 458784 | tf_op jit(solution)/shard_map/all_to_all | solution.py:546
  44.6 4.3 %all-to-all-start.1 = ((bf16[4,16,96,128]{3,2,1,0:T(8,128)(2,1)}), bf16[4,16,96,128]{3,2,1,0:T(8,128)(2,1)}, u32[]{:S(2)}, u32[]{:S(2)}) async-start(bf16[4,16,96,128]{3,2,1,0:T(8,128)(2,1)} %broadcast_in_dim.22), calls=%async_computation.1 | async-start | bytes 3145728 | tf_op jit(solution)/shard_map/all_to_all | solution.py:52
  49.0 3.4 %collective-permute-start.3 = (bf16[128,1152]{1,0:T(8,128)(2,1)S(1)}, bf16[128,1152]{1,0:T(8,128)(2,1)S(1)}, u32[]{:S(2)}, u32[]{:S(2)}) collective-permute-start(bf16[128,1152]{1,0:T(8,128)(2,1)S(1)} %maximum_select_fusion.2), channel_id=1, source_target_pairs={{0,64},{64,0},{1,65},{65,1},{2,66},{66,2},{3,67},{67,3},{4,68},{68... | collective-permute-start | bytes 884744 | tf_op jit(solution)/shard_map/ppermute | solution.py:59
  52.4 5.2 %collective-permute-done.3 = bf16[128,1152]{1,0:T(8,128)(2,1)S(1)} collective-permute-done((bf16[128,1152]{1,0:T(8,128)(2,1)S(1)}, bf16[128,1152]{1,0:T(8,128)(2,1)S(1)}, u32[]{:S(2)}, u32[]{:S(2)}) %collective-permute-start.3) | collective-permute-done | bytes 294944 | tf_op jit(solution)/shard_map/ppermute | solution.py:59
  59.7 1.9 collective-permute-done.4
  62.1 4.2 %all-to-all-done.1.all_ref = bf16[4,16,96,128]{3,2,1,0:T(8,128)(2,1)} async-done(((bf16[4,16,96,128]{3,2,1,0:T(8,128)(2,1)}), bf16[4,16,96,128]{3,2,1,0:T(8,128)(2,1)}, u32[]{:S(2)}, u32[]{:S(2)}) %all-to-all-start.1) | async-done | bytes 1572896 | tf_op jit(solution)/shard_map/all_to_all | solution.py:52
  66.3 9.1 %forward.1 = (bf16[512,128]{1,0:T(8,128)(2,1)S(1)}, f32[8,128]{1,0:T(8,128)S(1)}, f32[16,128]{1,0:T(8,128)S(1)}) custom-call(s32[4]{0:T(128)S(1)} %copy-done.1, s32[8]{0:T(128)S(1)} %bitcast.18, bf16[16,112,128]{2,1,0:T(8,128)(2,1)S(1)} %all-to-all-done.own_ref, bf16[4,16,96,128]{3,2,1,0:T(8,128)(2,1)} %all-to-all-done.1.all_ref), custom_call_target="tpu_custom_call" | custom-call | flops 4294967296 | bytes 3000000 | tf_op jit(solution)/shard_map/forward/pallas_call | solution.py:510
  75.4 3.6 %collective-permute-start.5 = (f32[16,128]{1,0:T(8,128)S(1)}, f32[16,128]{1,0:T(8,128)S(1)}, u32[]{:S(2)}, u32[]{:S(2)}) collective-permute-start(f32[16,128]{1,0:T(8,128)S(1)} %get-tuple-element.59.mine_ref), channel_id=1, source_target_pairs={{0,16},{16,0},{1,17},{17,1},{2,18},{18,2},{3,19},{19,3},{4,20},{20... | collective-permute-start | bytes 24584 | tf_op jit(solution)/shard_map/ppermute | solution.py:59
  79.0 2.1 collective-permute-done.5.other_ref
  81.8 9.6 %all-to-all-start.2 = ((f32[16,24,128]{2,1,0:T(8,128)}), f32[16,24,128]{2,1,0:T(8,128)S(1)}, u32[]{:S(2)}, u32[]{:S(2)}) async-start(f32[16,24,128]{2,1,0:T(8,128)} %plane.1), calls=%async_computation.2 | async-start | bytes 393216 | tf_op jit(solution)/shard_map/all_to_all | solution.py:574
  91.4 3.4 %collective-permute-start.6 = (bf16[512,128]{1,0:T(8,128)(2,1)S(1)}, bf16[512,128]{1,0:T(8,128)(2,1)S(1)}, u32[]{:S(2)}, u32[]{:S(2)}) collective-permute-start(bf16[512,128]{1,0:T(8,128)(2,1)S(1)} %get-tuple-element.62.spare_ref), channel_id=1, source_target_pairs={{0,16},{16,0},{1,17},{17,1},{2,18},{18,2},{3,19},{19,3},{4,20},{20... | collective-permute-start | bytes 393224 | tf_op jit(solution)/shard_map/ppermute | solution.py:59
  98.3 6.6 %all-to-all-done.2.means_ref = f32[16,24,128]{2,1,0:T(8,128)S(1)} async-done(((f32[16,24,128]{2,1,0:T(8,128)}), f32[16,24,128]{2,1,0:T(8,128)S(1)}, u32[]{:S(2)}, u32[]{:S(2)}) %all-to-all-start.2) | async-done | bytes 196640 | tf_op jit(solution)/shard_map/all_to_all | solution.py:574
  106.3 7.0 %all-to-all-start.3 = ((f32[16,8,128]{2,1,0:T(8,128)}), f32[16,8,128]{2,1,0:T(8,128)S(1)}, u32[]{:S(2)}, u32[]{:S(2)}) async-start(f32[16,8,128]{2,1,0:T(8,128)} %get-tuple-element.66), calls=%async_computation.3 | async-start | bytes 131072 | tf_op jit(solution)/shard_map/all_to_all | solution.py:591
  115.0 5.9 %all-to-all-done.3.sums_ref = f32[16,8,128]{2,1,0:T(8,128)S(1)} async-done(((f32[16,8,128]{2,1,0:T(8,128)}), f32[16,8,128]{2,1,0:T(8,128)S(1)}, u32[]{:S(2)}, u32[]{:S(2)}) %all-to-all-start.3) | async-done | bytes 65568 | tf_op jit(solution)/shard_map/all_to_all | solution.py:591
  122.3 6.0 %all-to-all-start.4 = ((f32[16,16,128]{2,1,0:T(8,128)}), f32[16,16,128]{2,1,0:T(8,128)S(1)}, u32[]{:S(2)}, u32[]{:S(2)}) async-start(f32[16,16,128]{2,1,0:T(8,128)} %loss.1), calls=%async_computation.4 | async-start | bytes 262144 | tf_op jit(solution)/shard_map/all_to_all | solution.py:603
  128.2 7.8 %mass.1 = (f32[8,8,128]{2,1,0:T(8,128)S(1)}, f32[8,4096]{1,0:T(8,128)S(1)}, bf16[4096,128]{1,0:T(8,128)(2,1)S(1)}) custom-call(s32[4]{0:T(128)S(1)} %copy-done.1, s32[8]{0:T(128)S(1)} %bitcast.19, bf16[16,112,128]{2,1,0:T(8,128)(2,1)S(1)} %all-to-all-done.own_ref, bf16[4,16,96,128]{3,2,1,0:T(8,128)(2,1)} %all-to-all-done.1.all_ref, ...), custom_call_target="tpu_custom_call" | custom-call | flops 4294967296 | bytes 2500000 | tf_op jit(solution)/shard_map/mass/pallas_call | solution.py:510
  137.0 5.4 %all-to-all-done.4.terms_ref = f32[16,16,128]{2,1,0:T(8,128)S(1)} async-done(((f32[16,16,128]{2,1,0:T(8,128)}), f32[16,16,128]{2,1,0:T(8,128)S(1)}, u32[]{:S(2)}, u32[]{:S(2)}) %all-to-all-start.4) | async-done | bytes 131104 | tf_op jit(solution)/shard_map/all_to_all | solution.py:603
  143.7 6.7 %all-to-all-start.5 = ((f32[16,8,128]{2,1,0:T(8,128)}), f32[16,8,128]{2,1,0:T(8,128)S(1)}, u32[]{:S(2)}, u32[]{:S(2)}) async-start(f32[16,8,128]{2,1,0:T(8,128)} %get-tuple-element.80), calls=%async_computation.5 | async-start | bytes 131072 | tf_op jit(solution)/shard_map/all_to_all | solution.py:624
  150.4 3.5 %collective-permute-start.7 = (f32[16,128]{1,0:T(8,128)S(1)}, f32[16,128]{1,0:T(8,128)S(1)}, u32[]{:S(2)}, u32[]{:S(2)}) collective-permute-start(f32[16,128]{1,0:T(8,128)S(1)} %get-tuple-element.84.delta_ref.mine_ref), channel_id=1, source_target_pairs={{0,1},{1,0},{2,3},{3,2},{4,5},{5,4},{6,7},{7,6},{8,9},{9,8},{10,11... | collective-permute-start | bytes 24584 | tf_op jit(solution)/shard_map/ppermute | solution.py:59
  154.0 8.6 %rows.1.grad_q_ref = bf16[1024,128]{1,0:T(8,128)(2,1)S(1)} custom-call(s32[4]{0:T(128)S(1)} %copy-done.1, s32[8]{0:T(128)S(1)} %bitcast.21, bf16[16,112,128]{2,1,0:T(8,128)(2,1)S(1)} %all-to-all-done.own_ref, bf16[4,16,96,128]{3,2,1,0:T(8,128)(2,1)} %all-to-all-done.1.all_ref, f32[8,128]{1,0:T(8,128)S(1)} %get-tuple-element.85.lse_ref, ...), custom_call_target="tpu_custom_call" | custom-call | flops 6442450944 | bytes 2000000 | tf_op jit(solution)/shard_map/rows/pallas_call | solution.py:510
  164.1 3.8 %all-to-all-start.7 = ((bf16[16,16,768]{2,1,0:T(8,128)(2,1)}), bf16[16,16,768]{2,1,0:T(8,128)(2,1)S(1)}, u32[]{:S(2)}, u32[]{:S(2)}) async-start(bf16[16,16,768]{2,1,0:T(8,128)(2,1)} %get-tuple-element.95), calls=%async_computation.7 | async-start | bytes 786432 | tf_op jit(solution)/shard_map/all_to_all | solution.py:643
  169.1 8.5 %columns.1 = bf16[16,64,128]{2,1,0:T(8,128)(2,1)} custom-call(s32[4]{0:T(128)S(1)} %copy-done.1, s32[8]{0:T(128)S(1)} %bitcast.23, bf16[16,112,128]{2,1,0:T(8,128)(2,1)S(1)} %all-to-all-done.own_ref, bf16[4096,128]{1,0:T(8,128)(2,1)S(1)} %copy-done.4, f32[16,128]{1,0:T(8,128)S(1)} %get-tuple-element.84.delta_ref.mine_ref, ...), custom_call_target="tpu_custom_call" | custom-call | flops 6442450944 | bytes 2500000 | tf_op jit(solution)/shard_map/columns/pallas_call | solution.py:510
  178.4 11.1 %all-to-all-start.6 = ((bf16[16,64,128]{2,1,0:T(8,128)(2,1)}), bf16[16,64,128]{2,1,0:T(8,128)(2,1)S(1)}, u32[]{:S(2)}, u32[]{:S(2)}) async-start(bf16[16,64,128]{2,1,0:T(8,128)(2,1)} %columns.1), calls=%async_computation.6 | async-start | bytes 524288 | tf_op jit(solution)/shard_map/all_to_all | solution.py:656
  193.7 14.2 %all-to-all-done.6.in_ref = bf16[16,64,128]{2,1,0:T(8,128)(2,1)S(1)} async-done(((bf16[16,64,128]{2,1,0:T(8,128)(2,1)}), bf16[16,64,128]{2,1,0:T(8,128)(2,1)S(1)}, u32[]{:S(2)}, u32[]{:S(2)}) %all-to-all-start.6) | async-done | bytes 262176 | tf_op jit(solution)/shard_map/all_to_all | solution.py:656
  (42 shorter events, 24.3 us)
Async XLA Ops:
  0.6 17.7 %copy-start.5 = (bf16[16,1024]{1,0:T(8,128)(2,1)S(1)}, bf16[16,1024]{1,0:T(8,128)(2,1)}, u32[]{:S(2)}) copy-start(bf16[16,1024]{1,0:T(8,128)(2,1)} %param.14) | copy-start | bytes 98308
  0.6 17.5 %copy-start.6 = (s32[16]{0:T(128)S(1)}, s32[16]{0:T(128)}, u32[]{:S(2)}) copy-start(s32[16]{0:T(128)} %param.15) | copy-start | bytes 196
  3.4 39.8 %all-to-all-start = ((bf16[16,112,128]{2,1,0:T(8,128)(2,1)}), bf16[16,112,128]{2,1,0:T(8,128)(2,1)S(1)}, u32[]{:S(2)}, u32[]{:S(2)}) async-start(bf16[16,112,128]{2,1,0:T(8,128)(2,1)} %pack.1), calls=%async_computation | async-start | bytes 917504 | tf_op jit(solution)/shard_map/all_to_all | solution.py:546
  18.3 7.4 %collective-permute-start = (bf16[16,1152]{1,0:T(8,128)(2,1)S(1)}, bf16[16,1152]{1,0:T(8,128)(2,1)S(1)}, u32[]{:S(2)}, u32[]{:S(2)}) collective-permute-start(bf16[16,1152]{1,0:T(8,128)(2,1)S(1)} %pad_maximum_fusion), channel_id=1, source_target_pairs={{0,256},{256,0},{1,257},{257,1},{2,258},{258,2},{3,259},{259,3},{4... | collective-permute-start | bytes 110600 | tf_op jit(solution)/shard_map/ppermute | solution.py:59
  25.7 6.2 %collective-permute-start.1 = (bf16[32,1152]{1,0:T(8,128)(2,1)S(1)}, bf16[32,1152]{1,0:T(8,128)(2,1)S(1)}, u32[]{:S(2)}, u32[]{:S(2)}) collective-permute-start(bf16[32,1152]{1,0:T(8,128)(2,1)S(1)} %maximum_select_fusion.4), channel_id=1, source_target_pairs={{0,16},{16,0},{1,17},{17,1},{2,18},{18,2},{3,19},{19,3},{4,20},{20... | collective-permute-start | bytes 221192 | tf_op jit(solution)/shard_map/ppermute | solution.py:59
  32.0 8.5 %collective-permute-start.2 = (bf16[64,1152]{1,0:T(8,128)(2,1)S(1)}, bf16[64,1152]{1,0:T(8,128)(2,1)S(1)}, u32[]{:S(2)}, u32[]{:S(2)}) collective-permute-start(bf16[64,1152]{1,0:T(8,128)(2,1)S(1)} %maximum_select_fusion.3), channel_id=1, source_target_pairs={{0,128},{128,0},{1,129},{129,1},{2,130},{130,2},{3,131},{131,3},{4... | collective-permute-start | bytes 442376 | tf_op jit(solution)/shard_map/ppermute | solution.py:59
  44.6 21.7 %all-to-all-start.1 = ((bf16[4,16,96,128]{3,2,1,0:T(8,128)(2,1)}), bf16[4,16,96,128]{3,2,1,0:T(8,128)(2,1)}, u32[]{:S(2)}, u32[]{:S(2)}) async-start(bf16[4,16,96,128]{3,2,1,0:T(8,128)(2,1)} %broadcast_in_dim.22), calls=%async_computation.1 | async-start | bytes 3145728 | tf_op jit(solution)/shard_map/all_to_all | solution.py:52
  49.0 8.6 %collective-permute-start.3 = (bf16[128,1152]{1,0:T(8,128)(2,1)S(1)}, bf16[128,1152]{1,0:T(8,128)(2,1)S(1)}, u32[]{:S(2)}, u32[]{:S(2)}) collective-permute-start(bf16[128,1152]{1,0:T(8,128)(2,1)S(1)} %maximum_select_fusion.2), channel_id=1, source_target_pairs={{0,64},{64,0},{1,65},{65,1},{2,66},{66,2},{3,67},{67,3},{4,68},{68... | collective-permute-start | bytes 884744 | tf_op jit(solution)/shard_map/ppermute | solution.py:59
  57.7 3.9 %collective-permute-start.4 = (bf16[256,1152]{1,0:T(8,128)(2,1)S(1)}, bf16[256,1152]{1,0:T(8,128)(2,1)S(1)}, u32[]{:S(2)}, u32[]{:S(2)}) collective-permute-start(bf16[256,1152]{1,0:T(8,128)(2,1)S(1)} %maximum_select_fusion.1), channel_id=1, source_target_pairs={{0,32},{32,0},{1,33},{33,1},{2,34},{34,2},{3,35},{35,3},{4,36},{36... | collective-permute-start | bytes 1769480 | tf_op jit(solution)/shard_map/ppermute | solution.py:59
  59.7 6.7 %copy-start.1 = (s32[4]{0:T(128)S(1)}, s32[4]{0:T(128)}, u32[]{:S(2)}) copy-start(s32[4]{0:T(128)} %pad_add_fusion.place_ref) | copy-start | bytes 52
  59.7 6.7 %copy-start.2 = (s32[1,8]{1,0:T(1,128)S(1)}, s32[1,8]{1,0:T(1,128)}, u32[]{:S(2)}) copy-start(s32[1,8]{1,0:T(1,128)} %param.13) | copy-start | bytes 100
  75.4 29.4 %copy-start = (bf16[512,1024]{1,0:T(8,128)(2,1)S(1)}, bf16[512,1024]{1,0:T(8,128)(2,1)}, u32[]{:S(2)}) copy-start(bf16[512,1024]{1,0:T(8,128)(2,1)} %w_ref.7) | copy-start | bytes 3145732
  75.4 5.7 %collective-permute-start.5 = (f32[16,128]{1,0:T(8,128)S(1)}, f32[16,128]{1,0:T(8,128)S(1)}, u32[]{:S(2)}, u32[]{:S(2)}) collective-permute-start(f32[16,128]{1,0:T(8,128)S(1)} %get-tuple-element.59.mine_ref), channel_id=1, source_target_pairs={{0,16},{16,0},{1,17},{17,1},{2,18},{18,2},{3,19},{19,3},{4,20},{20... | collective-permute-start | bytes 24584 | tf_op jit(solution)/shard_map/ppermute | solution.py:59
  81.8 23.1 %all-to-all-start.2 = ((f32[16,24,128]{2,1,0:T(8,128)}), f32[16,24,128]{2,1,0:T(8,128)S(1)}, u32[]{:S(2)}, u32[]{:S(2)}) async-start(f32[16,24,128]{2,1,0:T(8,128)} %plane.1), calls=%async_computation.2 | async-start | bytes 393216 | tf_op jit(solution)/shard_map/all_to_all | solution.py:574
  91.4 6.8 %collective-permute-start.6 = (bf16[512,128]{1,0:T(8,128)(2,1)S(1)}, bf16[512,128]{1,0:T(8,128)(2,1)S(1)}, u32[]{:S(2)}, u32[]{:S(2)}) collective-permute-start(bf16[512,128]{1,0:T(8,128)(2,1)S(1)} %get-tuple-element.62.spare_ref), channel_id=1, source_target_pairs={{0,16},{16,0},{1,17},{17,1},{2,18},{18,2},{3,19},{19,3},{4,20},{20... | collective-permute-start | bytes 393224 | tf_op jit(solution)/shard_map/ppermute | solution.py:59
  106.3 14.7 %all-to-all-start.3 = ((f32[16,8,128]{2,1,0:T(8,128)}), f32[16,8,128]{2,1,0:T(8,128)S(1)}, u32[]{:S(2)}, u32[]{:S(2)}) async-start(f32[16,8,128]{2,1,0:T(8,128)} %get-tuple-element.66), calls=%async_computation.3 | async-start | bytes 131072 | tf_op jit(solution)/shard_map/all_to_all | solution.py:591
  122.3 20.1 %all-to-all-start.4 = ((f32[16,16,128]{2,1,0:T(8,128)}), f32[16,16,128]{2,1,0:T(8,128)S(1)}, u32[]{:S(2)}, u32[]{:S(2)}) async-start(f32[16,16,128]{2,1,0:T(8,128)} %loss.1), calls=%async_computation.4 | async-start | bytes 262144 | tf_op jit(solution)/shard_map/all_to_all | solution.py:603
  136.0 1.0 copy-start.3
  143.7 18.8 %all-to-all-start.5 = ((f32[16,8,128]{2,1,0:T(8,128)}), f32[16,8,128]{2,1,0:T(8,128)S(1)}, u32[]{:S(2)}, u32[]{:S(2)}) async-start(f32[16,8,128]{2,1,0:T(8,128)} %get-tuple-element.80), calls=%async_computation.5 | async-start | bytes 131072 | tf_op jit(solution)/shard_map/all_to_all | solution.py:624
  150.4 13.7 %collective-permute-start.7 = (f32[16,128]{1,0:T(8,128)S(1)}, f32[16,128]{1,0:T(8,128)S(1)}, u32[]{:S(2)}, u32[]{:S(2)}) collective-permute-start(f32[16,128]{1,0:T(8,128)S(1)} %get-tuple-element.84.delta_ref.mine_ref), channel_id=1, source_target_pairs={{0,1},{1,0},{2,3},{3,2},{4,5},{5,4},{6,7},{7,6},{8,9},{9,8},{10,11... | collective-permute-start | bytes 24584 | tf_op jit(solution)/shard_map/ppermute | solution.py:59
  164.1 14.3 %all-to-all-start.7 = ((bf16[16,16,768]{2,1,0:T(8,128)(2,1)}), bf16[16,16,768]{2,1,0:T(8,128)(2,1)S(1)}, u32[]{:S(2)}, u32[]{:S(2)}) async-start(bf16[16,16,768]{2,1,0:T(8,128)(2,1)} %get-tuple-element.95), calls=%async_computation.7 | async-start | bytes 786432 | tf_op jit(solution)/shard_map/all_to_all | solution.py:643
  167.9 1.2 copy-start.4
  178.4 29.5 %all-to-all-start.6 = ((bf16[16,64,128]{2,1,0:T(8,128)(2,1)}), bf16[16,64,128]{2,1,0:T(8,128)(2,1)S(1)}, u32[]{:S(2)}, u32[]{:S(2)}) async-start(bf16[16,64,128]{2,1,0:T(8,128)(2,1)} %columns.1), calls=%async_computation.6 | async-start | bytes 524288 | tf_op jit(solution)/shard_map/all_to_all | solution.py:656
